TPU v7x, 256 devices: a whole 4x4x8 slice. The times are simulated.
256 devices in a mesh: ctx: 32 (over z, y_lo, core), head: 8 (over x, y_hi).
Axes of the slice: x: 4, y: 4 (y_hi: 2, y_lo: 2; y = y_hi * 2 + y_lo), z: 8, core: 2. Of those that a mesh axis runs over, the one named last changes fastest.
Arguments:
- queries: bfloat16 [16384, 4096], P('ctx', 'head'), may hold values from -180 to 180
- keys_values: bfloat16 [2, 16384, 1024], P(None, 'ctx', 'head'), may hold values from -6 to 6
- trace_lengths: int32 [7], replicated, may hold values from 1 to 4096, as said below
- step_rows: int32 [7, 32], replicated, may hold values from 0 to 16383, as said below
- prompt_ids: int32 [7], replicated, may hold values from 0 to 1
- cluster_ids: int32 [7], replicated, may hold values from 0 to 3
- step_stream: bfloat16 [224, 8192], P(None, 'ctx'), may hold values from -0.29882812 to 0.29882812
- out_weight: bfloat16 [4096, 8192], P('head', 'ctx'), may hold values from -3.59375 to 3.59375
- score_weight: bfloat16 [8192, 8192], P('ctx', 'head'), may hold values from -0.0625 to 0.0625
- class_weight: bfloat16 [8192, 2], P('head'), may hold values from -0.125 to 0.125
Outputs:
- attended: float32 [16384, 4096], P('ctx', 'head')
- step_scores: float32 [7, 32], replicated
- votes: float32 [2, 4], replicated
Inputs may be any that keep to these rules, and one draw needn't show every extreme that they name: `trace_lengths`: the traces lie end to end from row 0 and fill the context; one trace has exactly 4096 rows. `step_rows`: each trace's step rows lie inside that trace and rise strictly; the last one is the trace's last row.
All inputs are finite; a program needn't handle non-finite values.
Results may differ from a plain program's by a relative error of at most 0.033.
Values may be sent and summed in bfloat16 or wider, within the bound.
No kernel may reach another device: no remote copies, remote signals or barrier semaphores. Data moves between devices by JAX's collectives and lax.ppermute only.
A program may use at most 64 MiB of HBM per device.

v0:
```python
import functools
import math

import jax
import jax.numpy as jnp
from jax import lax
from jax.experimental import pallas as pl
from jax.experimental.pallas import tpu as pltpu
from jax.sharding import PartitionSpec as P

HD = 128
PROMPTS = 2
CLUSTERS = 4
TRACES = 7
STEPS = 32
PER_GROUP = 4
BLOCK = 512
TILE = 256
Z = 8
PLANE = 4
PAD = 8
GROUP = Z * PAD
WIDE = 1024
COEF = HD**-0.5 * math.log2(math.e)
LOW = -1e30
NONE = -60000.0
VMEM = pl.BlockSpec(memory_space=pltpu.VMEM)
SMEM = pl.BlockSpec(memory_space=pltpu.SMEM)
HBM = pl.BlockSpec(memory_space=pltpu.HBM)
BF16 = jnp.bfloat16
F32 = jnp.float32


def first_key(row, lengths):
    start = row * 0
    end = jnp.int32(0)
    for t in range(TRACES):
        end = end + lengths[t]
        start = jnp.where(row >= end, end, start)
    return start


def pick_kernel(me_ref, steps_hbm, q_hbm, keep_ref, pass_ref, send_ref, all_ref, steps_ref, q_ref, sems):
    steps_copy = pltpu.make_async_copy(steps_hbm, steps_ref, sems.at[0])
    q_copy = pltpu.make_async_copy(q_hbm, q_ref, sems.at[1])
    steps_copy.start()
    q_copy.start()
    steps_copy.wait()
    q_copy.wait()
    me = me_ref[0]
    core, side = me % 2, (me // 2) % 2
    at = lax.broadcasted_iota(jnp.int32, (TRACES, BLOCK), 1) + me * BLOCK
    none = jnp.zeros((PAD - TRACES, BLOCK), F32)
    steps = steps_ref[...]
    for c in range(2):
        for y in range(2):
            parts = []
            for z in range(Z):
                step = PLANE * z + 2 * y + c
                parts.append(jnp.where(steps[:, step : step + 1] == at, 1.0, 0.0))
                parts.append(none)
            chosen = jnp.concatenate(parts, axis=0).astype(BF16)
            got = jnp.dot(chosen, q_ref[...], preferred_element_type=F32)
            all_ref[pl.ds((2 * c + y) * GROUP, GROUP), :] = got.astype(BF16)

    def group(c, y):
        return all_ref[pl.ds(pl.multiple_of((2 * c + y) * GROUP, GROUP), GROUP), :]

    keep_ref[...] = group(core, side)
    pass_ref[...] = group(core, 1 - side)
    send_ref[:GROUP] = group(1 - core, side)
    send_ref[GROUP:] = group(1 - core, 1 - side)


def picked_kernel(me_ref, lengths_hbm, steps_hbm, q_ref, q1_ref, q2_ref, *refs):
    kv_refs, out_ref = refs[:PLANE], refs[PLANE]
    kv_s, lengths, steps_ref, sems = refs[-4:]
    lengths_copy = pltpu.make_async_copy(lengths_hbm, lengths, sems.at[PLANE])
    steps_copy = pltpu.make_async_copy(steps_hbm, steps_ref, sems.at[PLANE + 1])
    copies = [
        pltpu.make_async_copy(kv, kv_s.at[k], sems.at[k]) for k, kv in enumerate(kv_refs)
    ]
    for copy in [lengths_copy, steps_copy] + copies:
        copy.start()
    lengths_copy.wait()
    steps_copy.wait()
    me = me_ref[0]
    place = me % PLANE
    steps = steps_ref[...]
    lane = lax.broadcasted_iota(jnp.int32, (TRACES, STEPS), 1)
    none = jnp.full((PAD - TRACES, HD), -1, jnp.int32)
    parts = []
    for z in range(Z):
        mine = jnp.where(lane == PLANE * z + place, steps, 0)
        mine = jnp.sum(mine, axis=1, keepdims=True)
        parts.append(jnp.broadcast_to(mine, (TRACES, HD)))
        parts.append(none)
    row = jnp.concatenate(parts, axis=0)
    start = first_key(row, lengths)
    row = jnp.concatenate([row] * (BLOCK // HD), axis=1)
    start = jnp.concatenate([start] * (BLOCK // HD), axis=1)
    k_pos = lax.broadcasted_iota(jnp.int32, (GROUP, BLOCK), 1)
    q = (q_ref[...].astype(F32) + q1_ref[...].astype(F32) + q2_ref[...].astype(F32)).astype(BF16)
    q = jnp.concatenate([q[:, h * HD : (h + 1) * HD] for h in range(PER_GROUP)], axis=0)
    scores = []
    for k in range(PLANE):
        key0 = (me - place + (place ^ k)) * BLOCK
        mask = (k_pos <= row - key0) & (k_pos >= start - key0)
        mask = jnp.concatenate([mask] * PER_GROUP, axis=0)
        copies[k].wait()
        s = lax.dot_general(
            q, kv_s[k, 0], (((1,), (1,)), ((), ())), preferred_element_type=F32
        )
        scores.append(jnp.where(mask, s, LOW))
    top = jnp.maximum(jnp.maximum(scores[0], scores[1]), jnp.maximum(scores[2], scores[3]))
    top = jnp.maximum(jnp.max(top, axis=1, keepdims=True), 0.1 * LOW)
    ones = jnp.ones((BLOCK, HD), BF16)
    pv = jnp.zeros((PER_GROUP * GROUP, 2 * HD), F32)
    for k, s in enumerate(scores):
        p = jnp.exp2((s - top) * COEF).astype(BF16)
        ext = jnp.concatenate([kv_s[k, 1], ones], axis=1)
        pv = pv + jnp.dot(p, ext, preferred_element_type=F32)
    total = pv[:, HD:]
    some = total > 0.0
    total = jnp.where(some, total, 1.0)
    value = pv[:, :HD] / total
    size = jnp.where(some, top * COEF + jnp.log2(total), NONE)
    lanes = lax.broadcasted_iota(jnp.int32, (GROUP, HD), 1)
    stats = jnp.zeros((GROUP, HD), F32)
    for h in range(PER_GROUP):
        rows = slice(h * GROUP, (h + 1) * GROUP)
        out_ref[:, h * HD : (h + 1) * HD] = value[rows]
        rest = size[rows]
        for k in range(3):
            coarse = rest.astype(BF16).astype(F32)
            stats = jnp.where(lanes == PER_GROUP * k + h, coarse, stats)
            rest = rest - coarse
    for z in range(Z):
        packed = jnp.zeros((1, HD), F32)
        for t in range(TRACES):
            at = z * PAD + t
            packed = packed + pltpu.roll(stats[at : at + 1], 16 * t, 1)
        out_ref[z * PAD + TRACES : (z + 1) * PAD, :HD] = packed


def attend_kernel(slots, first, last, *refs):
    n = len(slots)
    arrays = 1 + max(slot[2] for slot in slots)
    me_ref, lengths_hbm, q_hbm = refs[:3]
    kv_hbm = [refs[3 + array].at[pl.ds(2 * at, 2)] for _, _, array, at in slots]
    if last:
        out_hbm = refs[-9]
    else:
        acc_hbm, ml_hbm = refs[-10:-8]
    if not first:
        acc_in, ml_in = refs[3 + arrays : 5 + arrays]
    q_ref, kv_ref, acc_ref, m_ref, l_ref, ml_ref, lengths, sems = refs[-8:]
    lengths_copy = pltpu.make_async_copy(lengths_hbm, lengths, sems.at[0])
    lengths_copy.start()
    lengths_copy.wait()
    me = me_ref[0]
    place = me % PLANE
    row0 = me * BLOCK
    ones = jnp.ones((BLOCK, HD), BF16)
    blocks = [me - place - back * PLANE + (place ^ flip) for back, flip, _, _ in slots]
    earliest = first_key(row0, lengths)
    active = [(block < me) & ((block + 1) * BLOCK > earliest) for block in blocks]

    def copy_in(source, target, k):
        return pltpu.make_async_copy(source, target, sems.at[k])

    def weigh(rows, count, keys, ext, mask, fresh):
        q = q_ref[rows, :]
        q = jnp.concatenate([q[:, h * HD : (h + 1) * HD] for h in range(PER_GROUP)], axis=0)
        s = lax.dot_general(q, keys, (((1,), (1,)), ((), ())), preferred_element_type=F32)
        for h in range(PER_GROUP):
            cols = slice(h * HD, (h + 1) * HD)
            mine = s[h * count : (h + 1) * count]
            if mask is not None:
                mine = jnp.where(mask, mine, LOW)
            top = jnp.max(mine, axis=1, keepdims=True)
            if fresh:
                top = jnp.broadcast_to(top, (count, HD))
            else:
                before = m_ref[rows, cols]
                top = jnp.maximum(before, top)
            wide = jnp.concatenate([top] * (mine.shape[1] // HD), axis=1)
            p = jnp.exp2((mine - wide) * COEF).astype(BF16)
            pv = jnp.dot(p, ext, preferred_element_type=F32)
            m_ref[rows, cols] = top
            if fresh:
                acc_ref[rows, cols] = pv[:, :HD]
                l_ref[rows, cols] = pv[:, HD:]
            else:
                scale = jnp.exp2((before - top) * COEF)
                acc_ref[rows, cols] = acc_ref[rows, cols] * scale + pv[:, :HD]
                l_ref[rows, cols] = l_ref[rows, cols] * scale + pv[:, HD:]

    def own_block(kv):
        for tile in range(BLOCK // TILE):
            width = (tile + 1) * TILE
            rows = slice(tile * TILE, width)
            keys = kv[0, :width, :]
            ext = jnp.concatenate([kv[1, :width, :], ones[:width]], axis=1)
            q_pos = row0 + tile * TILE + lax.broadcasted_iota(jnp.int32, (TILE, width), 0)
            k_pos = row0 + lax.broadcasted_iota(jnp.int32, (TILE, width), 1)
            starts = first_key(
                row0 + tile * TILE + lax.broadcasted_iota(jnp.int32, (TILE, HD), 0), lengths
            )
            starts = jnp.concatenate([starts] * (width // HD), axis=1)
            mask = (k_pos <= q_pos) & (k_pos >= starts)
            weigh(rows, TILE, keys, ext, mask, True)

    def other_tile(index, carry):
        tile, k = index % (BLOCK // TILE), index // (BLOCK // TILE)
        block = blocks[-1]
        for other in range(n - 1):
            block = jnp.where(k == other, blocks[other], block)
        key0 = block * BLOCK
        begin = pl.multiple_of(tile * TILE, TILE)
        rows = pl.ds(begin, TILE)
        low = first_key(row0 + begin, lengths)
        high = first_key(row0 + begin + TILE - 1, lengths)
        some = (block < me) & (key0 + BLOCK > low)
        every = key0 >= high

        def run(masked):
            keys = kv_ref[k, 0]
            ext = jnp.concatenate([kv_ref[k, 1], ones], axis=1)
            mask = None
            if masked:
                starts = first_key(
                    row0 + begin + lax.broadcasted_iota(jnp.int32, (TILE, HD), 0), lengths
                )
                starts = jnp.concatenate([starts] * (BLOCK // HD), axis=1)
                k_pos = key0 + lax.broadcasted_iota(jnp.int32, (TILE, BLOCK), 1)
                mask = k_pos >= starts
            weigh(rows, TILE, keys, ext, mask, False)

        pl.when(some & every)(functools.partial(run, False))
        pl.when(some & jnp.logical_not(every))(functools.partial(run, True))
        return carry

    def load_state():
        copies = [copy_in(acc_in, acc_ref, n), copy_in(ml_in, ml_ref, n + 1)]
        for copy in copies:
            copy.start()
        return copies

    def spread_state(copies):
        for copy in copies:
            copy.wait()
        for h in range(PER_GROUP):
            cols = slice(h * HD, (h + 1) * HD)
            m_ref[:, cols] = jnp.broadcast_to(ml_ref[:, h : h + 1], (BLOCK, HD))
            at = PER_GROUP + h
            l_ref[:, cols] = jnp.broadcast_to(ml_ref[:, at : at + 1], (BLOCK, HD))

    def store_state():
        lanes = lax.broadcasted_iota(jnp.int32, (BLOCK, HD), 1)
        ml = jnp.zeros((BLOCK, HD), F32)
        for h in range(PER_GROUP):
            cols = slice(h * HD, (h + 1) * HD)
            ml = jnp.where(lanes == h, m_ref[:, cols], ml)
            ml = jnp.where(lanes == PER_GROUP + h, l_ref[:, cols], ml)
        ml_ref[...] = ml
        copies = [copy_in(acc_ref, acc_hbm, n), copy_in(ml_ref, ml_hbm, n + 1)]
        for copy in copies:
            copy.start()
        for copy in copies:
            copy.wait()

    def work(loaded):
        q_copy = copy_in(q_hbm, q_ref, n + 2)
        q_copy.start()
        copies = [copy_in(kv, kv_ref.at[k], k) for k, kv in enumerate(kv_hbm)]
        for copy in copies:
            copy.start()
        if loaded:
            spread_state(loaded)
        q_copy.wait()
        for copy in copies:
            copy.wait()
        if first:
            own_block(kv_ref.at[0])
        lax.fori_loop((BLOCK // TILE) * int(first), (BLOCK // TILE) * n, other_tile, 0)

    some = functools.reduce(jnp.logical_or, active)
    if first:
        work(None)
        store_state()
    elif last:
        loaded = load_state()

        @pl.when(some)
        def _():
            work(loaded)

        @pl.when(jnp.logical_not(some))
        def _():
            spread_state(loaded)

        acc_ref[...] = acc_ref[...] / l_ref[...]
        copy = copy_in(acc_ref, out_hbm, n)
        copy.start()
        copy.wait()
    else:

        @pl.when(some)
        def _():
            work(load_state())
            store_state()


def attend(slots, me, lengths, queries, kvs, state, last=False):
    heads = pltpu.HBM((BLOCK, PER_GROUP * HD), F32)
    sizes = pltpu.HBM((BLOCK, HD), F32)
    operands = [me, *pinned([lengths, queries]), *kvs]
    aliases = {}
    if state is not None:
        if not last:
            aliases = {len(operands): 0, len(operands) + 1: 1}
        operands += pinned(state)
    shapes = (heads,) if last else (heads, sizes)
    work = PER_GROUP * BLOCK * BLOCK * len(slots)
    got = pl.pallas_call(
        functools.partial(attend_kernel, slots, state is None, last),
        out_shape=shapes,
        in_specs=[SMEM] + [HBM] * (len(operands) - 1),
        out_specs=[HBM] * len(shapes),
        scratch_shapes=[
            pltpu.VMEM((BLOCK, PER_GROUP * HD), BF16),
            pltpu.VMEM((len(slots), 2, BLOCK, HD), BF16),
            pltpu.VMEM((BLOCK, PER_GROUP * HD), F32),
            pltpu.VMEM((BLOCK, PER_GROUP * HD), F32),
            pltpu.VMEM((BLOCK, PER_GROUP * HD), F32),
            pltpu.VMEM((BLOCK, HD), F32),
            pltpu.SMEM((TRACES,), jnp.int32),
            pltpu.SemaphoreType.DMA((len(slots) + 3,)),
        ],
        input_output_aliases=aliases,
        compiler_params=pltpu.CompilerParams(vmem_limit_bytes=32 << 20),
        cost_estimate=pl.CostEstimate(
            flops=4 * HD * work, bytes_accessed=4 << 20, transcendentals=work
        ),
        name="attend_%d_%d" % slots[0][:2],
    )(*operands)
    return got[0] if last else got


def pinned(values):
    return [pltpu.with_memory_space_constraint(value, pltpu.HBM) for value in values]


def small_call(kernel, shape, operands, specs=None, **kw):
    return pl.pallas_call(
        kernel,
        out_shape=shape,
        in_specs=specs or [VMEM] * len(operands),
        out_specs=jax.tree.map(lambda _: VMEM, shape),
        compiler_params=pltpu.CompilerParams(vmem_limit_bytes=24 << 20),
        **kw,
    )(*operands)


def project_kernel(got_ref, *refs):
    packs, out_ref, weight_s, sems = refs[:PLANE], refs[PLANE], refs[-2], refs[-1]
    copies = [
        pltpu.make_async_copy(pack, weight_s.at[k], sems.at[k])
        for k, pack in enumerate(packs)
    ]
    for copy in copies:
        copy.start()
    sizes = []
    for z in range(Z):
        stats = []
        for step in range(Z):
            packed = got_ref[z, step * PAD + TRACES : (step + 1) * PAD, :HD]
            for t in range(PAD):
                stats.append(pltpu.roll(packed, (HD - 16 * t) % HD, 1))
        sizes.append(jnp.concatenate(stats, axis=0))
    sizes = [
        size
        + pltpu.roll(size, HD - PER_GROUP, 1)
        + pltpu.roll(size, HD - 2 * PER_GROUP, 1)
        for size in sizes
    ]
    top = functools.reduce(jnp.maximum, sizes)
    weights = [jnp.exp2(size - top) for size in sizes]
    total = functools.reduce(jnp.add, weights)
    weights = [weight / total for weight in weights]
    slot = lax.broadcasted_iota(jnp.int32, (GROUP, HD), 0)
    picked = []
    for h in range(PER_GROUP):
        joined = jnp.zeros((GROUP, HD), F32)
        for z in range(Z):
            joined = joined + got_ref[z, :, h * HD : (h + 1) * HD] * weights[z][:, h : h + 1]
        joined = jnp.where((slot & (PAD - 1)) < TRACES, joined, 0.0)
        picked.append(joined.astype(BF16))
    picked = jnp.concatenate(picked, axis=1)
    for k in range(PLANE):
        copies[k].wait()
        part = jnp.dot(picked, weight_s[k], preferred_element_type=F32)
        out_ref[:, k * 256 : (k + 1) * 256] = part


def inner_kernel(me_ref, total_ref, *refs):
    packs, out_ref, pack_s, sems = refs[:PLANE], refs[PLANE], refs[-2], refs[-1]
    copies = [
        pltpu.make_async_copy(pack, pack_s.at[k], sems.at[k])
        for k, pack in enumerate(packs)
    ]
    for copy in copies:
        copy.start()
    place = me_ref[0] % PLANE
    slot = lax.broadcasted_iota(jnp.int32, (GROUP, TRACES * STEPS), 0)
    at = lax.broadcasted_iota(jnp.int32, (GROUP, TRACES * STEPS), 1)
    trace = slot & (PAD - 1)
    wanted = trace * STEPS + PLANE * (slot >> 3) + place
    chosen = jnp.where((at == wanted) & (trace < TRACES), 1.0, 0.0).astype(BF16)
    for k in range(PLANE):
        copies[k].wait()
        base = jnp.dot(chosen, pack_s[k, WIDE:], preferred_element_type=F32)
        stream = (base + total_ref[:, k * 256 : (k + 1) * 256]).astype(BF16)
        for n in range(4):
            weight = pack_s[k, n * 256 : (n + 1) * 256]
            part = jnp.dot(stream, weight, preferred_element_type=F32)
            cols = slice(n * 256, (n + 1) * 256)
            out_ref[:, cols] = part if k == 0 else out_ref[:, cols] + part


def hidden_kernel(me_ref, inner_ref, class_ref, out_ref):
    hidden = jnp.maximum(inner_ref[...], 0.0).astype(BF16)
    logits = jnp.dot(hidden, class_ref[...], preferred_element_type=F32)
    gap = logits[:, 1:2] - logits[:, 0:1]
    lane = lax.broadcasted_iota(jnp.int32, (PAD, HD), 1)
    mine = jnp.where(lane == me_ref[0], gap, 0.0)
    for k in range(out_ref.shape[0]):
        out_ref[k] = mine


def vote_kernel(prompts, clusters, got_ref, scores_ref, votes_ref):
    gap = jnp.sum(got_ref[...], axis=0)
    scores = 1.0 / (1.0 + jnp.exp(-gap))
    scores_ref[...] = scores[:TRACES, :STEPS]
    lane = lax.broadcasted_iota(jnp.int32, (PAD, HD), 1)
    chain = jnp.min(jnp.where(lane < STEPS, scores, 2.0), axis=1, keepdims=True)
    prompt = lax.broadcasted_iota(jnp.int32, (PROMPTS, CLUSTERS), 0)
    cluster = lax.broadcasted_iota(jnp.int32, (PROMPTS, CLUSTERS), 1)
    votes = jnp.zeros((PROMPTS, CLUSTERS), F32)
    for t in range(TRACES):
        here = (prompt == prompts[t]) & (cluster == clusters[t])
        votes = votes + jnp.where(here, chain[t : t + 1, :], 0.0)
    votes_ref[...] = votes


def swapped(value, axis, bit):
    count = lax.axis_size(axis)
    return lax.ppermute(value, axis, [(s, s ^ bit) for s in range(count)])


def raised(value, planes):
    count = lax.axis_size("ctx")
    steps = planes * PLANE
    return lax.ppermute(value, "ctx", [(s, (s + steps) % count) for s in range(count)])


def per_device(
    queries,
    keys_values,
    trace_lengths,
    step_rows,
    prompt_ids,
    cluster_ids,
    step_stream,
    out_weight,
    score_weight,
    class_weight,
):
    me = lax.axis_index("ctx").astype(jnp.int32).reshape(1)
    columns = [[PLANE * z + j for z in range(Z)] for j in range(PLANE)]
    tie = lambda *values: lax.optimization_barrier(values)
    add = functools.partial(attend, me=me, lengths=trace_lengths, queries=queries)

    kv0 = keys_values
    core0 = swapped(kv0, "ctx", 1)
    kv1 = raised(kv0, 1)

    half = PER_GROUP * HD
    keep, passed, sent = small_call(
        pick_kernel,
        tuple(jax.ShapeDtypeStruct((n * GROUP, half), BF16) for n in (1, 1, 2)),
        [me, *pinned([step_rows, queries])],
        [SMEM, HBM, HBM],
        scratch_shapes=[
            pltpu.VMEM((PLANE * GROUP, half), BF16),
            pltpu.VMEM((TRACES, STEPS), jnp.int32),
            pltpu.VMEM((BLOCK, half), BF16),
            pltpu.SemaphoreType.DMA((2,)),
        ],
        name="pick",
    )
    arrived = swapped(sent, "ctx", 1)
    across = swapped(passed + arrived[GROUP:], "ctx", 2)
    wanted = keep + arrived[:GROUP] + across
    wanted, kv0y, core0, kv1 = tie(wanted, kv0, core0, kv1)
    wanted1, wanted2 = raised(wanted, -1), raised(wanted, -2)
    across0 = swapped(kv0y, "ctx", 2)
    core0y = swapped(core0, "ctx", 2)
    state = add([(0, 0, 0, 0), (0, 1, 1, 0)], kvs=[pinned([kv0y])[0], core0], state=None)
    wanted, wanted1, wanted2, state = tie(wanted, wanted1, wanted2, state)

    parts = small_call(
        picked_kernel,
        jax.ShapeDtypeStruct((GROUP, half), F32),
        [
            me,
            *pinned([trace_lengths, step_rows]),
            wanted,
            wanted1,
            wanted2,
            *pinned([kv0]),
            core0,
            across0,
            core0y,
        ],
        [SMEM, HBM, HBM] + [VMEM] * 3 + [HBM] * 4,
        scratch_shapes=[
            pltpu.VMEM((PLANE, 2, BLOCK, HD), BF16),
            pltpu.SMEM((TRACES,), jnp.int32),
            pltpu.VMEM((TRACES, STEPS), jnp.int32),
            pltpu.SemaphoreType.DMA((PLANE + 2,)),
        ],
        name="picked",
    )
    parts, state, kv1, across0, core0y, weight = tie(
        parts, state, kv1, across0, core0y, out_weight
    )
    across1 = swapped(kv1, "ctx", 2)

    firsts = [weight, swapped(weight, "ctx", 1), swapped(weight, "ctx", 2)]
    firsts.append(swapped(firsts[2], "ctx", 1))
    pack = jnp.concatenate(
        [score_weight[:, n * 256 : (n + 1) * 256] for n in range(4)] + [step_stream], axis=0
    )
    parts = jnp.broadcast_to(parts.astype(jnp.float16)[None], (Z, GROUP, half))
    parts = lax.all_to_all(parts, "ctx", 0, 0, axis_index_groups=columns).astype(F32)
    pair1 = jnp.concatenate([kv1, across1], axis=0)
    cores1 = swapped(pair1, "ctx", 1)
    state = add(
        [(0, 2, 0, 0), (0, 3, 1, 0), (1, 0, 2, 0), (1, 2, 2, 1)],
        kvs=[across0, core0y, pair1],
        state=state,
    )
    parts, state, pair1, cores1, pack = tie(parts, state, pair1, cores1, pack)
    packs = [pack, swapped(pack, "ctx", 1), swapped(pack, "ctx", 2)]
    packs.append(swapped(packs[2], "ctx", 1))

    projected = small_call(
        project_kernel,
        jax.ShapeDtypeStruct((GROUP, WIDE), F32),
        [parts, *firsts],
        [VMEM] + [HBM] * 4,
        scratch_shapes=[
            pltpu.VMEM((PLANE, BLOCK, 256), BF16),
            pltpu.SemaphoreType.DMA((PLANE,)),
        ],
        name="project",
    )
    projected, pair1 = tie((projected * 0.25).astype(jnp.float16), pair1)
    pair2 = raised(pair1, 1)
    projected = projected + swapped(projected, "head", 2)
    projected = projected + swapped(projected, "head", 4)
    projected, cores1 = tie(projected, cores1)
    other = swapped(projected, "head", 1)
    state = add([(1, 1, 0, 0), (1, 3, 0, 1)], kvs=[cores1], state=state)
    other, state, pair2 = tie(other, state, pair2)
    cores2 = swapped(pair2, "ctx", 1)
    projected = (projected.astype(F32) + other.astype(F32)) * 4.0

    inner = small_call(
        inner_kernel,
        jax.ShapeDtypeStruct((GROUP, WIDE), F32),
        [me, projected, *packs],
        [SMEM, VMEM] + [HBM] * 4,
        scratch_shapes=[
            pltpu.VMEM((PLANE, WIDE + TRACES * STEPS, 256), BF16),
            pltpu.SemaphoreType.DMA((PLANE,)),
        ],
        name="inner",
    )
    inner, state, pair2 = tie(inner, state, pair2)
    inner = (inner * 2.0**-10).astype(jnp.float16).reshape(Z, PAD, WIDE)
    state = add([(2, 0, 0, 0), (2, 2, 0, 1)], kvs=[pair2], state=state)
    inner = lax.all_to_all(inner, "ctx", 0, 0, axis_index_groups=columns)
    inner, state = tie(inner, state)
    inner = jnp.sum(inner.astype(F32), axis=0) * 2.0**10
    heads, count = lax.axis_size("head"), lax.axis_size("ctx")
    gap = small_call(
        hidden_kernel,
        jax.ShapeDtypeStruct((heads, PAD, HD), F32),
        [me, inner, class_weight],
        [SMEM, VMEM, VMEM],
        name="hidden",
    )
    gap, state, cores2 = tie(gap, state, cores2)
    attended = add([(2, 1, 0, 0), (2, 3, 0, 1)], kvs=[cores2], state=state, last=True)
    gap = lax.all_to_all(gap, "head", 0, 0)
    gap, attended = tie(gap, attended)
    gap = jnp.sum(gap, axis=0)
    gap = lax.all_to_all(jnp.broadcast_to(gap[None], (count, PAD, HD)), "ctx", 0, 0)
    step_scores, votes = small_call(
        vote_kernel,
        (
            jax.ShapeDtypeStruct((TRACES, STEPS), F32),
            jax.ShapeDtypeStruct((PROMPTS, CLUSTERS), F32),
        ),
        [prompt_ids, cluster_ids, gap],
        [SMEM, SMEM, VMEM],
        name="vote",
    )
    return (attended, step_scores, votes)


def solution(mesh):
    placed = (
        P("ctx", "head"),
        P(None, "ctx", "head"),
        P(),
        P(),
        P(),
        P(),
        P(None, "ctx"),
        P("head", "ctx"),
        P("ctx", "head"),
        P("head", None),
    )
    return jax.shard_map(
        per_device,
        mesh=mesh,
        in_specs=placed,
        out_specs=(P("ctx", "head"), P(), P()),
        check_vma=False,
    )
```

profile of v0, /device:TPU:1, one launch (start us, length us, event | category | flops | bytes accessed | tf_op | source)
XLA Modules:
  0.0 135.7 jit_solution(3749044340088923729)
XLA Ops:
  2.3 3.3 %collective-permute-start = (bf16[128,512]{1,0:T(8,128)(2,1)S(1)}, bf16[128,512]{1,0:T(8,128)(2,1)S(1)}, u32[]{:S(2)}, u32[]{:S(2)}) collective-permute-start(bf16[128,512]{1,0:T(8,128)(2,1)S(1)} %get-tuple-element.60), channel_id=1, source_target_pairs={{0,8},{8,0},{16,24},{24,16},{32,40},{40,32},{48,56},{56,48},{64,72... | collective-permute-start | bytes 393224 | tf_op jit(solution)/shard_map/ppermute | solution.py:459
  7.1 2.8 %collective-permute-done.1 = bf16[64,512]{1,0:T(8,128)(2,1)S(1)} collective-permute-done((bf16[64,512]{1,0:T(8,128)(2,1)S(1)}, bf16[64,512]{1,0:T(8,128)(2,1)S(1)}, u32[]{:S(2)}, u32[]{:S(2)}) %collective-permute-start.1) | collective-permute-done | bytes 65568 | tf_op jit(solution)/shard_map/ppermute | solution.py:459
  9.9 6.2 %collective-permute-done.3 = bf16[2,512,128]{2,1,0:T(8,128)(2,1)S(1)} collective-permute-done((bf16[2,512,128]{2,1,0:T(8,128)(2,1)}, bf16[2,512,128]{2,1,0:T(8,128)(2,1)S(1)}, u32[]{:S(2)}, u32[]{:S(2)}) %collective-permute-start.3) | collective-permute-done | bytes 262176 | tf_op jit(solution)/shard_map/ppermute | solution.py:465
  20.0 6.2 %attend_0_0.1 = (f32[512,512]{1,0:T(8,128)}, f32[512,128]{1,0:T(8,128)}) custom-call(s32[1]{0:T(128)} %bitcast.me_ref.refs_0_, s32[7]{0:T(128)} %refs_1_.9, bf16[512,512]{1,0:T(8,128)(2,1)} %refs_2_.9, bf16[2,512,128]{2,1,0:T(8,128)(2,1)} %refs_0_.1, bf16[2,512,128]{2,1,0:T(8,128)(2,1)S(1)} %collective-permute-done.2.refs_4_.refs_1_), custom_call_target="tpu_custom_call" | custom-call | flops 1073741824 | bytes 4194304 | tf_op jit(solution)/shard_map/attend_0_0/pallas_call | solution.py:326
  26.2 2.4 %collective-permute-done.6.refs_2_.refs_3_ = bf16[2,512,128]{2,1,0:T(8,128)(2,1)S(1)} collective-permute-done((bf16[2,512,128]{2,1,0:T(8,128)(2,1)S(1)}, bf16[2,512,128]{2,1,0:T(8,128)(2,1)S(1)}, u32[]{:S(2)}, u32[]{:S(2)}) %collective-permute-start.6) | collective-permute-done | bytes 262176 | tf_op jit(solution)/shard_map/ppermute | solution.py:459
  28.6 3.0 %picked.1 = f32[64,512]{1,0:T(8,128)S(1)} custom-call(s32[1]{0:T(128)} %bitcast.me_ref.refs_0_, s32[7]{0:T(128)} %refs_1_.9, s32[7,32]{1,0:T(8,128)} %steps_hbm.3, bf16[64,512]{1,0:T(8,128)(2,1)S(1)} %fusion.1.q_ref, bf16[64,512]{1,0:T(8,128)(2,1)S(1)} %collective-permute-done.4.q1_ref, bf16[64,512]{1,0:T(8,128)(2,1)S(1)} %collective-permute-done.5.q2_ref, ...), custom_call_target="tpu_custom_call" | custom-call | tf_op jit(solution)/shard_map/picked/pallas_call | solution.py:356
  33.9 4.6 %all-to-all-start = ((f16[8,64,512]{2,1,0:T(8,128)(2,1)}), f16[8,64,512]{2,1,0:T(8,128)(2,1)S(1)}, u32[]{:S(2)}, u32[]{:S(2)}) async-start(f16[8,64,512]{2,1,0:T(8,128)(2,1)} %broadcast_in_dim.4), calls=%async_computation | async-start | bytes 1048576 | tf_op jit(solution)/shard_map/all_to_all | solution.py:547
  38.6 2.8 %collective-permute-start.9 = (bf16[4,512,128]{2,1,0:T(8,128)(2,1)S(1)}, bf16[4,512,128]{2,1,0:T(8,128)(2,1)S(1)}, u32[]{:S(2)}, u32[]{:S(2)}) collective-permute-start(bf16[4,512,128]{2,1,0:T(8,128)(2,1)S(1)} %constant_dynamic-update-slice_fusion.refs_5_), channel_id=1, source_target_pairs={{0,8},{8,0},{16,24},{24,16},{32,40},{40,32},{48,56},{56,48},{64,72... | collective-permute-start | bytes 1572872 | tf_op jit(solution)/shard_map/ppermute | solution.py:459
  43.8 9.3 %all-to-all-done = f16[8,64,512]{2,1,0:T(8,128)(2,1)S(1)} async-done(((f16[8,64,512]{2,1,0:T(8,128)(2,1)}), f16[8,64,512]{2,1,0:T(8,128)(2,1)S(1)}, u32[]{:S(2)}, u32[]{:S(2)}) %all-to-all-start) | async-done | bytes 524320 | tf_op jit(solution)/shard_map/all_to_all | solution.py:547
  53.5 4.1 %collective-permute-start.10 = (bf16[512,256]{1,0:T(8,128)(2,1)S(1)}, bf16[512,256]{1,0:T(8,128)(2,1)S(1)}, u32[]{:S(2)}, u32[]{:S(2)}) collective-permute-start(bf16[512,256]{1,0:T(8,128)(2,1)S(1)} %copy-done), channel_id=1, source_target_pairs={{0,8},{8,0},{16,24},{24,16},{32,40},{40,32},{48,56},{56,48},{64,72... | collective-permute-start | bytes 786440 | tf_op jit(solution)/shard_map/ppermute | solution.py:459
  59.2 2.0 %project.1 = f32[64,1024]{1,0:T(8,128)S(1)} custom-call(f32[8,64,512]{2,1,0:T(8,128)S(1)} %convert_element_type.22.got_ref, bf16[512,256]{1,0:T(8,128)(2,1)S(1)} %copy-done, bf16[512,256]{1,0:T(8,128)(2,1)S(1)} %collective-permute-done.10.refs_1_, bf16[512,256]{1,0:T(8,128)(2,1)S(1)} %collective-permute-done.11.refs_2_, ...), custom_call_target="tpu_custom_call" | custom-call | tf_op jit(solution)/shard_map/project/pallas_call | solution.py:356
  62.2 3.3 %collective-permute-done.18.refs_2_ = bf16[1248,256]{1,0:T(8,128)(2,1)S(1)} collective-permute-done((bf16[1248,256]{1,0:T(8,128)(2,1)S(1)}, bf16[1248,256]{1,0:T(8,128)(2,1)S(1)}, u32[]{:S(2)}, u32[]{:S(2)}) %collective-permute-start.18) | collective-permute-done | bytes 639008 | tf_op jit(solution)/shard_map/ppermute | solution.py:459
  65.5 4.7 %collective-permute-start.19 = (bf16[1248,256]{1,0:T(8,128)(2,1)S(1)}, bf16[1248,256]{1,0:T(8,128)(2,1)S(1)}, u32[]{:S(2)}, u32[]{:S(2)}) collective-permute-start(bf16[1248,256]{1,0:T(8,128)(2,1)S(1)} %collective-permute-done.18.refs_2_), channel_id=1, source_target_pairs={{0,8},{8,0},{16,24},{24,16},{32,40},{40,32},{48,56},{56,48},{64,72... | collective-permute-start | bytes 1916936 | tf_op jit(solution)/shard_map/ppermute | solution.py:459
  71.4 3.9 %collective-permute-done.13 = f16[64,1024]{1,0:T(8,128)(2,1)S(1)} collective-permute-done((f16[64,1024]{1,0:T(8,128)(2,1)S(1)}, f16[64,1024]{1,0:T(8,128)(2,1)S(1)}, u32[]{:S(2)}, u32[]{:S(2)}) %collective-permute-start.13) | collective-permute-done | bytes 131104 | tf_op jit(solution)/shard_map/ppermute | solution.py:459
  75.3 2.8 %collective-permute-start.14 = (f16[64,1024]{1,0:T(8,128)(2,1)S(1)}, f16[64,1024]{1,0:T(8,128)(2,1)S(1)}, u32[]{:S(2)}, u32[]{:S(2)}) collective-permute-start(f16[64,1024]{1,0:T(8,128)(2,1)S(1)} %add.21), channel_id=1, source_target_pairs={{0,4},{1,5},{2,6},{3,7},{4,0},{5,1},{6,2},{7,3},{8,12},{9,13},{10,... | collective-permute-start | bytes 393224 | tf_op jit(solution)/shard_map/ppermute | solution.py:459
  78.2 3.0 %collective-permute-done.14 = f16[64,1024]{1,0:T(8,128)(2,1)S(1)} collective-permute-done((f16[64,1024]{1,0:T(8,128)(2,1)S(1)}, f16[64,1024]{1,0:T(8,128)(2,1)S(1)}, u32[]{:S(2)}, u32[]{:S(2)}) %collective-permute-start.14) | collective-permute-done | bytes 131104 | tf_op jit(solution)/shard_map/ppermute | solution.py:459
  81.2 2.7 %collective-permute-start.15 = (f16[64,1024]{1,0:T(8,128)(2,1)S(1)}, f16[64,1024]{1,0:T(8,128)(2,1)S(1)}, u32[]{:S(2)}, u32[]{:S(2)}) collective-permute-start(f16[64,1024]{1,0:T(8,128)(2,1)S(1)} %add.22), channel_id=1, source_target_pairs={{0,1},{1,0},{2,3},{3,2},{4,5},{5,4},{6,7},{7,6},{8,9},{9,8},{10,11... | collective-permute-start | bytes 393224 | tf_op jit(solution)/shard_map/ppermute | solution.py:459
  89.2 6.6 %all-to-all-start.1 = ((f16[8,8,1024]{2,1,0:T(8,128)(2,1)}), f16[8,8,1024]{2,1,0:T(8,128)(2,1)S(1)}, u32[]{:S(2)}, u32[]{:S(2)}) async-start(f16[8,8,1024]{2,1,0:T(8,128)(2,1)} %fusion), calls=%async_computation.1 | async-start | bytes 262144 | tf_op jit(solution)/shard_map/all_to_all | solution.py:595
  95.8 4.3 %collective-permute-start.20 = (bf16[4,512,128]{2,1,0:T(8,128)(2,1)S(1)}, bf16[4,512,128]{2,1,0:T(8,128)(2,1)S(1)}, u32[]{:S(2)}, u32[]{:S(2)}) collective-permute-start(bf16[4,512,128]{2,1,0:T(8,128)(2,1)S(1)} %collective-permute-done.16.refs_3_), channel_id=1, source_target_pairs={{0,8},{8,0},{16,24},{24,16},{32,40},{40,32},{48,56},{56,48},{64,72... | collective-permute-start | bytes 1572872 | tf_op jit(solution)/shard_map/ppermute | solution.py:459
  101.1 2.6 %all-to-all-done.1 = f16[8,8,1024]{2,1,0:T(8,128)(2,1)S(1)} async-done(((f16[8,8,1024]{2,1,0:T(8,128)(2,1)}), f16[8,8,1024]{2,1,0:T(8,128)(2,1)S(1)}, u32[]{:S(2)}, u32[]{:S(2)}) %all-to-all-start.1) | async-done | bytes 131104 | tf_op jit(solution)/shard_map/all_to_all | solution.py:595
  104.7 4.9 %all-to-all-start.2 = ((f32[8,8,128]{2,1,0:T(8,128)}), f32[8,8,128]{2,1,0:T(8,128)S(1)}, u32[]{:S(2)}, u32[]{:S(2)}) async-start(f32[8,8,128]{2,1,0:T(8,128)} %hidden.1), calls=%async_computation.2 | async-start | bytes 65536 | tf_op jit(solution)/shard_map/all_to_all | solution.py:608
  109.6 3.7 %attend_2_1.1 = f32[512,512]{1,0:T(8,128)} custom-call(s32[1]{0:T(128)} %bitcast.me_ref.refs_0_, s32[7]{0:T(128)} %refs_1_.9, bf16[512,512]{1,0:T(8,128)(2,1)} %refs_2_.9, bf16[4,512,128]{2,1,0:T(8,128)(2,1)S(1)} %collective-permute-done.20.refs_3_, f32[512,512]{1,0:T(8,128)} %get-tuple-element.109.refs_4_, f32[512,128]{1,0:T(8,128)} %get-tuple-element.110.refs_5_), custom_call_target="tpu_custom_call" | custom-call | flops 1073741824 | bytes 4194304 | tf_op jit(solution)/shard_map/attend_2_1/pallas_call | solution.py:326
  113.3 2.9 %all-to-all-done.2 = f32[8,8,128]{2,1,0:T(8,128)S(1)} async-done(((f32[8,8,128]{2,1,0:T(8,128)}), f32[8,8,128]{2,1,0:T(8,128)S(1)}, u32[]{:S(2)}, u32[]{:S(2)}) %all-to-all-start.2) | async-done | bytes 32800 | tf_op jit(solution)/shard_map/all_to_all | solution.py:608
  116.2 18.3 %all_to_all.20.got_ref = f32[32,8,128]{2,1,0:T(8,128)S(1)} all-to-all(f32[32,8,128]{2,1,0:T(8,128)S(1)} %broadcast_in_dim.5), channel_id=1, replica_groups=mesh['ctx'=32,'head'=8] {'ctx'}, dimensions={0} | all-to-all | bytes 262144 | tf_op jit(solution)/shard_map/all_to_all | solution.py:611
  (72 shorter events, 24.3 us)
Async XLA Ops:
  2.3 4.3 %collective-permute-start = (bf16[128,512]{1,0:T(8,128)(2,1)S(1)}, bf16[128,512]{1,0:T(8,128)(2,1)S(1)}, u32[]{:S(2)}, u32[]{:S(2)}) collective-permute-start(bf16[128,512]{1,0:T(8,128)(2,1)S(1)} %get-tuple-element.60), channel_id=1, source_target_pairs={{0,8},{8,0},{16,24},{24,16},{32,40},{40,32},{48,56},{56,48},{64,72... | collective-permute-start | bytes 393224 | tf_op jit(solution)/shard_map/ppermute | solution.py:459
  5.7 4.2 %collective-permute-start.2 = (bf16[2,512,128]{2,1,0:T(8,128)(2,1)}, bf16[2,512,128]{2,1,0:T(8,128)(2,1)S(1)}, u32[]{:S(2)}, u32[]{:S(2)}) collective-permute-start(bf16[2,512,128]{2,1,0:T(8,128)(2,1)} %refs_0_.1), channel_id=1, source_target_pairs={{0,8},{8,0},{16,24},{24,16},{32,40},{40,32},{48,56},{56,48},{64,72... | collective-permute-start | bytes 786440 | tf_op jit(solution)/shard_map/ppermute | solution.py:459
  5.8 10.4 %collective-permute-start.3 = (bf16[2,512,128]{2,1,0:T(8,128)(2,1)}, bf16[2,512,128]{2,1,0:T(8,128)(2,1)S(1)}, u32[]{:S(2)}, u32[]{:S(2)}) collective-permute-start(bf16[2,512,128]{2,1,0:T(8,128)(2,1)} %refs_0_.1), channel_id=1, source_target_pairs={{0,32},{8,40},{16,48},{24,56},{32,64},{40,72},{48,80},{56,88},{64,... | collective-permute-start | bytes 786440 | tf_op jit(solution)/shard_map/ppermute | solution.py:465
  6.7 3.2 %collective-permute-start.1 = (bf16[64,512]{1,0:T(8,128)(2,1)S(1)}, bf16[64,512]{1,0:T(8,128)(2,1)S(1)}, u32[]{:S(2)}, u32[]{:S(2)}) collective-permute-start(bf16[64,512]{1,0:T(8,128)(2,1)S(1)} %slice_add_fusion), channel_id=1, source_target_pairs={{0,16},{8,24},{16,0},{24,8},{32,48},{40,56},{48,32},{56,40},{64,80... | collective-permute-start | bytes 196616 | tf_op jit(solution)/shard_map/ppermute | solution.py:459
  16.1 10.1 %collective-permute-start.7 = (bf16[2,512,128]{2,1,0:T(8,128)(2,1)S(1)}, bf16[2,512,128]{2,1,0:T(8,128)(2,1)S(1)}, u32[]{:S(2)}, u32[]{:S(2)}) collective-permute-start(bf16[2,512,128]{2,1,0:T(8,128)(2,1)S(1)} %collective-permute-done.2.refs_4_.refs_1_), channel_id=1, source_target_pairs={{0,16},{8,24},{16,0},{24,8},{32,48},{40,56},{48,32},{56,40},{64,80... | collective-permute-start | bytes 786440 | tf_op jit(solution)/shard_map/ppermute | solution.py:459
  17.4 11.2 %collective-permute-start.6 = (bf16[2,512,128]{2,1,0:T(8,128)(2,1)S(1)}, bf16[2,512,128]{2,1,0:T(8,128)(2,1)S(1)}, u32[]{:S(2)}, u32[]{:S(2)}) collective-permute-start(bf16[2,512,128]{2,1,0:T(8,128)(2,1)S(1)} %copy-done.4), channel_id=1, source_target_pairs={{0,16},{8,24},{16,0},{24,8},{32,48},{40,56},{48,32},{56,40},{64,80... | collective-permute-start | bytes 786440 | tf_op jit(solution)/shard_map/ppermute | solution.py:459
  17.6 8.6 %collective-permute-start.4 = (bf16[64,512]{1,0:T(8,128)(2,1)S(1)}, bf16[64,512]{1,0:T(8,128)(2,1)S(1)}, u32[]{:S(2)}, u32[]{:S(2)}) collective-permute-start(bf16[64,512]{1,0:T(8,128)(2,1)S(1)} %fusion.1.q_ref), channel_id=1, source_target_pairs={{0,224},{8,232},{16,240},{24,248},{32,0},{40,8},{48,16},{56,24},{6... | collective-permute-start | bytes 196616 | tf_op jit(solution)/shard_map/ppermute | solution.py:465
  18.8 7.4 %collective-permute-start.5 = (bf16[64,512]{1,0:T(8,128)(2,1)S(1)}, bf16[64,512]{1,0:T(8,128)(2,1)S(1)}, u32[]{:S(2)}, u32[]{:S(2)}) collective-permute-start(bf16[64,512]{1,0:T(8,128)(2,1)S(1)} %fusion.1.q_ref), channel_id=1, source_target_pairs={{0,192},{8,200},{16,208},{24,216},{32,224},{40,232},{48,240},{56,2... | collective-permute-start | bytes 196616 | tf_op jit(solution)/shard_map/ppermute | solution.py:465
  31.6 6.9 %collective-permute-start.8 = (bf16[2,512,128]{2,1,0:T(8,128)(2,1)S(1)}, bf16[2,512,128]{2,1,0:T(8,128)(2,1)S(1)}, u32[]{:S(2)}, u32[]{:S(2)}) collective-permute-start(bf16[2,512,128]{2,1,0:T(8,128)(2,1)S(1)} %collective-permute-done.3), channel_id=1, source_target_pairs={{0,16},{8,24},{16,0},{24,8},{32,48},{40,56},{48,32},{56,40},{64,80... | collective-permute-start | bytes 786440 | tf_op jit(solution)/shard_map/ppermute | solution.py:459
  33.9 19.3 %all-to-all-start = ((f16[8,64,512]{2,1,0:T(8,128)(2,1)}), f16[8,64,512]{2,1,0:T(8,128)(2,1)S(1)}, u32[]{:S(2)}, u32[]{:S(2)}) async-start(f16[8,64,512]{2,1,0:T(8,128)(2,1)} %broadcast_in_dim.4), calls=%async_computation | async-start | bytes 1048576 | tf_op jit(solution)/shard_map/all_to_all | solution.py:547
  38.6 14.7 %collective-permute-start.9 = (bf16[4,512,128]{2,1,0:T(8,128)(2,1)S(1)}, bf16[4,512,128]{2,1,0:T(8,128)(2,1)S(1)}, u32[]{:S(2)}, u32[]{:S(2)}) collective-permute-start(bf16[4,512,128]{2,1,0:T(8,128)(2,1)S(1)} %constant_dynamic-update-slice_fusion.refs_5_), channel_id=1, source_target_pairs={{0,8},{8,0},{16,24},{24,16},{32,40},{40,32},{48,56},{56,48},{64,72... | collective-permute-start | bytes 1572872 | tf_op jit(solution)/shard_map/ppermute | solution.py:459
  42.4 15.3 %collective-permute-start.11 = (bf16[512,256]{1,0:T(8,128)(2,1)S(1)}, bf16[512,256]{1,0:T(8,128)(2,1)S(1)}, u32[]{:S(2)}, u32[]{:S(2)}) collective-permute-start(bf16[512,256]{1,0:T(8,128)(2,1)S(1)} %copy-done), channel_id=1, source_target_pairs={{0,16},{8,24},{16,0},{24,8},{32,48},{40,56},{48,32},{56,40},{64,80... | collective-permute-start | bytes 786440 | tf_op jit(solution)/shard_map/ppermute | solution.py:459
  53.3 12.2 %collective-permute-start.18 = (bf16[1248,256]{1,0:T(8,128)(2,1)S(1)}, bf16[1248,256]{1,0:T(8,128)(2,1)S(1)}, u32[]{:S(2)}, u32[]{:S(2)}) collective-permute-start(bf16[1248,256]{1,0:T(8,128)(2,1)S(1)} %constant_dynamic-update-slice_fusion.2.refs_0_), channel_id=1, source_target_pairs={{0,16},{8,24},{16,0},{24,8},{32,48},{40,56},{48,32},{56,40},{64,80... | collective-permute-start | bytes 1916936 | tf_op jit(solution)/shard_map/ppermute | solution.py:459
  53.5 5.2 %collective-permute-start.10 = (bf16[512,256]{1,0:T(8,128)(2,1)S(1)}, bf16[512,256]{1,0:T(8,128)(2,1)S(1)}, u32[]{:S(2)}, u32[]{:S(2)}) collective-permute-start(bf16[512,256]{1,0:T(8,128)(2,1)S(1)} %copy-done), channel_id=1, source_target_pairs={{0,8},{8,0},{16,24},{24,16},{32,40},{40,32},{48,56},{56,48},{64,72... | collective-permute-start | bytes 786440 | tf_op jit(solution)/shard_map/ppermute | solution.py:459
  57.6 1.5 %collective-permute-start.12 = (bf16[512,256]{1,0:T(8,128)(2,1)S(1)}, bf16[512,256]{1,0:T(8,128)(2,1)S(1)}, u32[]{:S(2)}, u32[]{:S(2)}) collective-permute-start(bf16[512,256]{1,0:T(8,128)(2,1)S(1)} %collective-permute-done.11.refs_2_), channel_id=1, source_target_pairs={{0,8},{8,0},{16,24},{24,16},{32,40},{40,32},{48,56},{56,48},{64,72... | collective-permute-start | bytes 786440 | tf_op jit(solution)/shard_map/ppermute | solution.py:459
  61.2 25.5 %collective-permute-start.16 = (bf16[4,512,128]{2,1,0:T(8,128)(2,1)S(1)}, bf16[4,512,128]{2,1,0:T(8,128)(2,1)S(1)}, u32[]{:S(2)}, u32[]{:S(2)}) collective-permute-start(bf16[4,512,128]{2,1,0:T(8,128)(2,1)S(1)} %constant_dynamic-update-slice_fusion.refs_5_), channel_id=1, source_target_pairs={{0,32},{8,40},{16,48},{24,56},{32,64},{40,72},{48,80},{56,88},{64,... | collective-permute-start | bytes 1572872 | tf_op jit(solution)/shard_map/ppermute | solution.py:465
  61.5 25.1 %collective-permute-start.17 = (bf16[1248,256]{1,0:T(8,128)(2,1)S(1)}, bf16[1248,256]{1,0:T(8,128)(2,1)S(1)}, u32[]{:S(2)}, u32[]{:S(2)}) collective-permute-start(bf16[1248,256]{1,0:T(8,128)(2,1)S(1)} %constant_dynamic-update-slice_fusion.2.refs_0_), channel_id=1, source_target_pairs={{0,8},{8,0},{16,24},{24,16},{32,40},{40,32},{48,56},{56,48},{64,72... | collective-permute-start | bytes 1916936 | tf_op jit(solution)/shard_map/ppermute | solution.py:459
  65.5 21.2 %collective-permute-start.19 = (bf16[1248,256]{1,0:T(8,128)(2,1)S(1)}, bf16[1248,256]{1,0:T(8,128)(2,1)S(1)}, u32[]{:S(2)}, u32[]{:S(2)}) collective-permute-start(bf16[1248,256]{1,0:T(8,128)(2,1)S(1)} %collective-permute-done.18.refs_2_), channel_id=1, source_target_pairs={{0,8},{8,0},{16,24},{24,16},{32,40},{40,32},{48,56},{56,48},{64,72... | collective-permute-start | bytes 1916936 | tf_op jit(solution)/shard_map/ppermute | solution.py:459
  70.2 5.1 %collective-permute-start.13 = (f16[64,1024]{1,0:T(8,128)(2,1)S(1)}, f16[64,1024]{1,0:T(8,128)(2,1)S(1)}, u32[]{:S(2)}, u32[]{:S(2)}) collective-permute-start(f16[64,1024]{1,0:T(8,128)(2,1)S(1)} %multiply_convert_fusion.1), channel_id=1, source_target_pairs={{0,2},{1,3},{2,0},{3,1},{4,6},{5,7},{6,4},{7,5},{8,10},{9,11},{10,... | collective-permute-start | bytes 393224 | tf_op jit(solution)/shard_map/ppermute | solution.py:459
  75.3 5.8 %collective-permute-start.14 = (f16[64,1024]{1,0:T(8,128)(2,1)S(1)}, f16[64,1024]{1,0:T(8,128)(2,1)S(1)}, u32[]{:S(2)}, u32[]{:S(2)}) collective-permute-start(f16[64,1024]{1,0:T(8,128)(2,1)S(1)} %add.21), channel_id=1, source_target_pairs={{0,4},{1,5},{2,6},{3,7},{4,0},{5,1},{6,2},{7,3},{8,12},{9,13},{10,... | collective-permute-start | bytes 393224 | tf_op jit(solution)/shard_map/ppermute | solution.py:459
  81.2 5.4 %collective-permute-start.15 = (f16[64,1024]{1,0:T(8,128)(2,1)S(1)}, f16[64,1024]{1,0:T(8,128)(2,1)S(1)}, u32[]{:S(2)}, u32[]{:S(2)}) collective-permute-start(f16[64,1024]{1,0:T(8,128)(2,1)S(1)} %add.22), channel_id=1, source_target_pairs={{0,1},{1,0},{2,3},{3,2},{4,5},{5,4},{6,7},{7,6},{8,9},{9,8},{10,11... | collective-permute-start | bytes 393224 | tf_op jit(solution)/shard_map/ppermute | solution.py:459
  89.2 14.6 %all-to-all-start.1 = ((f16[8,8,1024]{2,1,0:T(8,128)(2,1)}), f16[8,8,1024]{2,1,0:T(8,128)(2,1)S(1)}, u32[]{:S(2)}, u32[]{:S(2)}) async-start(f16[8,8,1024]{2,1,0:T(8,128)(2,1)} %fusion), calls=%async_computation.1 | async-start | bytes 262144 | tf_op jit(solution)/shard_map/all_to_all | solution.py:595
  95.8 8.9 %collective-permute-start.20 = (bf16[4,512,128]{2,1,0:T(8,128)(2,1)S(1)}, bf16[4,512,128]{2,1,0:T(8,128)(2,1)S(1)}, u32[]{:S(2)}, u32[]{:S(2)}) collective-permute-start(bf16[4,512,128]{2,1,0:T(8,128)(2,1)S(1)} %collective-permute-done.16.refs_3_), channel_id=1, source_target_pairs={{0,8},{8,0},{16,24},{24,16},{32,40},{40,32},{48,56},{56,48},{64,72... | collective-permute-start | bytes 1572872 | tf_op jit(solution)/shard_map/ppermute | solution.py:459
  104.7 11.5 %all-to-all-start.2 = ((f32[8,8,128]{2,1,0:T(8,128)}), f32[8,8,128]{2,1,0:T(8,128)S(1)}, u32[]{:S(2)}, u32[]{:S(2)}) async-start(f32[8,8,128]{2,1,0:T(8,128)} %hidden.1), calls=%async_computation.2 | async-start | bytes 65536 | tf_op jit(solution)/shard_map/all_to_all | solution.py:608
  (7 other events, 73.0 us)
where the time goes:
time: 136 us
  starting transfers between devices  49.9 us (37%)
  waiting for transfers between devices  40.8 us (30%)
  Pallas kernels  22.6 us (17%)
  blocking collectives  18.3 us (13%)
  local copies, waits for them, and re-layouts  2.13 us (2%)
    ppermute x17, starting transfers between devices, swapped(): return lax.ppermute(value, axis, [(s, s ^ bit) for s in range(count)])  30.9 us
    ppermute x17, waiting for transfers between devices, swapped(): return lax.ppermute(value, axis, [(s, s ^ bit) for s in range(count)])  19.8 us
    all_to_all x1, blocking collectives, per_device(): lax.all_to_all(jnp.broadcast_to(gap[None], (count, PAD, HD)), 'ctx', 0, 0)  18.3 us
    pallas_call x5, Pallas kernels, attend(): pl.pallas_call(functools.partial(attend_kernel, slots, state is None, las...  12.1 us
    pallas_call x6, Pallas kernels, small_call(): pl.pallas_call(kernel, out_shape=shape, in_specs=specs or [VMEM] * len(op...  10.5 us
    all_to_all x1, waiting for transfers between devices, per_device(): lax.all_to_all(parts, 'ctx', 0, 0, axis_index_groups=columns).astype(F32)  9.32 us
    all_to_all x1, starting transfers between devices, per_device(): inner = lax.all_to_all(inner, 'ctx', 0, 0, axis_index_groups=columns)  6.64 us
    ppermute x4, waiting for transfers between devices, raised(): lax.ppermute(value, 'ctx', [(s, (s + steps) % count) for s in range(count)])  6.25 us
  transfers between devices with their start and end apart: 24, of which 13 were waited for; matrix products, arithmetic and copies ran while one was open for 2% of the time, Pallas kernels for 11%

commit v1 on v0

--- a/solution.py
+++ b/solution.py
@@ -429,22 +429,22 @@
             out_ref[:, cols] = part if k == 0 else out_ref[:, cols] + part
 
 
-def hidden_kernel(me_ref, inner_ref, class_ref, out_ref):
+def hidden_kernel(inner_ref, class_ref, out_ref):
     hidden = jnp.maximum(inner_ref[...], 0.0).astype(BF16)
     logits = jnp.dot(hidden, class_ref[...], preferred_element_type=F32)
     gap = logits[:, 1:2] - logits[:, 0:1]
     lane = lax.broadcasted_iota(jnp.int32, (PAD, HD), 1)
-    mine = jnp.where(lane == me_ref[0], gap, 0.0)
+    row = lax.broadcasted_iota(jnp.int32, (PAD, HD), 0)
+    mine = jnp.sum(jnp.where(lane == row, gap, 0.0), axis=0, keepdims=True)
     for k in range(out_ref.shape[0]):
         out_ref[k] = mine
 
 
 def vote_kernel(prompts, clusters, got_ref, scores_ref, votes_ref):
-    gap = jnp.sum(got_ref[...], axis=0)
-    scores = 1.0 / (1.0 + jnp.exp(-gap))
-    scores_ref[...] = scores[:TRACES, :STEPS]
-    lane = lax.broadcasted_iota(jnp.int32, (PAD, HD), 1)
-    chain = jnp.min(jnp.where(lane < STEPS, scores, 2.0), axis=1, keepdims=True)
+    gap = jnp.concatenate([got_ref[k] for k in range(STEPS)], axis=0)
+    scores = 1.0 / (1.0 + jnp.exp(-gap.T[:PAD]))
+    scores_ref[...] = scores[:TRACES]
+    chain = jnp.min(scores, axis=1, keepdims=True)
     prompt = lax.broadcasted_iota(jnp.int32, (PROMPTS, CLUSTERS), 0)
     cluster = lax.broadcasted_iota(jnp.int32, (PROMPTS, CLUSTERS), 1)
     votes = jnp.zeros((PROMPTS, CLUSTERS), F32)
@@ -484,7 +484,6 @@
 
     kv0 = keys_values
     core0 = swapped(kv0, "ctx", 1)
-    kv1 = raised(kv0, 1)
 
     half = PER_GROUP * HD
     keep, passed, sent = small_call(
@@ -501,14 +500,22 @@
         name="pick",
     )
     arrived = swapped(sent, "ctx", 1)
+    across0 = swapped(kv0, "ctx", 2)
+    core0y = swapped(core0, "ctx", 2)
     across = swapped(passed + arrived[GROUP:], "ctx", 2)
     wanted = keep + arrived[:GROUP] + across
-    wanted, kv0y, core0, kv1 = tie(wanted, kv0, core0, kv1)
     wanted1, wanted2 = raised(wanted, -1), raised(wanted, -2)
-    across0 = swapped(kv0y, "ctx", 2)
-    core0y = swapped(core0, "ctx", 2)
-    state = add([(0, 0, 0, 0), (0, 1, 1, 0)], kvs=[pinned([kv0y])[0], core0], state=None)
+    wanted, own_kv, core0, across0 = tie(wanted, kv0, core0, across0)
+    state = add([(0, 0, 0, 0), (0, 1, 1, 0)], kvs=[pinned([own_kv])[0], core0], state=None)
     wanted, wanted1, wanted2, state = tie(wanted, wanted1, wanted2, state)
+
+    weight, wanted = tie(out_weight, wanted)
+    firsts = [weight, swapped(weight, "ctx", 1), swapped(weight, "ctx", 2)]
+    firsts.append(swapped(firsts[2], "ctx", 1))
+    pack = jnp.concatenate(
+        [score_weight[:, n * 256 : (n + 1) * 256] for n in range(4)] + [step_stream], axis=0
+    )
+    kv1, _ = tie(raised(kv0, 1), wanted)
 
     parts = small_call(
         picked_kernel,
@@ -533,19 +540,12 @@
         ],
         name="picked",
     )
-    parts, state, kv1, across0, core0y, weight = tie(
-        parts, state, kv1, across0, core0y, out_weight
-    )
+    parts, state, kv1, across0, core0y = tie(parts, state, kv1, across0, core0y)
     across1 = swapped(kv1, "ctx", 2)
-
-    firsts = [weight, swapped(weight, "ctx", 1), swapped(weight, "ctx", 2)]
-    firsts.append(swapped(firsts[2], "ctx", 1))
-    pack = jnp.concatenate(
-        [score_weight[:, n * 256 : (n + 1) * 256] for n in range(4)] + [step_stream], axis=0
-    )
     parts = jnp.broadcast_to(parts.astype(jnp.float16)[None], (Z, GROUP, half))
     parts = lax.all_to_all(parts, "ctx", 0, 0, axis_index_groups=columns).astype(F32)
     pair1 = jnp.concatenate([kv1, across1], axis=0)
+    *firsts, pair1, pack = tie(*firsts, pair1, pack)
     cores1 = swapped(pair1, "ctx", 1)
     state = add(
         [(0, 2, 0, 0), (0, 3, 1, 0), (1, 0, 2, 0), (1, 2, 2, 1)],
@@ -554,7 +554,6 @@
     )
     parts, state, pair1, cores1, pack = tie(parts, state, pair1, cores1, pack)
     packs = [pack, swapped(pack, "ctx", 1), swapped(pack, "ctx", 2)]
-    packs.append(swapped(packs[2], "ctx", 1))
 
     projected = small_call(
         project_kernel,
@@ -571,7 +570,8 @@
     pair2 = raised(pair1, 1)
     projected = projected + swapped(projected, "head", 2)
     projected = projected + swapped(projected, "head", 4)
-    projected, cores1 = tie(projected, cores1)
+    projected, cores1, packs[2] = tie(projected, cores1, packs[2])
+    packs.append(swapped(packs[2], "ctx", 1))
     other = swapped(projected, "head", 1)
     state = add([(1, 1, 0, 0), (1, 3, 0, 1)], kvs=[cores1], state=state)
     other, state, pair2 = tie(other, state, pair2)
@@ -598,9 +598,8 @@
     heads, count = lax.axis_size("head"), lax.axis_size("ctx")
     gap = small_call(
         hidden_kernel,
-        jax.ShapeDtypeStruct((heads, PAD, HD), F32),
-        [me, inner, class_weight],
-        [SMEM, VMEM, VMEM],
+        jax.ShapeDtypeStruct((heads, 1, HD), F32),
+        [inner, class_weight],
         name="hidden",
     )
     gap, state, cores2 = tie(gap, state, cores2)
@@ -608,7 +607,7 @@
     gap = lax.all_to_all(gap, "head", 0, 0)
     gap, attended = tie(gap, attended)
     gap = jnp.sum(gap, axis=0)
-    gap = lax.all_to_all(jnp.broadcast_to(gap[None], (count, PAD, HD)), "ctx", 0, 0)
+    gap = lax.all_to_all(jnp.broadcast_to(gap[None], (count, 1, HD)), "ctx", 0, 0)
     step_scores, votes = small_call(
         vote_kernel,
         (

time: 136 us -> 136 us (level)
  waiting for transfers between devices: 40.8 us -> 50.8 us
  starting transfers between devices: 49.9 us -> 42.3 us
  blocking collectives: 18.3 us -> 14.3 us
  other arithmetic: 1.02 us -> 3.08 us
    ppermute x17, starting transfers between devices: 30.9 us -> 22.3 us  [swapped(): return lax.ppermute(value, axis, [(s, s ^ bit) for s in range(count)])]
    ppermute x17, waiting for transfers between devices: 19.8 us -> 26.3 us  [swapped(): return lax.ppermute(value, axis, [(s, s ^ bit) for s in range(count)])]
    all_to_all x1, waiting for transfers between devices: 9.32 us -> 13.9 us  [per_device(): lax.all_to_all(parts, 'ctx', 0, 0, axis_index_groups=columns).astype(F32)]
    ppermute x4, waiting for transfers between devices: 6.25 us -> 1.79 us  [raised(): lax.ppermute(value, 'ctx', [(s, (s + steps) % count) for s in range(count)])]
    all_to_all x1, blocking collectives: 18.3 us -> 14.3 us  [per_device(): lax.all_to_all(jnp.broadcast_to(gap[None], (count, 1, HD)), 'ctx', 0, 0)]
    all_to_all x1, waiting for transfers between devices: 2.65 us -> 6.18 us  [per_device(): inner = lax.all_to_all(inner, 'ctx', 0, 0, axis_index_groups=columns)]
    ppermute x4, starting transfers between devices: 2.76 us -> 6.29 us  [raised(): lax.ppermute(value, 'ctx', [(s, (s + steps) % count) for s in range(count)])]
    all_to_all x1, starting transfers between devices: 6.64 us -> 4.26 us  [per_device(): inner = lax.all_to_all(inner, 'ctx', 0, 0, axis_index_groups=columns)]
  transfers between devices with their start and end apart: 24 -> 24, of which waited for: 13 -> 10; matrix products, arithmetic and copies ran while one was open for 2% -> 3% of each run, Pallas kernels for 11% -> 13%
where the time goes in v1:
time: 136 us; the launch traced here: 135 us
  waiting for transfers between devices  50.8 us (37%)
  starting transfers between devices  42.3 us (31%)
  Pallas kernels  22.7 us (17%)
  blocking collectives  14.3 us (11%)
  other arithmetic  3.08 us (2%)
    ppermute x17, waiting for transfers between devices, swapped(): return lax.ppermute(value, axis, [(s, s ^ bit) for s in range(count)])  26.3 us
    ppermute x17, starting transfers between devices, swapped(): return lax.ppermute(value, axis, [(s, s ^ bit) for s in range(count)])  22.3 us
    all_to_all x1, blocking collectives, per_device(): lax.all_to_all(jnp.broadcast_to(gap[None], (count, 1, HD)), 'ctx', 0, 0)  14.3 us
    all_to_all x1, waiting for transfers between devices, per_device(): lax.all_to_all(parts, 'ctx', 0, 0, axis_index_groups=columns).astype(F32)  13.9 us
    pallas_call x5, Pallas kernels, attend(): pl.pallas_call(functools.partial(attend_kernel, slots, state is None, las...  12.1 us
    pallas_call x6, Pallas kernels, small_call(): pl.pallas_call(kernel, out_shape=shape, in_specs=specs or [VMEM] * len(op...  10.6 us
    ppermute x4, starting transfers between devices, raised(): lax.ppermute(value, 'ctx', [(s, (s + steps) % count) for s in range(count)])  6.29 us
    all_to_all x1, waiting for transfers between devices, per_device(): inner = lax.all_to_all(inner, 'ctx', 0, 0, axis_index_groups=columns)  6.18 us
  transfers between devices with their start and end apart: 24, of which 10 were waited for; matrix products, arithmetic and copies ran while one was open for 3% of the time, Pallas kernels for 13%

profile of v1, /device:TPU:1, one launch (start us, length us, event | category | flops | bytes accessed | tf_op | source)
XLA Modules:
  0.0 135.4 jit_solution(3962489480332695529)
XLA Ops:
  0.6 1.7 %pick.1 = (bf16[64,512]{1,0:T(8,128)(2,1)S(1)}, bf16[64,512]{1,0:T(8,128)(2,1)S(1)}, bf16[128,512]{1,0:T(8,128)(2,1)S(1)}) custom-call(s32[1]{0:T(128)} %bitcast.me_ref.refs_0_, s32[7,32]{1,0:T(8,128)} %steps_hbm.3, bf16[512,512]{1,0:T(8,128)(2,1)} %refs_2_.9), custom_call_target="tpu_custom_call" | custom-call | tf_op jit(solution)/shard_map/pick/pallas_call | solution.py:356
  2.3 3.3 %collective-permute-start = (bf16[128,512]{1,0:T(8,128)(2,1)S(1)}, bf16[128,512]{1,0:T(8,128)(2,1)S(1)}, u32[]{:S(2)}, u32[]{:S(2)}) collective-permute-start(bf16[128,512]{1,0:T(8,128)(2,1)S(1)} %get-tuple-element.69), channel_id=1, source_target_pairs={{0,8},{8,0},{16,24},{24,16},{32,40},{40,32},{48,56},{56,48},{64,72... | collective-permute-start | bytes 393224 | tf_op jit(solution)/shard_map/ppermute | solution.py:459
  7.4 7.5 %collective-permute-done.1 = bf16[64,512]{1,0:T(8,128)(2,1)S(1)} collective-permute-done((bf16[64,512]{1,0:T(8,128)(2,1)S(1)}, bf16[64,512]{1,0:T(8,128)(2,1)S(1)}, u32[]{:S(2)}, u32[]{:S(2)}) %collective-permute-start.1) | collective-permute-done | bytes 65568 | tf_op jit(solution)/shard_map/ppermute | solution.py:459
  14.9 3.9 %collective-permute-start.4 = (bf16[64,512]{1,0:T(8,128)(2,1)S(1)}, bf16[64,512]{1,0:T(8,128)(2,1)S(1)}, u32[]{:S(2)}, u32[]{:S(2)}) collective-permute-start(bf16[64,512]{1,0:T(8,128)(2,1)S(1)} %fusion.1.q_ref), channel_id=1, source_target_pairs={{0,224},{8,232},{16,240},{24,248},{32,0},{40,8},{48,16},{56,24},{6... | collective-permute-start | bytes 196616 | tf_op jit(solution)/shard_map/ppermute | solution.py:465
  20.0 6.2 %attend_0_0.1 = (f32[512,512]{1,0:T(8,128)}, f32[512,128]{1,0:T(8,128)}) custom-call(s32[1]{0:T(128)} %bitcast.me_ref.refs_0_, s32[7]{0:T(128)} %refs_1_.9, bf16[512,512]{1,0:T(8,128)(2,1)} %refs_2_.9, bf16[2,512,128]{2,1,0:T(8,128)(2,1)} %refs_0_.1, bf16[2,512,128]{2,1,0:T(8,128)(2,1)S(1)} %collective-permute-done.2.refs_4_.refs_1_), custom_call_target="tpu_custom_call" | custom-call | flops 1073741824 | bytes 4194304 | tf_op jit(solution)/shard_map/attend_0_0/pallas_call | solution.py:326
  28.5 11.3 %collective-permute-done.6.refs_3_.refs_4_ = bf16[2,512,128]{2,1,0:T(8,128)(2,1)S(1)} collective-permute-done((bf16[2,512,128]{2,1,0:T(8,128)(2,1)S(1)}, bf16[2,512,128]{2,1,0:T(8,128)(2,1)S(1)}, u32[]{:S(2)}, u32[]{:S(2)}) %collective-permute-start.6) | collective-permute-done | bytes 262176 | tf_op jit(solution)/shard_map/ppermute | solution.py:459
  39.8 3.0 %picked.1 = f32[64,512]{1,0:T(8,128)S(1)} custom-call(s32[1]{0:T(128)} %bitcast.me_ref.refs_0_, s32[7]{0:T(128)} %refs_1_.9, s32[7,32]{1,0:T(8,128)} %steps_hbm.3, bf16[64,512]{1,0:T(8,128)(2,1)S(1)} %fusion.1.q_ref, bf16[64,512]{1,0:T(8,128)(2,1)S(1)} %collective-permute-done.4.q1_ref, bf16[64,512]{1,0:T(8,128)(2,1)S(1)} %collective-permute-done.5.q2_ref, ...), custom_call_target="tpu_custom_call" | custom-call | tf_op jit(solution)/shard_map/picked/pallas_call | solution.py:356
  42.8 1.7 %collective-permute-start.11 = (bf16[2,512,128]{2,1,0:T(8,128)(2,1)S(1)}, bf16[2,512,128]{2,1,0:T(8,128)(2,1)}, u32[]{:S(2)}, u32[]{:S(2)}) collective-permute-start(bf16[2,512,128]{2,1,0:T(8,128)(2,1)S(1)} %collective-permute-done.7), channel_id=1, source_target_pairs={{0,16},{8,24},{16,0},{24,8},{32,48},{40,56},{48,32},{56,40},{64,80... | collective-permute-start | bytes 786440 | tf_op jit(solution)/shard_map/ppermute | solution.py:459
  45.3 4.3 %all-to-all-start = ((f16[8,64,512]{2,1,0:T(8,128)(2,1)}), f16[8,64,512]{2,1,0:T(8,128)(2,1)}, u32[]{:S(2)}, u32[]{:S(2)}) async-start(f16[8,64,512]{2,1,0:T(8,128)(2,1)} %broadcast_in_dim.4), calls=%async_computation | async-start | bytes 1048576 | tf_op jit(solution)/shard_map/all_to_all | solution.py:546
  53.7 13.9 %all-to-all-done = f16[8,64,512]{2,1,0:T(8,128)(2,1)} async-done(((f16[8,64,512]{2,1,0:T(8,128)(2,1)}), f16[8,64,512]{2,1,0:T(8,128)(2,1)}, u32[]{:S(2)}, u32[]{:S(2)}) %all-to-all-start) | async-done | bytes 524320 | tf_op jit(solution)/shard_map/all_to_all | solution.py:546
  68.9 2.0 %project.1 = f32[64,1024]{1,0:T(8,128)S(1)} custom-call(f32[8,64,512]{2,1,0:T(8,128)S(1)} %convert_element_type.22.got_ref, bf16[512,256]{1,0:T(8,128)(2,1)S(1)} %copy-done, bf16[512,256]{1,0:T(8,128)(2,1)S(1)} %collective-permute-done.8.refs_1_, bf16[512,256]{1,0:T(8,128)(2,1)S(1)} %collective-permute-done.9.refs_2_, ...), custom_call_target="tpu_custom_call" | custom-call | tf_op jit(solution)/shard_map/project/pallas_call | solution.py:356
  72.2 3.0 %collective-permute-done.13 = f16[64,1024]{1,0:T(8,128)(2,1)S(1)} collective-permute-done((f16[64,1024]{1,0:T(8,128)(2,1)S(1)}, f16[64,1024]{1,0:T(8,128)(2,1)S(1)}, u32[]{:S(2)}, u32[]{:S(2)}) %collective-permute-start.13) | collective-permute-done | bytes 131104 | tf_op jit(solution)/shard_map/ppermute | solution.py:459
  75.3 2.8 %collective-permute-start.14 = (f16[64,1024]{1,0:T(8,128)(2,1)S(1)}, f16[64,1024]{1,0:T(8,128)(2,1)S(1)}, u32[]{:S(2)}, u32[]{:S(2)}) collective-permute-start(f16[64,1024]{1,0:T(8,128)(2,1)S(1)} %add.21), channel_id=1, source_target_pairs={{0,4},{1,5},{2,6},{3,7},{4,0},{5,1},{6,2},{7,3},{8,12},{9,13},{10,... | collective-permute-start | bytes 393224 | tf_op jit(solution)/shard_map/ppermute | solution.py:459
  78.1 3.3 %collective-permute-start.18 = (bf16[1248,256]{1,0:T(8,128)(2,1)S(1)}, bf16[1248,256]{1,0:T(8,128)(2,1)S(1)}, u32[]{:S(2)}, u32[]{:S(2)}) collective-permute-start(bf16[1248,256]{1,0:T(8,128)(2,1)S(1)} %constant_dynamic-update-slice_fusion.refs_0_), channel_id=1, source_target_pairs={{0,8},{8,0},{16,24},{24,16},{32,40},{40,32},{48,56},{56,48},{64,72... | collective-permute-start | bytes 1916936 | tf_op jit(solution)/shard_map/ppermute | solution.py:459
  81.5 2.8 %collective-permute-done.15.refs_2_ = bf16[1248,256]{1,0:T(8,128)(2,1)S(1)} collective-permute-done((bf16[1248,256]{1,0:T(8,128)(2,1)S(1)}, bf16[1248,256]{1,0:T(8,128)(2,1)S(1)}, u32[]{:S(2)}, u32[]{:S(2)}) %collective-permute-start.15) | collective-permute-done | bytes 639008 | tf_op jit(solution)/shard_map/ppermute | solution.py:459
  85.6 2.6 %collective-permute-start.16 = (f16[64,1024]{1,0:T(8,128)(2,1)S(1)}, f16[64,1024]{1,0:T(8,128)(2,1)S(1)}, u32[]{:S(2)}, u32[]{:S(2)}) collective-permute-start(f16[64,1024]{1,0:T(8,128)(2,1)S(1)} %add.22), channel_id=1, source_target_pairs={{0,1},{1,0},{2,3},{3,2},{4,5},{5,4},{6,7},{7,6},{8,9},{9,8},{10,11... | collective-permute-start | bytes 393224 | tf_op jit(solution)/shard_map/ppermute | solution.py:459
  89.0 1.8 %collective-permute-done.17.refs_3_ = bf16[4,512,128]{2,1,0:T(8,128)(2,1)S(1)} collective-permute-done((bf16[4,512,128]{2,1,0:T(8,128)(2,1)S(1)}, bf16[4,512,128]{2,1,0:T(8,128)(2,1)S(1)}, u32[]{:S(2)}, u32[]{:S(2)}) %collective-permute-start.17) | collective-permute-done | bytes 524320 | tf_op jit(solution)/shard_map/ppermute | solution.py:465
  92.3 1.8 %inner.1 = f32[64,1024]{1,0:T(8,128)S(1)} custom-call(s32[1]{0:T(128)} %bitcast.me_ref.refs_0_, f32[64,1024]{1,0:T(8,128)S(1)} %add_multiply_fusion.total_ref, bf16[1248,256]{1,0:T(8,128)(2,1)S(1)} %constant_dynamic-update-slice_fusion.refs_0_, bf16[1248,256]{1,0:T(8,128)(2,1)S(1)} %collective-permute-done.18.refs_1_, ...), custom_call_target="tpu_custom_call" | custom-call | tf_op jit(solution)/shard_map/inner/pallas_call | solution.py:356
  94.8 4.3 %all-to-all-start.1 = ((f16[8,8,1024]{2,1,0:T(8,128)(2,1)}), f16[8,8,1024]{2,1,0:T(8,128)(2,1)S(1)}, u32[]{:S(2)}, u32[]{:S(2)}) async-start(f16[8,8,1024]{2,1,0:T(8,128)(2,1)} %fusion), calls=%async_computation.1 | async-start | bytes 262144 | tf_op jit(solution)/shard_map/all_to_all | solution.py:595
  100.9 6.2 %all-to-all-done.1 = f16[8,8,1024]{2,1,0:T(8,128)(2,1)S(1)} async-done(((f16[8,8,1024]{2,1,0:T(8,128)(2,1)}), f16[8,8,1024]{2,1,0:T(8,128)(2,1)S(1)}, u32[]{:S(2)}, u32[]{:S(2)}) %all-to-all-start.1) | async-done | bytes 131104 | tf_op jit(solution)/shard_map/all_to_all | solution.py:595
  108.1 5.2 %all-to-all-start.2 = ((f32[8,1,128]{2,1,0:T(1,128)}), f32[8,1,128]{2,1,0:T(1,128)S(1)}, u32[]{:S(2)}, u32[]{:S(2)}) async-start(f32[8,1,128]{2,1,0:T(1,128)} %hidden.1), calls=%async_computation.2 | async-start | bytes 8192 | tf_op jit(solution)/shard_map/all_to_all | solution.py:607
  113.3 3.7 %attend_2_1.1 = f32[512,512]{1,0:T(8,128)} custom-call(s32[1]{0:T(128)} %bitcast.me_ref.refs_0_, s32[7]{0:T(128)} %refs_1_.9, bf16[512,512]{1,0:T(8,128)(2,1)} %refs_2_.9, bf16[4,512,128]{2,1,0:T(8,128)(2,1)S(1)} %collective-permute-done.20.refs_3_, f32[512,512]{1,0:T(8,128)} %get-tuple-element.127.refs_4_, f32[512,128]{1,0:T(8,128)} %get-tuple-element.128.refs_5_), custom_call_target="tpu_custom_call" | custom-call | flops 1073741824 | bytes 4194304 | tf_op jit(solution)/shard_map/attend_2_1/pallas_call | solution.py:326
  117.0 2.7 %all-to-all-done.2 = f32[8,1,128]{2,1,0:T(1,128)S(1)} async-done(((f32[8,1,128]{2,1,0:T(1,128)}), f32[8,1,128]{2,1,0:T(1,128)S(1)}, u32[]{:S(2)}, u32[]{:S(2)}) %all-to-all-start.2) | async-done | bytes 4128 | tf_op jit(solution)/shard_map/all_to_all | solution.py:607
  119.8 14.3 %all_to_all.20.got_ref = f32[32,1,128]{2,1,0:T(1,128)S(1)} all-to-all(f32[32,1,128]{2,1,0:T(1,128)S(1)} %broadcast_in_dim.5), channel_id=1, replica_groups=mesh['ctx'=32,'head'=8] {'ctx'}, dimensions={0} | all-to-all | bytes 32768 | tf_op jit(solution)/shard_map/all_to_all | solution.py:610
  (69 shorter events, 21.1 us)
Async XLA Ops:
  2.3 4.6 %collective-permute-start = (bf16[128,512]{1,0:T(8,128)(2,1)S(1)}, bf16[128,512]{1,0:T(8,128)(2,1)S(1)}, u32[]{:S(2)}, u32[]{:S(2)}) collective-permute-start(bf16[128,512]{1,0:T(8,128)(2,1)S(1)} %get-tuple-element.69), channel_id=1, source_target_pairs={{0,8},{8,0},{16,24},{24,16},{32,40},{40,32},{48,56},{56,48},{64,72... | collective-permute-start | bytes 393224 | tf_op jit(solution)/shard_map/ppermute | solution.py:459
  5.7 14.3 %collective-permute-start.2 = (bf16[2,512,128]{2,1,0:T(8,128)(2,1)}, bf16[2,512,128]{2,1,0:T(8,128)(2,1)S(1)}, u32[]{:S(2)}, u32[]{:S(2)}) collective-permute-start(bf16[2,512,128]{2,1,0:T(8,128)(2,1)} %refs_0_.1), channel_id=1, source_target_pairs={{0,8},{8,0},{16,24},{24,16},{32,40},{40,32},{48,56},{56,48},{64,72... | collective-permute-start | bytes 786440 | tf_op jit(solution)/shard_map/ppermute | solution.py:459
  5.8 14.2 %collective-permute-start.3 = (bf16[2,512,128]{2,1,0:T(8,128)(2,1)}, bf16[2,512,128]{2,1,0:T(8,128)(2,1)S(1)}, u32[]{:S(2)}, u32[]{:S(2)}) collective-permute-start(bf16[2,512,128]{2,1,0:T(8,128)(2,1)} %refs_0_.1), channel_id=1, source_target_pairs={{0,16},{8,24},{16,0},{24,8},{32,48},{40,56},{48,32},{56,40},{64,80... | collective-permute-start | bytes 786440 | tf_op jit(solution)/shard_map/ppermute | solution.py:459
  5.8 22.7 %collective-permute-start.7 = (bf16[2,512,128]{2,1,0:T(8,128)(2,1)}, bf16[2,512,128]{2,1,0:T(8,128)(2,1)S(1)}, u32[]{:S(2)}, u32[]{:S(2)}) collective-permute-start(bf16[2,512,128]{2,1,0:T(8,128)(2,1)} %refs_0_.1), channel_id=1, source_target_pairs={{0,32},{8,40},{16,48},{24,56},{32,64},{40,72},{48,80},{56,88},{64,... | collective-permute-start | bytes 786440 | tf_op jit(solution)/shard_map/ppermute | solution.py:465
  7.0 7.9 %collective-permute-start.1 = (bf16[64,512]{1,0:T(8,128)(2,1)S(1)}, bf16[64,512]{1,0:T(8,128)(2,1)S(1)}, u32[]{:S(2)}, u32[]{:S(2)}) collective-permute-start(bf16[64,512]{1,0:T(8,128)(2,1)S(1)} %slice_add_fusion), channel_id=1, source_target_pairs={{0,16},{8,24},{16,0},{24,8},{32,48},{40,56},{48,32},{56,40},{64,80... | collective-permute-start | bytes 196616 | tf_op jit(solution)/shard_map/ppermute | solution.py:459
  14.9 11.3 %collective-permute-start.4 = (bf16[64,512]{1,0:T(8,128)(2,1)S(1)}, bf16[64,512]{1,0:T(8,128)(2,1)S(1)}, u32[]{:S(2)}, u32[]{:S(2)}) collective-permute-start(bf16[64,512]{1,0:T(8,128)(2,1)S(1)} %fusion.1.q_ref), channel_id=1, source_target_pairs={{0,224},{8,232},{16,240},{24,248},{32,0},{40,8},{48,16},{56,24},{6... | collective-permute-start | bytes 196616 | tf_op jit(solution)/shard_map/ppermute | solution.py:465
  18.8 7.4 %collective-permute-start.5 = (bf16[64,512]{1,0:T(8,128)(2,1)S(1)}, bf16[64,512]{1,0:T(8,128)(2,1)S(1)}, u32[]{:S(2)}, u32[]{:S(2)}) collective-permute-start(bf16[64,512]{1,0:T(8,128)(2,1)S(1)} %fusion.1.q_ref), channel_id=1, source_target_pairs={{0,192},{8,200},{16,208},{24,216},{32,224},{40,232},{48,240},{56,2... | collective-permute-start | bytes 196616 | tf_op jit(solution)/shard_map/ppermute | solution.py:465
  26.2 23.4 %collective-permute-start.9 = (bf16[512,256]{1,0:T(8,128)(2,1)S(1)}, bf16[512,256]{1,0:T(8,128)(2,1)S(1)}, u32[]{:S(2)}, u32[]{:S(2)}) collective-permute-start(bf16[512,256]{1,0:T(8,128)(2,1)S(1)} %copy-done), channel_id=1, source_target_pairs={{0,16},{8,24},{16,0},{24,8},{32,48},{40,56},{48,32},{56,40},{64,80... | collective-permute-start | bytes 786440 | tf_op jit(solution)/shard_map/ppermute | solution.py:459
  27.7 12.1 %collective-permute-start.6 = (bf16[2,512,128]{2,1,0:T(8,128)(2,1)S(1)}, bf16[2,512,128]{2,1,0:T(8,128)(2,1)S(1)}, u32[]{:S(2)}, u32[]{:S(2)}) collective-permute-start(bf16[2,512,128]{2,1,0:T(8,128)(2,1)S(1)} %collective-permute-done.2.refs_4_.refs_1_), channel_id=1, source_target_pairs={{0,16},{8,24},{16,0},{24,8},{32,48},{40,56},{48,32},{56,40},{64,80... | collective-permute-start | bytes 786440 | tf_op jit(solution)/shard_map/ppermute | solution.py:459
  27.9 23.9 %collective-permute-start.8 = (bf16[512,256]{1,0:T(8,128)(2,1)S(1)}, bf16[512,256]{1,0:T(8,128)(2,1)S(1)}, u32[]{:S(2)}, u32[]{:S(2)}) collective-permute-start(bf16[512,256]{1,0:T(8,128)(2,1)S(1)} %copy-done), channel_id=1, source_target_pairs={{0,8},{8,0},{16,24},{24,16},{32,40},{40,32},{48,56},{56,48},{64,72... | collective-permute-start | bytes 786440 | tf_op jit(solution)/shard_map/ppermute | solution.py:459
  42.8 8.0 %collective-permute-start.11 = (bf16[2,512,128]{2,1,0:T(8,128)(2,1)S(1)}, bf16[2,512,128]{2,1,0:T(8,128)(2,1)}, u32[]{:S(2)}, u32[]{:S(2)}) collective-permute-start(bf16[2,512,128]{2,1,0:T(8,128)(2,1)S(1)} %collective-permute-done.7), channel_id=1, source_target_pairs={{0,16},{8,24},{16,0},{24,8},{32,48},{40,56},{48,32},{56,40},{64,80... | collective-permute-start | bytes 786440 | tf_op jit(solution)/shard_map/ppermute | solution.py:459
  45.3 22.3 %all-to-all-start = ((f16[8,64,512]{2,1,0:T(8,128)(2,1)}), f16[8,64,512]{2,1,0:T(8,128)(2,1)}, u32[]{:S(2)}, u32[]{:S(2)}) async-start(f16[8,64,512]{2,1,0:T(8,128)(2,1)} %broadcast_in_dim.4), calls=%async_computation | async-start | bytes 1048576 | tf_op jit(solution)/shard_map/all_to_all | solution.py:546
  49.7 2.2 %collective-permute-start.10 = (bf16[512,256]{1,0:T(8,128)(2,1)S(1)}, bf16[512,256]{1,0:T(8,128)(2,1)S(1)}, u32[]{:S(2)}, u32[]{:S(2)}) collective-permute-start(bf16[512,256]{1,0:T(8,128)(2,1)S(1)} %collective-permute-done.9.refs_2_), channel_id=1, source_target_pairs={{0,8},{8,0},{16,24},{24,16},{32,40},{40,32},{48,56},{56,48},{64,72... | collective-permute-start | bytes 786440 | tf_op jit(solution)/shard_map/ppermute | solution.py:459
  51.8 16.9 %collective-permute-start.12 = (bf16[4,512,128]{2,1,0:T(8,128)(2,1)S(1)}, bf16[4,512,128]{2,1,0:T(8,128)(2,1)S(1)}, u32[]{:S(2)}, u32[]{:S(2)}) collective-permute-start(bf16[4,512,128]{2,1,0:T(8,128)(2,1)S(1)} %pad_maximum_fusion.refs_5_), channel_id=1, source_target_pairs={{0,8},{8,0},{16,24},{24,16},{32,40},{40,32},{48,56},{56,48},{64,72... | collective-permute-start | bytes 1572872 | tf_op jit(solution)/shard_map/ppermute | solution.py:459
  68.8 15.5 %collective-permute-start.15 = (bf16[1248,256]{1,0:T(8,128)(2,1)S(1)}, bf16[1248,256]{1,0:T(8,128)(2,1)S(1)}, u32[]{:S(2)}, u32[]{:S(2)}) collective-permute-start(bf16[1248,256]{1,0:T(8,128)(2,1)S(1)} %constant_dynamic-update-slice_fusion.refs_0_), channel_id=1, source_target_pairs={{0,16},{8,24},{16,0},{24,8},{32,48},{40,56},{48,32},{56,40},{64,80... | collective-permute-start | bytes 1916936 | tf_op jit(solution)/shard_map/ppermute | solution.py:459
  70.9 4.3 %collective-permute-start.13 = (f16[64,1024]{1,0:T(8,128)(2,1)S(1)}, f16[64,1024]{1,0:T(8,128)(2,1)S(1)}, u32[]{:S(2)}, u32[]{:S(2)}) collective-permute-start(f16[64,1024]{1,0:T(8,128)(2,1)S(1)} %multiply_convert_fusion.1), channel_id=1, source_target_pairs={{0,2},{1,3},{2,0},{3,1},{4,6},{5,7},{6,4},{7,5},{8,10},{9,11},{10,... | collective-permute-start | bytes 393224 | tf_op jit(solution)/shard_map/ppermute | solution.py:459
  75.3 6.2 %collective-permute-start.14 = (f16[64,1024]{1,0:T(8,128)(2,1)S(1)}, f16[64,1024]{1,0:T(8,128)(2,1)S(1)}, u32[]{:S(2)}, u32[]{:S(2)}) collective-permute-start(f16[64,1024]{1,0:T(8,128)(2,1)S(1)} %add.21), channel_id=1, source_target_pairs={{0,4},{1,5},{2,6},{3,7},{4,0},{5,1},{6,2},{7,3},{8,12},{9,13},{10,... | collective-permute-start | bytes 393224 | tf_op jit(solution)/shard_map/ppermute | solution.py:459
  78.1 12.7 %collective-permute-start.17 = (bf16[4,512,128]{2,1,0:T(8,128)(2,1)S(1)}, bf16[4,512,128]{2,1,0:T(8,128)(2,1)S(1)}, u32[]{:S(2)}, u32[]{:S(2)}) collective-permute-start(bf16[4,512,128]{2,1,0:T(8,128)(2,1)S(1)} %pad_maximum_fusion.refs_5_), channel_id=1, source_target_pairs={{0,32},{8,40},{16,48},{24,56},{32,64},{40,72},{48,80},{56,88},{64,... | collective-permute-start | bytes 1572872 | tf_op jit(solution)/shard_map/ppermute | solution.py:465
  78.1 14.2 %collective-permute-start.18 = (bf16[1248,256]{1,0:T(8,128)(2,1)S(1)}, bf16[1248,256]{1,0:T(8,128)(2,1)S(1)}, u32[]{:S(2)}, u32[]{:S(2)}) collective-permute-start(bf16[1248,256]{1,0:T(8,128)(2,1)S(1)} %constant_dynamic-update-slice_fusion.refs_0_), channel_id=1, source_target_pairs={{0,8},{8,0},{16,24},{24,16},{32,40},{40,32},{48,56},{56,48},{64,72... | collective-permute-start | bytes 1916936 | tf_op jit(solution)/shard_map/ppermute | solution.py:459
  84.3 8.0 %collective-permute-start.19 = (bf16[1248,256]{1,0:T(8,128)(2,1)S(1)}, bf16[1248,256]{1,0:T(8,128)(2,1)S(1)}, u32[]{:S(2)}, u32[]{:S(2)}) collective-permute-start(bf16[1248,256]{1,0:T(8,128)(2,1)S(1)} %collective-permute-done.15.refs_2_), channel_id=1, source_target_pairs={{0,8},{8,0},{16,24},{24,16},{32,40},{40,32},{48,56},{56,48},{64,72... | collective-permute-start | bytes 1916936 | tf_op jit(solution)/shard_map/ppermute | solution.py:459
  85.6 6.6 %collective-permute-start.16 = (f16[64,1024]{1,0:T(8,128)(2,1)S(1)}, f16[64,1024]{1,0:T(8,128)(2,1)S(1)}, u32[]{:S(2)}, u32[]{:S(2)}) collective-permute-start(f16[64,1024]{1,0:T(8,128)(2,1)S(1)} %add.22), channel_id=1, source_target_pairs={{0,1},{1,0},{2,3},{3,2},{4,5},{5,4},{6,7},{7,6},{8,9},{9,8},{10,11... | collective-permute-start | bytes 393224 | tf_op jit(solution)/shard_map/ppermute | solution.py:459
  94.8 12.3 %all-to-all-start.1 = ((f16[8,8,1024]{2,1,0:T(8,128)(2,1)}), f16[8,8,1024]{2,1,0:T(8,128)(2,1)S(1)}, u32[]{:S(2)}, u32[]{:S(2)}) async-start(f16[8,8,1024]{2,1,0:T(8,128)(2,1)} %fusion), calls=%async_computation.1 | async-start | bytes 262144 | tf_op jit(solution)/shard_map/all_to_all | solution.py:595
  99.1 9.0 %collective-permute-start.20 = (bf16[4,512,128]{2,1,0:T(8,128)(2,1)S(1)}, bf16[4,512,128]{2,1,0:T(8,128)(2,1)S(1)}, u32[]{:S(2)}, u32[]{:S(2)}) collective-permute-start(bf16[4,512,128]{2,1,0:T(8,128)(2,1)S(1)} %collective-permute-done.17.refs_3_), channel_id=1, source_target_pairs={{0,8},{8,0},{16,24},{24,16},{32,40},{40,32},{48,56},{56,48},{64,72... | collective-permute-start | bytes 1572872 | tf_op jit(solution)/shard_map/ppermute | solution.py:459
  108.1 11.7 %all-to-all-start.2 = ((f32[8,1,128]{2,1,0:T(1,128)}), f32[8,1,128]{2,1,0:T(1,128)S(1)}, u32[]{:S(2)}, u32[]{:S(2)}) async-start(f32[8,1,128]{2,1,0:T(1,128)} %hidden.1), calls=%async_computation.2 | async-start | bytes 8192 | tf_op jit(solution)/shard_map/all_to_all | solution.py:607
  (6 other events, 53.0 us)

commit v2 on v1

--- a/solution.py
+++ b/solution.py
@@ -15,7 +15,8 @@
 STEPS = 32
 PER_GROUP = 4
 BLOCK = 512
-TILE = 256
+TILE = 512
+OWN_TILE = 256
 Z = 8
 PLANE = 4
 PAD = 8
@@ -146,28 +147,29 @@
 def attend_kernel(slots, first, last, *refs):
     n = len(slots)
     arrays = 1 + max(slot[2] for slot in slots)
-    me_ref, lengths_hbm, q_hbm = refs[:3]
+    me_ref, lengths_hbm, q_ref = refs[:3]
     kv_hbm = [refs[3 + array].at[pl.ds(2 * at, 2)] for _, _, array, at in slots]
-    if last:
-        out_hbm = refs[-9]
+    kv_ref, lengths, sems = refs[-3:]
+    if first:
+        q_hbm = q_ref
+        q_ref, m_ref, l_ref, acc_ref = refs[3 + arrays : 7 + arrays]
     else:
-        acc_hbm, ml_hbm = refs[-10:-8]
-    if not first:
-        acc_in, ml_in = refs[3 + arrays : 5 + arrays]
-    q_ref, kv_ref, acc_ref, m_ref, l_ref, ml_ref, lengths, sems = refs[-8:]
-    lengths_copy = pltpu.make_async_copy(lengths_hbm, lengths, sems.at[0])
-    lengths_copy.start()
-    lengths_copy.wait()
+        m_ref, l_ref, acc_ref = refs[3 + arrays : 6 + arrays]
+    copies = [
+        pltpu.make_async_copy(kv, kv_ref.at[k], sems.at[k]) for k, kv in enumerate(kv_hbm)
+    ]
+    copies.append(pltpu.make_async_copy(lengths_hbm, lengths, sems.at[n]))
+    if first:
+        copies.append(pltpu.make_async_copy(q_hbm, q_ref, sems.at[n + 1]))
+    for copy in copies:
+        copy.start()
+    for copy in copies:
+        copy.wait()
     me = me_ref[0]
     place = me % PLANE
     row0 = me * BLOCK
     ones = jnp.ones((BLOCK, HD), BF16)
     blocks = [me - place - back * PLANE + (place ^ flip) for back, flip, _, _ in slots]
-    earliest = first_key(row0, lengths)
-    active = [(block < me) & ((block + 1) * BLOCK > earliest) for block in blocks]
-
-    def copy_in(source, target, k):
-        return pltpu.make_async_copy(source, target, sems.at[k])
 
     def weigh(rows, count, keys, ext, mask, fresh):
         q = q_ref[rows, :]
@@ -196,20 +198,19 @@
                 acc_ref[rows, cols] = acc_ref[rows, cols] * scale + pv[:, :HD]
                 l_ref[rows, cols] = l_ref[rows, cols] * scale + pv[:, HD:]
 
-    def own_block(kv):
-        for tile in range(BLOCK // TILE):
-            width = (tile + 1) * TILE
-            rows = slice(tile * TILE, width)
-            keys = kv[0, :width, :]
-            ext = jnp.concatenate([kv[1, :width, :], ones[:width]], axis=1)
-            q_pos = row0 + tile * TILE + lax.broadcasted_iota(jnp.int32, (TILE, width), 0)
-            k_pos = row0 + lax.broadcasted_iota(jnp.int32, (TILE, width), 1)
-            starts = first_key(
-                row0 + tile * TILE + lax.broadcasted_iota(jnp.int32, (TILE, HD), 0), lengths
-            )
+    def own_block():
+        for tile in range(BLOCK // OWN_TILE):
+            width = (tile + 1) * OWN_TILE
+            rows = slice(tile * OWN_TILE, width)
+            keys = kv_ref[0, 0, :width, :]
+            ext = jnp.concatenate([kv_ref[0, 1, :width, :], ones[:width]], axis=1)
+            shape = (OWN_TILE, width)
+            q_pos = row0 + tile * OWN_TILE + lax.broadcasted_iota(jnp.int32, shape, 0)
+            k_pos = row0 + lax.broadcasted_iota(jnp.int32, shape, 1)
+            starts = first_key(q_pos[:, :HD], lengths)
             starts = jnp.concatenate([starts] * (width // HD), axis=1)
             mask = (k_pos <= q_pos) & (k_pos >= starts)
-            weigh(rows, TILE, keys, ext, mask, True)
+            weigh(rows, OWN_TILE, keys, ext, mask, True)
 
     def other_tile(index, carry):
         tile, k = index % (BLOCK // TILE), index // (BLOCK // TILE)
@@ -241,111 +242,54 @@
         pl.when(some & jnp.logical_not(every))(functools.partial(run, True))
         return carry
 
-    def load_state():
-        copies = [copy_in(acc_in, acc_ref, n), copy_in(ml_in, ml_ref, n + 1)]
-        for copy in copies:
-            copy.start()
-        return copies
-
-    def spread_state(copies):
-        for copy in copies:
-            copy.wait()
-        for h in range(PER_GROUP):
-            cols = slice(h * HD, (h + 1) * HD)
-            m_ref[:, cols] = jnp.broadcast_to(ml_ref[:, h : h + 1], (BLOCK, HD))
-            at = PER_GROUP + h
-            l_ref[:, cols] = jnp.broadcast_to(ml_ref[:, at : at + 1], (BLOCK, HD))
-
-    def store_state():
-        lanes = lax.broadcasted_iota(jnp.int32, (BLOCK, HD), 1)
-        ml = jnp.zeros((BLOCK, HD), F32)
-        for h in range(PER_GROUP):
-            cols = slice(h * HD, (h + 1) * HD)
-            ml = jnp.where(lanes == h, m_ref[:, cols], ml)
-            ml = jnp.where(lanes == PER_GROUP + h, l_ref[:, cols], ml)
-        ml_ref[...] = ml
-        copies = [copy_in(acc_ref, acc_hbm, n), copy_in(ml_ref, ml_hbm, n + 1)]
-        for copy in copies:
-            copy.start()
-        for copy in copies:
-            copy.wait()
-
-    def work(loaded):
-        q_copy = copy_in(q_hbm, q_ref, n + 2)
-        q_copy.start()
-        copies = [copy_in(kv, kv_ref.at[k], k) for k, kv in enumerate(kv_hbm)]
-        for copy in copies:
-            copy.start()
-        if loaded:
-            spread_state(loaded)
-        q_copy.wait()
-        for copy in copies:
-            copy.wait()
-        if first:
-            own_block(kv_ref.at[0])
-        lax.fori_loop((BLOCK // TILE) * int(first), (BLOCK // TILE) * n, other_tile, 0)
-
-    some = functools.reduce(jnp.logical_or, active)
     if first:
-        work(None)
-        store_state()
-    elif last:
-        loaded = load_state()
-
-        @pl.when(some)
-        def _():
-            work(loaded)
-
-        @pl.when(jnp.logical_not(some))
-        def _():
-            spread_state(loaded)
-
-        acc_ref[...] = acc_ref[...] / l_ref[...]
-        copy = copy_in(acc_ref, out_hbm, n)
-        copy.start()
-        copy.wait()
+        own_block()
+    tiles = BLOCK // TILE
+    lax.fori_loop(tiles * int(first), tiles * n, other_tile, 0)
+    if last:
+        out_ref = refs[-4]
+        out_ref[...] = acc_ref[...] / l_ref[...]
+
+
+def attend(slots, me, lengths, queries, kvs, state, last=False):
+    shape = (BLOCK, PER_GROUP * HD)
+    first = state is None
+    operands = [me, *pinned([lengths, queries] if first else [lengths]), *kvs]
+    specs = [SMEM] + [HBM] * (len(operands) - 1)
+    if not first:
+        q, *sums = [pltpu.with_memory_space_constraint(x, pltpu.VMEM) for x in state]
+        operands[2:2] = [q]
+        specs[2:2] = [VMEM]
+        at = len(operands)
+        operands += sums
+        specs += [VMEM] * 3
+    if last:
+        shapes, aliases = (jax.ShapeDtypeStruct(shape, F32),), {}
+    elif first:
+        shapes, aliases = (pltpu.VMEM(shape, BF16),) + (pltpu.VMEM(shape, F32),) * 3, {}
     else:
-
-        @pl.when(some)
-        def _():
-            work(load_state())
-            store_state()
-
-
-def attend(slots, me, lengths, queries, kvs, state, last=False):
-    heads = pltpu.HBM((BLOCK, PER_GROUP * HD), F32)
-    sizes = pltpu.HBM((BLOCK, HD), F32)
-    operands = [me, *pinned([lengths, queries]), *kvs]
-    aliases = {}
-    if state is not None:
-        if not last:
-            aliases = {len(operands): 0, len(operands) + 1: 1}
-        operands += pinned(state)
-    shapes = (heads,) if last else (heads, sizes)
+        shapes, aliases = (pltpu.VMEM(shape, F32),) * 3, {at + k: k for k in range(3)}
     work = PER_GROUP * BLOCK * BLOCK * len(slots)
     got = pl.pallas_call(
-        functools.partial(attend_kernel, slots, state is None, last),
+        functools.partial(attend_kernel, slots, first, last),
         out_shape=shapes,
-        in_specs=[SMEM] + [HBM] * (len(operands) - 1),
-        out_specs=[HBM] * len(shapes),
+        in_specs=specs,
+        out_specs=[VMEM] * len(shapes),
         scratch_shapes=[
-            pltpu.VMEM((BLOCK, PER_GROUP * HD), BF16),
             pltpu.VMEM((len(slots), 2, BLOCK, HD), BF16),
-            pltpu.VMEM((BLOCK, PER_GROUP * HD), F32),
-            pltpu.VMEM((BLOCK, PER_GROUP * HD), F32),
-            pltpu.VMEM((BLOCK, PER_GROUP * HD), F32),
-            pltpu.VMEM((BLOCK, HD), F32),
             pltpu.SMEM((TRACES,), jnp.int32),
-            pltpu.SemaphoreType.DMA((len(slots) + 3,)),
+            pltpu.SemaphoreType.DMA((len(slots) + 2,)),
         ],
         input_output_aliases=aliases,
         compiler_params=pltpu.CompilerParams(vmem_limit_bytes=32 << 20),
         cost_estimate=pl.CostEstimate(
-            flops=4 * HD * work, bytes_accessed=4 << 20, transcendentals=work
+            flops=4 * HD * work, bytes_accessed=1 << 20, transcendentals=work
         ),
         name="attend_%d_%d" % slots[0][:2],
     )(*operands)
-    return got[0] if last else got
+    if last:
+        return got[0]
+    return list(got) if first else [q, *got]
 
 
 def pinned(values):
@@ -500,14 +444,15 @@
         name="pick",
     )
     arrived = swapped(sent, "ctx", 1)
-    across0 = swapped(kv0, "ctx", 2)
-    core0y = swapped(core0, "ctx", 2)
     across = swapped(passed + arrived[GROUP:], "ctx", 2)
     wanted = keep + arrived[:GROUP] + across
+    wanted, kv0y, core0 = tie(wanted, kv0, core0)
     wanted1, wanted2 = raised(wanted, -1), raised(wanted, -2)
-    wanted, own_kv, core0, across0 = tie(wanted, kv0, core0, across0)
-    state = add([(0, 0, 0, 0), (0, 1, 1, 0)], kvs=[pinned([own_kv])[0], core0], state=None)
-    wanted, wanted1, wanted2, state = tie(wanted, wanted1, wanted2, state)
+    across0 = swapped(kv0y, "ctx", 2)
+    across0, wanted1 = tie(across0, wanted1)
+    core0y = swapped(across0, "ctx", 1)
+    state = add([(0, 0, 0, 0), (0, 1, 1, 0)], kvs=[pinned([kv0y])[0], core0], state=None)
+    wanted, wanted1, wanted2, *state = tie(wanted, wanted1, wanted2, *state)
 
     weight, wanted = tie(out_weight, wanted)
     firsts = [weight, swapped(weight, "ctx", 1), swapped(weight, "ctx", 2)]
@@ -540,7 +485,7 @@
         ],
         name="picked",
     )
-    parts, state, kv1, across0, core0y = tie(parts, state, kv1, across0, core0y)
+    parts, kv1, across0, core0y, *state = tie(parts, kv1, across0, core0y, *state)
     across1 = swapped(kv1, "ctx", 2)
     parts = jnp.broadcast_to(parts.astype(jnp.float16)[None], (Z, GROUP, half))
     parts = lax.all_to_all(parts, "ctx", 0, 0, axis_index_groups=columns).astype(F32)
@@ -552,7 +497,7 @@
         kvs=[across0, core0y, pair1],
         state=state,
     )
-    parts, state, pair1, cores1, pack = tie(parts, state, pair1, cores1, pack)
+    parts, pair1, cores1, pack, *state = tie(parts, pair1, cores1, pack, *state)
     packs = [pack, swapped(pack, "ctx", 1), swapped(pack, "ctx", 2)]
 
     projected = small_call(
@@ -574,7 +519,7 @@
     packs.append(swapped(packs[2], "ctx", 1))
     other = swapped(projected, "head", 1)
     state = add([(1, 1, 0, 0), (1, 3, 0, 1)], kvs=[cores1], state=state)
-    other, state, pair2 = tie(other, state, pair2)
+    other, pair2, *state = tie(other, pair2, *state)
     cores2 = swapped(pair2, "ctx", 1)
     projected = (projected.astype(F32) + other.astype(F32)) * 4.0
 
@@ -589,11 +534,11 @@
         ],
         name="inner",
     )
-    inner, state, pair2 = tie(inner, state, pair2)
+    inner, pair2, *state = tie(inner, pair2, *state)
     inner = (inner * 2.0**-10).astype(jnp.float16).reshape(Z, PAD, WIDE)
     state = add([(2, 0, 0, 0), (2, 2, 0, 1)], kvs=[pair2], state=state)
     inner = lax.all_to_all(inner, "ctx", 0, 0, axis_index_groups=columns)
-    inner, state = tie(inner, state)
+    inner, *state = tie(inner, *state)
     inner = jnp.sum(inner.astype(F32), axis=0) * 2.0**10
     heads, count = lax.axis_size("head"), lax.axis_size("ctx")
     gap = small_call(
@@ -602,7 +547,7 @@
         [inner, class_weight],
         name="hidden",
     )
-    gap, state, cores2 = tie(gap, state, cores2)
+    gap, cores2, *state = tie(gap, cores2, *state)
     attended = add([(2, 1, 0, 0), (2, 3, 0, 1)], kvs=[cores2], state=state, last=True)
     gap = lax.all_to_all(gap, "head", 0, 0)
     gap, attended = tie(gap, attended)

time: 136 us -> 121 us (0.89)
  waiting for transfers between devices: 50.8 us -> 27.7 us
  local copies, waits for them, and re-layouts: 1.17 us -> 8.84 us
  Pallas kernels: 22.7 us -> 20.2 us
  starting transfers between devices: 42.3 us -> 44 us
    ppermute x17, waiting for transfers between devices: 26.3 us -> 9.21 us  [swapped(): return lax.ppermute(value, axis, [(s, s ^ bit) for s in range(count)])]
    unnamed x17 -> x49, local copies, waits for them, and re-layouts: 0.31 us -> 7.31 us
    all_to_all x1, waiting for transfers between devices: 6.18 us -> 2.66 us  [per_device(): inner = lax.all_to_all(inner, 'ctx', 0, 0, axis_index_groups=columns)]
    all_to_all x1, waiting for transfers between devices: 13.9 us -> 10.6 us  [per_device(): lax.all_to_all(parts, 'ctx', 0, 0, axis_index_groups=columns).astype(F32)]
    pallas_call x5, Pallas kernels: 12.1 us -> 9.63 us  [attend(): pl.pallas_call(functools.partial(attend_kernel, slots, first, last), out_...]
  transfers between devices with their start and end apart: 24 -> 24, of which waited for: 10 -> 10; matrix products, arithmetic and copies ran while one was open for 3% -> 6% of each run, Pallas kernels for 13% -> 13%
where the time goes in v2:
time: 121 us; the launch traced here: 120 us
  starting transfers between devices  44 us (36%)
  waiting for transfers between devices  27.7 us (23%)
  Pallas kernels  20.2 us (17%)
  blocking collectives  14.3 us (12%)
  local copies, waits for them, and re-layouts  8.84 us (7%)
  other arithmetic  4.13 us (3%)
    ppermute x17, starting transfers between devices, swapped(): return lax.ppermute(value, axis, [(s, s ^ bit) for s in range(count)])  23.1 us
    all_to_all x1, blocking collectives, per_device(): lax.all_to_all(jnp.broadcast_to(gap[None], (count, 1, HD)), 'ctx', 0, 0)  14.3 us
    all_to_all x1, waiting for transfers between devices, per_device(): lax.all_to_all(parts, 'ctx', 0, 0, axis_index_groups=columns).astype(F32)  10.6 us
    pallas_call x6, Pallas kernels, small_call(): pl.pallas_call(kernel, out_shape=shape, in_specs=specs or [VMEM] * len(op...  10.6 us
    pallas_call x5, Pallas kernels, attend(): pl.pallas_call(functools.partial(attend_kernel, slots, first, last), out_...  9.63 us
    ppermute x17, waiting for transfers between devices, swapped(): return lax.ppermute(value, axis, [(s, s ^ bit) for s in range(count)])  9.21 us
    unnamed x49, local copies, waits for them, and re-layouts  7.31 us
    ppermute x4, starting transfers between devices, raised(): lax.ppermute(value, 'ctx', [(s, (s + steps) % count) for s in range(count)])  7.23 us
  transfers between devices with their start and end apart: 24, of which 10 were waited for; matrix products, arithmetic and copies ran while one was open for 6% of the time, Pallas kernels for 13%

profile of v2, /device:TPU:1, one launch (start us, length us, event | category | flops | bytes accessed | tf_op | source)
XLA Modules:
  0.0 120.3 jit_solution(5147680786934256678)
XLA Ops:
  0.6 1.7 %pick.1 = (bf16[64,512]{1,0:T(8,128)(2,1)S(1)}, bf16[64,512]{1,0:T(8,128)(2,1)S(1)}, bf16[128,512]{1,0:T(8,128)(2,1)S(1)}) custom-call(s32[1]{0:T(128)} %bitcast.me_ref.refs_0_, s32[7,32]{1,0:T(8,128)} %steps_hbm.3, bf16[512,512]{1,0:T(8,128)(2,1)} %refs_2_.1), custom_call_target="tpu_custom_call" | custom-call | tf_op jit(solution)/shard_map/pick/pallas_call | solution.py:300
  2.3 3.3 %collective-permute-start = (bf16[128,512]{1,0:T(8,128)(2,1)S(1)}, bf16[128,512]{1,0:T(8,128)(2,1)S(1)}, u32[]{:S(2)}, u32[]{:S(2)}) collective-permute-start(bf16[128,512]{1,0:T(8,128)(2,1)S(1)} %get-tuple-element.89), channel_id=1, source_target_pairs={{0,8},{8,0},{16,24},{24,16},{32,40},{40,32},{48,56},{56,48},{64,72... | collective-permute-start | bytes 393224 | tf_op jit(solution)/shard_map/ppermute | solution.py:403
  11.4 4.7 %collective-permute-start.4 = (bf16[64,512]{1,0:T(8,128)(2,1)S(1)}, bf16[64,512]{1,0:T(8,128)(2,1)S(1)}, u32[]{:S(2)}, u32[]{:S(2)}) collective-permute-start(bf16[64,512]{1,0:T(8,128)(2,1)S(1)} %fusion.1.q_ref), channel_id=1, source_target_pairs={{0,224},{8,232},{16,240},{24,248},{32,0},{40,8},{48,16},{56,24},{6... | collective-permute-start | bytes 196616 | tf_op jit(solution)/shard_map/ppermute | solution.py:409
  17.3 4.2 %attend_0_0.1 = (bf16[512,512]{1,0:T(8,128)(2,1)S(1)}, f32[512,512]{1,0:T(8,128)S(1)}, f32[512,512]{1,0:T(8,128)S(1)}, f32[512,512]{1,0:T(8,128)S(1)}) custom-call(s32[1]{0:T(128)} %bitcast.me_ref.refs_0_, s32[7]{0:T(128)} %refs_1_.9, bf16[512,512]{1,0:T(8,128)(2,1)} %refs_2_.1, bf16[2,512,128]{2,1,0:T(8,128)(2,1)} %refs_0_.1, ...), custom_call_target="tpu_custom_call" | custom-call | flops 1073741824 | bytes 1048576 | tf_op jit(solution)/shard_map/attend_0_0/pallas_call | solution.py:273
  21.5 1.9 %collective-permute-start.6 = (bf16[2,512,128]{2,1,0:T(8,128)(2,1)S(1)}, bf16[2,512,128]{2,1,0:T(8,128)(2,1)S(1)}, u32[]{:S(2)}, u32[]{:S(2)}) collective-permute-start(bf16[2,512,128]{2,1,0:T(8,128)(2,1)S(1)} %collective-permute-done.3.refs_2_.refs_3_), channel_id=1, source_target_pairs={{0,8},{8,0},{16,24},{24,16},{32,40},{40,32},{48,56},{56,48},{64,72... | collective-permute-start | bytes 786440 | tf_op jit(solution)/shard_map/ppermute | solution.py:403
  24.6 3.1 %picked.1 = f32[64,512]{1,0:T(8,128)S(1)} custom-call(s32[1]{0:T(128)} %bitcast.me_ref.refs_0_, s32[7]{0:T(128)} %refs_1_.9, s32[7,32]{1,0:T(8,128)} %steps_hbm.3, bf16[64,512]{1,0:T(8,128)(2,1)S(1)} %fusion.1.q_ref, bf16[64,512]{1,0:T(8,128)(2,1)S(1)} %collective-permute-done.4.q1_ref, bf16[64,512]{1,0:T(8,128)(2,1)S(1)} %collective-permute-done.5.q2_ref, ...), custom_call_target="tpu_custom_call" | custom-call | tf_op jit(solution)/shard_map/picked/pallas_call | solution.py:300
  30.2 4.1 %all-to-all-start = ((f16[8,64,512]{2,1,0:T(8,128)(2,1)}), f16[8,64,512]{2,1,0:T(8,128)(2,1)}, u32[]{:S(2)}, u32[]{:S(2)}) async-start(f16[8,64,512]{2,1,0:T(8,128)(2,1)} %broadcast_in_dim.4), calls=%async_computation | async-start | bytes 1048576 | tf_op jit(solution)/shard_map/all_to_all | solution.py:491
  37.5 2.0 %pad_maximum_fusion.refs_5_ = bf16[4,512,128]{2,1,0:T(8,128)(2,1)} fusion(bf16[2,512,128]{2,1,0:T(8,128)(2,1)} %collective-permute-done.11, bf16[2,512,128]{2,1,0:T(8,128)(2,1)} %collective-permute-done.7), kind=kLoop, calls=%fused_computation | loop fusion | flops 262144 | bytes 1048576 | tf_op jit(solution)/shard_map/concatenate | solution.py:492
  41.8 10.6 %all-to-all-done = f16[8,64,512]{2,1,0:T(8,128)(2,1)} async-done(((f16[8,64,512]{2,1,0:T(8,128)(2,1)}), f16[8,64,512]{2,1,0:T(8,128)(2,1)}, u32[]{:S(2)}, u32[]{:S(2)}) %all-to-all-start) | async-done | bytes 524320 | tf_op jit(solution)/shard_map/all_to_all | solution.py:491
  54.3 2.0 %project.1 = f32[64,1024]{1,0:T(8,128)S(1)} custom-call(f32[8,64,512]{2,1,0:T(8,128)S(1)} %convert_element_type.22.got_ref, bf16[512,256]{1,0:T(8,128)(2,1)S(1)} %copy-done.9, bf16[512,256]{1,0:T(8,128)(2,1)} %collective-permute-done.8.refs_1_, bf16[512,256]{1,0:T(8,128)(2,1)} %collective-permute-done.9.refs_2_, bf16[512,256]{1,0:T(8,128)(2,1)S(1)} %copy-done.11), custom_call_target="tpu_custom_call" | custom-call | tf_op jit(solution)/shard_map/project/pallas_call | solution.py:300
  57.6 3.0 %collective-permute-done.13 = f16[64,1024]{1,0:T(8,128)(2,1)S(1)} collective-permute-done((f16[64,1024]{1,0:T(8,128)(2,1)S(1)}, f16[64,1024]{1,0:T(8,128)(2,1)S(1)}, u32[]{:S(2)}, u32[]{:S(2)}) %collective-permute-start.13) | collective-permute-done | bytes 131104 | tf_op jit(solution)/shard_map/ppermute | solution.py:403
  60.7 2.8 %collective-permute-start.14 = (f16[64,1024]{1,0:T(8,128)(2,1)S(1)}, f16[64,1024]{1,0:T(8,128)(2,1)S(1)}, u32[]{:S(2)}, u32[]{:S(2)}) collective-permute-start(f16[64,1024]{1,0:T(8,128)(2,1)S(1)} %add.21), channel_id=1, source_target_pairs={{0,4},{1,5},{2,6},{3,7},{4,0},{5,1},{6,2},{7,3},{8,12},{9,13},{10,... | collective-permute-start | bytes 393224 | tf_op jit(solution)/shard_map/ppermute | solution.py:403
  63.5 2.9 %collective-permute-start.18 = (bf16[1248,256]{1,0:T(8,128)(2,1)S(1)}, bf16[1248,256]{1,0:T(8,128)(2,1)S(1)}, u32[]{:S(2)}, u32[]{:S(2)}) collective-permute-start(bf16[1248,256]{1,0:T(8,128)(2,1)S(1)} %copy-done.6), channel_id=1, source_target_pairs={{0,8},{8,0},{16,24},{24,16},{32,40},{40,32},{48,56},{56,48},{64,72... | collective-permute-start | bytes 1916936 | tf_op jit(solution)/shard_map/ppermute | solution.py:403
  66.5 2.7 %collective-permute-done.15.refs_2_ = bf16[1248,256]{1,0:T(8,128)(2,1)S(1)} collective-permute-done((bf16[1248,256]{1,0:T(8,128)(2,1)S(1)}, bf16[1248,256]{1,0:T(8,128)(2,1)S(1)}, u32[]{:S(2)}, u32[]{:S(2)}) %collective-permute-start.15) | collective-permute-done | bytes 639008 | tf_op jit(solution)/shard_map/ppermute | solution.py:403
  70.6 2.6 %collective-permute-start.16 = (f16[64,1024]{1,0:T(8,128)(2,1)S(1)}, f16[64,1024]{1,0:T(8,128)(2,1)S(1)}, u32[]{:S(2)}, u32[]{:S(2)}) collective-permute-start(f16[64,1024]{1,0:T(8,128)(2,1)S(1)} %add.22), channel_id=1, source_target_pairs={{0,1},{1,0},{2,3},{3,2},{4,5},{5,4},{6,7},{7,6},{8,9},{9,8},{10,11... | collective-permute-start | bytes 393224 | tf_op jit(solution)/shard_map/ppermute | solution.py:403
  74.3 2.1 %collective-permute-done.17.refs_3_ = bf16[4,512,128]{2,1,0:T(8,128)(2,1)S(1)} collective-permute-done((bf16[4,512,128]{2,1,0:T(8,128)(2,1)}, bf16[4,512,128]{2,1,0:T(8,128)(2,1)S(1)}, u32[]{:S(2)}, u32[]{:S(2)}) %collective-permute-start.17) | collective-permute-done | bytes 524320 | tf_op jit(solution)/shard_map/ppermute | solution.py:409
  77.3 1.8 %inner.1 = f32[64,1024]{1,0:T(8,128)S(1)} custom-call(s32[1]{0:T(128)} %bitcast.me_ref.refs_0_, f32[64,1024]{1,0:T(8,128)S(1)} %add_multiply_fusion.total_ref, bf16[1248,256]{1,0:T(8,128)(2,1)S(1)} %copy-done.6, bf16[1248,256]{1,0:T(8,128)(2,1)S(1)} %collective-permute-done.18.refs_1_, bf16[1248,256]{1,0:T(8,128)(2,1)S(1)} %collective-permute-done.15.refs_2_, ...), custom_call_target="tpu_custom_call" | custom-call | tf_op jit(solution)/shard_map/inner/pallas_call | solution.py:300
  79.7 3.5 %all-to-all-start.1 = ((f16[8,8,1024]{2,1,0:T(8,128)(2,1)}), f16[8,8,1024]{2,1,0:T(8,128)(2,1)S(1)}, u32[]{:S(2)}, u32[]{:S(2)}) async-start(f16[8,8,1024]{2,1,0:T(8,128)(2,1)} %fusion), calls=%async_computation.1 | async-start | bytes 262144 | tf_op jit(solution)/shard_map/all_to_all | solution.py:540
  83.2 2.2 %collective-permute-start.20 = (bf16[4,512,128]{2,1,0:T(8,128)(2,1)}, bf16[4,512,128]{2,1,0:T(8,128)(2,1)}, u32[]{:S(2)}, u32[]{:S(2)}) collective-permute-start(bf16[4,512,128]{2,1,0:T(8,128)(2,1)} %copy-done.7), channel_id=1, source_target_pairs={{0,8},{8,0},{16,24},{24,16},{32,40},{40,32},{48,56},{56,48},{64,72... | collective-permute-start | bytes 1572872 | tf_op jit(solution)/shard_map/ppermute | solution.py:403
  88.5 2.7 %all-to-all-done.1 = f16[8,8,1024]{2,1,0:T(8,128)(2,1)S(1)} async-done(((f16[8,8,1024]{2,1,0:T(8,128)(2,1)}), f16[8,8,1024]{2,1,0:T(8,128)(2,1)S(1)}, u32[]{:S(2)}, u32[]{:S(2)}) %all-to-all-start.1) | async-done | bytes 131104 | tf_op jit(solution)/shard_map/all_to_all | solution.py:540
  92.1 6.1 %all-to-all-start.2 = ((f32[8,1,128]{2,1,0:T(1,128)}), f32[8,1,128]{2,1,0:T(1,128)S(1)}, u32[]{:S(2)}, u32[]{:S(2)}) async-start(f32[8,1,128]{2,1,0:T(1,128)} %hidden.1), calls=%async_computation.2 | async-start | bytes 8192 | tf_op jit(solution)/shard_map/all_to_all | solution.py:552
  99.2 2.2 %attend_2_1.1 = f32[512,512]{1,0:T(8,128)} custom-call(s32[1]{0:T(128)} %bitcast.me_ref.refs_0_, s32[7]{0:T(128)} %refs_1_.9, bf16[512,512]{1,0:T(8,128)(2,1)S(1)} %copy-done.4, bf16[4,512,128]{2,1,0:T(8,128)(2,1)} %collective-permute-done.20.refs_3_, f32[512,512]{1,0:T(8,128)S(1)} %get-tuple-element.166.refs_4_, f32[512,512]{1,0:T(8,128)S(1)} %get-tuple-element.167.refs_5_, ...), custom_call_target="tpu_custom_call" | custom-call | flops 1073741824 | bytes 1048576 | tf_op jit(solution)/shard_map/attend_2_1/pallas_call | solution.py:273
  101.5 3.1 %all-to-all-done.2 = f32[8,1,128]{2,1,0:T(1,128)S(1)} async-done(((f32[8,1,128]{2,1,0:T(1,128)}), f32[8,1,128]{2,1,0:T(1,128)S(1)}, u32[]{:S(2)}, u32[]{:S(2)}) %all-to-all-start.2) | async-done | bytes 4128 | tf_op jit(solution)/shard_map/all_to_all | solution.py:552
  104.7 14.3 %all_to_all.20.got_ref = f32[32,1,128]{2,1,0:T(1,128)S(1)} all-to-all(f32[32,1,128]{2,1,0:T(1,128)S(1)} %broadcast_in_dim.5), channel_id=1, replica_groups=mesh['ctx'=32,'head'=8] {'ctx'}, dimensions={0} | all-to-all | bytes 32768 | tf_op jit(solution)/shard_map/all_to_all | solution.py:555
  (101 shorter events, 29.6 us)
Async XLA Ops:
  2.3 4.3 %collective-permute-start = (bf16[128,512]{1,0:T(8,128)(2,1)S(1)}, bf16[128,512]{1,0:T(8,128)(2,1)S(1)}, u32[]{:S(2)}, u32[]{:S(2)}) collective-permute-start(bf16[128,512]{1,0:T(8,128)(2,1)S(1)} %get-tuple-element.89), channel_id=1, source_target_pairs={{0,8},{8,0},{16,24},{24,16},{32,40},{40,32},{48,56},{56,48},{64,72... | collective-permute-start | bytes 393224 | tf_op jit(solution)/shard_map/ppermute | solution.py:403
  6.6 3.2 %collective-permute-start.1 = (bf16[64,512]{1,0:T(8,128)(2,1)S(1)}, bf16[64,512]{1,0:T(8,128)(2,1)S(1)}, u32[]{:S(2)}, u32[]{:S(2)}) collective-permute-start(bf16[64,512]{1,0:T(8,128)(2,1)S(1)} %slice_add_fusion), channel_id=1, source_target_pairs={{0,16},{8,24},{16,0},{24,8},{32,48},{40,56},{48,32},{56,40},{64,80... | collective-permute-start | bytes 196616 | tf_op jit(solution)/shard_map/ppermute | solution.py:403
  6.7 3.1 %collective-permute-start.2 = (bf16[2,512,128]{2,1,0:T(8,128)(2,1)S(1)}, bf16[2,512,128]{2,1,0:T(8,128)(2,1)S(1)}, u32[]{:S(2)}, u32[]{:S(2)}) collective-permute-start(bf16[2,512,128]{2,1,0:T(8,128)(2,1)S(1)} %copy-done.19), channel_id=1, source_target_pairs={{0,8},{8,0},{16,24},{24,16},{32,40},{40,32},{48,56},{56,48},{64,72... | collective-permute-start | bytes 786440 | tf_op jit(solution)/shard_map/ppermute | solution.py:403
  7.2 17.0 %collective-permute-start.7 = (bf16[2,512,128]{2,1,0:T(8,128)(2,1)S(1)}, bf16[2,512,128]{2,1,0:T(8,128)(2,1)}, u32[]{:S(2)}, u32[]{:S(2)}) collective-permute-start(bf16[2,512,128]{2,1,0:T(8,128)(2,1)S(1)} %copy-done.19), channel_id=1, source_target_pairs={{0,32},{8,40},{16,48},{24,56},{32,64},{40,72},{48,80},{56,88},{64,... | collective-permute-start | bytes 786440 | tf_op jit(solution)/shard_map/ppermute | solution.py:409
  9.9 11.6 %collective-permute-start.3 = (bf16[2,512,128]{2,1,0:T(8,128)(2,1)S(1)}, bf16[2,512,128]{2,1,0:T(8,128)(2,1)S(1)}, u32[]{:S(2)}, u32[]{:S(2)}) collective-permute-start(bf16[2,512,128]{2,1,0:T(8,128)(2,1)S(1)} %copy-done.19), channel_id=1, source_target_pairs={{0,16},{8,24},{16,0},{24,8},{32,48},{40,56},{48,32},{56,40},{64,80... | collective-permute-start | bytes 786440 | tf_op jit(solution)/shard_map/ppermute | solution.py:403
  11.4 10.1 %collective-permute-start.4 = (bf16[64,512]{1,0:T(8,128)(2,1)S(1)}, bf16[64,512]{1,0:T(8,128)(2,1)S(1)}, u32[]{:S(2)}, u32[]{:S(2)}) collective-permute-start(bf16[64,512]{1,0:T(8,128)(2,1)S(1)} %fusion.1.q_ref), channel_id=1, source_target_pairs={{0,224},{8,232},{16,240},{24,248},{32,0},{40,8},{48,16},{56,24},{6... | collective-permute-start | bytes 196616 | tf_op jit(solution)/shard_map/ppermute | solution.py:409
  16.1 5.4 %collective-permute-start.5 = (bf16[64,512]{1,0:T(8,128)(2,1)S(1)}, bf16[64,512]{1,0:T(8,128)(2,1)S(1)}, u32[]{:S(2)}, u32[]{:S(2)}) collective-permute-start(bf16[64,512]{1,0:T(8,128)(2,1)S(1)} %fusion.1.q_ref), channel_id=1, source_target_pairs={{0,192},{8,200},{16,208},{24,216},{32,224},{40,232},{48,240},{56,2... | collective-permute-start | bytes 196616 | tf_op jit(solution)/shard_map/ppermute | solution.py:409
  21.5 3.1 %collective-permute-start.6 = (bf16[2,512,128]{2,1,0:T(8,128)(2,1)S(1)}, bf16[2,512,128]{2,1,0:T(8,128)(2,1)S(1)}, u32[]{:S(2)}, u32[]{:S(2)}) collective-permute-start(bf16[2,512,128]{2,1,0:T(8,128)(2,1)S(1)} %collective-permute-done.3.refs_2_.refs_3_), channel_id=1, source_target_pairs={{0,8},{8,0},{16,24},{24,16},{32,40},{40,32},{48,56},{56,48},{64,72... | collective-permute-start | bytes 786440 | tf_op jit(solution)/shard_map/ppermute | solution.py:403
  23.4 10.9 %collective-permute-start.9 = (bf16[512,256]{1,0:T(8,128)(2,1)S(1)}, bf16[512,256]{1,0:T(8,128)(2,1)}, u32[]{:S(2)}, u32[]{:S(2)}) collective-permute-start(bf16[512,256]{1,0:T(8,128)(2,1)S(1)} %copy-done.9), channel_id=1, source_target_pairs={{0,16},{8,24},{16,0},{24,8},{32,48},{40,56},{48,32},{56,40},{64,80... | collective-permute-start | bytes 786440 | tf_op jit(solution)/shard_map/ppermute | solution.py:403
  23.7 15.8 %collective-permute-start.8 = (bf16[512,256]{1,0:T(8,128)(2,1)S(1)}, bf16[512,256]{1,0:T(8,128)(2,1)}, u32[]{:S(2)}, u32[]{:S(2)}) collective-permute-start(bf16[512,256]{1,0:T(8,128)(2,1)S(1)} %copy-done.9), channel_id=1, source_target_pairs={{0,8},{8,0},{16,24},{24,16},{32,40},{40,32},{48,56},{56,48},{64,72... | collective-permute-start | bytes 786440 | tf_op jit(solution)/shard_map/ppermute | solution.py:403
  28.4 9.1 %collective-permute-start.11 = (bf16[2,512,128]{2,1,0:T(8,128)(2,1)}, bf16[2,512,128]{2,1,0:T(8,128)(2,1)}, u32[]{:S(2)}, u32[]{:S(2)}) collective-permute-start(bf16[2,512,128]{2,1,0:T(8,128)(2,1)} %collective-permute-done.7), channel_id=1, source_target_pairs={{0,16},{8,24},{16,0},{24,8},{32,48},{40,56},{48,32},{56,40},{64,80... | collective-permute-start | bytes 786440 | tf_op jit(solution)/shard_map/ppermute | solution.py:403
  30.2 22.2 %all-to-all-start = ((f16[8,64,512]{2,1,0:T(8,128)(2,1)}), f16[8,64,512]{2,1,0:T(8,128)(2,1)}, u32[]{:S(2)}, u32[]{:S(2)}) async-start(f16[8,64,512]{2,1,0:T(8,128)(2,1)} %broadcast_in_dim.4), calls=%async_computation | async-start | bytes 1048576 | tf_op jit(solution)/shard_map/all_to_all | solution.py:491
  34.4 5.1 %collective-permute-start.10 = (bf16[512,256]{1,0:T(8,128)(2,1)}, bf16[512,256]{1,0:T(8,128)(2,1)S(1)}, u32[]{:S(2)}, u32[]{:S(2)}) collective-permute-start(bf16[512,256]{1,0:T(8,128)(2,1)} %collective-permute-done.9.refs_2_), channel_id=1, source_target_pairs={{0,8},{8,0},{16,24},{24,16},{32,40},{40,32},{48,56},{56,48},{64,72... | collective-permute-start | bytes 786440 | tf_op jit(solution)/shard_map/ppermute | solution.py:403
  40.2 13.5 %collective-permute-start.12 = (bf16[4,512,128]{2,1,0:T(8,128)(2,1)}, bf16[4,512,128]{2,1,0:T(8,128)(2,1)}, u32[]{:S(2)}, u32[]{:S(2)}) collective-permute-start(bf16[4,512,128]{2,1,0:T(8,128)(2,1)} %pad_maximum_fusion.refs_5_), channel_id=1, source_target_pairs={{0,8},{8,0},{16,24},{24,16},{32,40},{40,32},{48,56},{56,48},{64,72... | collective-permute-start | bytes 1572872 | tf_op jit(solution)/shard_map/ppermute | solution.py:403
  53.7 15.5 %collective-permute-start.15 = (bf16[1248,256]{1,0:T(8,128)(2,1)S(1)}, bf16[1248,256]{1,0:T(8,128)(2,1)S(1)}, u32[]{:S(2)}, u32[]{:S(2)}) collective-permute-start(bf16[1248,256]{1,0:T(8,128)(2,1)S(1)} %copy-done.6), channel_id=1, source_target_pairs={{0,16},{8,24},{16,0},{24,8},{32,48},{40,56},{48,32},{56,40},{64,80... | collective-permute-start | bytes 1916936 | tf_op jit(solution)/shard_map/ppermute | solution.py:403
  56.3 4.3 %collective-permute-start.13 = (f16[64,1024]{1,0:T(8,128)(2,1)S(1)}, f16[64,1024]{1,0:T(8,128)(2,1)S(1)}, u32[]{:S(2)}, u32[]{:S(2)}) collective-permute-start(f16[64,1024]{1,0:T(8,128)(2,1)S(1)} %multiply_convert_fusion.1), channel_id=1, source_target_pairs={{0,2},{1,3},{2,0},{3,1},{4,6},{5,7},{6,4},{7,5},{8,10},{9,11},{10,... | collective-permute-start | bytes 393224 | tf_op jit(solution)/shard_map/ppermute | solution.py:403
  60.7 5.8 %collective-permute-start.14 = (f16[64,1024]{1,0:T(8,128)(2,1)S(1)}, f16[64,1024]{1,0:T(8,128)(2,1)S(1)}, u32[]{:S(2)}, u32[]{:S(2)}) collective-permute-start(f16[64,1024]{1,0:T(8,128)(2,1)S(1)} %add.21), channel_id=1, source_target_pairs={{0,4},{1,5},{2,6},{3,7},{4,0},{5,1},{6,2},{7,3},{8,12},{9,13},{10,... | collective-permute-start | bytes 393224 | tf_op jit(solution)/shard_map/ppermute | solution.py:403
  63.5 12.9 %collective-permute-start.17 = (bf16[4,512,128]{2,1,0:T(8,128)(2,1)}, bf16[4,512,128]{2,1,0:T(8,128)(2,1)S(1)}, u32[]{:S(2)}, u32[]{:S(2)}) collective-permute-start(bf16[4,512,128]{2,1,0:T(8,128)(2,1)} %pad_maximum_fusion.refs_5_), channel_id=1, source_target_pairs={{0,32},{8,40},{16,48},{24,56},{32,64},{40,72},{48,80},{56,88},{64,... | collective-permute-start | bytes 1572872 | tf_op jit(solution)/shard_map/ppermute | solution.py:409
  63.5 13.7 %collective-permute-start.18 = (bf16[1248,256]{1,0:T(8,128)(2,1)S(1)}, bf16[1248,256]{1,0:T(8,128)(2,1)S(1)}, u32[]{:S(2)}, u32[]{:S(2)}) collective-permute-start(bf16[1248,256]{1,0:T(8,128)(2,1)S(1)} %copy-done.6), channel_id=1, source_target_pairs={{0,8},{8,0},{16,24},{24,16},{32,40},{40,32},{48,56},{56,48},{64,72... | collective-permute-start | bytes 1916936 | tf_op jit(solution)/shard_map/ppermute | solution.py:403
  69.2 8.0 %collective-permute-start.19 = (bf16[1248,256]{1,0:T(8,128)(2,1)S(1)}, bf16[1248,256]{1,0:T(8,128)(2,1)S(1)}, u32[]{:S(2)}, u32[]{:S(2)}) collective-permute-start(bf16[1248,256]{1,0:T(8,128)(2,1)S(1)} %collective-permute-done.15.refs_2_), channel_id=1, source_target_pairs={{0,8},{8,0},{16,24},{24,16},{32,40},{40,32},{48,56},{56,48},{64,72... | collective-permute-start | bytes 1916936 | tf_op jit(solution)/shard_map/ppermute | solution.py:403
  70.6 6.6 %collective-permute-start.16 = (f16[64,1024]{1,0:T(8,128)(2,1)S(1)}, f16[64,1024]{1,0:T(8,128)(2,1)S(1)}, u32[]{:S(2)}, u32[]{:S(2)}) collective-permute-start(f16[64,1024]{1,0:T(8,128)(2,1)S(1)} %add.22), channel_id=1, source_target_pairs={{0,1},{1,0},{2,3},{3,2},{4,5},{5,4},{6,7},{7,6},{8,9},{9,8},{10,11... | collective-permute-start | bytes 393224 | tf_op jit(solution)/shard_map/ppermute | solution.py:403
  79.7 11.4 %all-to-all-start.1 = ((f16[8,8,1024]{2,1,0:T(8,128)(2,1)}), f16[8,8,1024]{2,1,0:T(8,128)(2,1)S(1)}, u32[]{:S(2)}, u32[]{:S(2)}) async-start(f16[8,8,1024]{2,1,0:T(8,128)(2,1)} %fusion), calls=%async_computation.1 | async-start | bytes 262144 | tf_op jit(solution)/shard_map/all_to_all | solution.py:540
  83.2 8.9 %collective-permute-start.20 = (bf16[4,512,128]{2,1,0:T(8,128)(2,1)}, bf16[4,512,128]{2,1,0:T(8,128)(2,1)}, u32[]{:S(2)}, u32[]{:S(2)}) collective-permute-start(bf16[4,512,128]{2,1,0:T(8,128)(2,1)} %copy-done.7), channel_id=1, source_target_pairs={{0,8},{8,0},{16,24},{24,16},{32,40},{40,32},{48,56},{56,48},{64,72... | collective-permute-start | bytes 1572872 | tf_op jit(solution)/shard_map/ppermute | solution.py:403
  92.1 12.5 %all-to-all-start.2 = ((f32[8,1,128]{2,1,0:T(1,128)}), f32[8,1,128]{2,1,0:T(1,128)S(1)}, u32[]{:S(2)}, u32[]{:S(2)}) async-start(f32[8,1,128]{2,1,0:T(1,128)} %hidden.1), calls=%async_computation.2 | async-start | bytes 8192 | tf_op jit(solution)/shard_map/all_to_all | solution.py:552
  (22 other events, 116.9 us)

commit v3 on v2

--- a/solution.py
+++ b/solution.py
@@ -41,13 +41,19 @@
     return start
 
 
-def pick_kernel(me_ref, steps_hbm, q_hbm, keep_ref, pass_ref, send_ref, all_ref, steps_ref, q_ref, sems):
-    steps_copy = pltpu.make_async_copy(steps_hbm, steps_ref, sems.at[0])
-    q_copy = pltpu.make_async_copy(q_hbm, q_ref, sems.at[1])
-    steps_copy.start()
-    q_copy.start()
-    steps_copy.wait()
-    q_copy.wait()
+def pick_kernel(me_ref, steps_hbm, q_hbm, weight_hbm, stream_hbm, *refs):
+    keep_ref, pass_ref, send_ref, pack_hbm, all_ref, steps_ref, q_ref, sems = refs
+    copies = [pltpu.make_async_copy(steps_hbm, steps_ref, sems.at[0])]
+    for k in range(4):
+        part = pl.ds(k * BLOCK // 4, BLOCK // 4)
+        copies.append(pltpu.make_async_copy(q_hbm.at[part], q_ref.at[part], sems.at[1 + k]))
+    for k, (source, begin) in enumerate([(weight_hbm, 0), (stream_hbm, BLOCK)]):
+        target = pack_hbm.at[pl.ds(begin, source.shape[0])]
+        copies.append(pltpu.make_async_copy(source, target, sems.at[5 + k]))
+    for copy in copies:
+        copy.start()
+    for copy in copies[:5]:
+        copy.wait()
     me = me_ref[0]
     core, side = me % 2, (me // 2) % 2
     at = lax.broadcasted_iota(jnp.int32, (TRACES, BLOCK), 1) + me * BLOCK
@@ -71,15 +77,19 @@
     pass_ref[...] = group(core, 1 - side)
     send_ref[:GROUP] = group(1 - core, side)
     send_ref[GROUP:] = group(1 - core, 1 - side)
+    for copy in copies[5:]:
+        copy.wait()
 
 
 def picked_kernel(me_ref, lengths_hbm, steps_hbm, q_ref, q1_ref, q2_ref, *refs):
     kv_refs, out_ref = refs[:PLANE], refs[PLANE]
-    kv_s, lengths, steps_ref, sems = refs[-4:]
+    plane_ref, lengths, steps_ref, sems = refs[-4:]
+    kv_s = plane_ref
     lengths_copy = pltpu.make_async_copy(lengths_hbm, lengths, sems.at[PLANE])
     steps_copy = pltpu.make_async_copy(steps_hbm, steps_ref, sems.at[PLANE + 1])
     copies = [
-        pltpu.make_async_copy(kv, kv_s.at[k], sems.at[k]) for k, kv in enumerate(kv_refs)
+        pltpu.make_async_copy(kv, kv_s.at[pl.ds(2 * k, 2)], sems.at[k])
+        for k, kv in enumerate(kv_refs)
     ]
     for copy in [lengths_copy, steps_copy] + copies:
         copy.start()
@@ -110,7 +120,7 @@
         mask = jnp.concatenate([mask] * PER_GROUP, axis=0)
         copies[k].wait()
         s = lax.dot_general(
-            q, kv_s[k, 0], (((1,), (1,)), ((), ())), preferred_element_type=F32
+            q, kv_s[2 * k], (((1,), (1,)), ((), ())), preferred_element_type=F32
         )
         scores.append(jnp.where(mask, s, LOW))
     top = jnp.maximum(jnp.maximum(scores[0], scores[1]), jnp.maximum(scores[2], scores[3]))
@@ -119,7 +129,7 @@
     pv = jnp.zeros((PER_GROUP * GROUP, 2 * HD), F32)
     for k, s in enumerate(scores):
         p = jnp.exp2((s - top) * COEF).astype(BF16)
-        ext = jnp.concatenate([kv_s[k, 1], ones], axis=1)
+        ext = jnp.concatenate([kv_s[2 * k + 1], ones], axis=1)
         pv = pv + jnp.dot(p, ext, preferred_element_type=F32)
     total = pv[:, HD:]
     some = total > 0.0
@@ -144,7 +154,7 @@
         out_ref[z * PAD + TRACES : (z + 1) * PAD, :HD] = packed
 
 
-def attend_kernel(slots, first, last, *refs):
+def attend_kernel(slots, first, last, joined, *refs):
     n = len(slots)
     arrays = 1 + max(slot[2] for slot in slots)
     me_ref, lengths_hbm, q_ref = refs[:3]
@@ -155,13 +165,18 @@
         q_ref, m_ref, l_ref, acc_ref = refs[3 + arrays : 7 + arrays]
     else:
         m_ref, l_ref, acc_ref = refs[3 + arrays : 6 + arrays]
+    pair_copies = []
+    for k in range(joined):
+        source = refs[3 + arrays - joined + k]
+        target = refs[-4].at[pl.ds(2 * k, 2)]
+        pair_copies.append(pltpu.make_async_copy(source, target, sems.at[n + 2 + k]))
     copies = [
         pltpu.make_async_copy(kv, kv_ref.at[k], sems.at[k]) for k, kv in enumerate(kv_hbm)
     ]
     copies.append(pltpu.make_async_copy(lengths_hbm, lengths, sems.at[n]))
     if first:
         copies.append(pltpu.make_async_copy(q_hbm, q_ref, sems.at[n + 1]))
-    for copy in copies:
+    for copy in copies + pair_copies:
         copy.start()
     for copy in copies:
         copy.wait()
@@ -249,36 +264,43 @@
     if last:
         out_ref = refs[-4]
         out_ref[...] = acc_ref[...] / l_ref[...]
-
-
-def attend(slots, me, lengths, queries, kvs, state, last=False):
+    for copy in pair_copies:
+        copy.wait()
+
+
+def attend(slots, me, lengths, queries, kvs, state, last=False, in_vmem=0, joined=0):
     shape = (BLOCK, PER_GROUP * HD)
     first = state is None
-    operands = [me, *pinned([lengths, queries] if first else [lengths]), *kvs]
+    kept = [pltpu.with_memory_space_constraint(kv, pltpu.VMEM) for kv in kvs[:in_vmem]]
+    operands = [me, *pinned([lengths, queries] if first else [lengths]), *kept, *kvs[in_vmem:]]
     specs = [SMEM] + [HBM] * (len(operands) - 1)
     if not first:
         q, *sums = [pltpu.with_memory_space_constraint(x, pltpu.VMEM) for x in state]
         operands[2:2] = [q]
-        specs[2:2] = [VMEM]
+        specs[2:2] = [VMEM] + [VMEM] * in_vmem
+        del specs[3 + in_vmem : 3 + 2 * in_vmem]
         at = len(operands)
         operands += sums
         specs += [VMEM] * 3
+    shapes = (pltpu.VMEM(shape, BF16),) + (pltpu.VMEM(shape, F32),) * 3
+    out_specs, aliases = [VMEM] * 4, {}
     if last:
-        shapes, aliases = (jax.ShapeDtypeStruct(shape, F32),), {}
-    elif first:
-        shapes, aliases = (pltpu.VMEM(shape, BF16),) + (pltpu.VMEM(shape, F32),) * 3, {}
-    else:
-        shapes, aliases = (pltpu.VMEM(shape, F32),) * 3, {at + k: k for k in range(3)}
+        shapes, out_specs = (jax.ShapeDtypeStruct(shape, F32),), [VMEM]
+    elif not first:
+        aliases = {2: 0, at: 1, at + 1: 2, at + 2: 3}
+    if joined:
+        shapes += (pltpu.HBM((2 * joined, BLOCK, HD), BF16),)
+        out_specs.append(HBM)
     work = PER_GROUP * BLOCK * BLOCK * len(slots)
     got = pl.pallas_call(
-        functools.partial(attend_kernel, slots, first, last),
+        functools.partial(attend_kernel, slots, first, last, joined),
         out_shape=shapes,
         in_specs=specs,
-        out_specs=[VMEM] * len(shapes),
+        out_specs=out_specs,
         scratch_shapes=[
             pltpu.VMEM((len(slots), 2, BLOCK, HD), BF16),
             pltpu.SMEM((TRACES,), jnp.int32),
-            pltpu.SemaphoreType.DMA((len(slots) + 2,)),
+            pltpu.SemaphoreType.DMA((len(slots) + 2 + joined,)),
         ],
         input_output_aliases=aliases,
         compiler_params=pltpu.CompilerParams(vmem_limit_bytes=32 << 20),
@@ -289,19 +311,19 @@
     )(*operands)
     if last:
         return got[0]
-    return list(got) if first else [q, *got]
+    return (list(got[:4]), got[4]) if joined else list(got)
 
 
 def pinned(values):
     return [pltpu.with_memory_space_constraint(value, pltpu.HBM) for value in values]
 
 
-def small_call(kernel, shape, operands, specs=None, **kw):
+def small_call(kernel, shape, operands, specs=None, out_specs=None, **kw):
     return pl.pallas_call(
         kernel,
         out_shape=shape,
         in_specs=specs or [VMEM] * len(operands),
-        out_specs=jax.tree.map(lambda _: VMEM, shape),
+        out_specs=out_specs or ([VMEM] * len(shape) if type(shape) is tuple else VMEM),
         compiler_params=pltpu.CompilerParams(vmem_limit_bytes=24 << 20),
         **kw,
     )(*operands)
@@ -310,7 +332,7 @@
 def project_kernel(got_ref, *refs):
     packs, out_ref, weight_s, sems = refs[:PLANE], refs[PLANE], refs[-2], refs[-1]
     copies = [
-        pltpu.make_async_copy(pack, weight_s.at[k], sems.at[k])
+        pltpu.make_async_copy(pack.at[pl.ds(0, BLOCK)], weight_s.at[k], sems.at[k])
         for k, pack in enumerate(packs)
     ]
     for copy in copies:
@@ -349,11 +371,13 @@
 
 
 def inner_kernel(me_ref, total_ref, *refs):
-    packs, out_ref, pack_s, sems = refs[:PLANE], refs[PLANE], refs[-2], refs[-1]
-    copies = [
-        pltpu.make_async_copy(pack, pack_s.at[k], sems.at[k])
-        for k, pack in enumerate(packs)
-    ]
+    packs, weights, out_ref = refs[:PLANE], refs[PLANE : 2 * PLANE], refs[2 * PLANE]
+    stream_s, weight_s, sems = refs[-3:]
+    copies = []
+    for k in range(PLANE):
+        source = packs[k].at[pl.ds(BLOCK, TRACES * STEPS)]
+        copies.append(pltpu.make_async_copy(source, stream_s.at[k], sems.at[2 * k]))
+        copies.append(pltpu.make_async_copy(weights[k], weight_s.at[k], sems.at[2 * k + 1]))
     for copy in copies:
         copy.start()
     place = me_ref[0] % PLANE
@@ -363,14 +387,12 @@
     wanted = trace * STEPS + PLANE * (slot >> 3) + place
     chosen = jnp.where((at == wanted) & (trace < TRACES), 1.0, 0.0).astype(BF16)
     for k in range(PLANE):
-        copies[k].wait()
-        base = jnp.dot(chosen, pack_s[k, WIDE:], preferred_element_type=F32)
+        copies[2 * k].wait()
+        base = jnp.dot(chosen, stream_s[k], preferred_element_type=F32)
         stream = (base + total_ref[:, k * 256 : (k + 1) * 256]).astype(BF16)
-        for n in range(4):
-            weight = pack_s[k, n * 256 : (n + 1) * 256]
-            part = jnp.dot(stream, weight, preferred_element_type=F32)
-            cols = slice(n * 256, (n + 1) * 256)
-            out_ref[:, cols] = part if k == 0 else out_ref[:, cols] + part
+        copies[2 * k + 1].wait()
+        part = jnp.dot(stream, weight_s[k], preferred_element_type=F32)
+        out_ref[...] = part if k == 0 else out_ref[...] + part
 
 
 def hidden_kernel(inner_ref, class_ref, out_ref):
@@ -430,16 +452,19 @@
     core0 = swapped(kv0, "ctx", 1)
 
     half = PER_GROUP * HD
-    keep, passed, sent = small_call(
+    packed = (BLOCK + TRACES * STEPS, 256)
+    keep, passed, sent, weight = small_call(
         pick_kernel,
-        tuple(jax.ShapeDtypeStruct((n * GROUP, half), BF16) for n in (1, 1, 2)),
-        [me, *pinned([step_rows, queries])],
-        [SMEM, HBM, HBM],
+        tuple(jax.ShapeDtypeStruct((n * GROUP, half), BF16) for n in (1, 1, 2))
+        + (pltpu.HBM(packed, BF16),),
+        [me, *pinned([step_rows, queries, out_weight, step_stream])],
+        [SMEM] + [HBM] * 4,
+        [VMEM] * 3 + [HBM],
         scratch_shapes=[
             pltpu.VMEM((PLANE * GROUP, half), BF16),
             pltpu.VMEM((TRACES, STEPS), jnp.int32),
             pltpu.VMEM((BLOCK, half), BF16),
-            pltpu.SemaphoreType.DMA((2,)),
+            pltpu.SemaphoreType.DMA((7,)),
         ],
         name="pick",
     )
@@ -449,22 +474,18 @@
     wanted, kv0y, core0 = tie(wanted, kv0, core0)
     wanted1, wanted2 = raised(wanted, -1), raised(wanted, -2)
     across0 = swapped(kv0y, "ctx", 2)
-    across0, wanted1 = tie(across0, wanted1)
+    across0, wanted1, wanted2 = tie(across0, wanted1, wanted2)
     core0y = swapped(across0, "ctx", 1)
     state = add([(0, 0, 0, 0), (0, 1, 1, 0)], kvs=[pinned([kv0y])[0], core0], state=None)
     wanted, wanted1, wanted2, *state = tie(wanted, wanted1, wanted2, *state)
 
-    weight, wanted = tie(out_weight, wanted)
+    weight, wanted = tie(weight, wanted)
     firsts = [weight, swapped(weight, "ctx", 1), swapped(weight, "ctx", 2)]
-    firsts.append(swapped(firsts[2], "ctx", 1))
-    pack = jnp.concatenate(
-        [score_weight[:, n * 256 : (n + 1) * 256] for n in range(4)] + [step_stream], axis=0
-    )
     kv1, _ = tie(raised(kv0, 1), wanted)
 
-    parts = small_call(
+    parts, plane = small_call(
         picked_kernel,
-        jax.ShapeDtypeStruct((GROUP, half), F32),
+        (jax.ShapeDtypeStruct((GROUP, half), F32), pltpu.VMEM((2 * PLANE, BLOCK, HD), BF16)),
         [
             me,
             *pinned([trace_lengths, step_rows]),
@@ -478,27 +499,28 @@
         ],
         [SMEM, HBM, HBM] + [VMEM] * 3 + [HBM] * 4,
         scratch_shapes=[
-            pltpu.VMEM((PLANE, 2, BLOCK, HD), BF16),
             pltpu.SMEM((TRACES,), jnp.int32),
             pltpu.VMEM((TRACES, STEPS), jnp.int32),
             pltpu.SemaphoreType.DMA((PLANE + 2,)),
         ],
         name="picked",
     )
-    parts, kv1, across0, core0y, *state = tie(parts, kv1, across0, core0y, *state)
+    parts, kv1, plane, *state = tie(parts, kv1, plane, *state)
     across1 = swapped(kv1, "ctx", 2)
     parts = jnp.broadcast_to(parts.astype(jnp.float16)[None], (Z, GROUP, half))
     parts = lax.all_to_all(parts, "ctx", 0, 0, axis_index_groups=columns).astype(F32)
-    pair1 = jnp.concatenate([kv1, across1], axis=0)
-    *firsts, pair1, pack = tie(*firsts, pair1, pack)
+    firsts[2], across1 = tie(firsts[2], across1)
+    firsts.append(swapped(firsts[2], "ctx", 1))
+    state, pair1 = add(
+        [(0, 2, 0, 2), (0, 3, 0, 3), (1, 0, 1, 0), (1, 2, 2, 0)],
+        kvs=[plane, kv1, across1],
+        state=state,
+        in_vmem=1,
+        joined=2,
+    )
     cores1 = swapped(pair1, "ctx", 1)
-    state = add(
-        [(0, 2, 0, 0), (0, 3, 1, 0), (1, 0, 2, 0), (1, 2, 2, 1)],
-        kvs=[across0, core0y, pair1],
-        state=state,
-    )
-    parts, pair1, cores1, pack, *state = tie(parts, pair1, cores1, pack, *state)
-    packs = [pack, swapped(pack, "ctx", 1), swapped(pack, "ctx", 2)]
+    parts, pair1, weight, *state = tie(parts, pair1, score_weight, *state)
+    weights = [weight, swapped(weight, "ctx", 1), swapped(weight, "ctx", 2)]
 
     projected = small_call(
         project_kernel,
@@ -515,8 +537,8 @@
     pair2 = raised(pair1, 1)
     projected = projected + swapped(projected, "head", 2)
     projected = projected + swapped(projected, "head", 4)
-    projected, cores1, packs[2] = tie(projected, cores1, packs[2])
-    packs.append(swapped(packs[2], "ctx", 1))
+    projected, cores1, weights[2] = tie(projected, cores1, weights[2])
+    weights.append(swapped(weights[2], "ctx", 1))
     other = swapped(projected, "head", 1)
     state = add([(1, 1, 0, 0), (1, 3, 0, 1)], kvs=[cores1], state=state)
     other, pair2, *state = tie(other, pair2, *state)
@@ -526,11 +548,12 @@
     inner = small_call(
         inner_kernel,
         jax.ShapeDtypeStruct((GROUP, WIDE), F32),
-        [me, projected, *packs],
-        [SMEM, VMEM] + [HBM] * 4,
+        [me, projected, *firsts, *weights],
+        [SMEM, VMEM] + [HBM] * 8,
         scratch_shapes=[
-            pltpu.VMEM((PLANE, WIDE + TRACES * STEPS, 256), BF16),
-            pltpu.SemaphoreType.DMA((PLANE,)),
+            pltpu.VMEM((PLANE, TRACES * STEPS, 256), BF16),
+            pltpu.VMEM((PLANE, 256, WIDE), BF16),
+            pltpu.SemaphoreType.DMA((2 * PLANE,)),
         ],
         name="inner",
     )

time: 121 us -> 144 us (1.19)
  Pallas kernels: 20.2 us -> 31.4 us
  starting transfers between devices: 44 us -> 54 us
  waiting for transfers between devices: 27.7 us -> 30.9 us
  other arithmetic: 4.13 us -> 2.14 us
    ppermute x17, waiting for transfers between devices: 9.21 us -> 22.6 us  [swapped(): return lax.ppermute(value, axis, [(s, s ^ bit) for s in range(count)])]
    pallas_call x6, Pallas kernels: 10.6 us -> 22.1 us  [small_call(): pl.pallas_call(kernel, out_shape=shape, in_specs=specs or [VMEM] * len(op...]
    all_to_all x1, waiting for transfers between devices: 10.6 us -> 0.01 us  [per_device(): lax.all_to_all(parts, 'ctx', 0, 0, axis_index_groups=columns).astype(F32)]
    all_to_all x1, starting transfers between devices: 3.5 us -> 9.12 us  [per_device(): inner = lax.all_to_all(inner, 'ctx', 0, 0, axis_index_groups=columns)]
    ppermute x4, starting transfers between devices: 7.23 us -> 9.44 us  [raised(): lax.ppermute(value, 'ctx', [(s, (s + steps) % count) for s in range(count)])]
    ppermute x17, starting transfers between devices: 23.1 us -> 25.2 us  [swapped(): return lax.ppermute(value, axis, [(s, s ^ bit) for s in range(count)])]
    concatenate x1 -> x0, other arithmetic: 1.98 us -> none  [per_device(): pair1 = jnp.concatenate([kv1, across1], axis=0)]
    unnamed x49 -> x43, local copies, waits for them, and re-layouts: 7.31 us -> 9.14 us
  transfers between devices with their start and end apart: 24 -> 24, of which waited for: 10 -> 10; matrix products, arithmetic and copies ran while one was open for 6% -> 1% of each run, Pallas kernels for 13% -> 9%
where the time goes in v3:
time: 144 us
  starting transfers between devices  54 us (38%)
  Pallas kernels  31.4 us (22%)
  waiting for transfers between devices  30.9 us (21%)
  blocking collectives  14.5 us (10%)
  local copies, waits for them, and re-layouts  9.99 us (7%)
  other arithmetic  2.14 us (1%)
    ppermute x17, starting transfers between devices, swapped(): return lax.ppermute(value, axis, [(s, s ^ bit) for s in range(count)])  25.2 us
    ppermute x17, waiting for transfers between devices, swapped(): return lax.ppermute(value, axis, [(s, s ^ bit) for s in range(count)])  22.6 us
    pallas_call x6, Pallas kernels, small_call(): pl.pallas_call(kernel, out_shape=shape, in_specs=specs or [VMEM] * len(op...  22.1 us
    all_to_all x1, blocking collectives, per_device(): lax.all_to_all(jnp.broadcast_to(gap[None], (count, 1, HD)), 'ctx', 0, 0)  14.5 us
    ppermute x4, starting transfers between devices, raised(): lax.ppermute(value, 'ctx', [(s, (s + steps) % count) for s in range(count)])  9.44 us
    pallas_call x5, Pallas kernels, attend(): pl.pallas_call(functools.partial(attend_kernel, slots, first, last, joine...  9.3 us
    unnamed x43, local copies, waits for them, and re-layouts  9.14 us
    all_to_all x1, starting transfers between devices, per_device(): inner = lax.all_to_all(inner, 'ctx', 0, 0, axis_index_groups=columns)  9.12 us
  transfers between devices with their start and end apart: 24, of which 10 were waited for; matrix products, arithmetic and copies ran while one was open for 1% of the time, Pallas kernels for 9%

profile of v3, /device:TPU:1, one launch (start us, length us, event | category | flops | bytes accessed | tf_op | source)
XLA Modules:
  0.0 144.0 jit_solution(9402446707530681494)
XLA Ops:
  0.6 12.6 %pick.1 = (bf16[64,512]{1,0:T(8,128)(2,1)S(1)}, bf16[64,512]{1,0:T(8,128)(2,1)S(1)}, bf16[128,512]{1,0:T(8,128)(2,1)S(1)}, bf16[736,256]{1,0:T(8,128)(2,1)}) custom-call(s32[1]{0:T(128)} %bitcast.me_ref.refs_0_, s32[7,32]{1,0:T(8,128)} %steps_hbm.3, bf16[512,512]{1,0:T(8,128)(2,1)} %refs_2_.1, bf16[512,256]{1,0:T(8,128)(2,1)} %weight_hbm.1, ...), custom_call_target="tpu_custom_call" | custom-call | tf_op jit(solution)/shard_map/pick/pallas_call | solution.py:322
  13.2 3.3 %collective-permute-start = (bf16[128,512]{1,0:T(8,128)(2,1)S(1)}, bf16[128,512]{1,0:T(8,128)(2,1)S(1)}, u32[]{:S(2)}, u32[]{:S(2)}) collective-permute-start(bf16[128,512]{1,0:T(8,128)(2,1)S(1)} %get-tuple-element.92), channel_id=1, source_target_pairs={{0,8},{8,0},{16,24},{24,16},{32,40},{40,32},{48,56},{56,48},{64,72... | collective-permute-start | bytes 393224 | tf_op jit(solution)/shard_map/ppermute | solution.py:425
  18.1 2.6 %collective-permute-done.1 = bf16[64,512]{1,0:T(8,128)(2,1)S(1)} collective-permute-done((bf16[64,512]{1,0:T(8,128)(2,1)S(1)}, bf16[64,512]{1,0:T(8,128)(2,1)S(1)}, u32[]{:S(2)}, u32[]{:S(2)}) %collective-permute-start.1) | collective-permute-done | bytes 65568 | tf_op jit(solution)/shard_map/ppermute | solution.py:425
  21.4 4.6 %collective-permute-start.4 = (bf16[64,512]{1,0:T(8,128)(2,1)S(1)}, bf16[64,512]{1,0:T(8,128)(2,1)S(1)}, u32[]{:S(2)}, u32[]{:S(2)}) collective-permute-start(bf16[64,512]{1,0:T(8,128)(2,1)S(1)} %fusion.1.q_ref), channel_id=1, source_target_pairs={{0,224},{8,232},{16,240},{24,248},{32,0},{40,8},{48,16},{56,24},{6... | collective-permute-start | bytes 196616 | tf_op jit(solution)/shard_map/ppermute | solution.py:431
  27.9 2.2 %collective-permute-done.5.q2_ref = bf16[64,512]{1,0:T(8,128)(2,1)S(1)} collective-permute-done((bf16[64,512]{1,0:T(8,128)(2,1)S(1)}, bf16[64,512]{1,0:T(8,128)(2,1)S(1)}, u32[]{:S(2)}, u32[]{:S(2)}) %collective-permute-start.5) | collective-permute-done | bytes 65568 | tf_op jit(solution)/shard_map/ppermute | solution.py:431
  30.2 3.2 %collective-permute-start.6 = (bf16[2,512,128]{2,1,0:T(8,128)(2,1)S(1)}, bf16[2,512,128]{2,1,0:T(8,128)(2,1)S(1)}, u32[]{:S(2)}, u32[]{:S(2)}) collective-permute-start(bf16[2,512,128]{2,1,0:T(8,128)(2,1)S(1)} %collective-permute-done.3.refs_2_), channel_id=1, source_target_pairs={{0,8},{8,0},{16,24},{24,16},{32,40},{40,32},{48,56},{56,48},{64,72... | collective-permute-start | bytes 786440 | tf_op jit(solution)/shard_map/ppermute | solution.py:425
  33.4 4.2 %attend_0_0.1 = (bf16[512,512]{1,0:T(8,128)(2,1)S(1)}, f32[512,512]{1,0:T(8,128)S(1)}, f32[512,512]{1,0:T(8,128)S(1)}, f32[512,512]{1,0:T(8,128)S(1)}) custom-call(s32[1]{0:T(128)} %bitcast.me_ref.refs_0_, s32[7]{0:T(128)} %refs_1_.9, bf16[512,512]{1,0:T(8,128)(2,1)} %refs_2_.1, bf16[2,512,128]{2,1,0:T(8,128)(2,1)} %refs_0_.1, ...), custom_call_target="tpu_custom_call" | custom-call | flops 1073741824 | bytes 1048576 | tf_op jit(solution)/shard_map/attend_0_0/pallas_call | solution.py:295
  37.6 3.2 %picked.1 = (f32[64,512]{1,0:T(8,128)S(1)}, bf16[8,512,128]{2,1,0:T(8,128)(2,1)S(1)}) custom-call(s32[1]{0:T(128)} %bitcast.me_ref.refs_0_, s32[7]{0:T(128)} %refs_1_.9, s32[7,32]{1,0:T(8,128)} %steps_hbm.3, bf16[64,512]{1,0:T(8,128)(2,1)S(1)} %fusion.1.q_ref, bf16[64,512]{1,0:T(8,128)(2,1)S(1)} %collective-permute-done.4.q1_ref, ...), custom_call_target="tpu_custom_call" | custom-call | tf_op jit(solution)/shard_map/picked/pallas_call | solution.py:322
  42.6 4.3 %all-to-all-start = ((f16[8,64,512]{2,1,0:T(8,128)(2,1)}), f16[8,64,512]{2,1,0:T(8,128)(2,1)}, u32[]{:S(2)}, u32[]{:S(2)}) async-start(f16[8,64,512]{2,1,0:T(8,128)(2,1)} %broadcast_in_dim.4), calls=%async_computation | async-start | bytes 1048576 | tf_op jit(solution)/shard_map/all_to_all | solution.py:511
  48.7 9.4 %collective-permute-done.8.refs_2_ = bf16[736,256]{1,0:T(8,128)(2,1)} collective-permute-done((bf16[736,256]{1,0:T(8,128)(2,1)S(1)}, bf16[736,256]{1,0:T(8,128)(2,1)}, u32[]{:S(2)}, u32[]{:S(2)}) %collective-permute-start.8) | collective-permute-done | bytes 376864 | tf_op jit(solution)/shard_map/ppermute | solution.py:425
  58.1 5.5 %collective-permute-done.9.refs_5_ = bf16[2,512,128]{2,1,0:T(8,128)(2,1)S(1)} collective-permute-done((bf16[2,512,128]{2,1,0:T(8,128)(2,1)}, bf16[2,512,128]{2,1,0:T(8,128)(2,1)S(1)}, u32[]{:S(2)}, u32[]{:S(2)}) %collective-permute-start.9) | collective-permute-done | bytes 262176 | tf_op jit(solution)/shard_map/ppermute | solution.py:425
  70.3 3.6 %collective-permute-start.15 = (bf16[256,1024]{1,0:T(8,128)(2,1)S(1)}, bf16[256,1024]{1,0:T(8,128)(2,1)S(1)}, u32[]{:S(2)}, u32[]{:S(2)}) collective-permute-start(bf16[256,1024]{1,0:T(8,128)(2,1)S(1)} %copy-done.9), channel_id=1, source_target_pairs={{0,16},{8,24},{16,0},{24,8},{32,48},{40,56},{48,32},{56,40},{64,80... | collective-permute-start | bytes 1572872 | tf_op jit(solution)/shard_map/ppermute | solution.py:425
  74.0 2.1 %project.1 = f32[64,1024]{1,0:T(8,128)S(1)} custom-call(f32[8,64,512]{2,1,0:T(8,128)S(1)} %convert_element_type.22.got_ref, bf16[736,256]{1,0:T(8,128)(2,1)S(1)} %copy-done.8, bf16[736,256]{1,0:T(8,128)(2,1)} %collective-permute-done.10.refs_1_, bf16[736,256]{1,0:T(8,128)(2,1)} %collective-permute-done.8.refs_2_, ...), custom_call_target="tpu_custom_call" | custom-call | tf_op jit(solution)/shard_map/project/pallas_call | solution.py:322
  77.4 2.9 %collective-permute-start.17 = (bf16[4,512,128]{2,1,0:T(8,128)(2,1)S(1)}, bf16[4,512,128]{2,1,0:T(8,128)(2,1)S(1)}, u32[]{:S(2)}, u32[]{:S(2)}) collective-permute-start(bf16[4,512,128]{2,1,0:T(8,128)(2,1)S(1)} %copy-done.20), channel_id=1, source_target_pairs={{0,32},{8,40},{16,48},{24,56},{32,64},{40,72},{48,80},{56,88},{64,... | collective-permute-start | bytes 1572872 | tf_op jit(solution)/shard_map/ppermute | solution.py:431
  81.0 2.8 %collective-permute-start.13 = (f16[64,1024]{1,0:T(8,128)(2,1)S(1)}, f16[64,1024]{1,0:T(8,128)(2,1)S(1)}, u32[]{:S(2)}, u32[]{:S(2)}) collective-permute-start(f16[64,1024]{1,0:T(8,128)(2,1)S(1)} %add.21), channel_id=1, source_target_pairs={{0,4},{1,5},{2,6},{3,7},{4,0},{5,1},{6,2},{7,3},{8,12},{9,13},{10,... | collective-permute-start | bytes 393224 | tf_op jit(solution)/shard_map/ppermute | solution.py:425
  86.5 2.3 %collective-permute-start.19 = (bf16[256,1024]{1,0:T(8,128)(2,1)S(1)}, bf16[256,1024]{1,0:T(8,128)(2,1)S(1)}, u32[]{:S(2)}, u32[]{:S(2)}) collective-permute-start(bf16[256,1024]{1,0:T(8,128)(2,1)S(1)} %collective-permute-done.15.refs_6_), channel_id=1, source_target_pairs={{0,8},{8,0},{16,24},{24,16},{32,40},{40,32},{48,56},{56,48},{64,72... | collective-permute-start | bytes 1572872 | tf_op jit(solution)/shard_map/ppermute | solution.py:425
  88.8 2.9 %collective-permute-start.16 = (f16[64,1024]{1,0:T(8,128)(2,1)S(1)}, f16[64,1024]{1,0:T(8,128)(2,1)S(1)}, u32[]{:S(2)}, u32[]{:S(2)}) collective-permute-start(f16[64,1024]{1,0:T(8,128)(2,1)S(1)} %add.22), channel_id=1, source_target_pairs={{0,1},{1,0},{2,3},{3,2},{4,5},{5,4},{6,7},{7,6},{8,9},{9,8},{10,11... | collective-permute-start | bytes 393224 | tf_op jit(solution)/shard_map/ppermute | solution.py:425
  92.9 2.2 %collective-permute-done.16 = f16[64,1024]{1,0:T(8,128)(2,1)S(1)} collective-permute-done((f16[64,1024]{1,0:T(8,128)(2,1)S(1)}, f16[64,1024]{1,0:T(8,128)(2,1)S(1)}, u32[]{:S(2)}, u32[]{:S(2)}) %collective-permute-start.16) | collective-permute-done | bytes 131104 | tf_op jit(solution)/shard_map/ppermute | solution.py:425
  97.9 9.1 %all-to-all-start.1 = ((f16[8,8,1024]{2,1,0:T(8,128)(2,1)}), f16[8,8,1024]{2,1,0:T(8,128)(2,1)S(1)}, u32[]{:S(2)}, u32[]{:S(2)}) async-start(f16[8,8,1024]{2,1,0:T(8,128)(2,1)} %fusion), calls=%async_computation.1 | async-start | bytes 262144 | tf_op jit(solution)/shard_map/all_to_all | solution.py:563
  111.8 3.0 %all-to-all-done.1 = f16[8,8,1024]{2,1,0:T(8,128)(2,1)S(1)} async-done(((f16[8,8,1024]{2,1,0:T(8,128)(2,1)}), f16[8,8,1024]{2,1,0:T(8,128)(2,1)S(1)}, u32[]{:S(2)}, u32[]{:S(2)}) %all-to-all-start.1) | async-done | bytes 131104 | tf_op jit(solution)/shard_map/all_to_all | solution.py:563
  115.8 5.9 %all-to-all-start.2 = ((f32[8,1,128]{2,1,0:T(1,128)}), f32[8,1,128]{2,1,0:T(1,128)S(1)}, u32[]{:S(2)}, u32[]{:S(2)}) async-start(f32[8,1,128]{2,1,0:T(1,128)} %hidden.1), calls=%async_computation.2 | async-start | bytes 8192 | tf_op jit(solution)/shard_map/all_to_all | solution.py:575
  122.7 2.2 %attend_2_1.1 = f32[512,512]{1,0:T(8,128)} custom-call(s32[1]{0:T(128)} %bitcast.me_ref.refs_0_, s32[7]{0:T(128)} %refs_1_.9, bf16[512,512]{1,0:T(8,128)(2,1)S(1)} %copy-done.7, bf16[4,512,128]{2,1,0:T(8,128)(2,1)} %collective-permute-done.20.refs_3_, f32[512,512]{1,0:T(8,128)S(1)} %get-tuple-element.170.refs_4_, f32[512,512]{1,0:T(8,128)S(1)} %get-tuple-element.171.refs_5_, ...), custom_call_target="tpu_custom_call" | custom-call | flops 1073741824 | bytes 1048576 | tf_op jit(solution)/shard_map/attend_2_1/pallas_call | solution.py:295
  125.0 3.1 %all-to-all-done.2 = f32[8,1,128]{2,1,0:T(1,128)S(1)} async-done(((f32[8,1,128]{2,1,0:T(1,128)}), f32[8,1,128]{2,1,0:T(1,128)S(1)}, u32[]{:S(2)}, u32[]{:S(2)}) %all-to-all-start.2) | async-done | bytes 4128 | tf_op jit(solution)/shard_map/all_to_all | solution.py:575
  128.2 14.5 %all_to_all.20.got_ref = f32[32,1,128]{2,1,0:T(1,128)S(1)} all-to-all(f32[32,1,128]{2,1,0:T(1,128)S(1)} %broadcast_in_dim.5), channel_id=1, replica_groups=mesh['ctx'=32,'head'=8] {'ctx'}, dimensions={0} | all-to-all | bytes 32768 | tf_op jit(solution)/shard_map/all_to_all | solution.py:578
  (93 shorter events, 31.0 us)
Async XLA Ops:
  13.2 4.3 %collective-permute-start = (bf16[128,512]{1,0:T(8,128)(2,1)S(1)}, bf16[128,512]{1,0:T(8,128)(2,1)S(1)}, u32[]{:S(2)}, u32[]{:S(2)}) collective-permute-start(bf16[128,512]{1,0:T(8,128)(2,1)S(1)} %get-tuple-element.92), channel_id=1, source_target_pairs={{0,8},{8,0},{16,24},{24,16},{32,40},{40,32},{48,56},{56,48},{64,72... | collective-permute-start | bytes 393224 | tf_op jit(solution)/shard_map/ppermute | solution.py:425
  17.6 3.2 %collective-permute-start.1 = (bf16[64,512]{1,0:T(8,128)(2,1)S(1)}, bf16[64,512]{1,0:T(8,128)(2,1)S(1)}, u32[]{:S(2)}, u32[]{:S(2)}) collective-permute-start(bf16[64,512]{1,0:T(8,128)(2,1)S(1)} %slice_add_fusion), channel_id=1, source_target_pairs={{0,16},{8,24},{16,0},{24,8},{32,48},{40,56},{48,32},{56,40},{64,80... | collective-permute-start | bytes 196616 | tf_op jit(solution)/shard_map/ppermute | solution.py:425
  17.7 3.1 %collective-permute-start.2 = (bf16[2,512,128]{2,1,0:T(8,128)(2,1)S(1)}, bf16[2,512,128]{2,1,0:T(8,128)(2,1)S(1)}, u32[]{:S(2)}, u32[]{:S(2)}) collective-permute-start(bf16[2,512,128]{2,1,0:T(8,128)(2,1)S(1)} %copy-done.18), channel_id=1, source_target_pairs={{0,8},{8,0},{16,24},{24,16},{32,40},{40,32},{48,56},{56,48},{64,72... | collective-permute-start | bytes 786440 | tf_op jit(solution)/shard_map/ppermute | solution.py:425
  20.8 9.4 %collective-permute-start.3 = (bf16[2,512,128]{2,1,0:T(8,128)(2,1)S(1)}, bf16[2,512,128]{2,1,0:T(8,128)(2,1)S(1)}, u32[]{:S(2)}, u32[]{:S(2)}) collective-permute-start(bf16[2,512,128]{2,1,0:T(8,128)(2,1)S(1)} %copy-done.18), channel_id=1, source_target_pairs={{0,16},{8,24},{16,0},{24,8},{32,48},{40,56},{48,32},{56,40},{64,80... | collective-permute-start | bytes 786440 | tf_op jit(solution)/shard_map/ppermute | solution.py:425
  21.4 6.5 %collective-permute-start.4 = (bf16[64,512]{1,0:T(8,128)(2,1)S(1)}, bf16[64,512]{1,0:T(8,128)(2,1)S(1)}, u32[]{:S(2)}, u32[]{:S(2)}) collective-permute-start(bf16[64,512]{1,0:T(8,128)(2,1)S(1)} %fusion.1.q_ref), channel_id=1, source_target_pairs={{0,224},{8,232},{16,240},{24,248},{32,0},{40,8},{48,16},{56,24},{6... | collective-permute-start | bytes 196616 | tf_op jit(solution)/shard_map/ppermute | solution.py:431
  26.0 4.1 %collective-permute-start.5 = (bf16[64,512]{1,0:T(8,128)(2,1)S(1)}, bf16[64,512]{1,0:T(8,128)(2,1)S(1)}, u32[]{:S(2)}, u32[]{:S(2)}) collective-permute-start(bf16[64,512]{1,0:T(8,128)(2,1)S(1)} %fusion.1.q_ref), channel_id=1, source_target_pairs={{0,192},{8,200},{16,208},{24,216},{32,224},{40,232},{48,240},{56,2... | collective-permute-start | bytes 196616 | tf_op jit(solution)/shard_map/ppermute | solution.py:431
  27.2 10.4 %collective-permute-start.7 = (bf16[2,512,128]{2,1,0:T(8,128)(2,1)S(1)}, bf16[2,512,128]{2,1,0:T(8,128)(2,1)S(1)}, u32[]{:S(2)}, u32[]{:S(2)}) collective-permute-start(bf16[2,512,128]{2,1,0:T(8,128)(2,1)S(1)} %copy-done.18), channel_id=1, source_target_pairs={{0,32},{8,40},{16,48},{24,56},{32,64},{40,72},{48,80},{56,88},{64,... | collective-permute-start | bytes 786440 | tf_op jit(solution)/shard_map/ppermute | solution.py:431
  30.2 7.4 %collective-permute-start.6 = (bf16[2,512,128]{2,1,0:T(8,128)(2,1)S(1)}, bf16[2,512,128]{2,1,0:T(8,128)(2,1)S(1)}, u32[]{:S(2)}, u32[]{:S(2)}) collective-permute-start(bf16[2,512,128]{2,1,0:T(8,128)(2,1)S(1)} %collective-permute-done.3.refs_2_), channel_id=1, source_target_pairs={{0,8},{8,0},{16,24},{24,16},{32,40},{40,32},{48,56},{56,48},{64,72... | collective-permute-start | bytes 786440 | tf_op jit(solution)/shard_map/ppermute | solution.py:425
  42.6 26.4 %all-to-all-start = ((f16[8,64,512]{2,1,0:T(8,128)(2,1)}), f16[8,64,512]{2,1,0:T(8,128)(2,1)}, u32[]{:S(2)}, u32[]{:S(2)}) async-start(f16[8,64,512]{2,1,0:T(8,128)(2,1)} %broadcast_in_dim.4), calls=%async_computation | async-start | bytes 1048576 | tf_op jit(solution)/shard_map/all_to_all | solution.py:511
  46.9 11.2 %collective-permute-start.8 = (bf16[736,256]{1,0:T(8,128)(2,1)S(1)}, bf16[736,256]{1,0:T(8,128)(2,1)}, u32[]{:S(2)}, u32[]{:S(2)}) collective-permute-start(bf16[736,256]{1,0:T(8,128)(2,1)S(1)} %copy-done.8), channel_id=1, source_target_pairs={{0,16},{8,24},{16,0},{24,8},{32,48},{40,56},{48,32},{56,40},{64,80... | collective-permute-start | bytes 1130504 | tf_op jit(solution)/shard_map/ppermute | solution.py:425
  47.5 16.1 %collective-permute-start.9 = (bf16[2,512,128]{2,1,0:T(8,128)(2,1)}, bf16[2,512,128]{2,1,0:T(8,128)(2,1)S(1)}, u32[]{:S(2)}, u32[]{:S(2)}) collective-permute-start(bf16[2,512,128]{2,1,0:T(8,128)(2,1)} %copy-done.16), channel_id=1, source_target_pairs={{0,16},{8,24},{16,0},{24,8},{32,48},{40,56},{48,32},{56,40},{64,80... | collective-permute-start | bytes 786440 | tf_op jit(solution)/shard_map/ppermute | solution.py:425
  48.7 25.3 %collective-permute-start.10 = (bf16[736,256]{1,0:T(8,128)(2,1)S(1)}, bf16[736,256]{1,0:T(8,128)(2,1)}, u32[]{:S(2)}, u32[]{:S(2)}) collective-permute-start(bf16[736,256]{1,0:T(8,128)(2,1)S(1)} %copy-done.8), channel_id=1, source_target_pairs={{0,8},{8,0},{16,24},{24,16},{32,40},{40,32},{48,56},{56,48},{64,72... | collective-permute-start | bytes 1130504 | tf_op jit(solution)/shard_map/ppermute | solution.py:425
  63.6 10.4 %collective-permute-start.11 = (bf16[736,256]{1,0:T(8,128)(2,1)}, bf16[736,256]{1,0:T(8,128)(2,1)}, u32[]{:S(2)}, u32[]{:S(2)}) collective-permute-start(bf16[736,256]{1,0:T(8,128)(2,1)} %collective-permute-done.8.refs_2_), channel_id=1, source_target_pairs={{0,8},{8,0},{16,24},{24,16},{32,40},{40,32},{48,56},{56,48},{64,72... | collective-permute-start | bytes 1130504 | tf_op jit(solution)/shard_map/ppermute | solution.py:425
  68.7 17.8 %collective-permute-start.14 = (bf16[4,512,128]{2,1,0:T(8,128)(2,1)}, bf16[4,512,128]{2,1,0:T(8,128)(2,1)}, u32[]{:S(2)}, u32[]{:S(2)}) collective-permute-start(bf16[4,512,128]{2,1,0:T(8,128)(2,1)} %get-tuple-element.135), channel_id=1, source_target_pairs={{0,8},{8,0},{16,24},{24,16},{32,40},{40,32},{48,56},{56,48},{64,72... | collective-permute-start | bytes 1572872 | tf_op jit(solution)/shard_map/ppermute | solution.py:425
  70.3 16.2 %collective-permute-start.15 = (bf16[256,1024]{1,0:T(8,128)(2,1)S(1)}, bf16[256,1024]{1,0:T(8,128)(2,1)S(1)}, u32[]{:S(2)}, u32[]{:S(2)}) collective-permute-start(bf16[256,1024]{1,0:T(8,128)(2,1)S(1)} %copy-done.9), channel_id=1, source_target_pairs={{0,16},{8,24},{16,0},{24,8},{32,48},{40,56},{48,32},{56,40},{64,80... | collective-permute-start | bytes 1572872 | tf_op jit(solution)/shard_map/ppermute | solution.py:425
  76.1 4.9 %collective-permute-start.12 = (f16[64,1024]{1,0:T(8,128)(2,1)S(1)}, f16[64,1024]{1,0:T(8,128)(2,1)S(1)}, u32[]{:S(2)}, u32[]{:S(2)}) collective-permute-start(f16[64,1024]{1,0:T(8,128)(2,1)S(1)} %multiply_convert_fusion.1), channel_id=1, source_target_pairs={{0,2},{1,3},{2,0},{3,1},{4,6},{5,7},{6,4},{7,5},{8,10},{9,11},{10,... | collective-permute-start | bytes 393224 | tf_op jit(solution)/shard_map/ppermute | solution.py:425
  77.4 15.5 %collective-permute-start.17 = (bf16[4,512,128]{2,1,0:T(8,128)(2,1)S(1)}, bf16[4,512,128]{2,1,0:T(8,128)(2,1)S(1)}, u32[]{:S(2)}, u32[]{:S(2)}) collective-permute-start(bf16[4,512,128]{2,1,0:T(8,128)(2,1)S(1)} %copy-done.20), channel_id=1, source_target_pairs={{0,32},{8,40},{16,48},{24,56},{32,64},{40,72},{48,80},{56,88},{64,... | collective-permute-start | bytes 1572872 | tf_op jit(solution)/shard_map/ppermute | solution.py:431
  81.0 5.4 %collective-permute-start.13 = (f16[64,1024]{1,0:T(8,128)(2,1)S(1)}, f16[64,1024]{1,0:T(8,128)(2,1)S(1)}, u32[]{:S(2)}, u32[]{:S(2)}) collective-permute-start(f16[64,1024]{1,0:T(8,128)(2,1)S(1)} %add.21), channel_id=1, source_target_pairs={{0,4},{1,5},{2,6},{3,7},{4,0},{5,1},{6,2},{7,3},{8,12},{9,13},{10,... | collective-permute-start | bytes 393224 | tf_op jit(solution)/shard_map/ppermute | solution.py:425
  83.9 11.3 %collective-permute-start.18 = (bf16[256,1024]{1,0:T(8,128)(2,1)S(1)}, bf16[256,1024]{1,0:T(8,128)(2,1)S(1)}, u32[]{:S(2)}, u32[]{:S(2)}) collective-permute-start(bf16[256,1024]{1,0:T(8,128)(2,1)S(1)} %copy-done.9), channel_id=1, source_target_pairs={{0,8},{8,0},{16,24},{24,16},{32,40},{40,32},{48,56},{56,48},{64,72... | collective-permute-start | bytes 1572872 | tf_op jit(solution)/shard_map/ppermute | solution.py:425
  86.5 8.7 %collective-permute-start.19 = (bf16[256,1024]{1,0:T(8,128)(2,1)S(1)}, bf16[256,1024]{1,0:T(8,128)(2,1)S(1)}, u32[]{:S(2)}, u32[]{:S(2)}) collective-permute-start(bf16[256,1024]{1,0:T(8,128)(2,1)S(1)} %collective-permute-done.15.refs_6_), channel_id=1, source_target_pairs={{0,8},{8,0},{16,24},{24,16},{32,40},{40,32},{48,56},{56,48},{64,72... | collective-permute-start | bytes 1572872 | tf_op jit(solution)/shard_map/ppermute | solution.py:425
  88.8 6.3 %collective-permute-start.16 = (f16[64,1024]{1,0:T(8,128)(2,1)S(1)}, f16[64,1024]{1,0:T(8,128)(2,1)S(1)}, u32[]{:S(2)}, u32[]{:S(2)}) collective-permute-start(f16[64,1024]{1,0:T(8,128)(2,1)S(1)} %add.22), channel_id=1, source_target_pairs={{0,1},{1,0},{2,3},{3,2},{4,5},{5,4},{6,7},{7,6},{8,9},{9,8},{10,11... | collective-permute-start | bytes 393224 | tf_op jit(solution)/shard_map/ppermute | solution.py:425
  97.9 16.9 %all-to-all-start.1 = ((f16[8,8,1024]{2,1,0:T(8,128)(2,1)}), f16[8,8,1024]{2,1,0:T(8,128)(2,1)S(1)}, u32[]{:S(2)}, u32[]{:S(2)}) async-start(f16[8,8,1024]{2,1,0:T(8,128)(2,1)} %fusion), calls=%async_computation.1 | async-start | bytes 262144 | tf_op jit(solution)/shard_map/all_to_all | solution.py:563
  107.1 8.7 %collective-permute-start.20 = (bf16[4,512,128]{2,1,0:T(8,128)(2,1)}, bf16[4,512,128]{2,1,0:T(8,128)(2,1)}, u32[]{:S(2)}, u32[]{:S(2)}) collective-permute-start(bf16[4,512,128]{2,1,0:T(8,128)(2,1)} %copy-done.10), channel_id=1, source_target_pairs={{0,8},{8,0},{16,24},{24,16},{32,40},{40,32},{48,56},{56,48},{64,72... | collective-permute-start | bytes 1572872 | tf_op jit(solution)/shard_map/ppermute | solution.py:425
  115.8 12.4 %all-to-all-start.2 = ((f32[8,1,128]{2,1,0:T(1,128)}), f32[8,1,128]{2,1,0:T(1,128)S(1)}, u32[]{:S(2)}, u32[]{:S(2)}) async-start(f32[8,1,128]{2,1,0:T(1,128)} %hidden.1), calls=%async_computation.2 | async-start | bytes 8192 | tf_op jit(solution)/shard_map/all_to_all | solution.py:575
  (21 other events, 108.5 us)

commit v4 on v3

--- a/solution.py
+++ b/solution.py
@@ -42,13 +42,13 @@
 
 
 def pick_kernel(me_ref, steps_hbm, q_hbm, weight_hbm, stream_hbm, *refs):
-    keep_ref, pass_ref, send_ref, pack_hbm, all_ref, steps_ref, q_ref, sems = refs
+    keep_ref, pass_ref, send_ref, pack_ref, all_ref, steps_ref, q_ref, sems = refs
     copies = [pltpu.make_async_copy(steps_hbm, steps_ref, sems.at[0])]
     for k in range(4):
         part = pl.ds(k * BLOCK // 4, BLOCK // 4)
         copies.append(pltpu.make_async_copy(q_hbm.at[part], q_ref.at[part], sems.at[1 + k]))
     for k, (source, begin) in enumerate([(weight_hbm, 0), (stream_hbm, BLOCK)]):
-        target = pack_hbm.at[pl.ds(begin, source.shape[0])]
+        target = pack_ref.at[pl.ds(begin, source.shape[0])]
         copies.append(pltpu.make_async_copy(source, target, sems.at[5 + k]))
     for copy in copies:
         copy.start()
@@ -82,15 +82,16 @@
 
 
 def picked_kernel(me_ref, lengths_hbm, steps_hbm, q_ref, q1_ref, q2_ref, *refs):
-    kv_refs, out_ref = refs[:PLANE], refs[PLANE]
-    plane_ref, lengths, steps_ref, sems = refs[-4:]
-    kv_s = plane_ref
+    kv_refs, out_ref, moved_hbm = refs[:PLANE], refs[PLANE], refs[PLANE + 1]
+    kv_s, lengths, steps_ref, sems = refs[-4:]
     lengths_copy = pltpu.make_async_copy(lengths_hbm, lengths, sems.at[PLANE])
     steps_copy = pltpu.make_async_copy(steps_hbm, steps_ref, sems.at[PLANE + 1])
     copies = [
         pltpu.make_async_copy(kv, kv_s.at[pl.ds(2 * k, 2)], sems.at[k])
         for k, kv in enumerate(kv_refs)
     ]
+    half = pl.ds(PLANE, PLANE)
+    moved_copy = pltpu.make_async_copy(kv_s.at[half], moved_hbm, sems.at[PLANE + 2])
     for copy in [lengths_copy, steps_copy] + copies:
         copy.start()
     lengths_copy.wait()
@@ -123,6 +124,7 @@
             q, kv_s[2 * k], (((1,), (1,)), ((), ())), preferred_element_type=F32
         )
         scores.append(jnp.where(mask, s, LOW))
+    moved_copy.start()
     top = jnp.maximum(jnp.maximum(scores[0], scores[1]), jnp.maximum(scores[2], scores[3]))
     top = jnp.maximum(jnp.max(top, axis=1, keepdims=True), 0.1 * LOW)
     ones = jnp.ones((BLOCK, HD), BF16)
@@ -152,34 +154,37 @@
             at = z * PAD + t
             packed = packed + pltpu.roll(stats[at : at + 1], 16 * t, 1)
         out_ref[z * PAD + TRACES : (z + 1) * PAD, :HD] = packed
+    moved_copy.wait()
 
 
 def attend_kernel(slots, first, last, joined, *refs):
     n = len(slots)
     arrays = 1 + max(slot[2] for slot in slots)
-    me_ref, lengths_hbm, q_ref = refs[:3]
+    me_ref, lengths_hbm, q_hbm = refs[:3]
     kv_hbm = [refs[3 + array].at[pl.ds(2 * at, 2)] for _, _, array, at in slots]
-    kv_ref, lengths, sems = refs[-3:]
-    if first:
-        q_hbm = q_ref
-        q_ref, m_ref, l_ref, acc_ref = refs[3 + arrays : 7 + arrays]
-    else:
-        m_ref, l_ref, acc_ref = refs[3 + arrays : 6 + arrays]
-    pair_copies = []
-    for k in range(joined):
-        source = refs[3 + arrays - joined + k]
-        target = refs[-4].at[pl.ds(2 * k, 2)]
-        pair_copies.append(pltpu.make_async_copy(source, target, sems.at[n + 2 + k]))
+    m_ref, l_ref, acc_ref = refs[3 + arrays : 6 + arrays]
+    q_ref, kv_ref, lengths, sems = refs[-4:]
     copies = [
         pltpu.make_async_copy(kv, kv_ref.at[k], sems.at[k]) for k, kv in enumerate(kv_hbm)
     ]
     copies.append(pltpu.make_async_copy(lengths_hbm, lengths, sems.at[n]))
-    if first:
-        copies.append(pltpu.make_async_copy(q_hbm, q_ref, sems.at[n + 1]))
-    for copy in copies + pair_copies:
+    for k in range(4):
+        part = pl.ds(k * BLOCK // 4, BLOCK // 4)
+        copies.append(
+            pltpu.make_async_copy(q_hbm.at[part], q_ref.at[part], sems.at[n + 1 + k])
+        )
+    pair_copies = []
+    for k in range(joined):
+        target = refs[-5].at[pl.ds(2 * k, 2)]
+        pair_copies.append(
+            pltpu.make_async_copy(kv_ref.at[n - joined + k], target, sems.at[n + 5 + k])
+        )
+    for copy in copies:
         copy.start()
     for copy in copies:
         copy.wait()
+    for copy in pair_copies:
+        copy.start()
     me = me_ref[0]
     place = me % PLANE
     row0 = me * BLOCK
@@ -262,48 +267,41 @@
     tiles = BLOCK // TILE
     lax.fori_loop(tiles * int(first), tiles * n, other_tile, 0)
     if last:
-        out_ref = refs[-4]
+        out_ref = refs[-5]
         out_ref[...] = acc_ref[...] / l_ref[...]
     for copy in pair_copies:
         copy.wait()
 
 
-def attend(slots, me, lengths, queries, kvs, state, last=False, in_vmem=0, joined=0):
+def attend(slots, me, lengths, queries, kvs, state, last=False, joined=0):
     shape = (BLOCK, PER_GROUP * HD)
     first = state is None
-    kept = [pltpu.with_memory_space_constraint(kv, pltpu.VMEM) for kv in kvs[:in_vmem]]
-    operands = [me, *pinned([lengths, queries] if first else [lengths]), *kept, *kvs[in_vmem:]]
+    operands = [me, *pinned([lengths, queries]), *kvs]
     specs = [SMEM] + [HBM] * (len(operands) - 1)
+    shapes, aliases = (pltpu.VMEM(shape, F32),) * 3, {}
     if not first:
-        q, *sums = [pltpu.with_memory_space_constraint(x, pltpu.VMEM) for x in state]
-        operands[2:2] = [q]
-        specs[2:2] = [VMEM] + [VMEM] * in_vmem
-        del specs[3 + in_vmem : 3 + 2 * in_vmem]
         at = len(operands)
-        operands += sums
+        operands += [pltpu.with_memory_space_constraint(x, pltpu.VMEM) for x in state]
         specs += [VMEM] * 3
-    shapes = (pltpu.VMEM(shape, BF16),) + (pltpu.VMEM(shape, F32),) * 3
-    out_specs, aliases = [VMEM] * 4, {}
+        aliases = {at + k: k for k in range(3)}
     if last:
-        shapes, out_specs = (jax.ShapeDtypeStruct(shape, F32),), [VMEM]
-    elif not first:
-        aliases = {2: 0, at: 1, at + 1: 2, at + 2: 3}
+        shapes, aliases = (jax.ShapeDtypeStruct(shape, F32),), {}
     if joined:
-        shapes += (pltpu.HBM((2 * joined, BLOCK, HD), BF16),)
-        out_specs.append(HBM)
+        shapes += (pltpu.VMEM((2 * joined, BLOCK, HD), BF16),)
     work = PER_GROUP * BLOCK * BLOCK * len(slots)
     got = pl.pallas_call(
         functools.partial(attend_kernel, slots, first, last, joined),
         out_shape=shapes,
         in_specs=specs,
-        out_specs=out_specs,
+        out_specs=[VMEM] * len(shapes),
         scratch_shapes=[
+            pltpu.VMEM(shape, BF16),
             pltpu.VMEM((len(slots), 2, BLOCK, HD), BF16),
             pltpu.SMEM((TRACES,), jnp.int32),
-            pltpu.SemaphoreType.DMA((len(slots) + 2 + joined,)),
+            pltpu.SemaphoreType.DMA((len(slots) + 5 + joined,)),
         ],
         input_output_aliases=aliases,
-        compiler_params=pltpu.CompilerParams(vmem_limit_bytes=32 << 20),
+        compiler_params=pltpu.CompilerParams(vmem_limit_bytes=20 << 20),
         cost_estimate=pl.CostEstimate(
             flops=4 * HD * work, bytes_accessed=1 << 20, transcendentals=work
         ),
@@ -311,7 +309,7 @@
     )(*operands)
     if last:
         return got[0]
-    return (list(got[:4]), got[4]) if joined else list(got)
+    return (list(got[:3]), got[3]) if joined else list(got)
 
 
 def pinned(values):
@@ -324,7 +322,7 @@
         out_shape=shape,
         in_specs=specs or [VMEM] * len(operands),
         out_specs=out_specs or ([VMEM] * len(shape) if type(shape) is tuple else VMEM),
-        compiler_params=pltpu.CompilerParams(vmem_limit_bytes=24 << 20),
+        compiler_params=pltpu.CompilerParams(vmem_limit_bytes=16 << 20),
         **kw,
     )(*operands)
 
@@ -456,10 +454,10 @@
     keep, passed, sent, weight = small_call(
         pick_kernel,
         tuple(jax.ShapeDtypeStruct((n * GROUP, half), BF16) for n in (1, 1, 2))
-        + (pltpu.HBM(packed, BF16),),
+        + (pltpu.VMEM(packed, BF16),),
         [me, *pinned([step_rows, queries, out_weight, step_stream])],
         [SMEM] + [HBM] * 4,
-        [VMEM] * 3 + [HBM],
+        [VMEM] * 4,
         scratch_shapes=[
             pltpu.VMEM((PLANE * GROUP, half), BF16),
             pltpu.VMEM((TRACES, STEPS), jnp.int32),
@@ -479,13 +477,12 @@
     state = add([(0, 0, 0, 0), (0, 1, 1, 0)], kvs=[pinned([kv0y])[0], core0], state=None)
     wanted, wanted1, wanted2, *state = tie(wanted, wanted1, wanted2, *state)
 
-    weight, wanted = tie(weight, wanted)
-    firsts = [weight, swapped(weight, "ctx", 1), swapped(weight, "ctx", 2)]
-    kv1, _ = tie(raised(kv0, 1), wanted)
-
-    parts, plane = small_call(
+    kv1, wanted = tie(raised(kv0, 1), wanted)
+    across1 = swapped(kv1, "ctx", 2)
+
+    parts, moved = small_call(
         picked_kernel,
-        (jax.ShapeDtypeStruct((GROUP, half), F32), pltpu.VMEM((2 * PLANE, BLOCK, HD), BF16)),
+        (jax.ShapeDtypeStruct((GROUP, half), F32), pltpu.HBM((PLANE, BLOCK, HD), BF16)),
         [
             me,
             *pinned([trace_lengths, step_rows]),
@@ -498,27 +495,27 @@
             core0y,
         ],
         [SMEM, HBM, HBM] + [VMEM] * 3 + [HBM] * 4,
+        [VMEM, HBM],
         scratch_shapes=[
+            pltpu.VMEM((2 * PLANE, BLOCK, HD), BF16),
             pltpu.SMEM((TRACES,), jnp.int32),
             pltpu.VMEM((TRACES, STEPS), jnp.int32),
-            pltpu.SemaphoreType.DMA((PLANE + 2,)),
+            pltpu.SemaphoreType.DMA((PLANE + 3,)),
         ],
         name="picked",
     )
-    parts, kv1, plane, *state = tie(parts, kv1, plane, *state)
-    across1 = swapped(kv1, "ctx", 2)
+    parts, kv1, across1, weight, *state = tie(parts, kv1, across1, weight, *state)
+
+    firsts = [weight] + [swapped(weight, "ctx", bits) for bits in (1, 2, 3)]
+
     parts = jnp.broadcast_to(parts.astype(jnp.float16)[None], (Z, GROUP, half))
     parts = lax.all_to_all(parts, "ctx", 0, 0, axis_index_groups=columns).astype(F32)
-    firsts[2], across1 = tie(firsts[2], across1)
-    firsts.append(swapped(firsts[2], "ctx", 1))
     state, pair1 = add(
-        [(0, 2, 0, 2), (0, 3, 0, 3), (1, 0, 1, 0), (1, 2, 2, 0)],
-        kvs=[plane, kv1, across1],
+        [(0, 2, 0, 0), (0, 3, 0, 1), (1, 0, 1, 0), (1, 2, 2, 0)],
+        kvs=pinned([moved, kv1, across1]),
         state=state,
-        in_vmem=1,
         joined=2,
     )
-    cores1 = swapped(pair1, "ctx", 1)
     parts, pair1, weight, *state = tie(parts, pair1, score_weight, *state)
     weights = [weight, swapped(weight, "ctx", 1), swapped(weight, "ctx", 2)]
 
@@ -534,7 +531,7 @@
         name="project",
     )
     projected, pair1 = tie((projected * 0.25).astype(jnp.float16), pair1)
-    pair2 = raised(pair1, 1)
+    pair2, cores1 = raised(pair1, 1), swapped(pair1, "ctx", 1)
     projected = projected + swapped(projected, "head", 2)
     projected = projected + swapped(projected, "head", 4)
     projected, cores1, weights[2] = tie(projected, cores1, weights[2])
@@ -559,7 +556,7 @@
     )
     inner, pair2, *state = tie(inner, pair2, *state)
     inner = (inner * 2.0**-10).astype(jnp.float16).reshape(Z, PAD, WIDE)
-    state = add([(2, 0, 0, 0), (2, 2, 0, 1)], kvs=[pair2], state=state)
+    state = add([(2, 0, 0, 0), (2, 2, 0, 1)], kvs=pinned([pair2]), state=state)
     inner = lax.all_to_all(inner, "ctx", 0, 0, axis_index_groups=columns)
     inner, *state = tie(inner, *state)
     inner = jnp.sum(inner.astype(F32), axis=0) * 2.0**10

time: 144 us -> 128 us (0.89)
  Pallas kernels: 31.4 us -> 21.7 us
  starting transfers between devices: 54 us -> 45 us
  waiting for transfers between devices: 30.9 us -> 39.6 us
  local copies, waits for them, and re-layouts: 9.99 us -> 2.6 us
    all_to_all x1, waiting for transfers between devices: 0.01 us -> 11.3 us  [per_device(): lax.all_to_all(parts, 'ctx', 0, 0, axis_index_groups=columns).astype(F32)]
    pallas_call x6, Pallas kernels: 22.1 us -> 11 us  [small_call(): pl.pallas_call(kernel, out_shape=shape, in_specs=specs or [VMEM] * len(op...]
    unnamed x43 -> x21, local copies, waits for them, and re-layouts: 9.14 us -> 1.74 us
    ppermute x17, starting transfers between devices: 25.2 us -> 20.8 us  [swapped(): return lax.ppermute(value, axis, [(s, s ^ bit) for s in range(count)])]
    ppermute x17, waiting for transfers between devices: 22.6 us -> 18.9 us  [swapped(): return lax.ppermute(value, axis, [(s, s ^ bit) for s in range(count)])]
    all_to_all x1, starting transfers between devices: 9.12 us -> 5.75 us  [per_device(): inner = lax.all_to_all(inner, 'ctx', 0, 0, axis_index_groups=columns)]
    ppermute x4, starting transfers between devices: 9.44 us -> 6.95 us  [raised(): lax.ppermute(value, 'ctx', [(s, (s + steps) % count) for s in range(count)])]
    all_to_all x1, waiting for transfers between devices: 2.99 us -> 5.35 us  [per_device(): inner = lax.all_to_all(inner, 'ctx', 0, 0, axis_index_groups=columns)]
  transfers between devices with their start and end apart: 24 -> 24, of which waited for: 10 -> 12; matrix products, arithmetic and copies ran while one was open for 1% -> 2% of each run, Pallas kernels for 9% -> 11%
where the time goes in v4:
time: 128 us; the launch traced here: 127 us
  starting transfers between devices  45 us (35%)
  waiting for transfers between devices  39.6 us (31%)
  Pallas kernels  21.7 us (17%)
  blocking collectives  14.4 us (11%)
  other arithmetic  2.98 us (2%)
  local copies, waits for them, and re-layouts  2.6 us (2%)
    ppermute x17, starting transfers between devices, swapped(): return lax.ppermute(value, axis, [(s, s ^ bit) for s in range(count)])  20.8 us
    ppermute x17, waiting for transfers between devices, swapped(): return lax.ppermute(value, axis, [(s, s ^ bit) for s in range(count)])  18.9 us
    all_to_all x1, blocking collectives, per_device(): lax.all_to_all(jnp.broadcast_to(gap[None], (count, 1, HD)), 'ctx', 0, 0)  14.4 us
    all_to_all x1, waiting for transfers between devices, per_device(): lax.all_to_all(parts, 'ctx', 0, 0, axis_index_groups=columns).astype(F32)  11.3 us
    pallas_call x6, Pallas kernels, small_call(): pl.pallas_call(kernel, out_shape=shape, in_specs=specs or [VMEM] * len(op...  11 us
    pallas_call x5, Pallas kernels, attend(): pl.pallas_call(functools.partial(attend_kernel, slots, first, last, joine...  10.6 us
    ppermute x4, starting transfers between devices, raised(): lax.ppermute(value, 'ctx', [(s, (s + steps) % count) for s in range(count)])  6.95 us
    all_to_all x1, starting transfers between devices, per_device(): gap = lax.all_to_all(gap, 'head', 0, 0)  6.36 us
  transfers between devices with their start and end apart: 24, of which 12 were waited for; matrix products, arithmetic and copies ran while one was open for 2% of the time, Pallas kernels for 11%

profile of v4, /device:TPU:1, one launch (start us, length us, event | category | flops | bytes accessed | tf_op | source)
XLA Modules:
  0.0 127.2 jit_solution(7277473773313359953)
XLA Ops:
  0.6 1.8 %pick.1 = (bf16[64,512]{1,0:T(8,128)(2,1)S(1)}, bf16[64,512]{1,0:T(8,128)(2,1)S(1)}, bf16[128,512]{1,0:T(8,128)(2,1)S(1)}, bf16[736,256]{1,0:T(8,128)(2,1)S(1)}) custom-call(s32[1]{0:T(128)} %bitcast.me_ref.refs_0_, s32[7,32]{1,0:T(8,128)} %steps_hbm.3, bf16[512,512]{1,0:T(8,128)(2,1)} %refs_2_.9, bf16[512,256]{1,0:T(8,128)(2,1)} %weight_hbm.1, ...), custom_call_target="tpu_custom_call" | custom-call | tf_op jit(solution)/shard_map/pick/pallas_call | solution.py:320
  2.4 3.3 %collective-permute-start.1 = (bf16[128,512]{1,0:T(8,128)(2,1)S(1)}, bf16[128,512]{1,0:T(8,128)(2,1)S(1)}, u32[]{:S(2)}, u32[]{:S(2)}) collective-permute-start(bf16[128,512]{1,0:T(8,128)(2,1)S(1)} %get-tuple-element.78), channel_id=1, source_target_pairs={{0,8},{8,0},{16,24},{24,16},{32,40},{40,32},{48,56},{56,48},{64,72... | collective-permute-start | bytes 393224 | tf_op jit(solution)/shard_map/ppermute | solution.py:423
  7.3 2.6 %collective-permute-done.2 = bf16[64,512]{1,0:T(8,128)(2,1)S(1)} collective-permute-done((bf16[64,512]{1,0:T(8,128)(2,1)S(1)}, bf16[64,512]{1,0:T(8,128)(2,1)S(1)}, u32[]{:S(2)}, u32[]{:S(2)}) %collective-permute-start.2) | collective-permute-done | bytes 65568 | tf_op jit(solution)/shard_map/ppermute | solution.py:423
  11.3 3.9 %collective-permute-start.5 = (bf16[64,512]{1,0:T(8,128)(2,1)S(1)}, bf16[64,512]{1,0:T(8,128)(2,1)S(1)}, u32[]{:S(2)}, u32[]{:S(2)}) collective-permute-start(bf16[64,512]{1,0:T(8,128)(2,1)S(1)} %fusion.1.q_ref), channel_id=1, source_target_pairs={{0,224},{8,232},{16,240},{24,248},{32,0},{40,8},{48,16},{56,24},{6... | collective-permute-start | bytes 196616 | tf_op jit(solution)/shard_map/ppermute | solution.py:429
  15.2 1.9 %collective-permute-start.6 = (bf16[64,512]{1,0:T(8,128)(2,1)S(1)}, bf16[64,512]{1,0:T(8,128)(2,1)S(1)}, u32[]{:S(2)}, u32[]{:S(2)}) collective-permute-start(bf16[64,512]{1,0:T(8,128)(2,1)S(1)} %fusion.1.q_ref), channel_id=1, source_target_pairs={{0,192},{8,200},{16,208},{24,216},{32,224},{40,232},{48,240},{56,2... | collective-permute-start | bytes 196616 | tf_op jit(solution)/shard_map/ppermute | solution.py:429
  17.1 4.2 %attend_0_0.1 = (f32[512,512]{1,0:T(8,128)S(1)}, f32[512,512]{1,0:T(8,128)S(1)}, f32[512,512]{1,0:T(8,128)S(1)}) custom-call(s32[1]{0:T(128)} %bitcast.me_ref.refs_0_, s32[7]{0:T(128)} %refs_1_.9, bf16[512,512]{1,0:T(8,128)(2,1)} %refs_2_.9, bf16[2,512,128]{2,1,0:T(8,128)(2,1)} %refs_0_.1, bf16[2,512,128]{2,1,0:T(8,128)(2,1)S(1)} %collective-permute-done.3.refs_4_.refs_1_), custom_call_target="tpu_custom_call" | custom-call | flops 1073741824 | bytes 1048576 | tf_op jit(solution)/shard_map/attend_0_0/pallas_call | solution.py:292
  24.2 3.0 %picked.1 = (f32[64,512]{1,0:T(8,128)S(1)}, bf16[4,512,128]{2,1,0:T(8,128)(2,1)}) custom-call(s32[1]{0:T(128)} %bitcast.me_ref.refs_0_, s32[7]{0:T(128)} %refs_1_.9, s32[7,32]{1,0:T(8,128)} %steps_hbm.3, bf16[64,512]{1,0:T(8,128)(2,1)S(1)} %fusion.1.q_ref, bf16[64,512]{1,0:T(8,128)(2,1)S(1)} %collective-permute-done.5.q1_ref, ...), custom_call_target="tpu_custom_call" | custom-call | tf_op jit(solution)/shard_map/picked/pallas_call | solution.py:320
  27.2 3.5 %collective-permute-done.8.refs_5_ = bf16[2,512,128]{2,1,0:T(8,128)(2,1)S(1)} collective-permute-done((bf16[2,512,128]{2,1,0:T(8,128)(2,1)S(1)}, bf16[2,512,128]{2,1,0:T(8,128)(2,1)S(1)}, u32[]{:S(2)}, u32[]{:S(2)}) %collective-permute-start.8) | collective-permute-done | bytes 262176 | tf_op jit(solution)/shard_map/ppermute | solution.py:423
  32.2 5.2 %all-to-all-start = ((f16[8,64,512]{2,1,0:T(8,128)(2,1)}), f16[8,64,512]{2,1,0:T(8,128)(2,1)}, u32[]{:S(2)}, u32[]{:S(2)}) async-start(f16[8,64,512]{2,1,0:T(8,128)(2,1)} %broadcast_in_dim.4), calls=%async_computation | async-start | bytes 1048576 | tf_op jit(solution)/shard_map/all_to_all | solution.py:512
  37.5 2.8 %collective-permute-start.11 = (bf16[736,256]{1,0:T(8,128)(2,1)S(1)}, bf16[736,256]{1,0:T(8,128)(2,1)}, u32[]{:S(2)}, u32[]{:S(2)}) collective-permute-start(bf16[736,256]{1,0:T(8,128)(2,1)S(1)} %get-tuple-element.111.refs_0_), channel_id=1, source_target_pairs={{0,24},{8,16},{16,8},{24,0},{32,56},{40,48},{48,40},{56,32},{64,88... | collective-permute-start | bytes 1130504 | tf_op jit(solution)/shard_map/ppermute | solution.py:423
  42.8 11.3 %all-to-all-done = f16[8,64,512]{2,1,0:T(8,128)(2,1)} async-done(((f16[8,64,512]{2,1,0:T(8,128)(2,1)}), f16[8,64,512]{2,1,0:T(8,128)(2,1)}, u32[]{:S(2)}, u32[]{:S(2)}) %all-to-all-start) | async-done | bytes 524320 | tf_op jit(solution)/shard_map/all_to_all | solution.py:512
  56.0 2.1 %project.1 = f32[64,1024]{1,0:T(8,128)S(1)} custom-call(f32[8,64,512]{2,1,0:T(8,128)S(1)} %convert_element_type.22.got_ref, bf16[736,256]{1,0:T(8,128)(2,1)S(1)} %get-tuple-element.111.refs_0_, bf16[736,256]{1,0:T(8,128)(2,1)} %collective-permute-done.9.refs_1_, bf16[736,256]{1,0:T(8,128)(2,1)} %collective-permute-done.10.refs_2_, ...), custom_call_target="tpu_custom_call" | custom-call | tf_op jit(solution)/shard_map/project/pallas_call | solution.py:320
  61.2 3.1 %collective-permute-done.12 = f16[64,1024]{1,0:T(8,128)(2,1)S(1)} collective-permute-done((f16[64,1024]{1,0:T(8,128)(2,1)S(1)}, f16[64,1024]{1,0:T(8,128)(2,1)S(1)}, u32[]{:S(2)}, u32[]{:S(2)}) %collective-permute-start.12) | collective-permute-done | bytes 131104 | tf_op jit(solution)/shard_map/ppermute | solution.py:423
  64.3 2.8 %collective-permute-start.13 = (f16[64,1024]{1,0:T(8,128)(2,1)S(1)}, f16[64,1024]{1,0:T(8,128)(2,1)S(1)}, u32[]{:S(2)}, u32[]{:S(2)}) collective-permute-start(f16[64,1024]{1,0:T(8,128)(2,1)S(1)} %add.21), channel_id=1, source_target_pairs={{0,4},{1,5},{2,6},{3,7},{4,0},{5,1},{6,2},{7,3},{8,12},{9,13},{10,... | collective-permute-start | bytes 393224 | tf_op jit(solution)/shard_map/ppermute | solution.py:423
  69.8 3.1 %collective-permute-done.15.refs_6_ = bf16[256,1024]{1,0:T(8,128)(2,1)S(1)} collective-permute-done((bf16[256,1024]{1,0:T(8,128)(2,1)S(1)}, bf16[256,1024]{1,0:T(8,128)(2,1)S(1)}, u32[]{:S(2)}, u32[]{:S(2)}) %collective-permute-start.15) | collective-permute-done | bytes 524320 | tf_op jit(solution)/shard_map/ppermute | solution.py:423
  73.7 2.6 %collective-permute-start.16 = (f16[64,1024]{1,0:T(8,128)(2,1)S(1)}, f16[64,1024]{1,0:T(8,128)(2,1)S(1)}, u32[]{:S(2)}, u32[]{:S(2)}) collective-permute-start(f16[64,1024]{1,0:T(8,128)(2,1)S(1)} %add.22), channel_id=1, source_target_pairs={{0,1},{1,0},{2,3},{3,2},{4,5},{5,4},{6,7},{7,6},{8,9},{9,8},{10,11... | collective-permute-start | bytes 393224 | tf_op jit(solution)/shard_map/ppermute | solution.py:423
  77.6 2.8 %collective-permute-done.16 = f16[64,1024]{1,0:T(8,128)(2,1)S(1)} collective-permute-done((f16[64,1024]{1,0:T(8,128)(2,1)S(1)}, f16[64,1024]{1,0:T(8,128)(2,1)S(1)}, u32[]{:S(2)}, u32[]{:S(2)}) %collective-permute-start.16) | collective-permute-done | bytes 131104 | tf_op jit(solution)/shard_map/ppermute | solution.py:423
  80.4 2.1 %inner.1 = f32[64,1024]{1,0:T(8,128)S(1)} custom-call(s32[1]{0:T(128)} %bitcast.me_ref.refs_0_, f32[64,1024]{1,0:T(8,128)S(1)} %add_multiply_fusion.total_ref, bf16[736,256]{1,0:T(8,128)(2,1)S(1)} %get-tuple-element.111.refs_0_, bf16[736,256]{1,0:T(8,128)(2,1)} %collective-permute-done.9.refs_1_, bf16[736,256]{1,0:T(8,128)(2,1)} %collective-permute-done.10.refs_2_, ...), custom_call_target="tpu_custom_call" | custom-call | tf_op jit(solution)/shard_map/inner/pallas_call | solution.py:320
  83.2 5.8 %all-to-all-start.1 = ((f16[8,8,1024]{2,1,0:T(8,128)(2,1)}), f16[8,8,1024]{2,1,0:T(8,128)(2,1)}, u32[]{:S(2)}, u32[]{:S(2)}) async-start(f16[8,8,1024]{2,1,0:T(8,128)(2,1)} %fusion), calls=%async_computation.1 | async-start | bytes 262144 | tf_op jit(solution)/shard_map/all_to_all | solution.py:560
  91.5 5.3 %all-to-all-done.1 = f16[8,8,1024]{2,1,0:T(8,128)(2,1)} async-done(((f16[8,8,1024]{2,1,0:T(8,128)(2,1)}), f16[8,8,1024]{2,1,0:T(8,128)(2,1)}, u32[]{:S(2)}, u32[]{:S(2)}) %all-to-all-start.1) | async-done | bytes 131104 | tf_op jit(solution)/shard_map/all_to_all | solution.py:560
  98.6 6.4 %all-to-all-start.2 = ((f32[8,1,128]{2,1,0:T(1,128)}), f32[8,1,128]{2,1,0:T(1,128)S(1)}, u32[]{:S(2)}, u32[]{:S(2)}) async-start(f32[8,1,128]{2,1,0:T(1,128)} %hidden.1), calls=%async_computation.2 | async-start | bytes 8192 | tf_op jit(solution)/shard_map/all_to_all | solution.py:572
  105.0 2.4 %attend_2_1.1 = f32[512,512]{1,0:T(8,128)} custom-call(s32[1]{0:T(128)} %bitcast.me_ref.refs_0_, s32[7]{0:T(128)} %refs_1_.9, bf16[512,512]{1,0:T(8,128)(2,1)} %refs_2_.9, bf16[4,512,128]{2,1,0:T(8,128)(2,1)} %collective-permute-done.20.refs_3_, f32[512,512]{1,0:T(8,128)S(1)} %get-tuple-element.144.refs_4_, f32[512,512]{1,0:T(8,128)S(1)} %get-tuple-element.145.refs_5_, ...), custom_call_target="tpu_custom_call" | custom-call | flops 1073741824 | bytes 1048576 | tf_op jit(solution)/shard_map/attend_2_1/pallas_call | solution.py:292
  107.4 4.1 %all-to-all-done.2 = f32[8,1,128]{2,1,0:T(1,128)S(1)} async-done(((f32[8,1,128]{2,1,0:T(1,128)}), f32[8,1,128]{2,1,0:T(1,128)S(1)}, u32[]{:S(2)}, u32[]{:S(2)}) %all-to-all-start.2) | async-done | bytes 4128 | tf_op jit(solution)/shard_map/all_to_all | solution.py:572
  111.5 14.4 %all_to_all.20.got_ref = f32[32,1,128]{2,1,0:T(1,128)S(1)} all-to-all(f32[32,1,128]{2,1,0:T(1,128)S(1)} %broadcast_in_dim.5), channel_id=1, replica_groups=mesh['ctx'=32,'head'=8] {'ctx'}, dimensions={0} | all-to-all | bytes 32768 | tf_op jit(solution)/shard_map/all_to_all | solution.py:575
  (71 shorter events, 25.9 us)
Async XLA Ops:
  2.4 4.3 %collective-permute-start.1 = (bf16[128,512]{1,0:T(8,128)(2,1)S(1)}, bf16[128,512]{1,0:T(8,128)(2,1)S(1)}, u32[]{:S(2)}, u32[]{:S(2)}) collective-permute-start(bf16[128,512]{1,0:T(8,128)(2,1)S(1)} %get-tuple-element.78), channel_id=1, source_target_pairs={{0,8},{8,0},{16,24},{24,16},{32,40},{40,32},{48,56},{56,48},{64,72... | collective-permute-start | bytes 393224 | tf_op jit(solution)/shard_map/ppermute | solution.py:423
  6.7 3.2 %collective-permute-start.2 = (bf16[64,512]{1,0:T(8,128)(2,1)S(1)}, bf16[64,512]{1,0:T(8,128)(2,1)S(1)}, u32[]{:S(2)}, u32[]{:S(2)}) collective-permute-start(bf16[64,512]{1,0:T(8,128)(2,1)S(1)} %slice_add_fusion), channel_id=1, source_target_pairs={{0,16},{8,24},{16,0},{24,8},{32,48},{40,56},{48,32},{56,40},{64,80... | collective-permute-start | bytes 196616 | tf_op jit(solution)/shard_map/ppermute | solution.py:423
  6.8 3.1 %collective-permute-start.3 = (bf16[2,512,128]{2,1,0:T(8,128)(2,1)S(1)}, bf16[2,512,128]{2,1,0:T(8,128)(2,1)S(1)}, u32[]{:S(2)}, u32[]{:S(2)}) collective-permute-start(bf16[2,512,128]{2,1,0:T(8,128)(2,1)S(1)} %copy-done.6), channel_id=1, source_target_pairs={{0,8},{8,0},{16,24},{24,16},{32,40},{40,32},{48,56},{56,48},{64,72... | collective-permute-start | bytes 786440 | tf_op jit(solution)/shard_map/ppermute | solution.py:423
  10.0 11.4 %collective-permute-start.4 = (bf16[2,512,128]{2,1,0:T(8,128)(2,1)S(1)}, bf16[2,512,128]{2,1,0:T(8,128)(2,1)S(1)}, u32[]{:S(2)}, u32[]{:S(2)}) collective-permute-start(bf16[2,512,128]{2,1,0:T(8,128)(2,1)S(1)} %copy-done.6), channel_id=1, source_target_pairs={{0,16},{8,24},{16,0},{24,8},{32,48},{40,56},{48,32},{56,40},{64,80... | collective-permute-start | bytes 786440 | tf_op jit(solution)/shard_map/ppermute | solution.py:423
  10.6 12.4 %collective-permute-start = (bf16[2,512,128]{2,1,0:T(8,128)(2,1)S(1)}, bf16[2,512,128]{2,1,0:T(8,128)(2,1)S(1)}, u32[]{:S(2)}, u32[]{:S(2)}) collective-permute-start(bf16[2,512,128]{2,1,0:T(8,128)(2,1)S(1)} %copy-done.6), channel_id=1, source_target_pairs={{0,32},{8,40},{16,48},{24,56},{32,64},{40,72},{48,80},{56,88},{64,... | collective-permute-start | bytes 786440 | tf_op jit(solution)/shard_map/ppermute | solution.py:429
  11.3 10.1 %collective-permute-start.5 = (bf16[64,512]{1,0:T(8,128)(2,1)S(1)}, bf16[64,512]{1,0:T(8,128)(2,1)S(1)}, u32[]{:S(2)}, u32[]{:S(2)}) collective-permute-start(bf16[64,512]{1,0:T(8,128)(2,1)S(1)} %fusion.1.q_ref), channel_id=1, source_target_pairs={{0,224},{8,232},{16,240},{24,248},{32,0},{40,8},{48,16},{56,24},{6... | collective-permute-start | bytes 196616 | tf_op jit(solution)/shard_map/ppermute | solution.py:429
  15.2 6.2 %collective-permute-start.6 = (bf16[64,512]{1,0:T(8,128)(2,1)S(1)}, bf16[64,512]{1,0:T(8,128)(2,1)S(1)}, u32[]{:S(2)}, u32[]{:S(2)}) collective-permute-start(bf16[64,512]{1,0:T(8,128)(2,1)S(1)} %fusion.1.q_ref), channel_id=1, source_target_pairs={{0,192},{8,200},{16,208},{24,216},{32,224},{40,232},{48,240},{56,2... | collective-permute-start | bytes 196616 | tf_op jit(solution)/shard_map/ppermute | solution.py:429
  21.4 2.8 %collective-permute-start.7 = (bf16[2,512,128]{2,1,0:T(8,128)(2,1)S(1)}, bf16[2,512,128]{2,1,0:T(8,128)(2,1)S(1)}, u32[]{:S(2)}, u32[]{:S(2)}) collective-permute-start(bf16[2,512,128]{2,1,0:T(8,128)(2,1)S(1)} %collective-permute-done.4.refs_2_), channel_id=1, source_target_pairs={{0,8},{8,0},{16,24},{24,16},{32,40},{40,32},{48,56},{56,48},{64,72... | collective-permute-start | bytes 786440 | tf_op jit(solution)/shard_map/ppermute | solution.py:423
  23.0 7.6 %collective-permute-start.8 = (bf16[2,512,128]{2,1,0:T(8,128)(2,1)S(1)}, bf16[2,512,128]{2,1,0:T(8,128)(2,1)S(1)}, u32[]{:S(2)}, u32[]{:S(2)}) collective-permute-start(bf16[2,512,128]{2,1,0:T(8,128)(2,1)S(1)} %collective-permute-done.refs_4_), channel_id=1, source_target_pairs={{0,16},{8,24},{16,0},{24,8},{32,48},{40,56},{48,32},{56,40},{64,80... | collective-permute-start | bytes 786440 | tf_op jit(solution)/shard_map/ppermute | solution.py:423
  32.2 21.9 %all-to-all-start = ((f16[8,64,512]{2,1,0:T(8,128)(2,1)}), f16[8,64,512]{2,1,0:T(8,128)(2,1)}, u32[]{:S(2)}, u32[]{:S(2)}) async-start(f16[8,64,512]{2,1,0:T(8,128)(2,1)} %broadcast_in_dim.4), calls=%async_computation | async-start | bytes 1048576 | tf_op jit(solution)/shard_map/all_to_all | solution.py:512
  37.4 17.9 %collective-permute-start.10 = (bf16[736,256]{1,0:T(8,128)(2,1)S(1)}, bf16[736,256]{1,0:T(8,128)(2,1)}, u32[]{:S(2)}, u32[]{:S(2)}) collective-permute-start(bf16[736,256]{1,0:T(8,128)(2,1)S(1)} %get-tuple-element.111.refs_0_), channel_id=1, source_target_pairs={{0,16},{8,24},{16,0},{24,8},{32,48},{40,56},{48,32},{56,40},{64,80... | collective-permute-start | bytes 1130504 | tf_op jit(solution)/shard_map/ppermute | solution.py:423
  37.5 18.5 %collective-permute-start.11 = (bf16[736,256]{1,0:T(8,128)(2,1)S(1)}, bf16[736,256]{1,0:T(8,128)(2,1)}, u32[]{:S(2)}, u32[]{:S(2)}) collective-permute-start(bf16[736,256]{1,0:T(8,128)(2,1)S(1)} %get-tuple-element.111.refs_0_), channel_id=1, source_target_pairs={{0,24},{8,16},{16,8},{24,0},{32,56},{40,48},{48,40},{56,32},{64,88... | collective-permute-start | bytes 1130504 | tf_op jit(solution)/shard_map/ppermute | solution.py:423
  40.4 15.7 %collective-permute-start.9 = (bf16[736,256]{1,0:T(8,128)(2,1)S(1)}, bf16[736,256]{1,0:T(8,128)(2,1)}, u32[]{:S(2)}, u32[]{:S(2)}) collective-permute-start(bf16[736,256]{1,0:T(8,128)(2,1)S(1)} %get-tuple-element.111.refs_0_), channel_id=1, source_target_pairs={{0,8},{8,0},{16,24},{24,16},{32,40},{40,32},{48,56},{56,48},{64,72... | collective-permute-start | bytes 1130504 | tf_op jit(solution)/shard_map/ppermute | solution.py:423
  58.2 11.6 %collective-permute-start.14 = (bf16[4,512,128]{2,1,0:T(8,128)(2,1)S(1)}, bf16[4,512,128]{2,1,0:T(8,128)(2,1)S(1)}, u32[]{:S(2)}, u32[]{:S(2)}) collective-permute-start(bf16[4,512,128]{2,1,0:T(8,128)(2,1)S(1)} %copy-done.4), channel_id=1, source_target_pairs={{0,8},{8,0},{16,24},{24,16},{32,40},{40,32},{48,56},{56,48},{64,72... | collective-permute-start | bytes 1572872 | tf_op jit(solution)/shard_map/ppermute | solution.py:423
  59.4 13.5 %collective-permute-start.15 = (bf16[256,1024]{1,0:T(8,128)(2,1)S(1)}, bf16[256,1024]{1,0:T(8,128)(2,1)S(1)}, u32[]{:S(2)}, u32[]{:S(2)}) collective-permute-start(bf16[256,1024]{1,0:T(8,128)(2,1)S(1)} %copy-done), channel_id=1, source_target_pairs={{0,16},{8,24},{16,0},{24,8},{32,48},{40,56},{48,32},{56,40},{64,80... | collective-permute-start | bytes 1572872 | tf_op jit(solution)/shard_map/ppermute | solution.py:423
  59.6 4.7 %collective-permute-start.12 = (f16[64,1024]{1,0:T(8,128)(2,1)S(1)}, f16[64,1024]{1,0:T(8,128)(2,1)S(1)}, u32[]{:S(2)}, u32[]{:S(2)}) collective-permute-start(f16[64,1024]{1,0:T(8,128)(2,1)S(1)} %multiply_convert_fusion.1), channel_id=1, source_target_pairs={{0,2},{1,3},{2,0},{3,1},{4,6},{5,7},{6,4},{7,5},{8,10},{9,11},{10,... | collective-permute-start | bytes 393224 | tf_op jit(solution)/shard_map/ppermute | solution.py:423
  60.8 16.8 %collective-permute-start.17 = (bf16[4,512,128]{2,1,0:T(8,128)(2,1)S(1)}, bf16[4,512,128]{2,1,0:T(8,128)(2,1)S(1)}, u32[]{:S(2)}, u32[]{:S(2)}) collective-permute-start(bf16[4,512,128]{2,1,0:T(8,128)(2,1)S(1)} %copy-done.4), channel_id=1, source_target_pairs={{0,32},{8,40},{16,48},{24,56},{32,64},{40,72},{48,80},{56,88},{64,... | collective-permute-start | bytes 1572872 | tf_op jit(solution)/shard_map/ppermute | solution.py:429
  64.3 5.4 %collective-permute-start.13 = (f16[64,1024]{1,0:T(8,128)(2,1)S(1)}, f16[64,1024]{1,0:T(8,128)(2,1)S(1)}, u32[]{:S(2)}, u32[]{:S(2)}) collective-permute-start(f16[64,1024]{1,0:T(8,128)(2,1)S(1)} %add.21), channel_id=1, source_target_pairs={{0,4},{1,5},{2,6},{3,7},{4,0},{5,1},{6,2},{7,3},{8,12},{9,13},{10,... | collective-permute-start | bytes 393224 | tf_op jit(solution)/shard_map/ppermute | solution.py:423
  67.2 13.2 %collective-permute-start.18 = (bf16[256,1024]{1,0:T(8,128)(2,1)S(1)}, bf16[256,1024]{1,0:T(8,128)(2,1)S(1)}, u32[]{:S(2)}, u32[]{:S(2)}) collective-permute-start(bf16[256,1024]{1,0:T(8,128)(2,1)S(1)} %copy-done), channel_id=1, source_target_pairs={{0,8},{8,0},{16,24},{24,16},{32,40},{40,32},{48,56},{56,48},{64,72... | collective-permute-start | bytes 1572872 | tf_op jit(solution)/shard_map/ppermute | solution.py:423
  72.8 7.6 %collective-permute-start.19 = (bf16[256,1024]{1,0:T(8,128)(2,1)S(1)}, bf16[256,1024]{1,0:T(8,128)(2,1)S(1)}, u32[]{:S(2)}, u32[]{:S(2)}) collective-permute-start(bf16[256,1024]{1,0:T(8,128)(2,1)S(1)} %collective-permute-done.15.refs_6_), channel_id=1, source_target_pairs={{0,8},{8,0},{16,24},{24,16},{32,40},{40,32},{48,56},{56,48},{64,72... | collective-permute-start | bytes 1572872 | tf_op jit(solution)/shard_map/ppermute | solution.py:423
  73.7 6.6 %collective-permute-start.16 = (f16[64,1024]{1,0:T(8,128)(2,1)S(1)}, f16[64,1024]{1,0:T(8,128)(2,1)S(1)}, u32[]{:S(2)}, u32[]{:S(2)}) collective-permute-start(f16[64,1024]{1,0:T(8,128)(2,1)S(1)} %add.22), channel_id=1, source_target_pairs={{0,1},{1,0},{2,3},{3,2},{4,5},{5,4},{6,7},{7,6},{8,9},{9,8},{10,11... | collective-permute-start | bytes 393224 | tf_op jit(solution)/shard_map/ppermute | solution.py:423
  83.2 13.6 %all-to-all-start.1 = ((f16[8,8,1024]{2,1,0:T(8,128)(2,1)}), f16[8,8,1024]{2,1,0:T(8,128)(2,1)}, u32[]{:S(2)}, u32[]{:S(2)}) async-start(f16[8,8,1024]{2,1,0:T(8,128)(2,1)} %fusion), calls=%async_computation.1 | async-start | bytes 262144 | tf_op jit(solution)/shard_map/all_to_all | solution.py:560
  88.9 9.7 %collective-permute-start.20 = (bf16[4,512,128]{2,1,0:T(8,128)(2,1)}, bf16[4,512,128]{2,1,0:T(8,128)(2,1)}, u32[]{:S(2)}, u32[]{:S(2)}) collective-permute-start(bf16[4,512,128]{2,1,0:T(8,128)(2,1)} %copy-done.5), channel_id=1, source_target_pairs={{0,8},{8,0},{16,24},{24,16},{32,40},{40,32},{48,56},{56,48},{64,72... | collective-permute-start | bytes 1572872 | tf_op jit(solution)/shard_map/ppermute | solution.py:423
  98.6 12.8 %all-to-all-start.2 = ((f32[8,1,128]{2,1,0:T(1,128)}), f32[8,1,128]{2,1,0:T(1,128)S(1)}, u32[]{:S(2)}, u32[]{:S(2)}) async-start(f32[8,1,128]{2,1,0:T(1,128)} %hidden.1), calls=%async_computation.2 | async-start | bytes 8192 | tf_op jit(solution)/shard_map/all_to_all | solution.py:572
  (10 other events, 59.5 us)

commit v5 on v4

--- a/solution.py
+++ b/solution.py
@@ -474,11 +474,13 @@
     across0 = swapped(kv0y, "ctx", 2)
     across0, wanted1, wanted2 = tie(across0, wanted1, wanted2)
     core0y = swapped(across0, "ctx", 1)
-    state = add([(0, 0, 0, 0), (0, 1, 1, 0)], kvs=[pinned([kv0y])[0], core0], state=None)
+    kv1, own_core = tie(raised(kv0, 1), core0)
+    state = add([(0, 0, 0, 0), (0, 1, 1, 0)], kvs=[pinned([kv0y])[0], own_core], state=None)
     wanted, wanted1, wanted2, *state = tie(wanted, wanted1, wanted2, *state)
 
-    kv1, wanted = tie(raised(kv0, 1), wanted)
-    across1 = swapped(kv1, "ctx", 2)
+    weight, wanted = tie(weight, wanted)
+    firsts = [weight, swapped(weight, "ctx", 1), swapped(weight, "ctx", 2)]
+    firsts.append(swapped(firsts[2], "ctx", 1))
 
     parts, moved = small_call(
         picked_kernel,
@@ -504,20 +506,20 @@
         ],
         name="picked",
     )
-    parts, kv1, across1, weight, *state = tie(parts, kv1, across1, weight, *state)
-
-    firsts = [weight] + [swapped(weight, "ctx", bits) for bits in (1, 2, 3)]
-
+    parts, kv1, *state = tie(parts, kv1, *state)
+    across1 = swapped(kv1, "ctx", 2)
+    *firsts, across1, weight = tie(*firsts, across1, score_weight)
+    weights = [weight, None, swapped(weight, "ctx", 2)]
     parts = jnp.broadcast_to(parts.astype(jnp.float16)[None], (Z, GROUP, half))
     parts = lax.all_to_all(parts, "ctx", 0, 0, axis_index_groups=columns).astype(F32)
     state, pair1 = add(
         [(0, 2, 0, 0), (0, 3, 0, 1), (1, 0, 1, 0), (1, 2, 2, 0)],
-        kvs=pinned([moved, kv1, across1]),
+        kvs=[*pinned([moved]), kv1, across1],
         state=state,
         joined=2,
     )
-    parts, pair1, weight, *state = tie(parts, pair1, score_weight, *state)
-    weights = [weight, swapped(weight, "ctx", 1), swapped(weight, "ctx", 2)]
+    parts, pair1, weight, *state = tie(parts, pair1, weight, *state)
+    weights[1] = swapped(weight, "ctx", 1)
 
     projected = small_call(
         project_kernel,
@@ -533,8 +535,9 @@
     projected, pair1 = tie((projected * 0.25).astype(jnp.float16), pair1)
     pair2, cores1 = raised(pair1, 1), swapped(pair1, "ctx", 1)
     projected = projected + swapped(projected, "head", 2)
+    projected, weights[2] = tie(projected, weights[2])
     projected = projected + swapped(projected, "head", 4)
-    projected, cores1, weights[2] = tie(projected, cores1, weights[2])
+    projected, cores1 = tie(projected, cores1)
     weights.append(swapped(weights[2], "ctx", 1))
     other = swapped(projected, "head", 1)
     state = add([(1, 1, 0, 0), (1, 3, 0, 1)], kvs=[cores1], state=state)

time: 128 us -> 126 us (0.984)
  waiting for transfers between devices: 39.6 us -> 33.9 us
  blocking collectives: 14.4 us -> 17.8 us
    all_to_all x1, waiting for transfers between devices: 11.3 us -> 4.48 us  [per_device(): lax.all_to_all(parts, 'ctx', 0, 0, axis_index_groups=columns).astype(F32)]
    all_to_all x1, blocking collectives: 14.4 us -> 17.8 us  [per_device(): lax.all_to_all(jnp.broadcast_to(gap[None], (count, 1, HD)), 'ctx', 0, 0)]
    ppermute x4, waiting for transfers between devices: 0.01 us -> 3.17 us  [raised(): lax.ppermute(value, 'ctx', [(s, (s + steps) % count) for s in range(count)])]
    all_to_all x1, starting transfers between devices: 6.36 us -> 4.77 us  [per_device(): gap = lax.all_to_all(gap, 'head', 0, 0)]
    ppermute x17, waiting for transfers between devices: 18.9 us -> 17.4 us  [swapped(): return lax.ppermute(value, axis, [(s, s ^ bit) for s in range(count)])]
  transfers between devices with their start and end apart: 24 -> 24, of which waited for: 12 -> 11; matrix products, arithmetic and copies ran while one was open for 2% -> 3% of each run, Pallas kernels for 11% -> 13%
where the time goes in v5:
time: 126 us; the launch traced here: 125 us
  starting transfers between devices  44.9 us (36%)
  waiting for transfers between devices  33.9 us (27%)
  Pallas kernels  21.4 us (17%)
  blocking collectives  17.8 us (14%)
  local copies, waits for them, and re-layouts  3.4 us (3%)
  other arithmetic  3.06 us (2%)
    ppermute x17, starting transfers between devices, swapped(): return lax.ppermute(value, axis, [(s, s ^ bit) for s in range(count)])  21.8 us
    all_to_all x1, blocking collectives, per_device(): lax.all_to_all(jnp.broadcast_to(gap[None], (count, 1, HD)), 'ctx', 0, 0)  17.8 us
    ppermute x17, waiting for transfers between devices, swapped(): return lax.ppermute(value, axis, [(s, s ^ bit) for s in range(count)])  17.4 us
    pallas_call x6, Pallas kernels, small_call(): pl.pallas_call(kernel, out_shape=shape, in_specs=specs or [VMEM] * len(op...  10.9 us
    pallas_call x5, Pallas kernels, attend(): pl.pallas_call(functools.partial(attend_kernel, slots, first, last, joine...  10.5 us
    all_to_all x1, starting transfers between devices, per_device(): inner = lax.all_to_all(inner, 'ctx', 0, 0, axis_index_groups=columns)  6.61 us
    ppermute x4, starting transfers between devices, raised(): lax.ppermute(value, 'ctx', [(s, (s + steps) % count) for s in range(count)])  6.52 us
    all_to_all x1, starting transfers between devices, per_device(): lax.all_to_all(parts, 'ctx', 0, 0, axis_index_groups=columns).astype(F32)  5.16 us
  transfers between devices with their start and end apart: 24, of which 11 were waited for; matrix products, arithmetic and copies ran while one was open for 3% of the time, Pallas kernels for 13%

profile of v5, /device:TPU:1, one launch (start us, length us, event | category | flops | bytes accessed | tf_op | source)
XLA Modules:
  0.0 125.5 jit_solution(15711502940527608377)
XLA Ops:
  0.6 1.8 %pick.1 = (bf16[64,512]{1,0:T(8,128)(2,1)S(1)}, bf16[64,512]{1,0:T(8,128)(2,1)S(1)}, bf16[128,512]{1,0:T(8,128)(2,1)S(1)}, bf16[736,256]{1,0:T(8,128)(2,1)S(1)}) custom-call(s32[1]{0:T(128)} %bitcast.me_ref.refs_0_, s32[7,32]{1,0:T(8,128)} %steps_hbm.3, bf16[512,512]{1,0:T(8,128)(2,1)} %refs_2_.9, bf16[512,256]{1,0:T(8,128)(2,1)} %weight_hbm.1, ...), custom_call_target="tpu_custom_call" | custom-call | tf_op jit(solution)/shard_map/pick/pallas_call | solution.py:320
  2.4 3.3 %collective-permute-start = (bf16[128,512]{1,0:T(8,128)(2,1)S(1)}, bf16[128,512]{1,0:T(8,128)(2,1)S(1)}, u32[]{:S(2)}, u32[]{:S(2)}) collective-permute-start(bf16[128,512]{1,0:T(8,128)(2,1)S(1)} %get-tuple-element.86), channel_id=1, source_target_pairs={{0,8},{8,0},{16,24},{24,16},{32,40},{40,32},{48,56},{56,48},{64,72... | collective-permute-start | bytes 393224 | tf_op jit(solution)/shard_map/ppermute | solution.py:423
  7.3 2.6 %collective-permute-done.1 = bf16[64,512]{1,0:T(8,128)(2,1)S(1)} collective-permute-done((bf16[64,512]{1,0:T(8,128)(2,1)S(1)}, bf16[64,512]{1,0:T(8,128)(2,1)S(1)}, u32[]{:S(2)}, u32[]{:S(2)}) %collective-permute-start.1) | collective-permute-done | bytes 65568 | tf_op jit(solution)/shard_map/ppermute | solution.py:423
  11.3 3.9 %collective-permute-start.4 = (bf16[64,512]{1,0:T(8,128)(2,1)S(1)}, bf16[64,512]{1,0:T(8,128)(2,1)S(1)}, u32[]{:S(2)}, u32[]{:S(2)}) collective-permute-start(bf16[64,512]{1,0:T(8,128)(2,1)S(1)} %fusion.1.q_ref), channel_id=1, source_target_pairs={{0,224},{8,232},{16,240},{24,248},{32,0},{40,8},{48,16},{56,24},{6... | collective-permute-start | bytes 196616 | tf_op jit(solution)/shard_map/ppermute | solution.py:429
  15.2 1.9 %collective-permute-start.5 = (bf16[64,512]{1,0:T(8,128)(2,1)S(1)}, bf16[64,512]{1,0:T(8,128)(2,1)S(1)}, u32[]{:S(2)}, u32[]{:S(2)}) collective-permute-start(bf16[64,512]{1,0:T(8,128)(2,1)S(1)} %fusion.1.q_ref), channel_id=1, source_target_pairs={{0,192},{8,200},{16,208},{24,216},{32,224},{40,232},{48,240},{56,2... | collective-permute-start | bytes 196616 | tf_op jit(solution)/shard_map/ppermute | solution.py:429
  17.1 3.2 %collective-permute-done.5.q2_ref = bf16[64,512]{1,0:T(8,128)(2,1)S(1)} collective-permute-done((bf16[64,512]{1,0:T(8,128)(2,1)S(1)}, bf16[64,512]{1,0:T(8,128)(2,1)S(1)}, u32[]{:S(2)}, u32[]{:S(2)}) %collective-permute-start.5) | collective-permute-done | bytes 65568 | tf_op jit(solution)/shard_map/ppermute | solution.py:429
  20.3 2.7 %collective-permute-start.7 = (bf16[2,512,128]{2,1,0:T(8,128)(2,1)S(1)}, bf16[2,512,128]{2,1,0:T(8,128)(2,1)S(1)}, u32[]{:S(2)}, u32[]{:S(2)}) collective-permute-start(bf16[2,512,128]{2,1,0:T(8,128)(2,1)S(1)} %collective-permute-done.3.refs_2_), channel_id=1, source_target_pairs={{0,8},{8,0},{16,24},{24,16},{32,40},{40,32},{48,56},{56,48},{64,72... | collective-permute-start | bytes 786440 | tf_op jit(solution)/shard_map/ppermute | solution.py:423
  23.0 4.2 %attend_0_0.1 = (f32[512,512]{1,0:T(8,128)S(1)}, f32[512,512]{1,0:T(8,128)S(1)}, f32[512,512]{1,0:T(8,128)S(1)}) custom-call(s32[1]{0:T(128)} %bitcast.me_ref.refs_0_, s32[7]{0:T(128)} %refs_1_.9, bf16[512,512]{1,0:T(8,128)(2,1)} %refs_2_.9, bf16[2,512,128]{2,1,0:T(8,128)(2,1)} %refs_0_.1, bf16[2,512,128]{2,1,0:T(8,128)(2,1)S(1)} %collective-permute-done.2.refs_4_.refs_1_), custom_call_target="tpu_custom_call" | custom-call | flops 1073741824 | bytes 1048576 | tf_op jit(solution)/shard_map/attend_0_0/pallas_call | solution.py:292
  27.8 3.0 %picked.1 = (f32[64,512]{1,0:T(8,128)S(1)}, bf16[4,512,128]{2,1,0:T(8,128)(2,1)}) custom-call(s32[1]{0:T(128)} %bitcast.me_ref.refs_0_, s32[7]{0:T(128)} %refs_1_.9, s32[7,32]{1,0:T(8,128)} %steps_hbm.3, bf16[64,512]{1,0:T(8,128)(2,1)S(1)} %fusion.1.q_ref, bf16[64,512]{1,0:T(8,128)(2,1)S(1)} %collective-permute-done.4.q1_ref, ...), custom_call_target="tpu_custom_call" | custom-call | tf_op jit(solution)/shard_map/picked/pallas_call | solution.py:320
  31.7 5.2 %all-to-all-start = ((f16[8,64,512]{2,1,0:T(8,128)(2,1)}), f16[8,64,512]{2,1,0:T(8,128)(2,1)}, u32[]{:S(2)}, u32[]{:S(2)}) async-start(f16[8,64,512]{2,1,0:T(8,128)(2,1)} %broadcast_in_dim.4), calls=%async_computation | async-start | bytes 1048576 | tf_op jit(solution)/shard_map/all_to_all | solution.py:514
  39.3 6.1 %collective-permute-done.11.refs_5_ = bf16[2,512,128]{2,1,0:T(8,128)(2,1)S(1)} collective-permute-done((bf16[2,512,128]{2,1,0:T(8,128)(2,1)}, bf16[2,512,128]{2,1,0:T(8,128)(2,1)S(1)}, u32[]{:S(2)}, u32[]{:S(2)}) %collective-permute-start.11) | collective-permute-done | bytes 262176 | tf_op jit(solution)/shard_map/ppermute | solution.py:423
  49.8 4.5 %all-to-all-done = f16[8,64,512]{2,1,0:T(8,128)(2,1)} async-done(((f16[8,64,512]{2,1,0:T(8,128)(2,1)}), f16[8,64,512]{2,1,0:T(8,128)(2,1)}, u32[]{:S(2)}, u32[]{:S(2)}) %all-to-all-start) | async-done | bytes 524320 | tf_op jit(solution)/shard_map/all_to_all | solution.py:514
  55.6 2.0 %project.1 = f32[64,1024]{1,0:T(8,128)S(1)} custom-call(f32[8,64,512]{2,1,0:T(8,128)S(1)} %convert_element_type.22.got_ref, bf16[736,256]{1,0:T(8,128)(2,1)S(1)} %get-tuple-element.121.refs_0_, bf16[736,256]{1,0:T(8,128)(2,1)S(1)} %copy-done.1, bf16[736,256]{1,0:T(8,128)(2,1)} %collective-permute-done.9.refs_2_, bf16[736,256]{1,0:T(8,128)(2,1)S(1)} %copy-done.3), custom_call_target="tpu_custom_call" | custom-call | tf_op jit(solution)/shard_map/project/pallas_call | solution.py:320
  60.0 2.7 %collective-permute-done.12 = f16[64,1024]{1,0:T(8,128)(2,1)S(1)} collective-permute-done((f16[64,1024]{1,0:T(8,128)(2,1)S(1)}, f16[64,1024]{1,0:T(8,128)(2,1)S(1)}, u32[]{:S(2)}, u32[]{:S(2)}) %collective-permute-start.12) | collective-permute-done | bytes 131104 | tf_op jit(solution)/shard_map/ppermute | solution.py:423
  64.1 2.7 %collective-permute-start.14 = (f16[64,1024]{1,0:T(8,128)(2,1)S(1)}, f16[64,1024]{1,0:T(8,128)(2,1)S(1)}, u32[]{:S(2)}, u32[]{:S(2)}) collective-permute-start(f16[64,1024]{1,0:T(8,128)(2,1)S(1)} %add.21), channel_id=1, source_target_pairs={{0,4},{1,5},{2,6},{3,7},{4,0},{5,1},{6,2},{7,3},{8,12},{9,13},{10,... | collective-permute-start | bytes 393224 | tf_op jit(solution)/shard_map/ppermute | solution.py:423
  66.9 3.5 %collective-permute-done.14 = f16[64,1024]{1,0:T(8,128)(2,1)S(1)} collective-permute-done((f16[64,1024]{1,0:T(8,128)(2,1)S(1)}, f16[64,1024]{1,0:T(8,128)(2,1)S(1)}, u32[]{:S(2)}, u32[]{:S(2)}) %collective-permute-start.14) | collective-permute-done | bytes 131104 | tf_op jit(solution)/shard_map/ppermute | solution.py:423
  70.4 3.0 %collective-permute-start.16 = (f16[64,1024]{1,0:T(8,128)(2,1)S(1)}, f16[64,1024]{1,0:T(8,128)(2,1)S(1)}, u32[]{:S(2)}, u32[]{:S(2)}) collective-permute-start(f16[64,1024]{1,0:T(8,128)(2,1)S(1)} %add.22), channel_id=1, source_target_pairs={{0,1},{1,0},{2,3},{3,2},{4,5},{5,4},{6,7},{7,6},{8,9},{9,8},{10,11... | collective-permute-start | bytes 393224 | tf_op jit(solution)/shard_map/ppermute | solution.py:423
  75.9 2.0 %inner.1 = f32[64,1024]{1,0:T(8,128)S(1)} custom-call(s32[1]{0:T(128)} %bitcast.me_ref.refs_0_, f32[64,1024]{1,0:T(8,128)S(1)} %add_multiply_fusion.total_ref, bf16[736,256]{1,0:T(8,128)(2,1)S(1)} %get-tuple-element.121.refs_0_, bf16[736,256]{1,0:T(8,128)(2,1)S(1)} %copy-done.1, bf16[736,256]{1,0:T(8,128)(2,1)} %collective-permute-done.9.refs_2_, ...), custom_call_target="tpu_custom_call" | custom-call | tf_op jit(solution)/shard_map/inner/pallas_call | solution.py:320
  78.6 6.6 %all-to-all-start.1 = ((f16[8,8,1024]{2,1,0:T(8,128)(2,1)}), f16[8,8,1024]{2,1,0:T(8,128)(2,1)}, u32[]{:S(2)}, u32[]{:S(2)}) async-start(f16[8,8,1024]{2,1,0:T(8,128)(2,1)} %fusion), calls=%async_computation.1 | async-start | bytes 262144 | tf_op jit(solution)/shard_map/all_to_all | solution.py:563
  88.4 4.9 %all-to-all-done.1 = f16[8,8,1024]{2,1,0:T(8,128)(2,1)} async-done(((f16[8,8,1024]{2,1,0:T(8,128)(2,1)}), f16[8,8,1024]{2,1,0:T(8,128)(2,1)}, u32[]{:S(2)}, u32[]{:S(2)}) %all-to-all-start.1) | async-done | bytes 131104 | tf_op jit(solution)/shard_map/all_to_all | solution.py:563
  95.1 4.8 %all-to-all-start.2 = ((f32[8,1,128]{2,1,0:T(1,128)}), f32[8,1,128]{2,1,0:T(1,128)S(1)}, u32[]{:S(2)}, u32[]{:S(2)}) async-start(f32[8,1,128]{2,1,0:T(1,128)} %hidden.1), calls=%async_computation.2 | async-start | bytes 8192 | tf_op jit(solution)/shard_map/all_to_all | solution.py:575
  99.9 2.4 %attend_2_1.1 = f32[512,512]{1,0:T(8,128)} custom-call(s32[1]{0:T(128)} %bitcast.me_ref.refs_0_, s32[7]{0:T(128)} %refs_1_.9, bf16[512,512]{1,0:T(8,128)(2,1)} %refs_2_.9, bf16[4,512,128]{2,1,0:T(8,128)(2,1)} %collective-permute-done.20.refs_3_, f32[512,512]{1,0:T(8,128)S(1)} %get-tuple-element.158.refs_4_, f32[512,512]{1,0:T(8,128)S(1)} %get-tuple-element.159.refs_5_, ...), custom_call_target="tpu_custom_call" | custom-call | flops 1073741824 | bytes 1048576 | tf_op jit(solution)/shard_map/attend_2_1/pallas_call | solution.py:292
  102.3 4.1 %all-to-all-done.2 = f32[8,1,128]{2,1,0:T(1,128)S(1)} async-done(((f32[8,1,128]{2,1,0:T(1,128)}), f32[8,1,128]{2,1,0:T(1,128)S(1)}, u32[]{:S(2)}, u32[]{:S(2)}) %all-to-all-start.2) | async-done | bytes 4128 | tf_op jit(solution)/shard_map/all_to_all | solution.py:575
  106.4 17.8 %all_to_all.20.got_ref = f32[32,1,128]{2,1,0:T(1,128)S(1)} all-to-all(f32[32,1,128]{2,1,0:T(1,128)S(1)} %broadcast_in_dim.5), channel_id=1, replica_groups=mesh['ctx'=32,'head'=8] {'ctx'}, dimensions={0} | all-to-all | bytes 32768 | tf_op jit(solution)/shard_map/all_to_all | solution.py:578
  (75 shorter events, 25.7 us)
Async XLA Ops:
  2.4 4.3 %collective-permute-start = (bf16[128,512]{1,0:T(8,128)(2,1)S(1)}, bf16[128,512]{1,0:T(8,128)(2,1)S(1)}, u32[]{:S(2)}, u32[]{:S(2)}) collective-permute-start(bf16[128,512]{1,0:T(8,128)(2,1)S(1)} %get-tuple-element.86), channel_id=1, source_target_pairs={{0,8},{8,0},{16,24},{24,16},{32,40},{40,32},{48,56},{56,48},{64,72... | collective-permute-start | bytes 393224 | tf_op jit(solution)/shard_map/ppermute | solution.py:423
  6.7 3.2 %collective-permute-start.1 = (bf16[64,512]{1,0:T(8,128)(2,1)S(1)}, bf16[64,512]{1,0:T(8,128)(2,1)S(1)}, u32[]{:S(2)}, u32[]{:S(2)}) collective-permute-start(bf16[64,512]{1,0:T(8,128)(2,1)S(1)} %slice_add_fusion), channel_id=1, source_target_pairs={{0,16},{8,24},{16,0},{24,8},{32,48},{40,56},{48,32},{56,40},{64,80... | collective-permute-start | bytes 196616 | tf_op jit(solution)/shard_map/ppermute | solution.py:423
  6.8 3.1 %collective-permute-start.2 = (bf16[2,512,128]{2,1,0:T(8,128)(2,1)S(1)}, bf16[2,512,128]{2,1,0:T(8,128)(2,1)S(1)}, u32[]{:S(2)}, u32[]{:S(2)}) collective-permute-start(bf16[2,512,128]{2,1,0:T(8,128)(2,1)S(1)} %copy-done.10), channel_id=1, source_target_pairs={{0,8},{8,0},{16,24},{24,16},{32,40},{40,32},{48,56},{56,48},{64,72... | collective-permute-start | bytes 786440 | tf_op jit(solution)/shard_map/ppermute | solution.py:423
  10.0 10.3 %collective-permute-start.3 = (bf16[2,512,128]{2,1,0:T(8,128)(2,1)S(1)}, bf16[2,512,128]{2,1,0:T(8,128)(2,1)S(1)}, u32[]{:S(2)}, u32[]{:S(2)}) collective-permute-start(bf16[2,512,128]{2,1,0:T(8,128)(2,1)S(1)} %copy-done.10), channel_id=1, source_target_pairs={{0,16},{8,24},{16,0},{24,8},{32,48},{40,56},{48,32},{56,40},{64,80... | collective-permute-start | bytes 786440 | tf_op jit(solution)/shard_map/ppermute | solution.py:423
  10.6 12.4 %collective-permute-start.6 = (bf16[2,512,128]{2,1,0:T(8,128)(2,1)S(1)}, bf16[2,512,128]{2,1,0:T(8,128)(2,1)}, u32[]{:S(2)}, u32[]{:S(2)}) collective-permute-start(bf16[2,512,128]{2,1,0:T(8,128)(2,1)S(1)} %copy-done.10), channel_id=1, source_target_pairs={{0,32},{8,40},{16,48},{24,56},{32,64},{40,72},{48,80},{56,88},{64,... | collective-permute-start | bytes 786440 | tf_op jit(solution)/shard_map/ppermute | solution.py:429
  11.3 5.9 %collective-permute-start.4 = (bf16[64,512]{1,0:T(8,128)(2,1)S(1)}, bf16[64,512]{1,0:T(8,128)(2,1)S(1)}, u32[]{:S(2)}, u32[]{:S(2)}) collective-permute-start(bf16[64,512]{1,0:T(8,128)(2,1)S(1)} %fusion.1.q_ref), channel_id=1, source_target_pairs={{0,224},{8,232},{16,240},{24,248},{32,0},{40,8},{48,16},{56,24},{6... | collective-permute-start | bytes 196616 | tf_op jit(solution)/shard_map/ppermute | solution.py:429
  15.2 5.1 %collective-permute-start.5 = (bf16[64,512]{1,0:T(8,128)(2,1)S(1)}, bf16[64,512]{1,0:T(8,128)(2,1)S(1)}, u32[]{:S(2)}, u32[]{:S(2)}) collective-permute-start(bf16[64,512]{1,0:T(8,128)(2,1)S(1)} %fusion.1.q_ref), channel_id=1, source_target_pairs={{0,192},{8,200},{16,208},{24,216},{32,224},{40,232},{48,240},{56,2... | collective-permute-start | bytes 196616 | tf_op jit(solution)/shard_map/ppermute | solution.py:429
  20.3 7.5 %collective-permute-start.7 = (bf16[2,512,128]{2,1,0:T(8,128)(2,1)S(1)}, bf16[2,512,128]{2,1,0:T(8,128)(2,1)S(1)}, u32[]{:S(2)}, u32[]{:S(2)}) collective-permute-start(bf16[2,512,128]{2,1,0:T(8,128)(2,1)S(1)} %collective-permute-done.3.refs_2_), channel_id=1, source_target_pairs={{0,8},{8,0},{16,24},{24,16},{32,40},{40,32},{48,56},{56,48},{64,72... | collective-permute-start | bytes 786440 | tf_op jit(solution)/shard_map/ppermute | solution.py:423
  27.2 9.8 %collective-permute-start.9 = (bf16[736,256]{1,0:T(8,128)(2,1)S(1)}, bf16[736,256]{1,0:T(8,128)(2,1)}, u32[]{:S(2)}, u32[]{:S(2)}) collective-permute-start(bf16[736,256]{1,0:T(8,128)(2,1)S(1)} %get-tuple-element.121.refs_0_), channel_id=1, source_target_pairs={{0,16},{8,24},{16,0},{24,8},{32,48},{40,56},{48,32},{56,40},{64,80... | collective-permute-start | bytes 1130504 | tf_op jit(solution)/shard_map/ppermute | solution.py:423
  31.7 22.6 %all-to-all-start = ((f16[8,64,512]{2,1,0:T(8,128)(2,1)}), f16[8,64,512]{2,1,0:T(8,128)(2,1)}, u32[]{:S(2)}, u32[]{:S(2)}) async-start(f16[8,64,512]{2,1,0:T(8,128)(2,1)} %broadcast_in_dim.4), calls=%async_computation | async-start | bytes 1048576 | tf_op jit(solution)/shard_map/all_to_all | solution.py:514
  36.8 1.7 %collective-permute-start.8 = (bf16[736,256]{1,0:T(8,128)(2,1)S(1)}, bf16[736,256]{1,0:T(8,128)(2,1)S(1)}, u32[]{:S(2)}, u32[]{:S(2)}) collective-permute-start(bf16[736,256]{1,0:T(8,128)(2,1)S(1)} %get-tuple-element.121.refs_0_), channel_id=1, source_target_pairs={{0,8},{8,0},{16,24},{24,16},{32,40},{40,32},{48,56},{56,48},{64,72... | collective-permute-start | bytes 1130504 | tf_op jit(solution)/shard_map/ppermute | solution.py:423
  37.0 8.3 %collective-permute-start.10 = (bf16[736,256]{1,0:T(8,128)(2,1)}, bf16[736,256]{1,0:T(8,128)(2,1)S(1)}, u32[]{:S(2)}, u32[]{:S(2)}) collective-permute-start(bf16[736,256]{1,0:T(8,128)(2,1)} %collective-permute-done.9.refs_2_), channel_id=1, source_target_pairs={{0,8},{8,0},{16,24},{24,16},{32,40},{40,32},{48,56},{56,48},{64,72... | collective-permute-start | bytes 1130504 | tf_op jit(solution)/shard_map/ppermute | solution.py:423
  37.3 8.0 %collective-permute-start.11 = (bf16[2,512,128]{2,1,0:T(8,128)(2,1)}, bf16[2,512,128]{2,1,0:T(8,128)(2,1)S(1)}, u32[]{:S(2)}, u32[]{:S(2)}) collective-permute-start(bf16[2,512,128]{2,1,0:T(8,128)(2,1)} %collective-permute-done.6.refs_4_), channel_id=1, source_target_pairs={{0,16},{8,24},{16,0},{24,8},{32,48},{40,56},{48,32},{56,40},{64,80... | collective-permute-start | bytes 786440 | tf_op jit(solution)/shard_map/ppermute | solution.py:423
  46.1 16.6 %collective-permute-start.13 = (bf16[256,1024]{1,0:T(8,128)(2,1)}, bf16[256,1024]{1,0:T(8,128)(2,1)}, u32[]{:S(2)}, u32[]{:S(2)}) collective-permute-start(bf16[256,1024]{1,0:T(8,128)(2,1)} %refs_4_), channel_id=1, source_target_pairs={{0,16},{8,24},{16,0},{24,8},{32,48},{40,56},{48,32},{56,40},{64,80... | collective-permute-start | bytes 1572872 | tf_op jit(solution)/shard_map/ppermute | solution.py:423
  57.6 12.9 %collective-permute-start.15 = (bf16[4,512,128]{2,1,0:T(8,128)(2,1)S(1)}, bf16[4,512,128]{2,1,0:T(8,128)(2,1)S(1)}, u32[]{:S(2)}, u32[]{:S(2)}) collective-permute-start(bf16[4,512,128]{2,1,0:T(8,128)(2,1)S(1)} %copy-done.8), channel_id=1, source_target_pairs={{0,8},{8,0},{16,24},{24,16},{32,40},{40,32},{48,56},{56,48},{64,72... | collective-permute-start | bytes 1572872 | tf_op jit(solution)/shard_map/ppermute | solution.py:423
  58.1 16.6 %collective-permute-start.17 = (bf16[4,512,128]{2,1,0:T(8,128)(2,1)S(1)}, bf16[4,512,128]{2,1,0:T(8,128)(2,1)S(1)}, u32[]{:S(2)}, u32[]{:S(2)}) collective-permute-start(bf16[4,512,128]{2,1,0:T(8,128)(2,1)S(1)} %copy-done.8), channel_id=1, source_target_pairs={{0,32},{8,40},{16,48},{24,56},{32,64},{40,72},{48,80},{56,88},{64,... | collective-permute-start | bytes 1572872 | tf_op jit(solution)/shard_map/ppermute | solution.py:429
  58.1 4.6 %collective-permute-start.12 = (f16[64,1024]{1,0:T(8,128)(2,1)S(1)}, f16[64,1024]{1,0:T(8,128)(2,1)S(1)}, u32[]{:S(2)}, u32[]{:S(2)}) collective-permute-start(f16[64,1024]{1,0:T(8,128)(2,1)S(1)} %multiply_convert_fusion.1), channel_id=1, source_target_pairs={{0,2},{1,3},{2,0},{3,1},{4,6},{5,7},{6,4},{7,5},{8,10},{9,11},{10,... | collective-permute-start | bytes 393224 | tf_op jit(solution)/shard_map/ppermute | solution.py:423
  59.3 16.6 %collective-permute-start.18 = (bf16[256,1024]{1,0:T(8,128)(2,1)S(1)}, bf16[256,1024]{1,0:T(8,128)(2,1)S(1)}, u32[]{:S(2)}, u32[]{:S(2)}) collective-permute-start(bf16[256,1024]{1,0:T(8,128)(2,1)S(1)} %copy-done.4), channel_id=1, source_target_pairs={{0,8},{8,0},{16,24},{24,16},{32,40},{40,32},{48,56},{56,48},{64,72... | collective-permute-start | bytes 1572872 | tf_op jit(solution)/shard_map/ppermute | solution.py:423
  62.7 13.2 %collective-permute-start.19 = (bf16[256,1024]{1,0:T(8,128)(2,1)}, bf16[256,1024]{1,0:T(8,128)(2,1)S(1)}, u32[]{:S(2)}, u32[]{:S(2)}) collective-permute-start(bf16[256,1024]{1,0:T(8,128)(2,1)} %collective-permute-done.13.refs_6_), channel_id=1, source_target_pairs={{0,8},{8,0},{16,24},{24,16},{32,40},{40,32},{48,56},{56,48},{64,72... | collective-permute-start | bytes 1572872 | tf_op jit(solution)/shard_map/ppermute | solution.py:423
  64.1 6.3 %collective-permute-start.14 = (f16[64,1024]{1,0:T(8,128)(2,1)S(1)}, f16[64,1024]{1,0:T(8,128)(2,1)S(1)}, u32[]{:S(2)}, u32[]{:S(2)}) collective-permute-start(f16[64,1024]{1,0:T(8,128)(2,1)S(1)} %add.21), channel_id=1, source_target_pairs={{0,4},{1,5},{2,6},{3,7},{4,0},{5,1},{6,2},{7,3},{8,12},{9,13},{10,... | collective-permute-start | bytes 393224 | tf_op jit(solution)/shard_map/ppermute | solution.py:423
  70.4 5.4 %collective-permute-start.16 = (f16[64,1024]{1,0:T(8,128)(2,1)S(1)}, f16[64,1024]{1,0:T(8,128)(2,1)S(1)}, u32[]{:S(2)}, u32[]{:S(2)}) collective-permute-start(f16[64,1024]{1,0:T(8,128)(2,1)S(1)} %add.22), channel_id=1, source_target_pairs={{0,1},{1,0},{2,3},{3,2},{4,5},{5,4},{6,7},{7,6},{8,9},{9,8},{10,11... | collective-permute-start | bytes 393224 | tf_op jit(solution)/shard_map/ppermute | solution.py:423
  78.6 14.7 %all-to-all-start.1 = ((f16[8,8,1024]{2,1,0:T(8,128)(2,1)}), f16[8,8,1024]{2,1,0:T(8,128)(2,1)}, u32[]{:S(2)}, u32[]{:S(2)}) async-start(f16[8,8,1024]{2,1,0:T(8,128)(2,1)} %fusion), calls=%async_computation.1 | async-start | bytes 262144 | tf_op jit(solution)/shard_map/all_to_all | solution.py:563
  85.3 9.9 %collective-permute-start.20 = (bf16[4,512,128]{2,1,0:T(8,128)(2,1)}, bf16[4,512,128]{2,1,0:T(8,128)(2,1)}, u32[]{:S(2)}, u32[]{:S(2)}) collective-permute-start(bf16[4,512,128]{2,1,0:T(8,128)(2,1)} %copy-done.9), channel_id=1, source_target_pairs={{0,8},{8,0},{16,24},{24,16},{32,40},{40,32},{48,56},{56,48},{64,72... | collective-permute-start | bytes 1572872 | tf_op jit(solution)/shard_map/ppermute | solution.py:423
  95.1 11.2 %all-to-all-start.2 = ((f32[8,1,128]{2,1,0:T(1,128)}), f32[8,1,128]{2,1,0:T(1,128)S(1)}, u32[]{:S(2)}, u32[]{:S(2)}) async-start(f32[8,1,128]{2,1,0:T(1,128)} %hidden.1), calls=%async_computation.2 | async-start | bytes 8192 | tf_op jit(solution)/shard_map/all_to_all | solution.py:575
  (12 other events, 64.0 us)

commit v6 on v5

--- a/solution.py
+++ b/solution.py
@@ -157,7 +157,7 @@
     moved_copy.wait()
 
 
-def attend_kernel(slots, first, last, joined, *refs):
+def attend_kernel(slots, first, last, *refs):
     n = len(slots)
     arrays = 1 + max(slot[2] for slot in slots)
     me_ref, lengths_hbm, q_hbm = refs[:3]
@@ -173,18 +173,10 @@
         copies.append(
             pltpu.make_async_copy(q_hbm.at[part], q_ref.at[part], sems.at[n + 1 + k])
         )
-    pair_copies = []
-    for k in range(joined):
-        target = refs[-5].at[pl.ds(2 * k, 2)]
-        pair_copies.append(
-            pltpu.make_async_copy(kv_ref.at[n - joined + k], target, sems.at[n + 5 + k])
-        )
     for copy in copies:
         copy.start()
     for copy in copies:
         copy.wait()
-    for copy in pair_copies:
-        copy.start()
     me = me_ref[0]
     place = me % PLANE
     row0 = me * BLOCK
@@ -269,11 +261,9 @@
     if last:
         out_ref = refs[-5]
         out_ref[...] = acc_ref[...] / l_ref[...]
-    for copy in pair_copies:
-        copy.wait()
-
-
-def attend(slots, me, lengths, queries, kvs, state, last=False, joined=0):
+
+
+def attend(slots, me, lengths, queries, kvs, state, last=False):
     shape = (BLOCK, PER_GROUP * HD)
     first = state is None
     operands = [me, *pinned([lengths, queries]), *kvs]
@@ -286,11 +276,9 @@
         aliases = {at + k: k for k in range(3)}
     if last:
         shapes, aliases = (jax.ShapeDtypeStruct(shape, F32),), {}
-    if joined:
-        shapes += (pltpu.VMEM((2 * joined, BLOCK, HD), BF16),)
     work = PER_GROUP * BLOCK * BLOCK * len(slots)
     got = pl.pallas_call(
-        functools.partial(attend_kernel, slots, first, last, joined),
+        functools.partial(attend_kernel, slots, first, last),
         out_shape=shapes,
         in_specs=specs,
         out_specs=[VMEM] * len(shapes),
@@ -298,7 +286,7 @@
             pltpu.VMEM(shape, BF16),
             pltpu.VMEM((len(slots), 2, BLOCK, HD), BF16),
             pltpu.SMEM((TRACES,), jnp.int32),
-            pltpu.SemaphoreType.DMA((len(slots) + 5 + joined,)),
+            pltpu.SemaphoreType.DMA((len(slots) + 5,)),
         ],
         input_output_aliases=aliases,
         compiler_params=pltpu.CompilerParams(vmem_limit_bytes=20 << 20),
@@ -309,7 +297,7 @@
     )(*operands)
     if last:
         return got[0]
-    return (list(got[:3]), got[3]) if joined else list(got)
+    return list(got)
 
 
 def pinned(values):
@@ -328,11 +316,15 @@
 
 
 def project_kernel(got_ref, *refs):
-    packs, out_ref, weight_s, sems = refs[:PLANE], refs[PLANE], refs[-2], refs[-1]
+    packs, blocks, out_ref, pair_ref = refs[:PLANE], refs[PLANE:-4], refs[-4], refs[-3]
+    weight_s, sems = refs[-2:]
     copies = [
         pltpu.make_async_copy(pack.at[pl.ds(0, BLOCK)], weight_s.at[k], sems.at[k])
         for k, pack in enumerate(packs)
     ]
+    for k, block in enumerate(blocks):
+        target = pair_ref.at[pl.ds(2 * k, 2)]
+        copies.append(pltpu.make_async_copy(block, target, sems.at[PLANE + k]))
     for copy in copies:
         copy.start()
     sizes = []
@@ -366,6 +358,8 @@
         copies[k].wait()
         part = jnp.dot(picked, weight_s[k], preferred_element_type=F32)
         out_ref[:, k * 256 : (k + 1) * 256] = part
+    for copy in copies[PLANE:]:
+        copy.wait()
 
 
 def inner_kernel(me_ref, total_ref, *refs):
@@ -474,11 +468,10 @@
     across0 = swapped(kv0y, "ctx", 2)
     across0, wanted1, wanted2 = tie(across0, wanted1, wanted2)
     core0y = swapped(across0, "ctx", 1)
-    kv1, own_core = tie(raised(kv0, 1), core0)
-    state = add([(0, 0, 0, 0), (0, 1, 1, 0)], kvs=[pinned([kv0y])[0], own_core], state=None)
+    state = add([(0, 0, 0, 0), (0, 1, 1, 0)], kvs=[pinned([kv0y])[0], core0], state=None)
     wanted, wanted1, wanted2, *state = tie(wanted, wanted1, wanted2, *state)
 
-    weight, wanted = tie(weight, wanted)
+    kv1, weight, wanted = tie(raised(kv0, 1), weight, wanted)
     firsts = [weight, swapped(weight, "ctx", 1), swapped(weight, "ctx", 2)]
     firsts.append(swapped(firsts[2], "ctx", 1))
 
@@ -508,27 +501,24 @@
     )
     parts, kv1, *state = tie(parts, kv1, *state)
     across1 = swapped(kv1, "ctx", 2)
-    *firsts, across1, weight = tie(*firsts, across1, score_weight)
+    *firsts, moved, weight = tie(*firsts, moved, score_weight)
     weights = [weight, None, swapped(weight, "ctx", 2)]
     parts = jnp.broadcast_to(parts.astype(jnp.float16)[None], (Z, GROUP, half))
     parts = lax.all_to_all(parts, "ctx", 0, 0, axis_index_groups=columns).astype(F32)
-    state, pair1 = add(
-        [(0, 2, 0, 0), (0, 3, 0, 1), (1, 0, 1, 0), (1, 2, 2, 0)],
-        kvs=[*pinned([moved]), kv1, across1],
-        state=state,
-        joined=2,
-    )
-    parts, pair1, weight, *state = tie(parts, pair1, weight, *state)
+    state = add(
+        [(0, 2, 0, 0), (0, 3, 0, 1), (1, 0, 1, 0)], kvs=[*pinned([moved]), kv1], state=state
+    )
+    parts, weight, *state = tie(parts, weight, *state)
     weights[1] = swapped(weight, "ctx", 1)
 
-    projected = small_call(
+    projected, pair1 = small_call(
         project_kernel,
-        jax.ShapeDtypeStruct((GROUP, WIDE), F32),
-        [parts, *firsts],
-        [VMEM] + [HBM] * 4,
+        (jax.ShapeDtypeStruct((GROUP, WIDE), F32), pltpu.VMEM((4, BLOCK, HD), BF16)),
+        [parts, *firsts, kv1, across1],
+        [VMEM] + [HBM] * 6,
         scratch_shapes=[
             pltpu.VMEM((PLANE, BLOCK, 256), BF16),
-            pltpu.SemaphoreType.DMA((PLANE,)),
+            pltpu.SemaphoreType.DMA((PLANE + 2,)),
         ],
         name="project",
     )
@@ -559,7 +549,9 @@
     )
     inner, pair2, *state = tie(inner, pair2, *state)
     inner = (inner * 2.0**-10).astype(jnp.float16).reshape(Z, PAD, WIDE)
-    state = add([(2, 0, 0, 0), (2, 2, 0, 1)], kvs=pinned([pair2]), state=state)
+    state = add(
+        [(1, 2, 0, 1), (2, 0, 1, 0), (2, 2, 1, 1)], kvs=[pair1, *pinned([pair2])], state=state
+    )
     inner = lax.all_to_all(inner, "ctx", 0, 0, axis_index_groups=columns)
     inner, *state = tie(inner, *state)
     inner = jnp.sum(inner.astype(F32), axis=0) * 2.0**10

time: 126 us -> 130 us (1.032)
  waiting for transfers between devices: 33.9 us -> 36.5 us
  local copies, waits for them, and re-layouts: 3.4 us -> 5.36 us
  starting transfers between devices: 44.9 us -> 46.2 us
    ppermute x17, waiting for transfers between devices: 17.4 us -> 25.2 us  [swapped(): return lax.ppermute(value, axis, [(s, s ^ bit) for s in range(count)])]
    all_to_all x1, waiting for transfers between devices: 4.48 us -> 0.73 us  [per_device(): lax.all_to_all(parts, 'ctx', 0, 0, axis_index_groups=columns).astype(F32)]
    unnamed x25 -> x35, local copies, waits for them, and re-layouts: 2.55 us -> 4.5 us
    all_to_all x1, starting transfers between devices: 6.61 us -> 7.94 us  [per_device(): inner = lax.all_to_all(inner, 'ctx', 0, 0, axis_index_groups=columns)]
  transfers between devices with their start and end apart: 24 -> 24, of which waited for: 11 -> 12; matrix products, arithmetic and copies ran while one was open for 3% -> 2% of each run, Pallas kernels for 13% -> 10%
where the time goes in v6:
time: 130 us; the launch traced here: 131 us
  starting transfers between devices  46.2 us (36%)
  waiting for transfers between devices  36.5 us (28%)
  Pallas kernels  21.4 us (16%)
  blocking collectives  17 us (13%)
  local copies, waits for them, and re-layouts  5.36 us (4%)
  other arithmetic  3.11 us (2%)
    ppermute x17, waiting for transfers between devices, swapped(): return lax.ppermute(value, axis, [(s, s ^ bit) for s in range(count)])  25.2 us
    ppermute x17, starting transfers between devices, swapped(): return lax.ppermute(value, axis, [(s, s ^ bit) for s in range(count)])  21.5 us
    all_to_all x1, blocking collectives, per_device(): lax.all_to_all(jnp.broadcast_to(gap[None], (count, 1, HD)), 'ctx', 0, 0)  17 us
    pallas_call x6, Pallas kernels, small_call(): pl.pallas_call(kernel, out_shape=shape, in_specs=specs or [VMEM] * len(op...  11.1 us
    pallas_call x5, Pallas kernels, attend(): pl.pallas_call(functools.partial(attend_kernel, slots, first, last), out_...  10.3 us
    all_to_all x1, starting transfers between devices, per_device(): inner = lax.all_to_all(inner, 'ctx', 0, 0, axis_index_groups=columns)  7.94 us
    ppermute x4, starting transfers between devices, raised(): lax.ppermute(value, 'ctx', [(s, (s + steps) % count) for s in range(count)])  7.56 us
    all_to_all x1, starting transfers between devices, per_device(): gap = lax.all_to_all(gap, 'head', 0, 0)  5.08 us
  transfers between devices with their start and end apart: 24, of which 12 were waited for; matrix products, arithmetic and copies ran while one was open for 2% of the time, Pallas kernels for 10%

profile of v6, /device:TPU:1, one launch (start us, length us, event | category | flops | bytes accessed | tf_op | source)
XLA Modules:
  0.0 130.6 jit_solution(767171332296517254)
XLA Ops:
  0.6 1.8 %pick.1 = (bf16[64,512]{1,0:T(8,128)(2,1)S(1)}, bf16[64,512]{1,0:T(8,128)(2,1)S(1)}, bf16[128,512]{1,0:T(8,128)(2,1)S(1)}, bf16[736,256]{1,0:T(8,128)(2,1)S(1)}) custom-call(s32[1]{0:T(128)} %bitcast.me_ref.refs_0_, s32[7,32]{1,0:T(8,128)} %steps_hbm.3, bf16[512,512]{1,0:T(8,128)(2,1)} %refs_2_.9, bf16[512,256]{1,0:T(8,128)(2,1)} %weight_hbm.1, ...), custom_call_target="tpu_custom_call" | custom-call | tf_op jit(solution)/shard_map/pick/pallas_call | solution.py:308
  2.4 3.3 %collective-permute-start.1 = (bf16[128,512]{1,0:T(8,128)(2,1)S(1)}, bf16[128,512]{1,0:T(8,128)(2,1)S(1)}, u32[]{:S(2)}, u32[]{:S(2)}) collective-permute-start(bf16[128,512]{1,0:T(8,128)(2,1)S(1)} %get-tuple-element.85), channel_id=1, source_target_pairs={{0,8},{8,0},{16,24},{24,16},{32,40},{40,32},{48,56},{56,48},{64,72... | collective-permute-start | bytes 393224 | tf_op jit(solution)/shard_map/ppermute | solution.py:417
  7.3 2.6 %collective-permute-done.2 = bf16[64,512]{1,0:T(8,128)(2,1)S(1)} collective-permute-done((bf16[64,512]{1,0:T(8,128)(2,1)S(1)}, bf16[64,512]{1,0:T(8,128)(2,1)S(1)}, u32[]{:S(2)}, u32[]{:S(2)}) %collective-permute-start.2) | collective-permute-done | bytes 65568 | tf_op jit(solution)/shard_map/ppermute | solution.py:417
  10.6 4.6 %collective-permute-start.5 = (bf16[64,512]{1,0:T(8,128)(2,1)S(1)}, bf16[64,512]{1,0:T(8,128)(2,1)S(1)}, u32[]{:S(2)}, u32[]{:S(2)}) collective-permute-start(bf16[64,512]{1,0:T(8,128)(2,1)S(1)} %fusion.1.q_ref), channel_id=1, source_target_pairs={{0,224},{8,232},{16,240},{24,248},{32,0},{40,8},{48,16},{56,24},{6... | collective-permute-start | bytes 196616 | tf_op jit(solution)/shard_map/ppermute | solution.py:423
  17.1 2.2 %collective-permute-done.6.q2_ref = bf16[64,512]{1,0:T(8,128)(2,1)S(1)} collective-permute-done((bf16[64,512]{1,0:T(8,128)(2,1)S(1)}, bf16[64,512]{1,0:T(8,128)(2,1)S(1)}, u32[]{:S(2)}, u32[]{:S(2)}) %collective-permute-start.6) | collective-permute-done | bytes 65568 | tf_op jit(solution)/shard_map/ppermute | solution.py:423
  19.3 3.2 %collective-permute-start.7 = (bf16[2,512,128]{2,1,0:T(8,128)(2,1)S(1)}, bf16[2,512,128]{2,1,0:T(8,128)(2,1)S(1)}, u32[]{:S(2)}, u32[]{:S(2)}) collective-permute-start(bf16[2,512,128]{2,1,0:T(8,128)(2,1)S(1)} %collective-permute-done.4.refs_2_), channel_id=1, source_target_pairs={{0,8},{8,0},{16,24},{24,16},{32,40},{40,32},{48,56},{56,48},{64,72... | collective-permute-start | bytes 786440 | tf_op jit(solution)/shard_map/ppermute | solution.py:417
  22.5 4.2 %attend_0_0.1 = (f32[512,512]{1,0:T(8,128)S(1)}, f32[512,512]{1,0:T(8,128)S(1)}, f32[512,512]{1,0:T(8,128)S(1)}) custom-call(s32[1]{0:T(128)} %bitcast.me_ref.refs_0_, s32[7]{0:T(128)} %refs_1_.9, bf16[512,512]{1,0:T(8,128)(2,1)} %refs_2_.9, bf16[2,512,128]{2,1,0:T(8,128)(2,1)} %refs_0_.1, bf16[2,512,128]{2,1,0:T(8,128)(2,1)S(1)} %collective-permute-done.3.refs_4_.refs_1_), custom_call_target="tpu_custom_call" | custom-call | flops 1073741824 | bytes 1048576 | tf_op jit(solution)/shard_map/attend_0_0/pallas_call | solution.py:280
  26.8 3.1 %picked.1 = (f32[64,512]{1,0:T(8,128)S(1)}, bf16[4,512,128]{2,1,0:T(8,128)(2,1)}) custom-call(s32[1]{0:T(128)} %bitcast.me_ref.refs_0_, s32[7]{0:T(128)} %refs_1_.9, s32[7,32]{1,0:T(8,128)} %steps_hbm.3, bf16[64,512]{1,0:T(8,128)(2,1)S(1)} %fusion.1.q_ref, bf16[64,512]{1,0:T(8,128)(2,1)S(1)} %collective-permute-done.5.q1_ref, ...), custom_call_target="tpu_custom_call" | custom-call | tf_op jit(solution)/shard_map/picked/pallas_call | solution.py:308
  30.8 4.1 %all-to-all-start = ((f16[8,64,512]{2,1,0:T(8,128)(2,1)}), f16[8,64,512]{2,1,0:T(8,128)(2,1)}, u32[]{:S(2)}, u32[]{:S(2)}) async-start(f16[8,64,512]{2,1,0:T(8,128)(2,1)} %broadcast_in_dim.4), calls=%async_computation | async-start | bytes 1048576 | tf_op jit(solution)/shard_map/all_to_all | solution.py:507
  35.3 10.7 %collective-permute-done.9.refs_2_ = bf16[736,256]{1,0:T(8,128)(2,1)S(1)} collective-permute-done((bf16[736,256]{1,0:T(8,128)(2,1)S(1)}, bf16[736,256]{1,0:T(8,128)(2,1)S(1)}, u32[]{:S(2)}, u32[]{:S(2)}) %collective-permute-start.9) | collective-permute-done | bytes 376864 | tf_op jit(solution)/shard_map/ppermute | solution.py:417
  55.0 2.0 %project.1 = (f32[64,1024]{1,0:T(8,128)S(1)}, bf16[4,512,128]{2,1,0:T(8,128)(2,1)S(1)}) custom-call(f32[8,64,512]{2,1,0:T(8,128)S(1)} %convert_element_type.22.got_ref, bf16[736,256]{1,0:T(8,128)(2,1)S(1)} %get-tuple-element.118.refs_0_, bf16[736,256]{1,0:T(8,128)(2,1)S(1)} %copy-done.3, bf16[736,256]{1,0:T(8,128)(2,1)S(1)} %copy-done.1, ...), custom_call_target="tpu_custom_call" | custom-call | tf_op jit(solution)/shard_map/project/pallas_call | solution.py:308
  57.1 1.8 %collective-permute-start.15 = (bf16[4,512,128]{2,1,0:T(8,128)(2,1)S(1)}, bf16[4,512,128]{2,1,0:T(8,128)(2,1)S(1)}, u32[]{:S(2)}, u32[]{:S(2)}) collective-permute-start(bf16[4,512,128]{2,1,0:T(8,128)(2,1)S(1)} %get-tuple-element.126.refs_3_), channel_id=1, source_target_pairs={{0,8},{8,0},{16,24},{24,16},{32,40},{40,32},{48,56},{56,48},{64,72... | collective-permute-start | bytes 1572872 | tf_op jit(solution)/shard_map/ppermute | solution.py:417
  61.8 3.0 %collective-permute-done.12 = f16[64,1024]{1,0:T(8,128)(2,1)S(1)} collective-permute-done((f16[64,1024]{1,0:T(8,128)(2,1)S(1)}, f16[64,1024]{1,0:T(8,128)(2,1)S(1)}, u32[]{:S(2)}, u32[]{:S(2)}) %collective-permute-start.12) | collective-permute-done | bytes 131104 | tf_op jit(solution)/shard_map/ppermute | solution.py:417
  67.3 2.7 %collective-permute-start.14 = (f16[64,1024]{1,0:T(8,128)(2,1)S(1)}, f16[64,1024]{1,0:T(8,128)(2,1)S(1)}, u32[]{:S(2)}, u32[]{:S(2)}) collective-permute-start(f16[64,1024]{1,0:T(8,128)(2,1)S(1)} %add.21), channel_id=1, source_target_pairs={{0,4},{1,5},{2,6},{3,7},{4,0},{5,1},{6,2},{7,3},{8,12},{9,13},{10,... | collective-permute-start | bytes 393224 | tf_op jit(solution)/shard_map/ppermute | solution.py:417
  70.0 3.9 %collective-permute-done.14 = f16[64,1024]{1,0:T(8,128)(2,1)S(1)} collective-permute-done((f16[64,1024]{1,0:T(8,128)(2,1)S(1)}, f16[64,1024]{1,0:T(8,128)(2,1)S(1)}, u32[]{:S(2)}, u32[]{:S(2)}) %collective-permute-start.14) | collective-permute-done | bytes 131104 | tf_op jit(solution)/shard_map/ppermute | solution.py:417
  74.0 2.9 %collective-permute-start.16 = (f16[64,1024]{1,0:T(8,128)(2,1)S(1)}, f16[64,1024]{1,0:T(8,128)(2,1)S(1)}, u32[]{:S(2)}, u32[]{:S(2)}) collective-permute-start(f16[64,1024]{1,0:T(8,128)(2,1)S(1)} %add.22), channel_id=1, source_target_pairs={{0,1},{1,0},{2,3},{3,2},{4,5},{5,4},{6,7},{7,6},{8,9},{9,8},{10,11... | collective-permute-start | bytes 393224 | tf_op jit(solution)/shard_map/ppermute | solution.py:417
  78.1 1.9 %collective-permute-done.16 = f16[64,1024]{1,0:T(8,128)(2,1)S(1)} collective-permute-done((f16[64,1024]{1,0:T(8,128)(2,1)S(1)}, f16[64,1024]{1,0:T(8,128)(2,1)S(1)}, u32[]{:S(2)}, u32[]{:S(2)}) %collective-permute-start.16) | collective-permute-done | bytes 131104 | tf_op jit(solution)/shard_map/ppermute | solution.py:417
  80.1 2.1 %inner.1 = f32[64,1024]{1,0:T(8,128)S(1)} custom-call(s32[1]{0:T(128)} %bitcast.me_ref.refs_0_, f32[64,1024]{1,0:T(8,128)S(1)} %add_multiply_fusion.total_ref, bf16[736,256]{1,0:T(8,128)(2,1)S(1)} %get-tuple-element.118.refs_0_, bf16[736,256]{1,0:T(8,128)(2,1)S(1)} %copy-done.3, bf16[736,256]{1,0:T(8,128)(2,1)S(1)} %copy-done.1, ...), custom_call_target="tpu_custom_call" | custom-call | tf_op jit(solution)/shard_map/inner/pallas_call | solution.py:308
  82.9 7.9 %all-to-all-start.1 = ((f16[8,8,1024]{2,1,0:T(8,128)(2,1)}), f16[8,8,1024]{2,1,0:T(8,128)(2,1)}, u32[]{:S(2)}, u32[]{:S(2)}) async-start(f16[8,8,1024]{2,1,0:T(8,128)(2,1)} %fusion), calls=%async_computation.1 | async-start | bytes 262144 | tf_op jit(solution)/shard_map/all_to_all | solution.py:555
  94.6 4.3 %all-to-all-done.1 = f16[8,8,1024]{2,1,0:T(8,128)(2,1)} async-done(((f16[8,8,1024]{2,1,0:T(8,128)(2,1)}), f16[8,8,1024]{2,1,0:T(8,128)(2,1)}, u32[]{:S(2)}, u32[]{:S(2)}) %all-to-all-start.1) | async-done | bytes 131104 | tf_op jit(solution)/shard_map/all_to_all | solution.py:555
  100.7 5.1 %all-to-all-start.2 = ((f32[8,1,128]{2,1,0:T(1,128)}), f32[8,1,128]{2,1,0:T(1,128)S(1)}, u32[]{:S(2)}, u32[]{:S(2)}) async-start(f32[8,1,128]{2,1,0:T(1,128)} %hidden.1), calls=%async_computation.2 | async-start | bytes 8192 | tf_op jit(solution)/shard_map/all_to_all | solution.py:567
  105.8 2.4 %attend_2_1.1 = f32[512,512]{1,0:T(8,128)} custom-call(s32[1]{0:T(128)} %bitcast.me_ref.refs_0_, s32[7]{0:T(128)} %refs_1_.9, bf16[512,512]{1,0:T(8,128)(2,1)} %refs_2_.9, bf16[4,512,128]{2,1,0:T(8,128)(2,1)} %collective-permute-done.20.refs_3_, f32[512,512]{1,0:T(8,128)S(1)} %get-tuple-element.156.refs_4_, f32[512,512]{1,0:T(8,128)S(1)} %get-tuple-element.157.refs_5_, ...), custom_call_target="tpu_custom_call" | custom-call | flops 1073741824 | bytes 1048576 | tf_op jit(solution)/shard_map/attend_2_1/pallas_call | solution.py:280
  108.2 4.1 %all-to-all-done.2 = f32[8,1,128]{2,1,0:T(1,128)S(1)} async-done(((f32[8,1,128]{2,1,0:T(1,128)}), f32[8,1,128]{2,1,0:T(1,128)S(1)}, u32[]{:S(2)}, u32[]{:S(2)}) %all-to-all-start.2) | async-done | bytes 4128 | tf_op jit(solution)/shard_map/all_to_all | solution.py:567
  112.3 17.0 %all_to_all.20.got_ref = f32[32,1,128]{2,1,0:T(1,128)S(1)} all-to-all(f32[32,1,128]{2,1,0:T(1,128)S(1)} %broadcast_in_dim.5), channel_id=1, replica_groups=mesh['ctx'=32,'head'=8] {'ctx'}, dimensions={0} | all-to-all | bytes 32768 | tf_op jit(solution)/shard_map/all_to_all | solution.py:570
  (85 shorter events, 28.6 us)
Async XLA Ops:
  2.4 4.3 %collective-permute-start.1 = (bf16[128,512]{1,0:T(8,128)(2,1)S(1)}, bf16[128,512]{1,0:T(8,128)(2,1)S(1)}, u32[]{:S(2)}, u32[]{:S(2)}) collective-permute-start(bf16[128,512]{1,0:T(8,128)(2,1)S(1)} %get-tuple-element.85), channel_id=1, source_target_pairs={{0,8},{8,0},{16,24},{24,16},{32,40},{40,32},{48,56},{56,48},{64,72... | collective-permute-start | bytes 393224 | tf_op jit(solution)/shard_map/ppermute | solution.py:417
  6.7 3.2 %collective-permute-start.2 = (bf16[64,512]{1,0:T(8,128)(2,1)S(1)}, bf16[64,512]{1,0:T(8,128)(2,1)S(1)}, u32[]{:S(2)}, u32[]{:S(2)}) collective-permute-start(bf16[64,512]{1,0:T(8,128)(2,1)S(1)} %slice_add_fusion), channel_id=1, source_target_pairs={{0,16},{8,24},{16,0},{24,8},{32,48},{40,56},{48,32},{56,40},{64,80... | collective-permute-start | bytes 196616 | tf_op jit(solution)/shard_map/ppermute | solution.py:417
  6.8 3.1 %collective-permute-start.3 = (bf16[2,512,128]{2,1,0:T(8,128)(2,1)S(1)}, bf16[2,512,128]{2,1,0:T(8,128)(2,1)S(1)}, u32[]{:S(2)}, u32[]{:S(2)}) collective-permute-start(bf16[2,512,128]{2,1,0:T(8,128)(2,1)S(1)} %copy-done.14), channel_id=1, source_target_pairs={{0,8},{8,0},{16,24},{24,16},{32,40},{40,32},{48,56},{56,48},{64,72... | collective-permute-start | bytes 786440 | tf_op jit(solution)/shard_map/ppermute | solution.py:417
  10.0 9.4 %collective-permute-start.4 = (bf16[2,512,128]{2,1,0:T(8,128)(2,1)S(1)}, bf16[2,512,128]{2,1,0:T(8,128)(2,1)S(1)}, u32[]{:S(2)}, u32[]{:S(2)}) collective-permute-start(bf16[2,512,128]{2,1,0:T(8,128)(2,1)S(1)} %copy-done.14), channel_id=1, source_target_pairs={{0,16},{8,24},{16,0},{24,8},{32,48},{40,56},{48,32},{56,40},{64,80... | collective-permute-start | bytes 786440 | tf_op jit(solution)/shard_map/ppermute | solution.py:417
  10.6 6.5 %collective-permute-start.5 = (bf16[64,512]{1,0:T(8,128)(2,1)S(1)}, bf16[64,512]{1,0:T(8,128)(2,1)S(1)}, u32[]{:S(2)}, u32[]{:S(2)}) collective-permute-start(bf16[64,512]{1,0:T(8,128)(2,1)S(1)} %fusion.1.q_ref), channel_id=1, source_target_pairs={{0,224},{8,232},{16,240},{24,248},{32,0},{40,8},{48,16},{56,24},{6... | collective-permute-start | bytes 196616 | tf_op jit(solution)/shard_map/ppermute | solution.py:423
  15.2 4.1 %collective-permute-start.6 = (bf16[64,512]{1,0:T(8,128)(2,1)S(1)}, bf16[64,512]{1,0:T(8,128)(2,1)S(1)}, u32[]{:S(2)}, u32[]{:S(2)}) collective-permute-start(bf16[64,512]{1,0:T(8,128)(2,1)S(1)} %fusion.1.q_ref), channel_id=1, source_target_pairs={{0,192},{8,200},{16,208},{24,216},{32,224},{40,232},{48,240},{56,2... | collective-permute-start | bytes 196616 | tf_op jit(solution)/shard_map/ppermute | solution.py:423
  16.4 10.4 %collective-permute-start = (bf16[2,512,128]{2,1,0:T(8,128)(2,1)S(1)}, bf16[2,512,128]{2,1,0:T(8,128)(2,1)S(1)}, u32[]{:S(2)}, u32[]{:S(2)}) collective-permute-start(bf16[2,512,128]{2,1,0:T(8,128)(2,1)S(1)} %copy-done.14), channel_id=1, source_target_pairs={{0,32},{8,40},{16,48},{24,56},{32,64},{40,72},{48,80},{56,88},{64,... | collective-permute-start | bytes 786440 | tf_op jit(solution)/shard_map/ppermute | solution.py:423
  19.3 7.5 %collective-permute-start.7 = (bf16[2,512,128]{2,1,0:T(8,128)(2,1)S(1)}, bf16[2,512,128]{2,1,0:T(8,128)(2,1)S(1)}, u32[]{:S(2)}, u32[]{:S(2)}) collective-permute-start(bf16[2,512,128]{2,1,0:T(8,128)(2,1)S(1)} %collective-permute-done.4.refs_2_), channel_id=1, source_target_pairs={{0,8},{8,0},{16,24},{24,16},{32,40},{40,32},{48,56},{56,48},{64,72... | collective-permute-start | bytes 786440 | tf_op jit(solution)/shard_map/ppermute | solution.py:417
  30.8 22.2 %all-to-all-start = ((f16[8,64,512]{2,1,0:T(8,128)(2,1)}), f16[8,64,512]{2,1,0:T(8,128)(2,1)}, u32[]{:S(2)}, u32[]{:S(2)}) async-start(f16[8,64,512]{2,1,0:T(8,128)(2,1)} %broadcast_in_dim.4), calls=%async_computation | async-start | bytes 1048576 | tf_op jit(solution)/shard_map/all_to_all | solution.py:507
  34.9 11.1 %collective-permute-start.9 = (bf16[736,256]{1,0:T(8,128)(2,1)S(1)}, bf16[736,256]{1,0:T(8,128)(2,1)S(1)}, u32[]{:S(2)}, u32[]{:S(2)}) collective-permute-start(bf16[736,256]{1,0:T(8,128)(2,1)S(1)} %get-tuple-element.118.refs_0_), channel_id=1, source_target_pairs={{0,16},{8,24},{16,0},{24,8},{32,48},{40,56},{48,32},{56,40},{64,80... | collective-permute-start | bytes 1130504 | tf_op jit(solution)/shard_map/ppermute | solution.py:417
  35.3 11.9 %collective-permute-start.8 = (bf16[736,256]{1,0:T(8,128)(2,1)S(1)}, bf16[736,256]{1,0:T(8,128)(2,1)S(1)}, u32[]{:S(2)}, u32[]{:S(2)}) collective-permute-start(bf16[736,256]{1,0:T(8,128)(2,1)S(1)} %get-tuple-element.118.refs_0_), channel_id=1, source_target_pairs={{0,8},{8,0},{16,24},{24,16},{32,40},{40,32},{48,56},{56,48},{64,72... | collective-permute-start | bytes 1130504 | tf_op jit(solution)/shard_map/ppermute | solution.py:417
  46.0 1.9 %collective-permute-start.10 = (bf16[736,256]{1,0:T(8,128)(2,1)S(1)}, bf16[736,256]{1,0:T(8,128)(2,1)S(1)}, u32[]{:S(2)}, u32[]{:S(2)}) collective-permute-start(bf16[736,256]{1,0:T(8,128)(2,1)S(1)} %collective-permute-done.9.refs_2_), channel_id=1, source_target_pairs={{0,8},{8,0},{16,24},{24,16},{32,40},{40,32},{48,56},{56,48},{64,72... | collective-permute-start | bytes 1130504 | tf_op jit(solution)/shard_map/ppermute | solution.py:417
  47.0 8.0 %collective-permute-start.11 = (bf16[2,512,128]{2,1,0:T(8,128)(2,1)}, bf16[2,512,128]{2,1,0:T(8,128)(2,1)}, u32[]{:S(2)}, u32[]{:S(2)}) collective-permute-start(bf16[2,512,128]{2,1,0:T(8,128)(2,1)} %copy-done.7), channel_id=1, source_target_pairs={{0,16},{8,24},{16,0},{24,8},{32,48},{40,56},{48,32},{56,40},{64,80... | collective-permute-start | bytes 786440 | tf_op jit(solution)/shard_map/ppermute | solution.py:417
  48.7 17.5 %collective-permute-start.13 = (bf16[256,1024]{1,0:T(8,128)(2,1)}, bf16[256,1024]{1,0:T(8,128)(2,1)}, u32[]{:S(2)}, u32[]{:S(2)}) collective-permute-start(bf16[256,1024]{1,0:T(8,128)(2,1)} %refs_4_), channel_id=1, source_target_pairs={{0,16},{8,24},{16,0},{24,8},{32,48},{40,56},{48,32},{56,40},{64,80... | collective-permute-start | bytes 1572872 | tf_op jit(solution)/shard_map/ppermute | solution.py:417
  57.1 16.9 %collective-permute-start.15 = (bf16[4,512,128]{2,1,0:T(8,128)(2,1)S(1)}, bf16[4,512,128]{2,1,0:T(8,128)(2,1)S(1)}, u32[]{:S(2)}, u32[]{:S(2)}) collective-permute-start(bf16[4,512,128]{2,1,0:T(8,128)(2,1)S(1)} %get-tuple-element.126.refs_3_), channel_id=1, source_target_pairs={{0,8},{8,0},{16,24},{24,16},{32,40},{40,32},{48,56},{56,48},{64,72... | collective-permute-start | bytes 1572872 | tf_op jit(solution)/shard_map/ppermute | solution.py:417
  58.9 19.2 %collective-permute-start.17 = (bf16[4,512,128]{2,1,0:T(8,128)(2,1)S(1)}, bf16[4,512,128]{2,1,0:T(8,128)(2,1)S(1)}, u32[]{:S(2)}, u32[]{:S(2)}) collective-permute-start(bf16[4,512,128]{2,1,0:T(8,128)(2,1)S(1)} %get-tuple-element.126.refs_3_), channel_id=1, source_target_pairs={{0,32},{8,40},{16,48},{24,56},{32,64},{40,72},{48,80},{56,88},{64,... | collective-permute-start | bytes 1572872 | tf_op jit(solution)/shard_map/ppermute | solution.py:423
  60.0 4.8 %collective-permute-start.12 = (f16[64,1024]{1,0:T(8,128)(2,1)S(1)}, f16[64,1024]{1,0:T(8,128)(2,1)S(1)}, u32[]{:S(2)}, u32[]{:S(2)}) collective-permute-start(f16[64,1024]{1,0:T(8,128)(2,1)S(1)} %multiply_convert_fusion.1), channel_id=1, source_target_pairs={{0,2},{1,3},{2,0},{3,1},{4,6},{5,7},{6,4},{7,5},{8,10},{9,11},{10,... | collective-permute-start | bytes 393224 | tf_op jit(solution)/shard_map/ppermute | solution.py:417
  61.2 18.9 %collective-permute-start.18 = (bf16[256,1024]{1,0:T(8,128)(2,1)S(1)}, bf16[256,1024]{1,0:T(8,128)(2,1)S(1)}, u32[]{:S(2)}, u32[]{:S(2)}) collective-permute-start(bf16[256,1024]{1,0:T(8,128)(2,1)S(1)} %copy-done.6), channel_id=1, source_target_pairs={{0,8},{8,0},{16,24},{24,16},{32,40},{40,32},{48,56},{56,48},{64,72... | collective-permute-start | bytes 1572872 | tf_op jit(solution)/shard_map/ppermute | solution.py:417
  66.2 13.9 %collective-permute-start.19 = (bf16[256,1024]{1,0:T(8,128)(2,1)}, bf16[256,1024]{1,0:T(8,128)(2,1)S(1)}, u32[]{:S(2)}, u32[]{:S(2)}) collective-permute-start(bf16[256,1024]{1,0:T(8,128)(2,1)} %collective-permute-done.13.refs_6_), channel_id=1, source_target_pairs={{0,8},{8,0},{16,24},{24,16},{32,40},{40,32},{48,56},{56,48},{64,72... | collective-permute-start | bytes 1572872 | tf_op jit(solution)/shard_map/ppermute | solution.py:417
  67.3 6.6 %collective-permute-start.14 = (f16[64,1024]{1,0:T(8,128)(2,1)S(1)}, f16[64,1024]{1,0:T(8,128)(2,1)S(1)}, u32[]{:S(2)}, u32[]{:S(2)}) collective-permute-start(f16[64,1024]{1,0:T(8,128)(2,1)S(1)} %add.21), channel_id=1, source_target_pairs={{0,4},{1,5},{2,6},{3,7},{4,0},{5,1},{6,2},{7,3},{8,12},{9,13},{10,... | collective-permute-start | bytes 393224 | tf_op jit(solution)/shard_map/ppermute | solution.py:417
  74.0 6.1 %collective-permute-start.16 = (f16[64,1024]{1,0:T(8,128)(2,1)S(1)}, f16[64,1024]{1,0:T(8,128)(2,1)S(1)}, u32[]{:S(2)}, u32[]{:S(2)}) collective-permute-start(f16[64,1024]{1,0:T(8,128)(2,1)S(1)} %add.22), channel_id=1, source_target_pairs={{0,1},{1,0},{2,3},{3,2},{4,5},{5,4},{6,7},{7,6},{8,9},{9,8},{10,11... | collective-permute-start | bytes 393224 | tf_op jit(solution)/shard_map/ppermute | solution.py:417
  82.9 16.0 %all-to-all-start.1 = ((f16[8,8,1024]{2,1,0:T(8,128)(2,1)}), f16[8,8,1024]{2,1,0:T(8,128)(2,1)}, u32[]{:S(2)}, u32[]{:S(2)}) async-start(f16[8,8,1024]{2,1,0:T(8,128)(2,1)} %fusion), calls=%async_computation.1 | async-start | bytes 262144 | tf_op jit(solution)/shard_map/all_to_all | solution.py:555
  90.9 9.9 %collective-permute-start.20 = (bf16[4,512,128]{2,1,0:T(8,128)(2,1)}, bf16[4,512,128]{2,1,0:T(8,128)(2,1)}, u32[]{:S(2)}, u32[]{:S(2)}) collective-permute-start(bf16[4,512,128]{2,1,0:T(8,128)(2,1)} %copy-done.16), channel_id=1, source_target_pairs={{0,8},{8,0},{16,24},{24,16},{32,40},{40,32},{48,56},{56,48},{64,72... | collective-permute-start | bytes 1572872 | tf_op jit(solution)/shard_map/ppermute | solution.py:417
  100.7 11.5 %all-to-all-start.2 = ((f32[8,1,128]{2,1,0:T(1,128)}), f32[8,1,128]{2,1,0:T(1,128)S(1)}, u32[]{:S(2)}, u32[]{:S(2)}) async-start(f32[8,1,128]{2,1,0:T(1,128)} %hidden.1), calls=%async_computation.2 | async-start | bytes 8192 | tf_op jit(solution)/shard_map/all_to_all | solution.py:567
  (17 other events, 93.0 us)

commit v7 on v6

--- a/solution.py
+++ b/solution.py
@@ -466,14 +466,14 @@
     wanted, kv0y, core0 = tie(wanted, kv0, core0)
     wanted1, wanted2 = raised(wanted, -1), raised(wanted, -2)
     across0 = swapped(kv0y, "ctx", 2)
-    across0, wanted1, wanted2 = tie(across0, wanted1, wanted2)
+    state = add([(0, 0, 0, 0), (0, 1, 1, 0)], kvs=[pinned([kv0y])[0], core0], state=None)
+    kv1 = raised(kv0, 1)
+    across0, wanted1, wanted2, kv1, *state = tie(across0, wanted1, wanted2, kv1, *state)
     core0y = swapped(across0, "ctx", 1)
-    state = add([(0, 0, 0, 0), (0, 1, 1, 0)], kvs=[pinned([kv0y])[0], core0], state=None)
     wanted, wanted1, wanted2, *state = tie(wanted, wanted1, wanted2, *state)
 
-    kv1, weight, wanted = tie(raised(kv0, 1), weight, wanted)
+    weight, wanted = tie(weight, wanted)
     firsts = [weight, swapped(weight, "ctx", 1), swapped(weight, "ctx", 2)]
-    firsts.append(swapped(firsts[2], "ctx", 1))
 
     parts, moved = small_call(
         picked_kernel,
@@ -502,11 +502,12 @@
     parts, kv1, *state = tie(parts, kv1, *state)
     across1 = swapped(kv1, "ctx", 2)
     *firsts, moved, weight = tie(*firsts, moved, score_weight)
+    firsts = [*pinned(firsts), swapped(firsts[2], "ctx", 1)]
     weights = [weight, None, swapped(weight, "ctx", 2)]
     parts = jnp.broadcast_to(parts.astype(jnp.float16)[None], (Z, GROUP, half))
     parts = lax.all_to_all(parts, "ctx", 0, 0, axis_index_groups=columns).astype(F32)
     state = add(
-        [(0, 2, 0, 0), (0, 3, 0, 1), (1, 0, 1, 0)], kvs=[*pinned([moved]), kv1], state=state
+        [(0, 2, 0, 0), (0, 3, 0, 1), (1, 0, 1, 0)], kvs=pinned([moved, kv1]), state=state
     )
     parts, weight, *state = tie(parts, weight, *state)
     weights[1] = swapped(weight, "ctx", 1)
@@ -514,7 +515,7 @@
     projected, pair1 = small_call(
         project_kernel,
         (jax.ShapeDtypeStruct((GROUP, WIDE), F32), pltpu.VMEM((4, BLOCK, HD), BF16)),
-        [parts, *firsts, kv1, across1],
+        [parts, *firsts, *pinned([kv1]), across1],
         [VMEM] + [HBM] * 6,
         scratch_shapes=[
             pltpu.VMEM((PLANE, BLOCK, 256), BF16),
@@ -550,7 +551,7 @@
     inner, pair2, *state = tie(inner, pair2, *state)
     inner = (inner * 2.0**-10).astype(jnp.float16).reshape(Z, PAD, WIDE)
     state = add(
-        [(1, 2, 0, 1), (2, 0, 1, 0), (2, 2, 1, 1)], kvs=[pair1, *pinned([pair2])], state=state
+        [(1, 2, 0, 1), (2, 0, 1, 0), (2, 2, 1, 1)], kvs=pinned([pair1, pair2]), state=state
     )
     inner = lax.all_to_all(inner, "ctx", 0, 0, axis_index_groups=columns)
     inner, *state = tie(inner, *state)

time: 130 us -> 125 us (0.962)
  local copies, waits for them, and re-layouts: 5.36 us -> 1.11 us
  blocking collectives: 17 us -> 15.1 us
    unnamed x35 -> x21, local copies, waits for them, and re-layouts: 4.5 us -> 0.25 us
    all_to_all x1, waiting for transfers between devices: 0.73 us -> 3.16 us  [per_device(): lax.all_to_all(parts, 'ctx', 0, 0, axis_index_groups=columns).astype(F32)]
    ppermute x4, waiting for transfers between devices: 2.22 us -> 0.01 us  [raised(): lax.ppermute(value, 'ctx', [(s, (s + steps) % count) for s in range(count)])]
    all_to_all x1, blocking collectives: 17 us -> 15.1 us  [per_device(): lax.all_to_all(jnp.broadcast_to(gap[None], (count, 1, HD)), 'ctx', 0, 0)]
  transfers between devices with their start and end apart: 24 -> 24, of which waited for: 12 -> 13; matrix products, arithmetic and copies ran while one was open for 2% -> 1% of each run, Pallas kernels for 10% -> 11%
where the time goes in v7:
time: 125 us
  starting transfers between devices  46.7 us (37%)
  waiting for transfers between devices  37.4 us (30%)
  Pallas kernels  21.4 us (17%)
  blocking collectives  15.1 us (12%)
  other arithmetic  2.07 us (2%)
    ppermute x17, waiting for transfers between devices, swapped(): return lax.ppermute(value, axis, [(s, s ^ bit) for s in range(count)])  25 us
    ppermute x17, starting transfers between devices, swapped(): return lax.ppermute(value, axis, [(s, s ^ bit) for s in range(count)])  20.3 us
    all_to_all x1, blocking collectives, per_device(): lax.all_to_all(jnp.broadcast_to(gap[None], (count, 1, HD)), 'ctx', 0, 0)  15.1 us
    pallas_call x6, Pallas kernels, small_call(): pl.pallas_call(kernel, out_shape=shape, in_specs=specs or [VMEM] * len(op...  11 us
    pallas_call x5, Pallas kernels, attend(): pl.pallas_call(functools.partial(attend_kernel, slots, first, last), out_...  10.4 us
    ppermute x4, starting transfers between devices, raised(): lax.ppermute(value, 'ctx', [(s, (s + steps) % count) for s in range(count)])  8.76 us
    all_to_all x1, starting transfers between devices, per_device(): inner = lax.all_to_all(inner, 'ctx', 0, 0, axis_index_groups=columns)  8.55 us
    all_to_all x1, waiting for transfers between devices, per_device(): inner = lax.all_to_all(inner, 'ctx', 0, 0, axis_index_groups=columns)  5.15 us
  transfers between devices with their start and end apart: 24, of which 13 were waited for; matrix products, arithmetic and copies ran while one was open for 1% of the time, Pallas kernels for 11%

profile of v7, /device:TPU:1, one launch (start us, length us, event | category | flops | bytes accessed | tf_op | source)
XLA Modules:
  0.0 124.8 jit_solution(9617417390344844048)
XLA Ops:
  0.6 1.8 %pick.1 = (bf16[64,512]{1,0:T(8,128)(2,1)S(1)}, bf16[64,512]{1,0:T(8,128)(2,1)S(1)}, bf16[128,512]{1,0:T(8,128)(2,1)S(1)}, bf16[736,256]{1,0:T(8,128)(2,1)S(1)}) custom-call(s32[1]{0:T(128)} %bitcast.me_ref.refs_0_, s32[7,32]{1,0:T(8,128)} %steps_hbm.3, bf16[512,512]{1,0:T(8,128)(2,1)} %refs_2_.9, bf16[512,256]{1,0:T(8,128)(2,1)} %weight_hbm.1, ...), custom_call_target="tpu_custom_call" | custom-call | tf_op jit(solution)/shard_map/pick/pallas_call | solution.py:308
  2.4 3.3 %collective-permute-start = (bf16[128,512]{1,0:T(8,128)(2,1)S(1)}, bf16[128,512]{1,0:T(8,128)(2,1)S(1)}, u32[]{:S(2)}, u32[]{:S(2)}) collective-permute-start(bf16[128,512]{1,0:T(8,128)(2,1)S(1)} %get-tuple-element.87), channel_id=1, source_target_pairs={{0,8},{8,0},{16,24},{24,16},{32,40},{40,32},{48,56},{56,48},{64,72... | collective-permute-start | bytes 393224 | tf_op jit(solution)/shard_map/ppermute | solution.py:417
  10.6 4.6 %collective-permute-start.4 = (bf16[64,512]{1,0:T(8,128)(2,1)S(1)}, bf16[64,512]{1,0:T(8,128)(2,1)S(1)}, u32[]{:S(2)}, u32[]{:S(2)}) collective-permute-start(bf16[64,512]{1,0:T(8,128)(2,1)S(1)} %fusion.1.q_ref), channel_id=1, source_target_pairs={{0,224},{8,232},{16,240},{24,248},{32,0},{40,8},{48,16},{56,24},{6... | collective-permute-start | bytes 196616 | tf_op jit(solution)/shard_map/ppermute | solution.py:423
  16.4 4.2 %attend_0_0.1 = (f32[512,512]{1,0:T(8,128)S(1)}, f32[512,512]{1,0:T(8,128)S(1)}, f32[512,512]{1,0:T(8,128)S(1)}) custom-call(s32[1]{0:T(128)} %bitcast.me_ref.refs_0_, s32[7]{0:T(128)} %refs_1_.9, bf16[512,512]{1,0:T(8,128)(2,1)} %refs_2_.9, bf16[2,512,128]{2,1,0:T(8,128)(2,1)} %refs_0_.1, bf16[2,512,128]{2,1,0:T(8,128)(2,1)S(1)} %collective-permute-done.2.refs_4_.refs_1_), custom_call_target="tpu_custom_call" | custom-call | flops 1073741824 | bytes 1048576 | tf_op jit(solution)/shard_map/attend_0_0/pallas_call | solution.py:280
  20.7 1.9 %collective-permute-start.7 = (bf16[2,512,128]{2,1,0:T(8,128)(2,1)S(1)}, bf16[2,512,128]{2,1,0:T(8,128)(2,1)S(1)}, u32[]{:S(2)}, u32[]{:S(2)}) collective-permute-start(bf16[2,512,128]{2,1,0:T(8,128)(2,1)S(1)} %collective-permute-done.3.refs_2_), channel_id=1, source_target_pairs={{0,8},{8,0},{16,24},{24,16},{32,40},{40,32},{48,56},{56,48},{64,72... | collective-permute-start | bytes 786440 | tf_op jit(solution)/shard_map/ppermute | solution.py:417
  23.7 3.0 %picked.1 = (f32[64,512]{1,0:T(8,128)S(1)}, bf16[4,512,128]{2,1,0:T(8,128)(2,1)}) custom-call(s32[1]{0:T(128)} %bitcast.me_ref.refs_0_, s32[7]{0:T(128)} %refs_1_.9, s32[7,32]{1,0:T(8,128)} %steps_hbm.3, bf16[64,512]{1,0:T(8,128)(2,1)S(1)} %fusion.1.q_ref, bf16[64,512]{1,0:T(8,128)(2,1)S(1)} %collective-permute-done.4.q1_ref, ...), custom_call_target="tpu_custom_call" | custom-call | tf_op jit(solution)/shard_map/picked/pallas_call | solution.py:308
  27.6 4.1 %all-to-all-start = ((f16[8,64,512]{2,1,0:T(8,128)(2,1)}), f16[8,64,512]{2,1,0:T(8,128)(2,1)}, u32[]{:S(2)}, u32[]{:S(2)}) async-start(f16[8,64,512]{2,1,0:T(8,128)(2,1)} %broadcast_in_dim.4), calls=%async_computation | async-start | bytes 1048576 | tf_op jit(solution)/shard_map/all_to_all | solution.py:508
  33.8 9.1 %collective-permute-done.9.refs_2_ = bf16[736,256]{1,0:T(8,128)(2,1)} collective-permute-done((bf16[736,256]{1,0:T(8,128)(2,1)S(1)}, bf16[736,256]{1,0:T(8,128)(2,1)}, u32[]{:S(2)}, u32[]{:S(2)}) %collective-permute-start.9) | collective-permute-done | bytes 376864 | tf_op jit(solution)/shard_map/ppermute | solution.py:417
  46.6 3.2 %all-to-all-done = f16[8,64,512]{2,1,0:T(8,128)(2,1)} async-done(((f16[8,64,512]{2,1,0:T(8,128)(2,1)}), f16[8,64,512]{2,1,0:T(8,128)(2,1)}, u32[]{:S(2)}, u32[]{:S(2)}) %all-to-all-start) | async-done | bytes 524320 | tf_op jit(solution)/shard_map/all_to_all | solution.py:508
  52.0 2.0 %project.1 = (f32[64,1024]{1,0:T(8,128)S(1)}, bf16[4,512,128]{2,1,0:T(8,128)(2,1)S(1)}) custom-call(f32[8,64,512]{2,1,0:T(8,128)S(1)} %convert_element_type.22.got_ref, bf16[736,256]{1,0:T(8,128)(2,1)} %copy-done, bf16[736,256]{1,0:T(8,128)(2,1)} %copy-done.5, bf16[736,256]{1,0:T(8,128)(2,1)} %collective-permute-done.9.refs_2_, ...), custom_call_target="tpu_custom_call" | custom-call | tf_op jit(solution)/shard_map/project/pallas_call | solution.py:308
  55.3 1.6 %collective-permute-start.17 = (bf16[4,512,128]{2,1,0:T(8,128)(2,1)S(1)}, bf16[4,512,128]{2,1,0:T(8,128)(2,1)S(1)}, u32[]{:S(2)}, u32[]{:S(2)}) collective-permute-start(bf16[4,512,128]{2,1,0:T(8,128)(2,1)S(1)} %get-tuple-element.130.refs_3_), channel_id=1, source_target_pairs={{0,32},{8,40},{16,48},{24,56},{32,64},{40,72},{48,80},{56,88},{64,... | collective-permute-start | bytes 1572872 | tf_op jit(solution)/shard_map/ppermute | solution.py:423
  58.8 3.0 %collective-permute-done.12 = f16[64,1024]{1,0:T(8,128)(2,1)S(1)} collective-permute-done((f16[64,1024]{1,0:T(8,128)(2,1)S(1)}, f16[64,1024]{1,0:T(8,128)(2,1)S(1)}, u32[]{:S(2)}, u32[]{:S(2)}) %collective-permute-start.12) | collective-permute-done | bytes 131104 | tf_op jit(solution)/shard_map/ppermute | solution.py:417
  61.8 1.5 %collective-permute-done.13.refs_6_ = bf16[256,1024]{1,0:T(8,128)(2,1)} collective-permute-done((bf16[256,1024]{1,0:T(8,128)(2,1)}, bf16[256,1024]{1,0:T(8,128)(2,1)}, u32[]{:S(2)}, u32[]{:S(2)}) %collective-permute-start.13) | collective-permute-done | bytes 524320 | tf_op jit(solution)/shard_map/ppermute | solution.py:417
  64.1 2.7 %collective-permute-start.14 = (f16[64,1024]{1,0:T(8,128)(2,1)S(1)}, f16[64,1024]{1,0:T(8,128)(2,1)S(1)}, u32[]{:S(2)}, u32[]{:S(2)}) collective-permute-start(f16[64,1024]{1,0:T(8,128)(2,1)S(1)} %add.21), channel_id=1, source_target_pairs={{0,4},{1,5},{2,6},{3,7},{4,0},{5,1},{6,2},{7,3},{8,12},{9,13},{10,... | collective-permute-start | bytes 393224 | tf_op jit(solution)/shard_map/ppermute | solution.py:417
  66.8 3.9 %collective-permute-done.14 = f16[64,1024]{1,0:T(8,128)(2,1)S(1)} collective-permute-done((f16[64,1024]{1,0:T(8,128)(2,1)S(1)}, f16[64,1024]{1,0:T(8,128)(2,1)S(1)}, u32[]{:S(2)}, u32[]{:S(2)}) %collective-permute-start.14) | collective-permute-done | bytes 131104 | tf_op jit(solution)/shard_map/ppermute | solution.py:417
  70.8 2.9 %collective-permute-start.16 = (f16[64,1024]{1,0:T(8,128)(2,1)S(1)}, f16[64,1024]{1,0:T(8,128)(2,1)S(1)}, u32[]{:S(2)}, u32[]{:S(2)}) collective-permute-start(f16[64,1024]{1,0:T(8,128)(2,1)S(1)} %add.22), channel_id=1, source_target_pairs={{0,1},{1,0},{2,3},{3,2},{4,5},{5,4},{6,7},{7,6},{8,9},{9,8},{10,11... | collective-permute-start | bytes 393224 | tf_op jit(solution)/shard_map/ppermute | solution.py:417
  74.9 1.9 %collective-permute-done.16 = f16[64,1024]{1,0:T(8,128)(2,1)S(1)} collective-permute-done((f16[64,1024]{1,0:T(8,128)(2,1)S(1)}, f16[64,1024]{1,0:T(8,128)(2,1)S(1)}, u32[]{:S(2)}, u32[]{:S(2)}) %collective-permute-start.16) | collective-permute-done | bytes 131104 | tf_op jit(solution)/shard_map/ppermute | solution.py:417
  76.9 2.1 %inner.1 = f32[64,1024]{1,0:T(8,128)S(1)} custom-call(s32[1]{0:T(128)} %bitcast.me_ref.refs_0_, f32[64,1024]{1,0:T(8,128)S(1)} %add_multiply_fusion.total_ref, bf16[736,256]{1,0:T(8,128)(2,1)} %copy-done, bf16[736,256]{1,0:T(8,128)(2,1)} %copy-done.5, bf16[736,256]{1,0:T(8,128)(2,1)} %collective-permute-done.9.refs_2_, ...), custom_call_target="tpu_custom_call" | custom-call | tf_op jit(solution)/shard_map/inner/pallas_call | solution.py:308
  79.7 8.5 %all-to-all-start.1 = ((f16[8,8,1024]{2,1,0:T(8,128)(2,1)}), f16[8,8,1024]{2,1,0:T(8,128)(2,1)S(1)}, u32[]{:S(2)}, u32[]{:S(2)}) async-start(f16[8,8,1024]{2,1,0:T(8,128)(2,1)} %fusion), calls=%async_computation.1 | async-start | bytes 262144 | tf_op jit(solution)/shard_map/all_to_all | solution.py:556
  90.9 5.2 %all-to-all-done.1 = f16[8,8,1024]{2,1,0:T(8,128)(2,1)S(1)} async-done(((f16[8,8,1024]{2,1,0:T(8,128)(2,1)}), f16[8,8,1024]{2,1,0:T(8,128)(2,1)S(1)}, u32[]{:S(2)}, u32[]{:S(2)}) %all-to-all-start.1) | async-done | bytes 131104 | tf_op jit(solution)/shard_map/all_to_all | solution.py:556
  97.0 5.0 %all-to-all-start.2 = ((f32[8,1,128]{2,1,0:T(1,128)}), f32[8,1,128]{2,1,0:T(1,128)S(1)}, u32[]{:S(2)}, u32[]{:S(2)}) async-start(f32[8,1,128]{2,1,0:T(1,128)} %hidden.1), calls=%async_computation.2 | async-start | bytes 8192 | tf_op jit(solution)/shard_map/all_to_all | solution.py:568
  101.9 2.4 %attend_2_1.1 = f32[512,512]{1,0:T(8,128)} custom-call(s32[1]{0:T(128)} %bitcast.me_ref.refs_0_, s32[7]{0:T(128)} %refs_1_.9, bf16[512,512]{1,0:T(8,128)(2,1)} %refs_2_.9, bf16[4,512,128]{2,1,0:T(8,128)(2,1)} %collective-permute-done.20.refs_3_, f32[512,512]{1,0:T(8,128)S(1)} %get-tuple-element.160.refs_4_, f32[512,512]{1,0:T(8,128)S(1)} %get-tuple-element.161.refs_5_, ...), custom_call_target="tpu_custom_call" | custom-call | flops 1073741824 | bytes 1048576 | tf_op jit(solution)/shard_map/attend_2_1/pallas_call | solution.py:280
  104.3 4.1 %all-to-all-done.2 = f32[8,1,128]{2,1,0:T(1,128)S(1)} async-done(((f32[8,1,128]{2,1,0:T(1,128)}), f32[8,1,128]{2,1,0:T(1,128)S(1)}, u32[]{:S(2)}, u32[]{:S(2)}) %all-to-all-start.2) | async-done | bytes 4128 | tf_op jit(solution)/shard_map/all_to_all | solution.py:568
  108.4 15.1 %all_to_all.20.got_ref = f32[32,1,128]{2,1,0:T(1,128)S(1)} all-to-all(f32[32,1,128]{2,1,0:T(1,128)S(1)} %broadcast_in_dim.5), channel_id=1, replica_groups=mesh['ctx'=32,'head'=8] {'ctx'}, dimensions={0} | all-to-all | bytes 32768 | tf_op jit(solution)/shard_map/all_to_all | solution.py:571
  (71 shorter events, 26.8 us)
Async XLA Ops:
  2.4 4.3 %collective-permute-start = (bf16[128,512]{1,0:T(8,128)(2,1)S(1)}, bf16[128,512]{1,0:T(8,128)(2,1)S(1)}, u32[]{:S(2)}, u32[]{:S(2)}) collective-permute-start(bf16[128,512]{1,0:T(8,128)(2,1)S(1)} %get-tuple-element.87), channel_id=1, source_target_pairs={{0,8},{8,0},{16,24},{24,16},{32,40},{40,32},{48,56},{56,48},{64,72... | collective-permute-start | bytes 393224 | tf_op jit(solution)/shard_map/ppermute | solution.py:417
  6.7 3.2 %collective-permute-start.1 = (bf16[64,512]{1,0:T(8,128)(2,1)S(1)}, bf16[64,512]{1,0:T(8,128)(2,1)S(1)}, u32[]{:S(2)}, u32[]{:S(2)}) collective-permute-start(bf16[64,512]{1,0:T(8,128)(2,1)S(1)} %slice_add_fusion), channel_id=1, source_target_pairs={{0,16},{8,24},{16,0},{24,8},{32,48},{40,56},{48,32},{56,40},{64,80... | collective-permute-start | bytes 196616 | tf_op jit(solution)/shard_map/ppermute | solution.py:417
  6.9 3.1 %collective-permute-start.2 = (bf16[2,512,128]{2,1,0:T(8,128)(2,1)S(1)}, bf16[2,512,128]{2,1,0:T(8,128)(2,1)S(1)}, u32[]{:S(2)}, u32[]{:S(2)}) collective-permute-start(bf16[2,512,128]{2,1,0:T(8,128)(2,1)S(1)} %copy-done.7), channel_id=1, source_target_pairs={{0,8},{8,0},{16,24},{24,16},{32,40},{40,32},{48,56},{56,48},{64,72... | collective-permute-start | bytes 786440 | tf_op jit(solution)/shard_map/ppermute | solution.py:417
  7.3 13.3 %collective-permute-start.6 = (bf16[2,512,128]{2,1,0:T(8,128)(2,1)S(1)}, bf16[2,512,128]{2,1,0:T(8,128)(2,1)S(1)}, u32[]{:S(2)}, u32[]{:S(2)}) collective-permute-start(bf16[2,512,128]{2,1,0:T(8,128)(2,1)S(1)} %copy-done.7), channel_id=1, source_target_pairs={{0,32},{8,40},{16,48},{24,56},{32,64},{40,72},{48,80},{56,88},{64,... | collective-permute-start | bytes 786440 | tf_op jit(solution)/shard_map/ppermute | solution.py:423
  10.0 10.7 %collective-permute-start.3 = (bf16[2,512,128]{2,1,0:T(8,128)(2,1)S(1)}, bf16[2,512,128]{2,1,0:T(8,128)(2,1)S(1)}, u32[]{:S(2)}, u32[]{:S(2)}) collective-permute-start(bf16[2,512,128]{2,1,0:T(8,128)(2,1)S(1)} %copy-done.7), channel_id=1, source_target_pairs={{0,16},{8,24},{16,0},{24,8},{32,48},{40,56},{48,32},{56,40},{64,80... | collective-permute-start | bytes 786440 | tf_op jit(solution)/shard_map/ppermute | solution.py:417
  10.6 10.0 %collective-permute-start.4 = (bf16[64,512]{1,0:T(8,128)(2,1)S(1)}, bf16[64,512]{1,0:T(8,128)(2,1)S(1)}, u32[]{:S(2)}, u32[]{:S(2)}) collective-permute-start(bf16[64,512]{1,0:T(8,128)(2,1)S(1)} %fusion.1.q_ref), channel_id=1, source_target_pairs={{0,224},{8,232},{16,240},{24,248},{32,0},{40,8},{48,16},{56,24},{6... | collective-permute-start | bytes 196616 | tf_op jit(solution)/shard_map/ppermute | solution.py:423
  15.2 5.4 %collective-permute-start.5 = (bf16[64,512]{1,0:T(8,128)(2,1)S(1)}, bf16[64,512]{1,0:T(8,128)(2,1)S(1)}, u32[]{:S(2)}, u32[]{:S(2)}) collective-permute-start(bf16[64,512]{1,0:T(8,128)(2,1)S(1)} %fusion.1.q_ref), channel_id=1, source_target_pairs={{0,192},{8,200},{16,208},{24,216},{32,224},{40,232},{48,240},{56,2... | collective-permute-start | bytes 196616 | tf_op jit(solution)/shard_map/ppermute | solution.py:423
  20.7 3.0 %collective-permute-start.7 = (bf16[2,512,128]{2,1,0:T(8,128)(2,1)S(1)}, bf16[2,512,128]{2,1,0:T(8,128)(2,1)S(1)}, u32[]{:S(2)}, u32[]{:S(2)}) collective-permute-start(bf16[2,512,128]{2,1,0:T(8,128)(2,1)S(1)} %collective-permute-done.3.refs_2_), channel_id=1, source_target_pairs={{0,8},{8,0},{16,24},{24,16},{32,40},{40,32},{48,56},{56,48},{64,72... | collective-permute-start | bytes 786440 | tf_op jit(solution)/shard_map/ppermute | solution.py:417
  27.6 22.2 %all-to-all-start = ((f16[8,64,512]{2,1,0:T(8,128)(2,1)}), f16[8,64,512]{2,1,0:T(8,128)(2,1)}, u32[]{:S(2)}, u32[]{:S(2)}) async-start(f16[8,64,512]{2,1,0:T(8,128)(2,1)} %broadcast_in_dim.4), calls=%async_computation | async-start | bytes 1048576 | tf_op jit(solution)/shard_map/all_to_all | solution.py:508
  31.7 2.1 %collective-permute-start.8 = (bf16[736,256]{1,0:T(8,128)(2,1)S(1)}, bf16[736,256]{1,0:T(8,128)(2,1)S(1)}, u32[]{:S(2)}, u32[]{:S(2)}) collective-permute-start(bf16[736,256]{1,0:T(8,128)(2,1)S(1)} %get-tuple-element.123.refs_0_), channel_id=1, source_target_pairs={{0,8},{8,0},{16,24},{24,16},{32,40},{40,32},{48,56},{56,48},{64,72... | collective-permute-start | bytes 1130504 | tf_op jit(solution)/shard_map/ppermute | solution.py:417
  32.5 10.4 %collective-permute-start.9 = (bf16[736,256]{1,0:T(8,128)(2,1)S(1)}, bf16[736,256]{1,0:T(8,128)(2,1)}, u32[]{:S(2)}, u32[]{:S(2)}) collective-permute-start(bf16[736,256]{1,0:T(8,128)(2,1)S(1)} %get-tuple-element.123.refs_0_), channel_id=1, source_target_pairs={{0,16},{8,24},{16,0},{24,8},{32,48},{40,56},{48,32},{56,40},{64,80... | collective-permute-start | bytes 1130504 | tf_op jit(solution)/shard_map/ppermute | solution.py:417
  42.9 9.1 %collective-permute-start.10 = (bf16[736,256]{1,0:T(8,128)(2,1)}, bf16[736,256]{1,0:T(8,128)(2,1)S(1)}, u32[]{:S(2)}, u32[]{:S(2)}) collective-permute-start(bf16[736,256]{1,0:T(8,128)(2,1)} %collective-permute-done.9.refs_2_), channel_id=1, source_target_pairs={{0,8},{8,0},{16,24},{24,16},{32,40},{40,32},{48,56},{56,48},{64,72... | collective-permute-start | bytes 1130504 | tf_op jit(solution)/shard_map/ppermute | solution.py:417
  43.8 8.3 %collective-permute-start.11 = (bf16[2,512,128]{2,1,0:T(8,128)(2,1)}, bf16[2,512,128]{2,1,0:T(8,128)(2,1)}, u32[]{:S(2)}, u32[]{:S(2)}) collective-permute-start(bf16[2,512,128]{2,1,0:T(8,128)(2,1)} %copy-done.6), channel_id=1, source_target_pairs={{0,16},{8,24},{16,0},{24,8},{32,48},{40,56},{48,32},{56,40},{64,80... | collective-permute-start | bytes 786440 | tf_op jit(solution)/shard_map/ppermute | solution.py:417
  44.0 19.3 %collective-permute-start.13 = (bf16[256,1024]{1,0:T(8,128)(2,1)}, bf16[256,1024]{1,0:T(8,128)(2,1)}, u32[]{:S(2)}, u32[]{:S(2)}) collective-permute-start(bf16[256,1024]{1,0:T(8,128)(2,1)} %refs_4_), channel_id=1, source_target_pairs={{0,16},{8,24},{16,0},{24,8},{32,48},{40,56},{48,32},{56,40},{64,80... | collective-permute-start | bytes 1572872 | tf_op jit(solution)/shard_map/ppermute | solution.py:417
  54.0 16.7 %collective-permute-start.15 = (bf16[4,512,128]{2,1,0:T(8,128)(2,1)S(1)}, bf16[4,512,128]{2,1,0:T(8,128)(2,1)S(1)}, u32[]{:S(2)}, u32[]{:S(2)}) collective-permute-start(bf16[4,512,128]{2,1,0:T(8,128)(2,1)S(1)} %get-tuple-element.130.refs_3_), channel_id=1, source_target_pairs={{0,8},{8,0},{16,24},{24,16},{32,40},{40,32},{48,56},{56,48},{64,72... | collective-permute-start | bytes 1572872 | tf_op jit(solution)/shard_map/ppermute | solution.py:417
  55.3 19.6 %collective-permute-start.17 = (bf16[4,512,128]{2,1,0:T(8,128)(2,1)S(1)}, bf16[4,512,128]{2,1,0:T(8,128)(2,1)S(1)}, u32[]{:S(2)}, u32[]{:S(2)}) collective-permute-start(bf16[4,512,128]{2,1,0:T(8,128)(2,1)S(1)} %get-tuple-element.130.refs_3_), channel_id=1, source_target_pairs={{0,32},{8,40},{16,48},{24,56},{32,64},{40,72},{48,80},{56,88},{64,... | collective-permute-start | bytes 1572872 | tf_op jit(solution)/shard_map/ppermute | solution.py:423
  56.9 4.8 %collective-permute-start.12 = (f16[64,1024]{1,0:T(8,128)(2,1)S(1)}, f16[64,1024]{1,0:T(8,128)(2,1)S(1)}, u32[]{:S(2)}, u32[]{:S(2)}) collective-permute-start(f16[64,1024]{1,0:T(8,128)(2,1)S(1)} %multiply_convert_fusion.1), channel_id=1, source_target_pairs={{0,2},{1,3},{2,0},{3,1},{4,6},{5,7},{6,4},{7,5},{8,10},{9,11},{10,... | collective-permute-start | bytes 393224 | tf_op jit(solution)/shard_map/ppermute | solution.py:417
  58.1 18.7 %collective-permute-start.18 = (bf16[256,1024]{1,0:T(8,128)(2,1)S(1)}, bf16[256,1024]{1,0:T(8,128)(2,1)S(1)}, u32[]{:S(2)}, u32[]{:S(2)}) collective-permute-start(bf16[256,1024]{1,0:T(8,128)(2,1)S(1)} %copy-done.1), channel_id=1, source_target_pairs={{0,8},{8,0},{16,24},{24,16},{32,40},{40,32},{48,56},{56,48},{64,72... | collective-permute-start | bytes 1572872 | tf_op jit(solution)/shard_map/ppermute | solution.py:417
  63.3 13.6 %collective-permute-start.19 = (bf16[256,1024]{1,0:T(8,128)(2,1)}, bf16[256,1024]{1,0:T(8,128)(2,1)S(1)}, u32[]{:S(2)}, u32[]{:S(2)}) collective-permute-start(bf16[256,1024]{1,0:T(8,128)(2,1)} %collective-permute-done.13.refs_6_), channel_id=1, source_target_pairs={{0,8},{8,0},{16,24},{24,16},{32,40},{40,32},{48,56},{56,48},{64,72... | collective-permute-start | bytes 1572872 | tf_op jit(solution)/shard_map/ppermute | solution.py:417
  64.1 6.6 %collective-permute-start.14 = (f16[64,1024]{1,0:T(8,128)(2,1)S(1)}, f16[64,1024]{1,0:T(8,128)(2,1)S(1)}, u32[]{:S(2)}, u32[]{:S(2)}) collective-permute-start(f16[64,1024]{1,0:T(8,128)(2,1)S(1)} %add.21), channel_id=1, source_target_pairs={{0,4},{1,5},{2,6},{3,7},{4,0},{5,1},{6,2},{7,3},{8,12},{9,13},{10,... | collective-permute-start | bytes 393224 | tf_op jit(solution)/shard_map/ppermute | solution.py:417
  70.8 6.1 %collective-permute-start.16 = (f16[64,1024]{1,0:T(8,128)(2,1)S(1)}, f16[64,1024]{1,0:T(8,128)(2,1)S(1)}, u32[]{:S(2)}, u32[]{:S(2)}) collective-permute-start(f16[64,1024]{1,0:T(8,128)(2,1)S(1)} %add.22), channel_id=1, source_target_pairs={{0,1},{1,0},{2,3},{3,2},{4,5},{5,4},{6,7},{7,6},{8,9},{9,8},{10,11... | collective-permute-start | bytes 393224 | tf_op jit(solution)/shard_map/ppermute | solution.py:417
  79.7 16.3 %all-to-all-start.1 = ((f16[8,8,1024]{2,1,0:T(8,128)(2,1)}), f16[8,8,1024]{2,1,0:T(8,128)(2,1)S(1)}, u32[]{:S(2)}, u32[]{:S(2)}) async-start(f16[8,8,1024]{2,1,0:T(8,128)(2,1)} %fusion), calls=%async_computation.1 | async-start | bytes 262144 | tf_op jit(solution)/shard_map/all_to_all | solution.py:556
  88.3 8.7 %collective-permute-start.20 = (bf16[4,512,128]{2,1,0:T(8,128)(2,1)}, bf16[4,512,128]{2,1,0:T(8,128)(2,1)}, u32[]{:S(2)}, u32[]{:S(2)}) collective-permute-start(bf16[4,512,128]{2,1,0:T(8,128)(2,1)} %copy-done.9), channel_id=1, source_target_pairs={{0,8},{8,0},{16,24},{24,16},{32,40},{40,32},{48,56},{56,48},{64,72... | collective-permute-start | bytes 1572872 | tf_op jit(solution)/shard_map/ppermute | solution.py:417
  97.0 11.4 %all-to-all-start.2 = ((f32[8,1,128]{2,1,0:T(1,128)}), f32[8,1,128]{2,1,0:T(1,128)S(1)}, u32[]{:S(2)}, u32[]{:S(2)}) async-start(f32[8,1,128]{2,1,0:T(1,128)} %hidden.1), calls=%async_computation.2 | async-start | bytes 8192 | tf_op jit(solution)/shard_map/all_to_all | solution.py:568
  (10 other events, 120.4 us)

commit v8 on v7

--- a/solution.py
+++ b/solution.py
@@ -472,7 +472,7 @@
     core0y = swapped(across0, "ctx", 1)
     wanted, wanted1, wanted2, *state = tie(wanted, wanted1, wanted2, *state)
 
-    weight, wanted = tie(weight, wanted)
+    weight, *state = tie(weight, *state)
     firsts = [weight, swapped(weight, "ctx", 1), swapped(weight, "ctx", 2)]
 
     parts, moved = small_call(
@@ -499,9 +499,9 @@
         ],
         name="picked",
     )
-    parts, kv1, *state = tie(parts, kv1, *state)
+    parts, kv1, *firsts = tie(parts, kv1, *firsts)
     across1 = swapped(kv1, "ctx", 2)
-    *firsts, moved, weight = tie(*firsts, moved, score_weight)
+    weight, parts = tie(score_weight, parts)
     firsts = [*pinned(firsts), swapped(firsts[2], "ctx", 1)]
     weights = [weight, None, swapped(weight, "ctx", 2)]
     parts = jnp.broadcast_to(parts.astype(jnp.float16)[None], (Z, GROUP, half))

time: 125 us -> 125 us (level)
  starting transfers between devices: 46.7 us -> 42.8 us
  waiting for transfers between devices: 37.4 us -> 40 us
    all_to_all x1, waiting for transfers between devices: 3.16 us -> 14 us  [per_device(): lax.all_to_all(parts, 'ctx', 0, 0, axis_index_groups=columns).astype(F32)]
    ppermute x17, waiting for transfers between devices: 25 us -> 17.5 us  [swapped(): return lax.ppermute(value, axis, [(s, s ^ bit) for s in range(count)])]
    all_to_all x1, starting transfers between devices: 8.55 us -> 3.8 us  [per_device(): inner = lax.all_to_all(inner, 'ctx', 0, 0, axis_index_groups=columns)]
    all_to_all x1, starting transfers between devices: 4.97 us -> 6.36 us  [per_device(): gap = lax.all_to_all(gap, 'head', 0, 0)]
    ppermute x4, starting transfers between devices: 8.76 us -> 7.45 us  [raised(): lax.ppermute(value, 'ctx', [(s, (s + steps) % count) for s in range(count)])]
  transfers between devices with their start and end apart: 24 -> 24, of which waited for: 13 -> 10; matrix products, arithmetic and copies ran while one was open for 1% -> 1% of each run, Pallas kernels for 11% -> 13%
where the time goes in v8:
time: 125 us; the launch traced here: 124 us
  starting transfers between devices  42.8 us (34%)
  waiting for transfers between devices  40 us (32%)
  Pallas kernels  21.4 us (17%)
  blocking collectives  15.1 us (12%)
  other arithmetic  2.08 us (2%)
  local copies, waits for them, and re-layouts  1.84 us (1%)
    ppermute x17, starting transfers between devices, swapped(): return lax.ppermute(value, axis, [(s, s ^ bit) for s in range(count)])  21.1 us
    ppermute x17, waiting for transfers between devices, swapped(): return lax.ppermute(value, axis, [(s, s ^ bit) for s in range(count)])  17.5 us
    all_to_all x1, blocking collectives, per_device(): lax.all_to_all(jnp.broadcast_to(gap[None], (count, 1, HD)), 'ctx', 0, 0)  15.1 us
    all_to_all x1, waiting for transfers between devices, per_device(): lax.all_to_all(parts, 'ctx', 0, 0, axis_index_groups=columns).astype(F32)  14 us
    pallas_call x6, Pallas kernels, small_call(): pl.pallas_call(kernel, out_shape=shape, in_specs=specs or [VMEM] * len(op...  11 us
    pallas_call x5, Pallas kernels, attend(): pl.pallas_call(functools.partial(attend_kernel, slots, first, last), out_...  10.4 us
    ppermute x4, starting transfers between devices, raised(): lax.ppermute(value, 'ctx', [(s, (s + steps) % count) for s in range(count)])  7.45 us
    all_to_all x1, starting transfers between devices, per_device(): gap = lax.all_to_all(gap, 'head', 0, 0)  6.36 us
  transfers between devices with their start and end apart: 24, of which 10 were waited for; matrix products, arithmetic and copies ran while one was open for 1% of the time, Pallas kernels for 13%

profile of v8, /device:TPU:1, one launch (start us, length us, event | category | flops | bytes accessed | tf_op | source)
XLA Modules:
  0.0 124.3 jit_solution(11770022611869827963)
XLA Ops:
  0.6 1.8 %pick.1 = (bf16[64,512]{1,0:T(8,128)(2,1)S(1)}, bf16[64,512]{1,0:T(8,128)(2,1)S(1)}, bf16[128,512]{1,0:T(8,128)(2,1)S(1)}, bf16[736,256]{1,0:T(8,128)(2,1)S(1)}) custom-call(s32[1]{0:T(128)} %bitcast.me_ref.refs_0_, s32[7,32]{1,0:T(8,128)} %steps_hbm.3, bf16[512,512]{1,0:T(8,128)(2,1)} %refs_2_.9, bf16[512,256]{1,0:T(8,128)(2,1)} %weight_hbm.1, ...), custom_call_target="tpu_custom_call" | custom-call | tf_op jit(solution)/shard_map/pick/pallas_call | solution.py:308
  2.4 3.3 %collective-permute-start = (bf16[128,512]{1,0:T(8,128)(2,1)S(1)}, bf16[128,512]{1,0:T(8,128)(2,1)S(1)}, u32[]{:S(2)}, u32[]{:S(2)}) collective-permute-start(bf16[128,512]{1,0:T(8,128)(2,1)S(1)} %get-tuple-element.85), channel_id=1, source_target_pairs={{0,8},{8,0},{16,24},{24,16},{32,40},{40,32},{48,56},{56,48},{64,72... | collective-permute-start | bytes 393224 | tf_op jit(solution)/shard_map/ppermute | solution.py:417
  7.3 1.4 %collective-permute-start.6 = (bf16[2,512,128]{2,1,0:T(8,128)(2,1)S(1)}, bf16[2,512,128]{2,1,0:T(8,128)(2,1)S(1)}, u32[]{:S(2)}, u32[]{:S(2)}) collective-permute-start(bf16[2,512,128]{2,1,0:T(8,128)(2,1)S(1)} %copy-done.8), channel_id=1, source_target_pairs={{0,32},{8,40},{16,48},{24,56},{32,64},{40,72},{48,80},{56,88},{64,... | collective-permute-start | bytes 786440 | tf_op jit(solution)/shard_map/ppermute | solution.py:423
  10.6 4.6 %collective-permute-start.4 = (bf16[64,512]{1,0:T(8,128)(2,1)S(1)}, bf16[64,512]{1,0:T(8,128)(2,1)S(1)}, u32[]{:S(2)}, u32[]{:S(2)}) collective-permute-start(bf16[64,512]{1,0:T(8,128)(2,1)S(1)} %fusion.1.q_ref), channel_id=1, source_target_pairs={{0,224},{8,232},{16,240},{24,248},{32,0},{40,8},{48,16},{56,24},{6... | collective-permute-start | bytes 196616 | tf_op jit(solution)/shard_map/ppermute | solution.py:423
  16.4 4.2 %attend_0_0.1 = (f32[512,512]{1,0:T(8,128)S(1)}, f32[512,512]{1,0:T(8,128)S(1)}, f32[512,512]{1,0:T(8,128)S(1)}) custom-call(s32[1]{0:T(128)} %bitcast.me_ref.refs_0_, s32[7]{0:T(128)} %refs_1_.9, bf16[512,512]{1,0:T(8,128)(2,1)} %refs_2_.9, bf16[2,512,128]{2,1,0:T(8,128)(2,1)} %refs_0_.1, bf16[2,512,128]{2,1,0:T(8,128)(2,1)S(1)} %collective-permute-done.2.refs_4_.refs_1_), custom_call_target="tpu_custom_call" | custom-call | flops 1073741824 | bytes 1048576 | tf_op jit(solution)/shard_map/attend_0_0/pallas_call | solution.py:280
  20.7 1.9 %collective-permute-start.8 = (bf16[736,256]{1,0:T(8,128)(2,1)S(1)}, bf16[736,256]{1,0:T(8,128)(2,1)S(1)}, u32[]{:S(2)}, u32[]{:S(2)}) collective-permute-start(bf16[736,256]{1,0:T(8,128)(2,1)S(1)} %get-tuple-element.121.refs_0_), channel_id=1, source_target_pairs={{0,8},{8,0},{16,24},{24,16},{32,40},{40,32},{48,56},{56,48},{64,72... | collective-permute-start | bytes 1130504 | tf_op jit(solution)/shard_map/ppermute | solution.py:417
  24.3 3.0 %picked.1 = (f32[64,512]{1,0:T(8,128)S(1)}, bf16[4,512,128]{2,1,0:T(8,128)(2,1)}) custom-call(s32[1]{0:T(128)} %bitcast.me_ref.refs_0_, s32[7]{0:T(128)} %refs_1_.9, s32[7,32]{1,0:T(8,128)} %steps_hbm.3, bf16[64,512]{1,0:T(8,128)(2,1)S(1)} %fusion.1.q_ref, bf16[64,512]{1,0:T(8,128)(2,1)S(1)} %collective-permute-done.4.q1_ref, ...), custom_call_target="tpu_custom_call" | custom-call | tf_op jit(solution)/shard_map/picked/pallas_call | solution.py:308
  27.3 5.6 %collective-permute-done.9.refs_2_ = bf16[736,256]{1,0:T(8,128)(2,1)S(1)} collective-permute-done((bf16[736,256]{1,0:T(8,128)(2,1)S(1)}, bf16[736,256]{1,0:T(8,128)(2,1)S(1)}, u32[]{:S(2)}, u32[]{:S(2)}) %collective-permute-start.9) | collective-permute-done | bytes 376864 | tf_op jit(solution)/shard_map/ppermute | solution.py:417
  34.5 4.1 %all-to-all-start = ((f16[8,64,512]{2,1,0:T(8,128)(2,1)}), f16[8,64,512]{2,1,0:T(8,128)(2,1)}, u32[]{:S(2)}, u32[]{:S(2)}) async-start(f16[8,64,512]{2,1,0:T(8,128)(2,1)} %broadcast_in_dim.4), calls=%async_computation | async-start | bytes 1048576 | tf_op jit(solution)/shard_map/all_to_all | solution.py:508
  42.6 14.0 %all-to-all-done = f16[8,64,512]{2,1,0:T(8,128)(2,1)} async-done(((f16[8,64,512]{2,1,0:T(8,128)(2,1)}), f16[8,64,512]{2,1,0:T(8,128)(2,1)}, u32[]{:S(2)}, u32[]{:S(2)}) %all-to-all-start) | async-done | bytes 524320 | tf_op jit(solution)/shard_map/all_to_all | solution.py:508
  57.7 2.0 %project.1 = (f32[64,1024]{1,0:T(8,128)S(1)}, bf16[4,512,128]{2,1,0:T(8,128)(2,1)S(1)}) custom-call(f32[8,64,512]{2,1,0:T(8,128)S(1)} %convert_element_type.22.got_ref, bf16[736,256]{1,0:T(8,128)(2,1)} %copy-done, bf16[736,256]{1,0:T(8,128)(2,1)} %copy-done.5, bf16[736,256]{1,0:T(8,128)(2,1)} %copy-done.6, ...), custom_call_target="tpu_custom_call" | custom-call | tf_op jit(solution)/shard_map/project/pallas_call | solution.py:308
  62.6 2.9 %collective-permute-done.12 = f16[64,1024]{1,0:T(8,128)(2,1)S(1)} collective-permute-done((f16[64,1024]{1,0:T(8,128)(2,1)S(1)}, f16[64,1024]{1,0:T(8,128)(2,1)S(1)}, u32[]{:S(2)}, u32[]{:S(2)}) %collective-permute-start.12) | collective-permute-done | bytes 131104 | tf_op jit(solution)/shard_map/ppermute | solution.py:417
  66.8 2.8 %collective-permute-start.14 = (f16[64,1024]{1,0:T(8,128)(2,1)S(1)}, f16[64,1024]{1,0:T(8,128)(2,1)S(1)}, u32[]{:S(2)}, u32[]{:S(2)}) collective-permute-start(f16[64,1024]{1,0:T(8,128)(2,1)S(1)} %add.21), channel_id=1, source_target_pairs={{0,4},{1,5},{2,6},{3,7},{4,0},{5,1},{6,2},{7,3},{8,12},{9,13},{10,... | collective-permute-start | bytes 393224 | tf_op jit(solution)/shard_map/ppermute | solution.py:417
  69.6 3.8 %collective-permute-done.14 = f16[64,1024]{1,0:T(8,128)(2,1)S(1)} collective-permute-done((f16[64,1024]{1,0:T(8,128)(2,1)S(1)}, f16[64,1024]{1,0:T(8,128)(2,1)S(1)}, u32[]{:S(2)}, u32[]{:S(2)}) %collective-permute-start.14) | collective-permute-done | bytes 131104 | tf_op jit(solution)/shard_map/ppermute | solution.py:417
  73.4 2.9 %collective-permute-start.16 = (f16[64,1024]{1,0:T(8,128)(2,1)S(1)}, f16[64,1024]{1,0:T(8,128)(2,1)S(1)}, u32[]{:S(2)}, u32[]{:S(2)}) collective-permute-start(f16[64,1024]{1,0:T(8,128)(2,1)S(1)} %add.22), channel_id=1, source_target_pairs={{0,1},{1,0},{2,3},{3,2},{4,5},{5,4},{6,7},{7,6},{8,9},{9,8},{10,11... | collective-permute-start | bytes 393224 | tf_op jit(solution)/shard_map/ppermute | solution.py:417
  77.6 1.8 %collective-permute-done.16 = f16[64,1024]{1,0:T(8,128)(2,1)S(1)} collective-permute-done((f16[64,1024]{1,0:T(8,128)(2,1)S(1)}, f16[64,1024]{1,0:T(8,128)(2,1)S(1)}, u32[]{:S(2)}, u32[]{:S(2)}) %collective-permute-start.16) | collective-permute-done | bytes 131104 | tf_op jit(solution)/shard_map/ppermute | solution.py:417
  79.5 2.1 %inner.1 = f32[64,1024]{1,0:T(8,128)S(1)} custom-call(s32[1]{0:T(128)} %bitcast.me_ref.refs_0_, f32[64,1024]{1,0:T(8,128)S(1)} %add_multiply_fusion.total_ref, bf16[736,256]{1,0:T(8,128)(2,1)} %copy-done, bf16[736,256]{1,0:T(8,128)(2,1)} %copy-done.5, bf16[736,256]{1,0:T(8,128)(2,1)} %copy-done.6, bf16[736,256]{1,0:T(8,128)(2,1)S(1)} %collective-permute-done.10.refs_3_, ...), custom_call_target="tpu_custom_call" | custom-call | tf_op jit(solution)/shard_map/inner/pallas_call | solution.py:308
  82.3 3.8 %all-to-all-start.1 = ((f16[8,8,1024]{2,1,0:T(8,128)(2,1)}), f16[8,8,1024]{2,1,0:T(8,128)(2,1)S(1)}, u32[]{:S(2)}, u32[]{:S(2)}) async-start(f16[8,8,1024]{2,1,0:T(8,128)(2,1)} %fusion), calls=%async_computation.1 | async-start | bytes 262144 | tf_op jit(solution)/shard_map/all_to_all | solution.py:556
  86.1 2.1 %collective-permute-start.20 = (bf16[4,512,128]{2,1,0:T(8,128)(2,1)}, bf16[4,512,128]{2,1,0:T(8,128)(2,1)}, u32[]{:S(2)}, u32[]{:S(2)}) collective-permute-start(bf16[4,512,128]{2,1,0:T(8,128)(2,1)} %copy-done.10), channel_id=1, source_target_pairs={{0,8},{8,0},{16,24},{24,16},{32,40},{40,32},{48,56},{56,48},{64,72... | collective-permute-start | bytes 1572872 | tf_op jit(solution)/shard_map/ppermute | solution.py:417
  89.7 4.4 %all-to-all-done.1 = f16[8,8,1024]{2,1,0:T(8,128)(2,1)S(1)} async-done(((f16[8,8,1024]{2,1,0:T(8,128)(2,1)}), f16[8,8,1024]{2,1,0:T(8,128)(2,1)S(1)}, u32[]{:S(2)}, u32[]{:S(2)}) %all-to-all-start.1) | async-done | bytes 131104 | tf_op jit(solution)/shard_map/all_to_all | solution.py:556
  95.1 6.4 %all-to-all-start.2 = ((f32[8,1,128]{2,1,0:T(1,128)}), f32[8,1,128]{2,1,0:T(1,128)S(1)}, u32[]{:S(2)}, u32[]{:S(2)}) async-start(f32[8,1,128]{2,1,0:T(1,128)} %hidden.1), calls=%async_computation.2 | async-start | bytes 8192 | tf_op jit(solution)/shard_map/all_to_all | solution.py:568
  101.4 2.4 %attend_2_1.1 = f32[512,512]{1,0:T(8,128)} custom-call(s32[1]{0:T(128)} %bitcast.me_ref.refs_0_, s32[7]{0:T(128)} %refs_1_.9, bf16[512,512]{1,0:T(8,128)(2,1)} %refs_2_.9, bf16[4,512,128]{2,1,0:T(8,128)(2,1)} %collective-permute-done.20.refs_3_, f32[512,512]{1,0:T(8,128)S(1)} %get-tuple-element.158.refs_4_, f32[512,512]{1,0:T(8,128)S(1)} %get-tuple-element.159.refs_5_, ...), custom_call_target="tpu_custom_call" | custom-call | flops 1073741824 | bytes 1048576 | tf_op jit(solution)/shard_map/attend_2_1/pallas_call | solution.py:280
  103.8 4.1 %all-to-all-done.2 = f32[8,1,128]{2,1,0:T(1,128)S(1)} async-done(((f32[8,1,128]{2,1,0:T(1,128)}), f32[8,1,128]{2,1,0:T(1,128)S(1)}, u32[]{:S(2)}, u32[]{:S(2)}) %all-to-all-start.2) | async-done | bytes 4128 | tf_op jit(solution)/shard_map/all_to_all | solution.py:568
  107.9 15.1 %all_to_all.20.got_ref = f32[32,1,128]{2,1,0:T(1,128)S(1)} all-to-all(f32[32,1,128]{2,1,0:T(1,128)S(1)} %broadcast_in_dim.5), channel_id=1, replica_groups=mesh['ctx'=32,'head'=8] {'ctx'}, dimensions={0} | all-to-all | bytes 32768 | tf_op jit(solution)/shard_map/all_to_all | solution.py:571
  (73 shorter events, 23.0 us)
Async XLA Ops:
  2.4 4.3 %collective-permute-start = (bf16[128,512]{1,0:T(8,128)(2,1)S(1)}, bf16[128,512]{1,0:T(8,128)(2,1)S(1)}, u32[]{:S(2)}, u32[]{:S(2)}) collective-permute-start(bf16[128,512]{1,0:T(8,128)(2,1)S(1)} %get-tuple-element.85), channel_id=1, source_target_pairs={{0,8},{8,0},{16,24},{24,16},{32,40},{40,32},{48,56},{56,48},{64,72... | collective-permute-start | bytes 393224 | tf_op jit(solution)/shard_map/ppermute | solution.py:417
  6.7 3.2 %collective-permute-start.1 = (bf16[64,512]{1,0:T(8,128)(2,1)S(1)}, bf16[64,512]{1,0:T(8,128)(2,1)S(1)}, u32[]{:S(2)}, u32[]{:S(2)}) collective-permute-start(bf16[64,512]{1,0:T(8,128)(2,1)S(1)} %slice_add_fusion), channel_id=1, source_target_pairs={{0,16},{8,24},{16,0},{24,8},{32,48},{40,56},{48,32},{56,40},{64,80... | collective-permute-start | bytes 196616 | tf_op jit(solution)/shard_map/ppermute | solution.py:417
  6.9 3.1 %collective-permute-start.2 = (bf16[2,512,128]{2,1,0:T(8,128)(2,1)S(1)}, bf16[2,512,128]{2,1,0:T(8,128)(2,1)S(1)}, u32[]{:S(2)}, u32[]{:S(2)}) collective-permute-start(bf16[2,512,128]{2,1,0:T(8,128)(2,1)S(1)} %copy-done.8), channel_id=1, source_target_pairs={{0,8},{8,0},{16,24},{24,16},{32,40},{40,32},{48,56},{56,48},{64,72... | collective-permute-start | bytes 786440 | tf_op jit(solution)/shard_map/ppermute | solution.py:417
  7.3 13.3 %collective-permute-start.6 = (bf16[2,512,128]{2,1,0:T(8,128)(2,1)S(1)}, bf16[2,512,128]{2,1,0:T(8,128)(2,1)S(1)}, u32[]{:S(2)}, u32[]{:S(2)}) collective-permute-start(bf16[2,512,128]{2,1,0:T(8,128)(2,1)S(1)} %copy-done.8), channel_id=1, source_target_pairs={{0,32},{8,40},{16,48},{24,56},{32,64},{40,72},{48,80},{56,88},{64,... | collective-permute-start | bytes 786440 | tf_op jit(solution)/shard_map/ppermute | solution.py:423
  10.0 10.7 %collective-permute-start.3 = (bf16[2,512,128]{2,1,0:T(8,128)(2,1)S(1)}, bf16[2,512,128]{2,1,0:T(8,128)(2,1)S(1)}, u32[]{:S(2)}, u32[]{:S(2)}) collective-permute-start(bf16[2,512,128]{2,1,0:T(8,128)(2,1)S(1)} %copy-done.8), channel_id=1, source_target_pairs={{0,16},{8,24},{16,0},{24,8},{32,48},{40,56},{48,32},{56,40},{64,80... | collective-permute-start | bytes 786440 | tf_op jit(solution)/shard_map/ppermute | solution.py:417
  10.6 10.0 %collective-permute-start.4 = (bf16[64,512]{1,0:T(8,128)(2,1)S(1)}, bf16[64,512]{1,0:T(8,128)(2,1)S(1)}, u32[]{:S(2)}, u32[]{:S(2)}) collective-permute-start(bf16[64,512]{1,0:T(8,128)(2,1)S(1)} %fusion.1.q_ref), channel_id=1, source_target_pairs={{0,224},{8,232},{16,240},{24,248},{32,0},{40,8},{48,16},{56,24},{6... | collective-permute-start | bytes 196616 | tf_op jit(solution)/shard_map/ppermute | solution.py:423
  15.2 5.4 %collective-permute-start.5 = (bf16[64,512]{1,0:T(8,128)(2,1)S(1)}, bf16[64,512]{1,0:T(8,128)(2,1)S(1)}, u32[]{:S(2)}, u32[]{:S(2)}) collective-permute-start(bf16[64,512]{1,0:T(8,128)(2,1)S(1)} %fusion.1.q_ref), channel_id=1, source_target_pairs={{0,192},{8,200},{16,208},{24,216},{32,224},{40,232},{48,240},{56,2... | collective-permute-start | bytes 196616 | tf_op jit(solution)/shard_map/ppermute | solution.py:423
  20.7 6.6 %collective-permute-start.8 = (bf16[736,256]{1,0:T(8,128)(2,1)S(1)}, bf16[736,256]{1,0:T(8,128)(2,1)S(1)}, u32[]{:S(2)}, u32[]{:S(2)}) collective-permute-start(bf16[736,256]{1,0:T(8,128)(2,1)S(1)} %get-tuple-element.121.refs_0_), channel_id=1, source_target_pairs={{0,8},{8,0},{16,24},{24,16},{32,40},{40,32},{48,56},{56,48},{64,72... | collective-permute-start | bytes 1130504 | tf_op jit(solution)/shard_map/ppermute | solution.py:417
  22.5 10.3 %collective-permute-start.9 = (bf16[736,256]{1,0:T(8,128)(2,1)S(1)}, bf16[736,256]{1,0:T(8,128)(2,1)S(1)}, u32[]{:S(2)}, u32[]{:S(2)}) collective-permute-start(bf16[736,256]{1,0:T(8,128)(2,1)S(1)} %get-tuple-element.121.refs_0_), channel_id=1, source_target_pairs={{0,16},{8,24},{16,0},{24,8},{32,48},{40,56},{48,32},{56,40},{64,80... | collective-permute-start | bytes 1130504 | tf_op jit(solution)/shard_map/ppermute | solution.py:417
  22.7 1.5 %collective-permute-start.7 = (bf16[2,512,128]{2,1,0:T(8,128)(2,1)S(1)}, bf16[2,512,128]{2,1,0:T(8,128)(2,1)S(1)}, u32[]{:S(2)}, u32[]{:S(2)}) collective-permute-start(bf16[2,512,128]{2,1,0:T(8,128)(2,1)S(1)} %collective-permute-done.3.refs_2_), channel_id=1, source_target_pairs={{0,8},{8,0},{16,24},{24,16},{32,40},{40,32},{48,56},{56,48},{64,72... | collective-permute-start | bytes 786440 | tf_op jit(solution)/shard_map/ppermute | solution.py:417
  34.5 22.1 %all-to-all-start = ((f16[8,64,512]{2,1,0:T(8,128)(2,1)}), f16[8,64,512]{2,1,0:T(8,128)(2,1)}, u32[]{:S(2)}, u32[]{:S(2)}) async-start(f16[8,64,512]{2,1,0:T(8,128)(2,1)} %broadcast_in_dim.4), calls=%async_computation | async-start | bytes 1048576 | tf_op jit(solution)/shard_map/all_to_all | solution.py:508
  38.6 19.1 %collective-permute-start.10 = (bf16[736,256]{1,0:T(8,128)(2,1)}, bf16[736,256]{1,0:T(8,128)(2,1)S(1)}, u32[]{:S(2)}, u32[]{:S(2)}) collective-permute-start(bf16[736,256]{1,0:T(8,128)(2,1)} %copy-done.6), channel_id=1, source_target_pairs={{0,8},{8,0},{16,24},{24,16},{32,40},{40,32},{48,56},{56,48},{64,72... | collective-permute-start | bytes 1130504 | tf_op jit(solution)/shard_map/ppermute | solution.py:417
  39.7 18.0 %collective-permute-start.11 = (bf16[2,512,128]{2,1,0:T(8,128)(2,1)}, bf16[2,512,128]{2,1,0:T(8,128)(2,1)}, u32[]{:S(2)}, u32[]{:S(2)}) collective-permute-start(bf16[2,512,128]{2,1,0:T(8,128)(2,1)} %copy-done.7), channel_id=1, source_target_pairs={{0,16},{8,24},{16,0},{24,8},{32,48},{40,56},{48,32},{56,40},{64,80... | collective-permute-start | bytes 786440 | tf_op jit(solution)/shard_map/ppermute | solution.py:417
  39.9 25.6 %collective-permute-start.13 = (bf16[256,1024]{1,0:T(8,128)(2,1)}, bf16[256,1024]{1,0:T(8,128)(2,1)}, u32[]{:S(2)}, u32[]{:S(2)}) collective-permute-start(bf16[256,1024]{1,0:T(8,128)(2,1)} %refs_4_), channel_id=1, source_target_pairs={{0,16},{8,24},{16,0},{24,8},{32,48},{40,56},{48,32},{56,40},{64,80... | collective-permute-start | bytes 1572872 | tf_op jit(solution)/shard_map/ppermute | solution.py:417
  59.7 13.7 %collective-permute-start.15 = (bf16[4,512,128]{2,1,0:T(8,128)(2,1)S(1)}, bf16[4,512,128]{2,1,0:T(8,128)(2,1)S(1)}, u32[]{:S(2)}, u32[]{:S(2)}) collective-permute-start(bf16[4,512,128]{2,1,0:T(8,128)(2,1)S(1)} %get-tuple-element.128.refs_3_), channel_id=1, source_target_pairs={{0,8},{8,0},{16,24},{24,16},{32,40},{40,32},{48,56},{56,48},{64,72... | collective-permute-start | bytes 1572872 | tf_op jit(solution)/shard_map/ppermute | solution.py:417
  60.4 17.1 %collective-permute-start.17 = (bf16[4,512,128]{2,1,0:T(8,128)(2,1)S(1)}, bf16[4,512,128]{2,1,0:T(8,128)(2,1)S(1)}, u32[]{:S(2)}, u32[]{:S(2)}) collective-permute-start(bf16[4,512,128]{2,1,0:T(8,128)(2,1)S(1)} %get-tuple-element.128.refs_3_), channel_id=1, source_target_pairs={{0,32},{8,40},{16,48},{24,56},{32,64},{40,72},{48,80},{56,88},{64,... | collective-permute-start | bytes 1572872 | tf_op jit(solution)/shard_map/ppermute | solution.py:423
  60.7 4.7 %collective-permute-start.12 = (f16[64,1024]{1,0:T(8,128)(2,1)S(1)}, f16[64,1024]{1,0:T(8,128)(2,1)S(1)}, u32[]{:S(2)}, u32[]{:S(2)}) collective-permute-start(f16[64,1024]{1,0:T(8,128)(2,1)S(1)} %multiply_convert_fusion.1), channel_id=1, source_target_pairs={{0,2},{1,3},{2,0},{3,1},{4,6},{5,7},{6,4},{7,5},{8,10},{9,11},{10,... | collective-permute-start | bytes 393224 | tf_op jit(solution)/shard_map/ppermute | solution.py:417
  62.0 17.5 %collective-permute-start.18 = (bf16[256,1024]{1,0:T(8,128)(2,1)S(1)}, bf16[256,1024]{1,0:T(8,128)(2,1)S(1)}, u32[]{:S(2)}, u32[]{:S(2)}) collective-permute-start(bf16[256,1024]{1,0:T(8,128)(2,1)S(1)} %copy-done.1), channel_id=1, source_target_pairs={{0,8},{8,0},{16,24},{24,16},{32,40},{40,32},{48,56},{56,48},{64,72... | collective-permute-start | bytes 1572872 | tf_op jit(solution)/shard_map/ppermute | solution.py:417
  65.5 13.9 %collective-permute-start.19 = (bf16[256,1024]{1,0:T(8,128)(2,1)}, bf16[256,1024]{1,0:T(8,128)(2,1)S(1)}, u32[]{:S(2)}, u32[]{:S(2)}) collective-permute-start(bf16[256,1024]{1,0:T(8,128)(2,1)} %collective-permute-done.13.refs_6_), channel_id=1, source_target_pairs={{0,8},{8,0},{16,24},{24,16},{32,40},{40,32},{48,56},{56,48},{64,72... | collective-permute-start | bytes 1572872 | tf_op jit(solution)/shard_map/ppermute | solution.py:417
  66.8 6.6 %collective-permute-start.14 = (f16[64,1024]{1,0:T(8,128)(2,1)S(1)}, f16[64,1024]{1,0:T(8,128)(2,1)S(1)}, u32[]{:S(2)}, u32[]{:S(2)}) collective-permute-start(f16[64,1024]{1,0:T(8,128)(2,1)S(1)} %add.21), channel_id=1, source_target_pairs={{0,4},{1,5},{2,6},{3,7},{4,0},{5,1},{6,2},{7,3},{8,12},{9,13},{10,... | collective-permute-start | bytes 393224 | tf_op jit(solution)/shard_map/ppermute | solution.py:417
  73.4 6.0 %collective-permute-start.16 = (f16[64,1024]{1,0:T(8,128)(2,1)S(1)}, f16[64,1024]{1,0:T(8,128)(2,1)S(1)}, u32[]{:S(2)}, u32[]{:S(2)}) collective-permute-start(f16[64,1024]{1,0:T(8,128)(2,1)S(1)} %add.22), channel_id=1, source_target_pairs={{0,1},{1,0},{2,3},{3,2},{4,5},{5,4},{6,7},{7,6},{8,9},{9,8},{10,11... | collective-permute-start | bytes 393224 | tf_op jit(solution)/shard_map/ppermute | solution.py:417
  82.3 11.8 %all-to-all-start.1 = ((f16[8,8,1024]{2,1,0:T(8,128)(2,1)}), f16[8,8,1024]{2,1,0:T(8,128)(2,1)S(1)}, u32[]{:S(2)}, u32[]{:S(2)}) async-start(f16[8,8,1024]{2,1,0:T(8,128)(2,1)} %fusion), calls=%async_computation.1 | async-start | bytes 262144 | tf_op jit(solution)/shard_map/all_to_all | solution.py:556
  86.1 9.0 %collective-permute-start.20 = (bf16[4,512,128]{2,1,0:T(8,128)(2,1)}, bf16[4,512,128]{2,1,0:T(8,128)(2,1)}, u32[]{:S(2)}, u32[]{:S(2)}) collective-permute-start(bf16[4,512,128]{2,1,0:T(8,128)(2,1)} %copy-done.10), channel_id=1, source_target_pairs={{0,8},{8,0},{16,24},{24,16},{32,40},{40,32},{48,56},{56,48},{64,72... | collective-permute-start | bytes 1572872 | tf_op jit(solution)/shard_map/ppermute | solution.py:417
  95.1 12.8 %all-to-all-start.2 = ((f32[8,1,128]{2,1,0:T(1,128)}), f32[8,1,128]{2,1,0:T(1,128)S(1)}, u32[]{:S(2)}, u32[]{:S(2)}) async-start(f32[8,1,128]{2,1,0:T(1,128)} %hidden.1), calls=%async_computation.2 | async-start | bytes 8192 | tf_op jit(solution)/shard_map/all_to_all | solution.py:568
  (11 other events, 97.6 us)

commit v9 on v8

--- a/solution.py
+++ b/solution.py
@@ -472,8 +472,9 @@
     core0y = swapped(across0, "ctx", 1)
     wanted, wanted1, wanted2, *state = tie(wanted, wanted1, wanted2, *state)
 
-    weight, *state = tie(weight, *state)
+    weight, _ = tie(weight, kv0y)
     firsts = [weight, swapped(weight, "ctx", 1), swapped(weight, "ctx", 2)]
+    wanted, firsts[2] = tie(wanted, firsts[2])
 
     parts, moved = small_call(
         picked_kernel,
@@ -499,10 +500,10 @@
         ],
         name="picked",
     )
-    parts, kv1, *firsts = tie(parts, kv1, *firsts)
+    parts, kv1, firsts[2] = tie(parts, kv1, firsts[2])
     across1 = swapped(kv1, "ctx", 2)
     weight, parts = tie(score_weight, parts)
-    firsts = [*pinned(firsts), swapped(firsts[2], "ctx", 1)]
+    firsts.append(swapped(firsts[2], "ctx", 1))
     weights = [weight, None, swapped(weight, "ctx", 2)]
     parts = jnp.broadcast_to(parts.astype(jnp.float16)[None], (Z, GROUP, half))
     parts = lax.all_to_all(parts, "ctx", 0, 0, axis_index_groups=columns).astype(F32)

time: 125 us -> 123 us (0.984)
  waiting for transfers between devices: 40 us -> 31 us
  starting transfers between devices: 42.8 us -> 48.5 us
    ppermute x17, waiting for transfers between devices: 17.5 us -> 12.2 us  [swapped(): return lax.ppermute(value, axis, [(s, s ^ bit) for s in range(count)])]
    all_to_all x1, waiting for transfers between devices: 14 us -> 10.2 us  [per_device(): lax.all_to_all(parts, 'ctx', 0, 0, axis_index_groups=columns).astype(F32)]
    ppermute x17, starting transfers between devices: 21.1 us -> 24.6 us  [swapped(): return lax.ppermute(value, axis, [(s, s ^ bit) for s in range(count)])]
    all_to_all x1, starting transfers between devices: 4.15 us -> 6.9 us  [per_device(): lax.all_to_all(parts, 'ctx', 0, 0, axis_index_groups=columns).astype(F32)]
    all_to_all x1, starting transfers between devices: 3.8 us -> 5.42 us  [per_device(): inner = lax.all_to_all(inner, 'ctx', 0, 0, axis_index_groups=columns)]
    all_to_all x1, starting transfers between devices: 6.36 us -> 4.9 us  [per_device(): gap = lax.all_to_all(gap, 'head', 0, 0)]
  transfers between devices with their start and end apart: 24 -> 24, of which waited for: 10 -> 9; matrix products, arithmetic and copies ran while one was open for 1% -> 2% of each run, Pallas kernels for 13% -> 11%
where the time goes in v9:
time: 123 us; the launch traced here: 122 us
  starting transfers between devices  48.5 us (39%)
  waiting for transfers between devices  31 us (25%)
  Pallas kernels  21.5 us (17%)
  blocking collectives  15.1 us (12%)
  local copies, waits for them, and re-layouts  2.72 us (2%)
  other arithmetic  2.13 us (2%)
    ppermute x17, starting transfers between devices, swapped(): return lax.ppermute(value, axis, [(s, s ^ bit) for s in range(count)])  24.6 us
    all_to_all x1, blocking collectives, per_device(): lax.all_to_all(jnp.broadcast_to(gap[None], (count, 1, HD)), 'ctx', 0, 0)  15.1 us
    ppermute x17, waiting for transfers between devices, swapped(): return lax.ppermute(value, axis, [(s, s ^ bit) for s in range(count)])  12.2 us
    pallas_call x6, Pallas kernels, small_call(): pl.pallas_call(kernel, out_shape=shape, in_specs=specs or [VMEM] * len(op...  11.1 us
    pallas_call x5, Pallas kernels, attend(): pl.pallas_call(functools.partial(attend_kernel, slots, first, last), out_...  10.4 us
    all_to_all x1, waiting for transfers between devices, per_device(): lax.all_to_all(parts, 'ctx', 0, 0, axis_index_groups=columns).astype(F32)  10.2 us
    all_to_all x1, starting transfers between devices, per_device(): lax.all_to_all(parts, 'ctx', 0, 0, axis_index_groups=columns).astype(F32)  6.9 us
    ppermute x4, starting transfers between devices, raised(): lax.ppermute(value, 'ctx', [(s, (s + steps) % count) for s in range(count)])  6.68 us
  transfers between devices with their start and end apart: 24, of which 9 were waited for; matrix products, arithmetic and copies ran while one was open for 2% of the time, Pallas kernels for 11%

profile of v9, /device:TPU:1, one launch (start us, length us, event | category | flops | bytes accessed | tf_op | source)
XLA Modules:
  0.0 122.0 jit_solution(6114087349274182008)
XLA Ops:
  0.6 1.8 %pick.1 = (bf16[64,512]{1,0:T(8,128)(2,1)S(1)}, bf16[64,512]{1,0:T(8,128)(2,1)S(1)}, bf16[128,512]{1,0:T(8,128)(2,1)S(1)}, bf16[736,256]{1,0:T(8,128)(2,1)S(1)}) custom-call(s32[1]{0:T(128)} %bitcast.me_ref.refs_0_, s32[7,32]{1,0:T(8,128)} %steps_hbm.3, bf16[512,512]{1,0:T(8,128)(2,1)} %refs_2_.9, bf16[512,256]{1,0:T(8,128)(2,1)} %weight_hbm.1, ...), custom_call_target="tpu_custom_call" | custom-call | tf_op jit(solution)/shard_map/pick/pallas_call | solution.py:308
  2.4 3.3 %collective-permute-start = (bf16[128,512]{1,0:T(8,128)(2,1)S(1)}, bf16[128,512]{1,0:T(8,128)(2,1)S(1)}, u32[]{:S(2)}, u32[]{:S(2)}) collective-permute-start(bf16[128,512]{1,0:T(8,128)(2,1)S(1)} %get-tuple-element.82), channel_id=1, source_target_pairs={{0,8},{8,0},{16,24},{24,16},{32,40},{40,32},{48,56},{56,48},{64,72... | collective-permute-start | bytes 393224 | tf_op jit(solution)/shard_map/ppermute | solution.py:417
  11.5 3.8 %collective-permute-start.4 = (bf16[64,512]{1,0:T(8,128)(2,1)S(1)}, bf16[64,512]{1,0:T(8,128)(2,1)S(1)}, u32[]{:S(2)}, u32[]{:S(2)}) collective-permute-start(bf16[64,512]{1,0:T(8,128)(2,1)S(1)} %fusion.1.q_ref), channel_id=1, source_target_pairs={{0,224},{8,232},{16,240},{24,248},{32,0},{40,8},{48,16},{56,24},{6... | collective-permute-start | bytes 196616 | tf_op jit(solution)/shard_map/ppermute | solution.py:423
  16.5 4.2 %attend_0_0.1 = (f32[512,512]{1,0:T(8,128)S(1)}, f32[512,512]{1,0:T(8,128)S(1)}, f32[512,512]{1,0:T(8,128)S(1)}) custom-call(s32[1]{0:T(128)} %bitcast.me_ref.refs_0_, s32[7]{0:T(128)} %refs_1_.9, bf16[512,512]{1,0:T(8,128)(2,1)} %refs_2_.9, bf16[2,512,128]{2,1,0:T(8,128)(2,1)} %refs_0_.1, bf16[2,512,128]{2,1,0:T(8,128)(2,1)S(1)} %collective-permute-done.2.refs_4_.refs_1_), custom_call_target="tpu_custom_call" | custom-call | flops 1073741824 | bytes 1048576 | tf_op jit(solution)/shard_map/attend_0_0/pallas_call | solution.py:280
  20.8 2.2 %collective-permute-start.8 = (bf16[2,512,128]{2,1,0:T(8,128)(2,1)S(1)}, bf16[2,512,128]{2,1,0:T(8,128)(2,1)S(1)}, u32[]{:S(2)}, u32[]{:S(2)}) collective-permute-start(bf16[2,512,128]{2,1,0:T(8,128)(2,1)S(1)} %collective-permute-done.3.refs_2_), channel_id=1, source_target_pairs={{0,8},{8,0},{16,24},{24,16},{32,40},{40,32},{48,56},{56,48},{64,72... | collective-permute-start | bytes 786440 | tf_op jit(solution)/shard_map/ppermute | solution.py:417
  23.0 1.4 %collective-permute-done.7.refs_2_ = bf16[736,256]{1,0:T(8,128)(2,1)S(1)} collective-permute-done((bf16[736,256]{1,0:T(8,128)(2,1)S(1)}, bf16[736,256]{1,0:T(8,128)(2,1)S(1)}, u32[]{:S(2)}, u32[]{:S(2)}) %collective-permute-start.7) | collective-permute-done | bytes 376864 | tf_op jit(solution)/shard_map/ppermute | solution.py:417
  24.4 3.1 %picked.1 = (f32[64,512]{1,0:T(8,128)S(1)}, bf16[4,512,128]{2,1,0:T(8,128)(2,1)}) custom-call(s32[1]{0:T(128)} %bitcast.me_ref.refs_0_, s32[7]{0:T(128)} %refs_1_.9, s32[7,32]{1,0:T(8,128)} %steps_hbm.3, bf16[64,512]{1,0:T(8,128)(2,1)S(1)} %fusion.1.q_ref, bf16[64,512]{1,0:T(8,128)(2,1)S(1)} %collective-permute-done.4.q1_ref, ...), custom_call_target="tpu_custom_call" | custom-call | tf_op jit(solution)/shard_map/picked/pallas_call | solution.py:308
  28.4 6.9 %all-to-all-start = ((f16[8,64,512]{2,1,0:T(8,128)(2,1)}), f16[8,64,512]{2,1,0:T(8,128)(2,1)}, u32[]{:S(2)}, u32[]{:S(2)}) async-start(f16[8,64,512]{2,1,0:T(8,128)(2,1)} %broadcast_in_dim.4), calls=%async_computation | async-start | bytes 1048576 | tf_op jit(solution)/shard_map/all_to_all | solution.py:509
  35.3 2.3 %collective-permute-start.9 = (bf16[736,256]{1,0:T(8,128)(2,1)S(1)}, bf16[736,256]{1,0:T(8,128)(2,1)}, u32[]{:S(2)}, u32[]{:S(2)}) collective-permute-start(bf16[736,256]{1,0:T(8,128)(2,1)S(1)} %get-tuple-element.97.refs_0_), channel_id=1, source_target_pairs={{0,8},{8,0},{16,24},{24,16},{32,40},{40,32},{48,56},{56,48},{64,72... | collective-permute-start | bytes 1130504 | tf_op jit(solution)/shard_map/ppermute | solution.py:417
  40.5 10.2 %all-to-all-done = f16[8,64,512]{2,1,0:T(8,128)(2,1)} async-done(((f16[8,64,512]{2,1,0:T(8,128)(2,1)}), f16[8,64,512]{2,1,0:T(8,128)(2,1)}, u32[]{:S(2)}, u32[]{:S(2)}) %all-to-all-start) | async-done | bytes 524320 | tf_op jit(solution)/shard_map/all_to_all | solution.py:509
  52.0 2.0 %project.1 = (f32[64,1024]{1,0:T(8,128)S(1)}, bf16[4,512,128]{2,1,0:T(8,128)(2,1)S(1)}) custom-call(f32[8,64,512]{2,1,0:T(8,128)S(1)} %convert_element_type.22.got_ref, bf16[736,256]{1,0:T(8,128)(2,1)S(1)} %get-tuple-element.97.refs_0_, bf16[736,256]{1,0:T(8,128)(2,1)} %collective-permute-done.9.refs_1_, bf16[736,256]{1,0:T(8,128)(2,1)S(1)} %copy-done.1, ...), custom_call_target="tpu_custom_call" | custom-call | tf_op jit(solution)/shard_map/project/pallas_call | solution.py:308
  54.0 3.3 %collective-permute-start.15 = (bf16[4,512,128]{2,1,0:T(8,128)(2,1)S(1)}, bf16[4,512,128]{2,1,0:T(8,128)(2,1)S(1)}, u32[]{:S(2)}, u32[]{:S(2)}) collective-permute-start(bf16[4,512,128]{2,1,0:T(8,128)(2,1)S(1)} %get-tuple-element.122.refs_3_), channel_id=1, source_target_pairs={{0,8},{8,0},{16,24},{24,16},{32,40},{40,32},{48,56},{56,48},{64,72... | collective-permute-start | bytes 1572872 | tf_op jit(solution)/shard_map/ppermute | solution.py:417
  59.4 2.9 %collective-permute-done.12 = f16[64,1024]{1,0:T(8,128)(2,1)S(1)} collective-permute-done((f16[64,1024]{1,0:T(8,128)(2,1)S(1)}, f16[64,1024]{1,0:T(8,128)(2,1)S(1)}, u32[]{:S(2)}, u32[]{:S(2)}) %collective-permute-start.12) | collective-permute-done | bytes 131104 | tf_op jit(solution)/shard_map/ppermute | solution.py:417
  63.6 2.8 %collective-permute-start.14 = (f16[64,1024]{1,0:T(8,128)(2,1)S(1)}, f16[64,1024]{1,0:T(8,128)(2,1)S(1)}, u32[]{:S(2)}, u32[]{:S(2)}) collective-permute-start(f16[64,1024]{1,0:T(8,128)(2,1)S(1)} %add.21), channel_id=1, source_target_pairs={{0,4},{1,5},{2,6},{3,7},{4,0},{5,1},{6,2},{7,3},{8,12},{9,13},{10,... | collective-permute-start | bytes 393224 | tf_op jit(solution)/shard_map/ppermute | solution.py:417
  66.4 3.8 %collective-permute-done.14 = f16[64,1024]{1,0:T(8,128)(2,1)S(1)} collective-permute-done((f16[64,1024]{1,0:T(8,128)(2,1)S(1)}, f16[64,1024]{1,0:T(8,128)(2,1)S(1)}, u32[]{:S(2)}, u32[]{:S(2)}) %collective-permute-start.14) | collective-permute-done | bytes 131104 | tf_op jit(solution)/shard_map/ppermute | solution.py:417
  70.3 2.9 %collective-permute-start.16 = (f16[64,1024]{1,0:T(8,128)(2,1)S(1)}, f16[64,1024]{1,0:T(8,128)(2,1)S(1)}, u32[]{:S(2)}, u32[]{:S(2)}) collective-permute-start(f16[64,1024]{1,0:T(8,128)(2,1)S(1)} %add.22), channel_id=1, source_target_pairs={{0,1},{1,0},{2,3},{3,2},{4,5},{5,4},{6,7},{7,6},{8,9},{9,8},{10,11... | collective-permute-start | bytes 393224 | tf_op jit(solution)/shard_map/ppermute | solution.py:417
  74.4 1.8 %collective-permute-done.16 = f16[64,1024]{1,0:T(8,128)(2,1)S(1)} collective-permute-done((f16[64,1024]{1,0:T(8,128)(2,1)S(1)}, f16[64,1024]{1,0:T(8,128)(2,1)S(1)}, u32[]{:S(2)}, u32[]{:S(2)}) %collective-permute-start.16) | collective-permute-done | bytes 131104 | tf_op jit(solution)/shard_map/ppermute | solution.py:417
  76.3 2.1 %inner.1 = f32[64,1024]{1,0:T(8,128)S(1)} custom-call(s32[1]{0:T(128)} %bitcast.me_ref.refs_0_, f32[64,1024]{1,0:T(8,128)S(1)} %add_multiply_fusion.total_ref, bf16[736,256]{1,0:T(8,128)(2,1)S(1)} %get-tuple-element.97.refs_0_, bf16[736,256]{1,0:T(8,128)(2,1)} %collective-permute-done.9.refs_1_, bf16[736,256]{1,0:T(8,128)(2,1)S(1)} %copy-done.1, ...), custom_call_target="tpu_custom_call" | custom-call | tf_op jit(solution)/shard_map/inner/pallas_call | solution.py:308
  79.0 5.4 %all-to-all-start.1 = ((f16[8,8,1024]{2,1,0:T(8,128)(2,1)}), f16[8,8,1024]{2,1,0:T(8,128)(2,1)S(1)}, u32[]{:S(2)}, u32[]{:S(2)}) async-start(f16[8,8,1024]{2,1,0:T(8,128)(2,1)} %fusion), calls=%async_computation.1 | async-start | bytes 262144 | tf_op jit(solution)/shard_map/all_to_all | solution.py:557
  87.8 4.5 %all-to-all-done.1 = f16[8,8,1024]{2,1,0:T(8,128)(2,1)S(1)} async-done(((f16[8,8,1024]{2,1,0:T(8,128)(2,1)}), f16[8,8,1024]{2,1,0:T(8,128)(2,1)S(1)}, u32[]{:S(2)}, u32[]{:S(2)}) %all-to-all-start.1) | async-done | bytes 131104 | tf_op jit(solution)/shard_map/all_to_all | solution.py:557
  94.2 4.9 %all-to-all-start.2 = ((f32[8,1,128]{2,1,0:T(1,128)}), f32[8,1,128]{2,1,0:T(1,128)S(1)}, u32[]{:S(2)}, u32[]{:S(2)}) async-start(f32[8,1,128]{2,1,0:T(1,128)} %hidden.1), calls=%async_computation.2 | async-start | bytes 8192 | tf_op jit(solution)/shard_map/all_to_all | solution.py:569
  99.1 2.4 %attend_2_1.1 = f32[512,512]{1,0:T(8,128)} custom-call(s32[1]{0:T(128)} %bitcast.me_ref.refs_0_, s32[7]{0:T(128)} %refs_1_.9, bf16[512,512]{1,0:T(8,128)(2,1)} %refs_2_.9, bf16[4,512,128]{2,1,0:T(8,128)(2,1)} %collective-permute-done.20.refs_3_, f32[512,512]{1,0:T(8,128)S(1)} %get-tuple-element.152.refs_4_, f32[512,512]{1,0:T(8,128)S(1)} %get-tuple-element.153.refs_5_, ...), custom_call_target="tpu_custom_call" | custom-call | flops 1073741824 | bytes 1048576 | tf_op jit(solution)/shard_map/attend_2_1/pallas_call | solution.py:280
  101.5 4.1 %all-to-all-done.2 = f32[8,1,128]{2,1,0:T(1,128)S(1)} async-done(((f32[8,1,128]{2,1,0:T(1,128)}), f32[8,1,128]{2,1,0:T(1,128)S(1)}, u32[]{:S(2)}, u32[]{:S(2)}) %all-to-all-start.2) | async-done | bytes 4128 | tf_op jit(solution)/shard_map/all_to_all | solution.py:569
  105.6 15.1 %all_to_all.20.got_ref = f32[32,1,128]{2,1,0:T(1,128)S(1)} all-to-all(f32[32,1,128]{2,1,0:T(1,128)S(1)} %broadcast_in_dim.5), channel_id=1, replica_groups=mesh['ctx'=32,'head'=8] {'ctx'}, dimensions={0} | all-to-all | bytes 32768 | tf_op jit(solution)/shard_map/all_to_all | solution.py:572
  (73 shorter events, 23.9 us)
Async XLA Ops:
  2.4 4.3 %collective-permute-start = (bf16[128,512]{1,0:T(8,128)(2,1)S(1)}, bf16[128,512]{1,0:T(8,128)(2,1)S(1)}, u32[]{:S(2)}, u32[]{:S(2)}) collective-permute-start(bf16[128,512]{1,0:T(8,128)(2,1)S(1)} %get-tuple-element.82), channel_id=1, source_target_pairs={{0,8},{8,0},{16,24},{24,16},{32,40},{40,32},{48,56},{56,48},{64,72... | collective-permute-start | bytes 393224 | tf_op jit(solution)/shard_map/ppermute | solution.py:417
  6.7 3.2 %collective-permute-start.1 = (bf16[64,512]{1,0:T(8,128)(2,1)S(1)}, bf16[64,512]{1,0:T(8,128)(2,1)S(1)}, u32[]{:S(2)}, u32[]{:S(2)}) collective-permute-start(bf16[64,512]{1,0:T(8,128)(2,1)S(1)} %slice_add_fusion), channel_id=1, source_target_pairs={{0,16},{8,24},{16,0},{24,8},{32,48},{40,56},{48,32},{56,40},{64,80... | collective-permute-start | bytes 196616 | tf_op jit(solution)/shard_map/ppermute | solution.py:417
  6.8 3.1 %collective-permute-start.2 = (bf16[2,512,128]{2,1,0:T(8,128)(2,1)S(1)}, bf16[2,512,128]{2,1,0:T(8,128)(2,1)S(1)}, u32[]{:S(2)}, u32[]{:S(2)}) collective-permute-start(bf16[2,512,128]{2,1,0:T(8,128)(2,1)S(1)} %copy-done.8), channel_id=1, source_target_pairs={{0,8},{8,0},{16,24},{24,16},{32,40},{40,32},{48,56},{56,48},{64,72... | collective-permute-start | bytes 786440 | tf_op jit(solution)/shard_map/ppermute | solution.py:417
  7.3 13.5 %collective-permute-start.6 = (bf16[2,512,128]{2,1,0:T(8,128)(2,1)S(1)}, bf16[2,512,128]{2,1,0:T(8,128)(2,1)S(1)}, u32[]{:S(2)}, u32[]{:S(2)}) collective-permute-start(bf16[2,512,128]{2,1,0:T(8,128)(2,1)S(1)} %copy-done.8), channel_id=1, source_target_pairs={{0,32},{8,40},{16,48},{24,56},{32,64},{40,72},{48,80},{56,88},{64,... | collective-permute-start | bytes 786440 | tf_op jit(solution)/shard_map/ppermute | solution.py:423
  10.0 10.8 %collective-permute-start.3 = (bf16[2,512,128]{2,1,0:T(8,128)(2,1)S(1)}, bf16[2,512,128]{2,1,0:T(8,128)(2,1)S(1)}, u32[]{:S(2)}, u32[]{:S(2)}) collective-permute-start(bf16[2,512,128]{2,1,0:T(8,128)(2,1)S(1)} %copy-done.8), channel_id=1, source_target_pairs={{0,16},{8,24},{16,0},{24,8},{32,48},{40,56},{48,32},{56,40},{64,80... | collective-permute-start | bytes 786440 | tf_op jit(solution)/shard_map/ppermute | solution.py:417
  10.6 13.8 %collective-permute-start.7 = (bf16[736,256]{1,0:T(8,128)(2,1)S(1)}, bf16[736,256]{1,0:T(8,128)(2,1)S(1)}, u32[]{:S(2)}, u32[]{:S(2)}) collective-permute-start(bf16[736,256]{1,0:T(8,128)(2,1)S(1)} %get-tuple-element.97.refs_0_), channel_id=1, source_target_pairs={{0,16},{8,24},{16,0},{24,8},{32,48},{40,56},{48,32},{56,40},{64,80... | collective-permute-start | bytes 1130504 | tf_op jit(solution)/shard_map/ppermute | solution.py:417
  11.5 9.3 %collective-permute-start.4 = (bf16[64,512]{1,0:T(8,128)(2,1)S(1)}, bf16[64,512]{1,0:T(8,128)(2,1)S(1)}, u32[]{:S(2)}, u32[]{:S(2)}) collective-permute-start(bf16[64,512]{1,0:T(8,128)(2,1)S(1)} %fusion.1.q_ref), channel_id=1, source_target_pairs={{0,224},{8,232},{16,240},{24,248},{32,0},{40,8},{48,16},{56,24},{6... | collective-permute-start | bytes 196616 | tf_op jit(solution)/shard_map/ppermute | solution.py:423
  15.4 5.4 %collective-permute-start.5 = (bf16[64,512]{1,0:T(8,128)(2,1)S(1)}, bf16[64,512]{1,0:T(8,128)(2,1)S(1)}, u32[]{:S(2)}, u32[]{:S(2)}) collective-permute-start(bf16[64,512]{1,0:T(8,128)(2,1)S(1)} %fusion.1.q_ref), channel_id=1, source_target_pairs={{0,192},{8,200},{16,208},{24,216},{32,224},{40,232},{48,240},{56,2... | collective-permute-start | bytes 196616 | tf_op jit(solution)/shard_map/ppermute | solution.py:423
  20.8 3.6 %collective-permute-start.8 = (bf16[2,512,128]{2,1,0:T(8,128)(2,1)S(1)}, bf16[2,512,128]{2,1,0:T(8,128)(2,1)S(1)}, u32[]{:S(2)}, u32[]{:S(2)}) collective-permute-start(bf16[2,512,128]{2,1,0:T(8,128)(2,1)S(1)} %collective-permute-done.3.refs_2_), channel_id=1, source_target_pairs={{0,8},{8,0},{16,24},{24,16},{32,40},{40,32},{48,56},{56,48},{64,72... | collective-permute-start | bytes 786440 | tf_op jit(solution)/shard_map/ppermute | solution.py:417
  28.4 22.3 %all-to-all-start = ((f16[8,64,512]{2,1,0:T(8,128)(2,1)}), f16[8,64,512]{2,1,0:T(8,128)(2,1)}, u32[]{:S(2)}, u32[]{:S(2)}) async-start(f16[8,64,512]{2,1,0:T(8,128)(2,1)} %broadcast_in_dim.4), calls=%async_computation | async-start | bytes 1048576 | tf_op jit(solution)/shard_map/all_to_all | solution.py:509
  35.3 16.6 %collective-permute-start.9 = (bf16[736,256]{1,0:T(8,128)(2,1)S(1)}, bf16[736,256]{1,0:T(8,128)(2,1)}, u32[]{:S(2)}, u32[]{:S(2)}) collective-permute-start(bf16[736,256]{1,0:T(8,128)(2,1)S(1)} %get-tuple-element.97.refs_0_), channel_id=1, source_target_pairs={{0,8},{8,0},{16,24},{24,16},{32,40},{40,32},{48,56},{56,48},{64,72... | collective-permute-start | bytes 1130504 | tf_op jit(solution)/shard_map/ppermute | solution.py:417
  37.6 14.4 %collective-permute-start.10 = (bf16[736,256]{1,0:T(8,128)(2,1)}, bf16[736,256]{1,0:T(8,128)(2,1)}, u32[]{:S(2)}, u32[]{:S(2)}) collective-permute-start(bf16[736,256]{1,0:T(8,128)(2,1)} %copy-done), channel_id=1, source_target_pairs={{0,8},{8,0},{16,24},{24,16},{32,40},{40,32},{48,56},{56,48},{64,72... | collective-permute-start | bytes 1130504 | tf_op jit(solution)/shard_map/ppermute | solution.py:417
  37.7 14.3 %collective-permute-start.11 = (bf16[2,512,128]{2,1,0:T(8,128)(2,1)}, bf16[2,512,128]{2,1,0:T(8,128)(2,1)}, u32[]{:S(2)}, u32[]{:S(2)}) collective-permute-start(bf16[2,512,128]{2,1,0:T(8,128)(2,1)} %copy-done.7), channel_id=1, source_target_pairs={{0,16},{8,24},{16,0},{24,8},{32,48},{40,56},{48,32},{56,40},{64,80... | collective-permute-start | bytes 786440 | tf_op jit(solution)/shard_map/ppermute | solution.py:417
  39.0 23.4 %collective-permute-start.13 = (bf16[256,1024]{1,0:T(8,128)(2,1)}, bf16[256,1024]{1,0:T(8,128)(2,1)}, u32[]{:S(2)}, u32[]{:S(2)}) collective-permute-start(bf16[256,1024]{1,0:T(8,128)(2,1)} %refs_4_), channel_id=1, source_target_pairs={{0,16},{8,24},{16,0},{24,8},{32,48},{40,56},{48,32},{56,40},{64,80... | collective-permute-start | bytes 1572872 | tf_op jit(solution)/shard_map/ppermute | solution.py:417
  54.0 16.2 %collective-permute-start.15 = (bf16[4,512,128]{2,1,0:T(8,128)(2,1)S(1)}, bf16[4,512,128]{2,1,0:T(8,128)(2,1)S(1)}, u32[]{:S(2)}, u32[]{:S(2)}) collective-permute-start(bf16[4,512,128]{2,1,0:T(8,128)(2,1)S(1)} %get-tuple-element.122.refs_3_), channel_id=1, source_target_pairs={{0,8},{8,0},{16,24},{24,16},{32,40},{40,32},{48,56},{56,48},{64,72... | collective-permute-start | bytes 1572872 | tf_op jit(solution)/shard_map/ppermute | solution.py:417
  57.3 17.1 %collective-permute-start.17 = (bf16[4,512,128]{2,1,0:T(8,128)(2,1)S(1)}, bf16[4,512,128]{2,1,0:T(8,128)(2,1)S(1)}, u32[]{:S(2)}, u32[]{:S(2)}) collective-permute-start(bf16[4,512,128]{2,1,0:T(8,128)(2,1)S(1)} %get-tuple-element.122.refs_3_), channel_id=1, source_target_pairs={{0,32},{8,40},{16,48},{24,56},{32,64},{40,72},{48,80},{56,88},{64,... | collective-permute-start | bytes 1572872 | tf_op jit(solution)/shard_map/ppermute | solution.py:423
  57.6 4.7 %collective-permute-start.12 = (f16[64,1024]{1,0:T(8,128)(2,1)S(1)}, f16[64,1024]{1,0:T(8,128)(2,1)S(1)}, u32[]{:S(2)}, u32[]{:S(2)}) collective-permute-start(f16[64,1024]{1,0:T(8,128)(2,1)S(1)} %multiply_convert_fusion.1), channel_id=1, source_target_pairs={{0,2},{1,3},{2,0},{3,1},{4,6},{5,7},{6,4},{7,5},{8,10},{9,11},{10,... | collective-permute-start | bytes 393224 | tf_op jit(solution)/shard_map/ppermute | solution.py:417
  58.8 17.5 %collective-permute-start.18 = (bf16[256,1024]{1,0:T(8,128)(2,1)S(1)}, bf16[256,1024]{1,0:T(8,128)(2,1)S(1)}, u32[]{:S(2)}, u32[]{:S(2)}) collective-permute-start(bf16[256,1024]{1,0:T(8,128)(2,1)S(1)} %copy-done.3), channel_id=1, source_target_pairs={{0,8},{8,0},{16,24},{24,16},{32,40},{40,32},{48,56},{56,48},{64,72... | collective-permute-start | bytes 1572872 | tf_op jit(solution)/shard_map/ppermute | solution.py:417
  62.4 13.9 %collective-permute-start.19 = (bf16[256,1024]{1,0:T(8,128)(2,1)}, bf16[256,1024]{1,0:T(8,128)(2,1)S(1)}, u32[]{:S(2)}, u32[]{:S(2)}) collective-permute-start(bf16[256,1024]{1,0:T(8,128)(2,1)} %collective-permute-done.13.refs_6_), channel_id=1, source_target_pairs={{0,8},{8,0},{16,24},{24,16},{32,40},{40,32},{48,56},{56,48},{64,72... | collective-permute-start | bytes 1572872 | tf_op jit(solution)/shard_map/ppermute | solution.py:417
  63.6 6.6 %collective-permute-start.14 = (f16[64,1024]{1,0:T(8,128)(2,1)S(1)}, f16[64,1024]{1,0:T(8,128)(2,1)S(1)}, u32[]{:S(2)}, u32[]{:S(2)}) collective-permute-start(f16[64,1024]{1,0:T(8,128)(2,1)S(1)} %add.21), channel_id=1, source_target_pairs={{0,4},{1,5},{2,6},{3,7},{4,0},{5,1},{6,2},{7,3},{8,12},{9,13},{10,... | collective-permute-start | bytes 393224 | tf_op jit(solution)/shard_map/ppermute | solution.py:417
  70.3 6.0 %collective-permute-start.16 = (f16[64,1024]{1,0:T(8,128)(2,1)S(1)}, f16[64,1024]{1,0:T(8,128)(2,1)S(1)}, u32[]{:S(2)}, u32[]{:S(2)}) collective-permute-start(f16[64,1024]{1,0:T(8,128)(2,1)S(1)} %add.22), channel_id=1, source_target_pairs={{0,1},{1,0},{2,3},{3,2},{4,5},{5,4},{6,7},{7,6},{8,9},{9,8},{10,11... | collective-permute-start | bytes 393224 | tf_op jit(solution)/shard_map/ppermute | solution.py:417
  79.0 13.3 %all-to-all-start.1 = ((f16[8,8,1024]{2,1,0:T(8,128)(2,1)}), f16[8,8,1024]{2,1,0:T(8,128)(2,1)S(1)}, u32[]{:S(2)}, u32[]{:S(2)}) async-start(f16[8,8,1024]{2,1,0:T(8,128)(2,1)} %fusion), calls=%async_computation.1 | async-start | bytes 262144 | tf_op jit(solution)/shard_map/all_to_all | solution.py:557
  84.5 9.7 %collective-permute-start.20 = (bf16[4,512,128]{2,1,0:T(8,128)(2,1)}, bf16[4,512,128]{2,1,0:T(8,128)(2,1)}, u32[]{:S(2)}, u32[]{:S(2)}) collective-permute-start(bf16[4,512,128]{2,1,0:T(8,128)(2,1)} %copy-done.10), channel_id=1, source_target_pairs={{0,8},{8,0},{16,24},{24,16},{32,40},{40,32},{48,56},{56,48},{64,72... | collective-permute-start | bytes 1572872 | tf_op jit(solution)/shard_map/ppermute | solution.py:417
  94.2 11.3 %all-to-all-start.2 = ((f32[8,1,128]{2,1,0:T(1,128)}), f32[8,1,128]{2,1,0:T(1,128)S(1)}, u32[]{:S(2)}, u32[]{:S(2)}) async-start(f32[8,1,128]{2,1,0:T(1,128)} %hidden.1), calls=%async_computation.2 | async-start | bytes 8192 | tf_op jit(solution)/shard_map/all_to_all | solution.py:569
  (11 other events, 82.3 us)
